TPU v7x, 32 devices: a whole 2x2x4 slice. The times are simulated.
32 devices in a mesh: rep: 4 (over x, core), fsdp: 8 (over z, y).
Axes of the slice: x: 2, y: 2, z: 4, core: 2. Of those that a mesh axis runs over, the one named last changes fastest.
Arguments:
- tokens: bfloat16 [4096, 2048], P(('rep', 'fsdp')), may hold values from -6 to 6
- w_query: bfloat16 [2048, 2048], P('fsdp'), may hold values from -0.125 to 0.125
- w_key: bfloat16 [2048, 2048], P('fsdp'), may hold values from -0.125 to 0.125
- w_value: bfloat16 [2048, 4096], P('fsdp'), may hold values from -0.125 to 0.125
- w_gate: bfloat16 [2048, 4096], P('fsdp'), may hold values from -0.125 to 0.125
- w_out: bfloat16 [4096, 2048], P('fsdp'), may hold values from -0.09375 to 0.09375
- norm1_gain: bfloat16 [2048], P('fsdp'), may hold values from 0.5 to 1.5
- norm1_bias: bfloat16 [2048], P('fsdp'), may hold values from -3 to 3
- w_ffn_gate: bfloat16 [2048, 4096], P('fsdp'), may hold values from -0.125 to 0.125
- w_ffn_up: bfloat16 [2048, 4096], P('fsdp'), may hold values from -0.125 to 0.125
- w_ffn_down: bfloat16 [4096, 2048], P('fsdp'), may hold values from -0.09375 to 0.09375
- norm2_gain: bfloat16 [2048], P('fsdp'), may hold values from 0.5 to 1.5
- norm2_bias: bfloat16 [2048], P('fsdp'), may hold values from -3 to 3
- cotangent: bfloat16 [4096, 2048], P(('rep', 'fsdp')), may hold values from -6 to 6
Outputs:
- output: bfloat16 [4096, 2048], P(('rep', 'fsdp'))
- grad_tokens: float32 [4096, 2048], P(('rep', 'fsdp'))
- grad_w_query: float32 [2048, 2048], P('fsdp')
- grad_w_key: float32 [2048, 2048], P('fsdp')
- grad_w_value: float32 [2048, 4096], P('fsdp')
- grad_w_gate: float32 [2048, 4096], P('fsdp')
- grad_w_out: float32 [4096, 2048], P('fsdp')
- grad_norm1_gain: float32 [2048], P('fsdp')
- grad_norm1_bias: float32 [2048], P('fsdp')
- grad_w_ffn_gate: float32 [2048, 4096], P('fsdp')
- grad_w_ffn_up: float32 [2048, 4096], P('fsdp')
- grad_w_ffn_down: float32 [4096, 2048], P('fsdp')
- grad_norm2_gain: float32 [2048], P('fsdp')
- grad_norm2_bias: float32 [2048], P('fsdp')
All inputs are finite; a program needn't handle non-finite values.
Results may differ from a plain program's by a relative error of at most 0.02.
Values may be sent and summed in bfloat16 or wider, within the bound.
No kernel may reach another device: no remote copies, remote signals or barrier semaphores. Data moves between devices by JAX's collectives and lax.ppermute only.
A program may use at most 576 MiB of HBM per device.

v0:
```python
import math

import jax
import jax.numpy as jnp
from jax import lax
from jax.sharding import PartitionSpec as P

D = 2048
HEADS = 8
FF = 4096
DK = 256
VD = 4096
DV = 512


epsilon = 1e-05
head_epsilon = 1.0
highest = lax.Precision.HIGHEST


def prefix(value, axis, combine, identity):
    devices, position = (lax.axis_size(axis), lax.axis_index(axis))
    everything = jax.tree.map(lambda part: lax.all_gather(part, axis), value)
    start = jax.tree.map(
        lambda part, zero: jnp.broadcast_to(jnp.asarray(zero, part.dtype), part.shape),
        value,
        identity,
    )

    def turn(k, before):
        reached = k < position
        new = combine(before, jax.tree.map(lambda part: part[k], everything))
        return jax.tree.map(lambda a, b: jnp.where(reached, a, b), new, before)

    return lax.fori_loop(0, devices, turn, start)


def prefix_2(value, axis, join, neutral):
    count = lax.axis_size(axis)
    place = lax.axis_index(axis)
    ahead = count - 1 - place
    gathered = jax.tree.map(
        lambda a, kind: lax.all_gather(a.astype(kind), axis),
        value,
        jax.tree.map(lambda a: jnp.bfloat16 if a.dtype == jnp.float32 else a.dtype, value),
    )
    state = jax.tree.map(lambda a, e: jnp.zeros_like(a) + jnp.asarray(e, a.dtype), value, neutral)

    def one(turn, state):
        source = count - 1 - turn
        return join(
            state,
            jax.tree.map(
                lambda a, own: lax.dynamic_index_in_dim(a, source, 0, False).astype(own.dtype),
                gathered,
                value,
            ),
        )

    return lax.fori_loop(0, ahead, one, state)


def normalize(values):
    center = values - jnp.mean(values, axis=-1, keepdims=True)
    spread = jnp.mean(center * center, axis=-1, keepdims=True)
    return center * lax.rsqrt(spread + epsilon)


def head_norm(values):
    center = values - jnp.mean(values, axis=-1, keepdims=True)
    spread = jnp.mean(center * center, axis=-1, keepdims=True)
    return center * lax.rsqrt(spread + head_epsilon)


def layer_norm(values, gain, shift):
    return normalize(values) * gain + shift


def rotate(tensor, positions):
    half = tensor.shape[-1] // 2
    freqs = jnp.exp(-jnp.arange(half, dtype=jnp.float32) * (math.log(10000.0) / half))
    angles = positions[:, None] * freqs[None, :]
    cosine = jnp.cos(angles)[:, None, :]
    sine = jnp.sin(angles)[:, None, :]
    first = tensor[..., :half]
    second = tensor[..., half:]
    return jnp.concatenate(
        [first * cosine - second * sine, second * cosine + first * sine], axis=-1
    )


def decay_tables(heads, length):
    logs = jnp.log(1.0 - 2.0 ** (-5.0 - jnp.arange(heads, dtype=jnp.float32)))
    index = jnp.arange(length, dtype=jnp.float32)
    differ = index[:, None] - index[None, :]
    mask = jnp.where(
        differ[None] >= 0, jnp.exp(jnp.maximum(differ, 0.0)[None] * logs[:, None, None]), 0.0
    )
    query_decay = jnp.exp((index[None, :] + 1.0) * logs[:, None])
    key_decay = jnp.exp((length - 1.0 - index[None, :]) * logs[:, None])
    block_decay = jnp.exp(length * logs)
    return (mask, query_decay, key_decay, block_decay)


def contract_last(left, right):
    return lax.dot_general(
        left, right, (((1,), (1,)), ((), ())), preferred_element_type=jnp.float32
    )


def contract_first(left, right):
    return lax.dot_general(
        left, right, (((0,), (0,)), ((), ())), preferred_element_type=jnp.float32
    )


def chain(earlier, later):
    return (earlier[0] * later[0], later[0][:, None, None] * earlier[1] + later[1])


def on_device(
    tokens,
    w_query,
    w_key,
    w_value,
    w_gate,
    w_out,
    norm1_gain,
    norm1_bias,
    w_ffn_gate,
    w_ffn_up,
    w_ffn_down,
    norm2_gain,
    norm2_bias,
    cotangent,
):
    row_total = tokens.shape[0]
    inputs = tokens.astype(jnp.float32)
    normed_first = normalize(inputs)
    piece_query = lax.all_gather(w_query, "fsdp", axis=0, tiled=True)
    piece_key = lax.all_gather(w_key, "fsdp", axis=0, tiled=True)
    piece_value = lax.all_gather(w_value, "fsdp", axis=0, tiled=True)
    piece_gate = lax.all_gather(w_gate, "fsdp", axis=0, tiled=True)
    piece_gain = lax.all_gather(norm1_gain, "fsdp", axis=0, tiled=True)
    piece_bias = lax.all_gather(norm1_bias, "fsdp", axis=0, tiled=True)
    normed_part = normed_first
    z_part = (normed_part * piece_gain.astype(jnp.float32) + piece_bias.astype(jnp.float32)).astype(
        jnp.bfloat16
    )
    updated = (
        jnp.dot(z_part, piece_query, preferred_element_type=jnp.float32),
        jnp.dot(z_part, piece_key, preferred_element_type=jnp.float32),
        jnp.dot(z_part, piece_value, preferred_element_type=jnp.float32),
        jnp.dot(z_part, piece_gate, preferred_element_type=jnp.float32),
        z_part,
        piece_gain,
        piece_bias,
    )
    mixer_out = updated
    query_pre, key_pre, value_pre, gate_pre, z_first, gain_first, bias_first = mixer_out[:7]
    positions = (
        lax.axis_index("fsdp") * row_total + jnp.arange(row_total, dtype=jnp.int32)
    ).astype(jnp.float32)
    key_scale = DK ** (-0.5)
    query_heads = query_pre.reshape(row_total, HEADS, DK)
    query_low = rotate(query_heads, positions).astype(jnp.bfloat16)
    key_low = (rotate(key_pre.reshape(row_total, HEADS, DK), positions) * key_scale).astype(
        jnp.bfloat16
    )
    value_low = value_pre.astype(jnp.bfloat16)
    query_full = query_low.astype(jnp.float32)
    key_full = key_low.astype(jnp.float32)
    value_full = value_low.astype(jnp.float32).reshape(row_total, HEADS, DV)
    mask, query_decay, key_decay, block_decay = decay_tables(HEADS, row_total)
    scores = (
        jnp.einsum("ihd,jhd->hij", query_low, key_low, preferred_element_type=jnp.float32) * mask
    )
    intra = jnp.einsum("hij,jhe->ihe", scores, value_full, precision=highest)
    key_weighted = key_full * key_decay.T[:, :, None]
    local_state = jnp.einsum("jhd,jhe->hde", key_weighted, value_full, precision=highest)
    identity = (jnp.ones((HEADS,), jnp.float32), jnp.zeros_like(local_state))
    prior = prefix((block_decay, local_state), "fsdp", chain, identity)
    state_in = prior[1]
    query_weighted = query_full * query_decay.T[:, :, None]
    retained = intra + jnp.einsum("ihd,hde->ihe", query_weighted, state_in, precision=highest)

    def mix_values(retained_in, gate_in):
        return head_norm(retained_in).reshape(row_total, VD) * jax.nn.silu(gate_in)

    mixed, mix_pull = jax.vjp(mix_values, retained, gate_pre)
    mixed_low = mixed.astype(jnp.bfloat16)
    mixed_part = mixed_low
    updated = (
        jnp.dot(
            mixed_part,
            lax.all_gather(w_out, "fsdp", axis=0, tiled=True),
            preferred_element_type=jnp.float32,
        ),
    )
    output_fold = updated
    resid = inputs + output_fold[0]
    normed_second = normalize(resid)
    piece_gate = lax.all_gather(w_ffn_gate, "fsdp", axis=0, tiled=True)
    piece_up = lax.all_gather(w_ffn_up, "fsdp", axis=0, tiled=True)
    piece_gain = lax.all_gather(norm2_gain, "fsdp", axis=0, tiled=True)
    piece_bias = lax.all_gather(norm2_bias, "fsdp", axis=0, tiled=True)
    normed_part = normed_second
    z_part = (normed_part * piece_gain.astype(jnp.float32) + piece_bias.astype(jnp.float32)).astype(
        jnp.bfloat16
    )
    updated = (
        jnp.dot(z_part, piece_gate, preferred_element_type=jnp.float32),
        jnp.dot(z_part, piece_up, preferred_element_type=jnp.float32),
        z_part,
        piece_gain,
        piece_bias,
    )
    expand_out = updated
    gate_ffn, up_ffn, z_second, gain_second, bias_second = expand_out[:5]

    def gated_unit(gate_in, up_in):
        return jax.nn.gelu(gate_in, approximate=False) * up_in

    hidden, gated_pull = jax.vjp(gated_unit, gate_ffn, up_ffn)
    hidden_low = hidden.astype(jnp.bfloat16)
    hidden_part = hidden_low
    updated = (
        jnp.dot(
            hidden_part,
            lax.all_gather(w_ffn_down, "fsdp", axis=0, tiled=True),
            preferred_element_type=jnp.float32,
        ),
    )
    result = resid + updated[0]
    output = result.astype(jnp.bfloat16)
    grad_result = cotangent.astype(jnp.float32)
    grad_hidden = contract_last(cotangent, lax.all_gather(w_ffn_down, "fsdp", axis=0, tiled=True))
    grad_gate_ffn, grad_up_ffn = gated_pull(grad_hidden.astype(jnp.bfloat16).astype(jnp.float32))
    gate_ffn_low = grad_gate_ffn.astype(jnp.bfloat16)
    up_ffn_low = grad_up_ffn.astype(jnp.bfloat16)
    pieces = (
        lax.all_gather(w_ffn_gate, "fsdp", axis=0, tiled=True),
        lax.all_gather(w_ffn_up, "fsdp", axis=0, tiled=True),
    )
    update = contract_last(gate_ffn_low, pieces[0]) + contract_last(up_ffn_low, pieces[1])
    grad_z_second = update
    _, second_pull = jax.vjp(
        layer_norm, resid, gain_second.astype(jnp.float32), bias_second.astype(jnp.float32)
    )
    grad_resid_norm, grad_gain_second, grad_bias_second = second_pull(grad_z_second)
    grad_resid = grad_result + grad_resid_norm
    grad_branch = grad_resid.astype(jnp.bfloat16)
    grad_mixed = contract_last(grad_branch, lax.all_gather(w_out, "fsdp", axis=0, tiled=True))
    grad_retained, grad_gate = mix_pull(grad_mixed.astype(jnp.bfloat16).astype(jnp.float32))
    gate_grad_low = grad_gate.astype(jnp.bfloat16)
    grad_scores = jnp.einsum("ihe,jhe->hij", grad_retained, value_full, precision=highest) * mask
    grad_query = jnp.einsum("hij,jhd->ihd", grad_scores, key_full, precision=highest)
    grad_query = (
        grad_query
        + jnp.einsum("ihe,hde->ihd", grad_retained, state_in, precision=highest)
        * query_decay.T[:, :, None]
    )
    grad_key = jnp.einsum("hij,ihd->jhd", grad_scores, query_full, precision=highest)
    grad_value = jnp.einsum("hij,ihe->jhe", scores, grad_retained, precision=highest)
    grad_state_in = jnp.einsum("ihd,ihe->hde", query_weighted, grad_retained, precision=highest)
    later = prefix_2((block_decay, grad_state_in), "fsdp", chain, identity)
    grad_local = later[1]
    grad_key = (
        grad_key
        + jnp.einsum("jhe,hde->jhd", value_full, grad_local, precision=highest)
        * key_decay.T[:, :, None]
    )
    grad_value = grad_value + jnp.einsum(
        "jhd,hde->jhe", key_weighted, grad_local, precision=highest
    )
    _, rotate_pull = jax.vjp(lambda tensor: rotate(tensor, positions), query_heads)
    query_grad_low = rotate_pull(grad_query)[0].reshape(row_total, D).astype(jnp.bfloat16)
    key_grad_low = rotate_pull(grad_key * key_scale)[0].reshape(row_total, D).astype(jnp.bfloat16)
    value_grad_low = grad_value.reshape(row_total, VD).astype(jnp.bfloat16)
    pieces = (
        lax.all_gather(w_query, "fsdp", axis=0, tiled=True),
        lax.all_gather(w_key, "fsdp", axis=0, tiled=True),
        lax.all_gather(w_value, "fsdp", axis=0, tiled=True),
        lax.all_gather(w_gate, "fsdp", axis=0, tiled=True),
    )
    update = (
        contract_last(query_grad_low, pieces[0])
        + contract_last(key_grad_low, pieces[1])
        + contract_last(value_grad_low, pieces[2])
        + contract_last(gate_grad_low, pieces[3])
    )
    _, first_pull = jax.vjp(
        layer_norm, inputs, gain_first.astype(jnp.float32), bias_first.astype(jnp.float32)
    )
    grad_input_norm, grad_gain_first, grad_bias_first = first_pull(update)
    grad_tokens = grad_resid + grad_input_norm
    hidden_part = hidden_low
    mixed_part = mixed_low
    output_rows = lax.psum_scatter(
        jnp.concatenate(
            [contract_first(hidden_part, cotangent), contract_first(mixed_part, grad_branch)],
            axis=1,
        ).astype(jnp.bfloat16),
        "fsdp",
        scatter_dimension=0,
        tiled=True,
    )
    input_rows = lax.psum_scatter(
        jnp.concatenate(
            [
                contract_first(z_first, query_grad_low),
                contract_first(z_first, key_grad_low),
                contract_first(z_first, value_grad_low),
                contract_first(z_first, gate_grad_low),
                contract_first(z_second, gate_ffn_low),
                contract_first(z_second, up_ffn_low),
            ],
            axis=1,
        ).astype(jnp.bfloat16),
        "fsdp",
        scatter_dimension=0,
        tiled=True,
    )
    gain_stack = jnp.stack([grad_gain_first, grad_bias_first, grad_gain_second, grad_bias_second])
    gain_rows = lax.psum_scatter(
        gain_stack.astype(jnp.bfloat16), "fsdp", scatter_dimension=1, tiled=True
    )
    summed = (
        lax.psum(input_rows, "rep").astype(jnp.float32),
        lax.psum(output_rows, "rep").astype(jnp.float32),
        lax.psum(gain_rows, "rep").astype(jnp.float32),
    )
    input_total, output_total, gain_total = summed
    return (
        output,
        grad_tokens,
        input_total[:, :D],
        input_total[:, D : 2 * D],
        input_total[:, 2 * D : 2 * D + VD],
        input_total[:, 2 * D + VD : 2 * D + 2 * VD],
        output_total[:, D:],
        gain_total[0],
        gain_total[1],
        input_total[:, 2 * D + 2 * VD : 2 * D + 2 * VD + FF],
        input_total[:, 2 * D + 2 * VD + FF :],
        output_total[:, :D],
        gain_total[2],
        gain_total[3],
    )


def solution(mesh):
    in_specs = (
        P(("rep", "fsdp"), None),
        P("fsdp", None),
        P("fsdp", None),
        P("fsdp", None),
        P("fsdp", None),
        P("fsdp", None),
        P("fsdp"),
        P("fsdp"),
        P("fsdp", None),
        P("fsdp", None),
        P("fsdp", None),
        P("fsdp"),
        P("fsdp"),
        P(("rep", "fsdp"), None),
    )
    out_specs = (
        P(("rep", "fsdp"), None),
        P(("rep", "fsdp"), None),
        P("fsdp", None),
        P("fsdp", None),
        P("fsdp", None),
        P("fsdp", None),
        P("fsdp", None),
        P("fsdp"),
        P("fsdp"),
        P("fsdp", None),
        P("fsdp", None),
        P("fsdp", None),
        P("fsdp"),
        P("fsdp"),
    )
    return jax.shard_map(
        on_device, mesh=mesh, in_specs=in_specs, out_specs=out_specs, check_vma=False
    )
```

profile of v0, /device:TPU:0, one launch (start us, length us, event | category | flops | bytes accessed | tf_op | source)
XLA Modules:
  0.0 4780.3 jit_solution(11625595537723999888)
XLA Ops:
  9.5 22.4 all-gather.3
  32.0 16.6 all-gather.2
  50.0 87.9 %all-gather.21.cloned.1.call-done = bf16[2048,2048]{1,0:T(8,128)(2,1)} async-done(((bf16[256,2048]{1,0:T(8,128)(2,1)}), bf16[2048,2048]{1,0:T(8,128)(2,1)}) %all-gather.21.cloned.1.call-update) | async-done | bytes 8388624 | tf_op jit(solution)/shard_map/all_gather | solution.py:140
  143.0 120.2 %all-gather.23.cloned.1.call-done = bf16[2048,2048]{1,0:T(8,128)(2,1)} async-done(((bf16[256,2048]{1,0:T(8,128)(2,1)}), bf16[2048,2048]{1,0:T(8,128)(2,1)}) %all-gather.23.cloned.1.call-update) | async-done | bytes 8388624 | tf_op jit(solution)/shard_map/all_gather | solution.py:141
  268.9 222.3 %all-gather.19.cloned.1.call-done = bf16[2048,4096]{1,0:T(8,128)(2,1)} async-done(((bf16[256,4096]{1,0:T(8,128)(2,1)}), bf16[2048,4096]{1,0:T(8,128)(2,1)}) %all-gather.19.cloned.1.call-update) | async-done | bytes 16777232 | tf_op jit(solution)/shard_map/all_gather | solution.py:142
  491.2 8.2 convolution_convert_fusion.6
  508.1 58.6 %all-gather.6 = bf16[8,1,256]{2,1,0:T(2,128)(2,1)S(1)} all-gather(bf16[1,1,256]{2,1,0:T(2,128)(2,1)S(1)} %reshape.365), channel_id=1, replica_groups=mesh['rep'=4,'fsdp'=8] {'fsdp'}, dimensions={0}, use_global_device_ids=true | all-gather | bytes 4608 | tf_op jit(solution)/shard_map/all_gather | solution.py:206
  566.8 25.4 all-gather.5
  592.3 24.0 all-gather.4
  616.7 524.4 %all-gather.35.cloned.1.call-done = f32[64,256,512]{2,1,0:T(8,128)} async-done(((f32[8,256,512]{2,1,0:T(8,128)}), f32[64,256,512]{2,1,0:T(8,128)}) %all-gather.35.cloned.1.call-update) | async-done | bytes 33554448 | tf_op jit(solution)/shard_map/all_gather | solution.py:23
  1141.1 52.5 %while.29 = (s32[]{:T(128)}, f32[8,256,512]{2,1,0:T(8,128)}, s32[]{:T(128)}, f32[8,8]{1,0:T(8,128)S(1)}, f32[8,8,256,512]{3,2,1,0:T(8,128)}, /*index=5*/s32[]{:T(128)}, s32[]{:T(128)}) while((s32[]{:T(128)}, f32[8,256,512]{2,1,0:T(8,128)}, s32[]{:T(128)}, f32[8,8]{1,0:T(8,128)S(1)}, f32[8,8,256,512]{3,2,1,0:T(8,128)}, ...), condition=%wide.region_3.4_spmd.clone, body=%wide.region_2.3_spmd.clone.sunk | while | flops 4194308 | bytes 12583121 | solution.py:35
  1193.6 8.8 fusion.58
  1208.6 162.0 %all-gather.25.cloned.1.call-done = bf16[2048,4096]{1,0:T(8,128)(2,1)} async-done(((bf16[256,4096]{1,0:T(8,128)(2,1)}), bf16[2048,4096]{1,0:T(8,128)(2,1)}) %all-gather.25.cloned.1.call-update) | async-done | bytes 16777232 | tf_op jit(solution)/shard_map/all_gather | solution.py:143
  1370.7 10.8 multiply_convert_fusion.2
  1381.4 217.0 %all-gather.27.cloned.1.call-done = bf16[4096,2048]{1,0:T(8,128)(2,1)} async-done(((bf16[512,2048]{1,0:T(8,128)(2,1)}), bf16[4096,2048]{1,0:T(8,128)(2,1)}) %all-gather.27.cloned.1.call-update) | async-done | bytes 16777232 | tf_op jit(solution)/shard_map/all_gather | solution.py:196
  1598.5 8.5 fusion.96
  1608.2 218.2 %all-gather.29.cloned.1.call-done = bf16[2048,4096]{1,0:T(8,128)(2,1)} async-done(((bf16[256,4096]{1,0:T(8,128)(2,1)}), bf16[2048,4096]{1,0:T(8,128)(2,1)}) %all-gather.29.cloned.1.call-update) | async-done | bytes 16777232 | tf_op jit(solution)/shard_map/all_gather | solution.py:203
  1826.4 9.4 fusion.97
  1835.8 218.5 %all-gather.33.cloned.1.call-done = bf16[4096,2048]{1,0:T(8,128)(2,1)} async-done(((bf16[512,2048]{1,0:T(8,128)(2,1)}), bf16[4096,2048]{1,0:T(8,128)(2,1)}) %all-gather.33.cloned.1.call-update) | async-done | bytes 16777232 | tf_op jit(solution)/shard_map/all_gather | solution.py:230
  2054.4 14.8 multiply_convert_fusion
  2069.1 213.2 %all-gather.31.cloned.1.call-done = bf16[2048,4096]{1,0:T(8,128)(2,1)} async-done(((bf16[256,4096]{1,0:T(8,128)(2,1)}), bf16[2048,4096]{1,0:T(8,128)(2,1)}) %all-gather.31.cloned.1.call-update) | async-done | bytes 16777232 | tf_op jit(solution)/shard_map/all_gather | solution.py:204
  2282.3 12.6 add_convert_fusion.1
  2294.9 12.7 fusion.98
  2307.6 13.9 multiply_reduce_fusion.2
  2325.5 15.2 fusion.68
  2353.7 10.7 convolution_convert_fusion
  2364.5 9.3 convolution_convert_fusion.1
  2373.8 23.6 pad_maximum_fusion
  2397.6 17.5 all-gather.7
  2429.6 148.9 %all-gather.37.cloned.1.call-done = bf16[64,256,512]{2,1,0:T(8,128)(2,1)} async-done(((bf16[8,256,512]{2,1,0:T(8,128)(2,1)}), bf16[64,256,512]{2,1,0:T(8,128)(2,1)}) %all-gather.37.cloned.1.call-update) | async-done | bytes 16777232 | tf_op jit(solution)/shard_map/all_gather | solution.py:43
  2581.0 42.1 while.28
  2636.6 12.8 copy.112
  2655.0 12.4 copy.113
  2667.5 9.8 add_convert_fusion
  2677.3 8.4 constant_dynamic-update-slice_fusion.1
  2685.7 8.4 constant_dynamic-update-slice_fusion
  2694.1 8.5 convert_dynamic-update-slice_fusion.3
  2702.6 9.7 convert_dynamic-update-slice_fusion.2
  2712.3 8.3 convert_dynamic-update-slice_fusion.1
  2720.6 8.5 convert_dynamic-update-slice_fusion
  2729.8 12.9 fusion.101
  2750.0 12.8 fusion.100
  2773.3 350.2 %reduce-scatter.8.cloned.1.call-done = bf16[512,4096]{0,1:T(8,128)(2,1)} async-done(((bf16[4096,4096]{0,1:T(8,128)(2,1)}), bf16[512,4096]{0,1:T(8,128)(2,1)}) %reduce-scatter.8.cloned.1.call-update) | async-done | bytes 4194320 | tf_op jit(solution)/shard_map/reduce_scatter | solution.py:299
  3123.5 1298.1 %reduce-scatter.12.cloned.1.call-done = bf16[256,20480]{1,0:T(8,128)(2,1)} async-done(((bf16[2048,20480]{1,0:T(8,128)(2,1)}), bf16[256,20480]{1,0:T(8,128)(2,1)}) %reduce-scatter.12.cloned.1.call-update) | async-done | bytes 10485776
  4423.2 9.1 fusion.5
  4433.8 53.3 %reduce-scatter.10.cloned.1.call-done = bf16[256,4]{1,0:T(8,128)(2,1)} async-done(((bf16[2048,4]{1,0:T(8,128)(2,1)}), bf16[256,4]{1,0:T(8,128)(2,1)}) %reduce-scatter.10.cloned.1.call-update) | async-done | bytes 2064
  4494.2 249.3 %all-reduce.8.cloned.1.call-done = (bf16[256,20480]{1,0:T(8,128)(2,1)}, bf16[512,4096]{0,1:T(8,128)(2,1)}) async-done(((bf16[256,20480]{1,0:T(8,128)(2,1)}, bf16[512,4096]{0,1:T(8,128)(2,1)}), (bf16[256,20480]{1,0:T(8,128)(2,1)}, bf16[512,4096]{0,1:T(8,128)(2,1)})) %all-reduce.8.cloned.1.call-update) | async-done | bytes 14680080 | tf_op jit(solution)/shard_map/psum | solution.py:329
  4747.6 10.4 fusion.90
  (256 shorter events, 226.4 us)
Async XLA Ops:
  7.2 24.8 copy-start.53
  7.2 41.4 copy-start.1
  7.2 130.7 %all-gather.21.cloned.1.call-start = ((), (), s32[]{:S(2)}) async-start(), calls=%async_computation.4 | async-start | bytes 9437184 | tf_op jit(solution)/shard_map/all_gather | solution.py:140
  7.9 255.3 %all-gather.23.cloned.1.call-start = ((), (), s32[]{:S(2)}) async-start(), calls=%async_computation.5 | async-start | bytes 9437184 | tf_op jit(solution)/shard_map/all_gather | solution.py:141
  8.7 482.5 %all-gather.19.cloned.1.call-start = ((), (), s32[]{:S(2)}) async-start(), calls=%async_computation.3 | async-start | bytes 18874368 | tf_op jit(solution)/shard_map/all_gather | solution.py:142
  9.4 1131.6 %all-gather.35.cloned.1.call-start = ((), (), s32[]{:S(2)}) async-start(), calls=%async_computation.12 | async-start | bytes 37748736 | tf_op jit(solution)/shard_map/all_gather | solution.py:23
  48.6 567.8 %copy-start.46 = (f32[8]{0:T(128)}, f32[8]{0:T(128)S(1)}, u32[]{:S(2)}) copy-start(f32[8]{0:T(128)S(1)} %subtract_log_fusion) | copy-start | bytes 100
  49.7 449.7 %copy-start.40 = (f32[128,8]{0,1:T(8,128)}, f32[128,8]{0,1:T(8,128)S(1)}, u32[]{:S(2)}) copy-start(f32[128,8]{0,1:T(8,128)S(1)} %get-tuple-element.323) | copy-start | bytes 12292
  50.0 218.4 %copy-start.36 = (f32[128,128]{1,0:T(8,128)}, f32[128,128]{1,0:T(8,128)S(1)}, u32[]{:S(2)}) copy-start(f32[128,128]{1,0:T(8,128)S(1)} %get-tuple-element.320) | copy-start | bytes 196612
  50.0 218.4 %copy-start.38 = (f32[128,128]{1,0:T(8,128)}, f32[128,128]{1,0:T(8,128)S(1)}, u32[]{:S(2)}) copy-start(f32[128,128]{1,0:T(8,128)S(1)} %get-tuple-element.321) | copy-start | bytes 196612
  268.8 924.8 %copy-start.30 = (bf16[128,8,128]{2,0,1:T(8,128)(2,1)}, bf16[128,8,128]{2,0,1:T(8,128)(2,1)S(1)}, u32[]{:S(2)}) copy-start(bf16[128,8,128]{2,0,1:T(8,128)(2,1)S(1)} %get-tuple-element.305) | copy-start | bytes 786436
  268.9 347.5 %copy-start.18 = (bf16[128,8,256]{2,0,1:T(8,128)(2,1)}, bf16[128,8,256]{2,0,1:T(8,128)(2,1)S(1)}, u32[]{:S(2)}) copy-start(bf16[128,8,256]{2,0,1:T(8,128)(2,1)S(1)} %fusion.53) | copy-start | bytes 1572868
  504.6 866.0 %all-gather.25.cloned.1.call-start = ((), (), s32[]{:S(2)}) async-start(), calls=%async_computation.6 | async-start | bytes 18874368 | tf_op jit(solution)/shard_map/all_gather | solution.py:143
  505.2 1093.2 %all-gather.27.cloned.1.call-start = ((), (), s32[]{:S(2)}) async-start(), calls=%async_computation.7 | async-start | bytes 18874368 | tf_op jit(solution)/shard_map/all_gather | solution.py:196
  505.8 1320.6 %all-gather.29.cloned.1.call-start = ((), (), s32[]{:S(2)}) async-start(), calls=%async_computation.8 | async-start | bytes 18874368 | tf_op jit(solution)/shard_map/all_gather | solution.py:203
  506.6 60.2 %copy-start.55 = (bf16[256]{0:T(256)(128)(2,1)S(1)}, bf16[256]{0:T(256)(128)(2,1)}, u32[]{:S(2)}) copy-start(bf16[256]{0:T(256)(128)(2,1)} %param.29) | copy-start | bytes 1540
  506.6 1547.8 %all-gather.33.cloned.1.call-start = ((), (), s32[]{:S(2)}) async-start(), calls=%async_computation.10 | async-start | bytes 18874368 | tf_op jit(solution)/shard_map/all_gather | solution.py:230
  507.3 1775.0 %all-gather.31.cloned.1.call-start = ((), (), s32[]{:S(2)}) async-start(), calls=%async_computation.9 | async-start | bytes 18874368 | tf_op jit(solution)/shard_map/all_gather | solution.py:204
  508.1 2070.4 %all-gather.37.cloned.1.call-start = ((), (), s32[]{:S(2)}) async-start(), calls=%async_computation.13 | async-start | bytes 18874368 | tf_op jit(solution)/shard_map/all_gather | solution.py:43
  616.7 585.7 %copy-start.34 = (f32[8,128,128]{2,1,0:T(8,128)}, f32[8,128,128]{2,1,0:T(8,128)S(1)}, u32[]{:S(2)}) copy-start(f32[8,128,128]{2,1,0:T(8,128)S(1)} %convolution_multiply_fusion) | copy-start | bytes 1572868
  1193.6 8.8 copy-start.7
  2307.6 14.0 copy-start.49
  2323.6 17.1 copy-start.44
  2352.5 11.9 copy-start.11
  2352.5 771.0 %reduce-scatter.8.cloned.1.call-start = ((), (), s32[]{:S(2)}) async-start(), calls=%async_computation.11 | async-start | bytes 37748736 | tf_op jit(solution)/shard_map/reduce_scatter | solution.py:299
  2397.4 17.6 copy-start.3
  2397.5 17.6 copy-start.47
  2397.5 2024.2 %reduce-scatter.12.cloned.1.call-start = ((), (), s32[]{:S(2)}) async-start(), calls=%async_computation.15 | async-start | bytes 94371840
  2397.5 20.8 copy-start.32
  2415.1 4.9 copy-start
  2581.0 42.1 copy-start.8
  2581.0 42.1 copy-start.28
  2581.0 42.1 copy-start.41
  2630.5 6.0 copy-start.24
  2630.9 18.5 copy-start.22
  2655.0 12.4 copy-start.20
  2702.6 9.7 copy-start.13
  2712.3 8.3 copy-start.33
  2729.1 1758.0 %reduce-scatter.10.cloned.1.call-start = ((), (), s32[]{:S(2)}) async-start(), calls=%async_computation.14 | async-start | bytes 589824
  2729.8 12.9 copy-start.25
  2750.0 12.8 copy-start.23
  2762.8 7.8 copy-start.51
  2773.2 1970.3 %all-reduce.8.cloned.1.call-start = ((), (), s32[]{:S(2)}) async-start(), calls=%async_computation.16 | async-start | bytes 29360128 | tf_op jit(solution)/shard_map/psum | solution.py:329
  4423.2 9.1 copy-start.15
  4423.2 9.1 copy-start.17
  4423.2 9.1 copy-start.27
  4423.2 9.1 copy-start.45
  4747.6 10.4 copy-start.10
  (22 other events, 43.3 us)
Sparse Core Ops, SparseCore 0:
  10.2 127.7 all-gather.20
  140.1 123.1 all-gather.22
  265.3 225.7 all-gather.18
  504.8 636.2 all-gather.34
  1143.0 227.5 all-gather.24
  1372.6 225.7 all-gather.26
  1600.6 225.7 all-gather.28
  1828.5 225.7 all-gather.32
  2056.5 225.7 all-gather.30
  2352.6 225.7 all-gather.36
  2582.2 541.2 reduce-scatter.7
  3127.2 1294.3 reduce-scatter.11
  4425.9 61.0 reduce-scatter.9
  4489.6 253.8 all-reduce.7
where the time goes:
time: 4790 us; the launch traced here: 4780 us
  waiting for transfers between devices  4090 us (85%)
  matrix products  280 us (6%)
  blocking collectives  170 us (4%)
  other arithmetic  131 us (3%)
  local copies, waits for them, and re-layouts  94.3 us (2%)
    unnamed x16, waiting for transfers between devices  1360 us
    all_gather x1, waiting for transfers between devices, prefix(): everything = jax.tree.map(lambda part: lax.all_gather(part, axis), value)  524 us
    reduce_scatter x1, waiting for transfers between devices, on_device(): lax.psum_scatter(jnp.concatenate([contract_first(hidden_part, cotangent),...  350 us
    psum x1, waiting for transfers between devices, on_device(): lax.psum(input_rows, 'rep').astype(jnp.float32)  249 us
    all_gather x1, waiting for transfers between devices, on_device(): piece_value = lax.all_gather(w_value, 'fsdp', axis=0, tiled=True)  222 us
    all_gather x1, waiting for transfers between devices, on_device(): lax.all_gather(w_ffn_down, 'fsdp', axis=0, tiled=True)  219 us
    all_gather x1, waiting for transfers between devices, on_device(): piece_gate = lax.all_gather(w_ffn_gate, 'fsdp', axis=0, tiled=True)  218 us
    all_gather x1, waiting for transfers between devices, on_device(): lax.all_gather(w_out, 'fsdp', axis=0, tiled=True)  217 us
  transfers between devices with their start and end apart: 14, of which 14 were waited for; matrix products, arithmetic and copies ran while one was open for 8% of the time, Pallas kernels for 0%

commit v1 on v0

v1 whole, which is shorter than its diff:
```python
import math

import jax
import jax.numpy as jnp
from jax import lax
from jax.sharding import PartitionSpec as P

HEADS = 8
epsilon = 1e-05
head_epsilon = 1.0
f32 = jnp.float32
bf16 = jnp.bfloat16


def dot(a, b, ca=1, cb=0, kind=f32):
    return lax.dot_general(a, b, (((ca,), (cb,)), ((), ())), preferred_element_type=kind)


class Ring:
    def __init__(self, axis):
        self.axis = axis
        self.n = n = lax.axis_size(axis)
        self.order = list(range(0, n, 2)) + list(range(n - 1, 0, -2))
        place = [0] * n
        for i, device in enumerate(self.order):
            place[device] = i
        self.place = jnp.array(place, jnp.int32)[lax.axis_index(axis)]
        self.forward = [(self.order[i], self.order[(i + 1) % n]) for i in range(n)]
        self.backward = [(b, a) for a, b in self.forward]
        self.half = n // 2
        self.offsets = [0]
        for s in range(1, self.half):
            self.offsets += [-s, s]
        self.offsets.append(self.half)

    def send(self, value, forward):
        return lax.ppermute(value, self.axis, self.forward if forward else self.backward)

    def owners(self):
        places = (self.place + jnp.array(self.offsets, jnp.int32)) % self.n
        return jnp.array(self.order, jnp.int32)[places]

    def gather(self, block):
        rows = block.shape[0] // 2
        blocks = [block]
        ahead = behind = block
        for _ in range(1, self.half):
            ahead = self.send(ahead, True)
            behind = self.send(behind, False)
            blocks += [ahead, behind]
        blocks.append(
            jnp.concatenate([self.send(ahead[:rows], True), self.send(behind[rows:], False)])
        )
        return blocks

    def scatter(self, parts):
        term = dict(zip(self.offsets, parts))
        rows = parts[0].shape[0] // 2
        far = term[self.half]
        ahead = self.send(far[:rows].astype(bf16), True).astype(f32)
        behind = self.send(far[rows:].astype(bf16), False).astype(f32)
        nothing = jnp.zeros_like(ahead)
        ahead = jnp.concatenate([ahead, nothing])
        behind = jnp.concatenate([nothing, behind])
        for s in range(self.half - 1, 0, -1):
            ahead = self.send((term[s] + ahead).astype(bf16), True).astype(f32)
            behind = self.send((term[-s] + behind).astype(bf16), False).astype(f32)
        return term[0] + ahead + behind


class Cube:
    def __init__(self, axis):
        self.axis = axis
        self.n = lax.axis_size(axis)
        self.bits = self.n.bit_length() - 1
        self.index = lax.axis_index(axis)

    def swap(self, value, bit):
        return lax.ppermute(value, self.axis, [(i, i ^ (1 << bit)) for i in range(self.n)])

    def mine(self, bit):
        return (self.index >> bit) & 1

    def gather(self, value, dim):
        for bit in reversed(range(self.bits)):
            other = self.swap(value, bit)
            low = self.mine(bit) == 0
            shape = list(value.shape)
            first = jnp.where(low, value, other)
            second = jnp.where(low, other, value)
            value = jnp.stack([first, second], dim + 1)
            shape[dim] *= 2
            value = value.reshape(shape)
        return value

    def scatter(self, value, dim):
        for bit in range(self.bits):
            shape = list(value.shape)
            value = value.reshape(shape[:dim] + [shape[dim] // 2, 2] + shape[dim + 1 :])
            mine = self.mine(bit)
            given = lax.dynamic_index_in_dim(value, 1 - mine, dim + 1, False).astype(bf16)
            kept = lax.dynamic_index_in_dim(value, mine, dim + 1, False)
            value = kept + self.swap(given, bit).astype(f32)
        return value


def normalize(values):
    center = values - jnp.mean(values, axis=-1, keepdims=True)
    spread = jnp.mean(center * center, axis=-1, keepdims=True)
    return center * lax.rsqrt(spread + epsilon)


def layer_norm(values, gain, shift):
    return normalize(values) * gain + shift


def head_norm(values):
    center = values - jnp.mean(values, axis=-1, keepdims=True)
    spread = jnp.mean(center * center, axis=-1, keepdims=True)
    return center * lax.rsqrt(spread + head_epsilon)


def turn(values, cosine, sine):
    half = values.shape[-1] // 2
    first, second = values[:, :half], values[:, half:]
    return jnp.concatenate([first * cosine - second * sine, second * cosine + first * sine], -1)


def turn_back(values, cosine, sine):
    return turn(values, cosine, -sine)


def on_device(
    tokens,
    w_query,
    w_key,
    w_value,
    w_gate,
    w_out,
    norm1_gain,
    norm1_bias,
    w_ffn_gate,
    w_ffn_up,
    w_ffn_down,
    norm2_gain,
    norm2_bias,
    cotangent,
):
    ring = Ring("fsdp")
    cube = Cube("rep")
    n = ring.n
    assert n == HEADS
    rows, width = tokens.shape
    depth = w_query.shape[0]
    part = depth // cube.n

    def columns_of(*weights):
        mine = [
            lax.dynamic_slice_in_dim(w, cube.index * part, part, 0)
            .reshape(part, n, w.shape[1] // n)
            .transpose(1, 0, 2)
            for w in weights
        ]
        sent = jnp.concatenate(mine, -1)
        got = lax.all_to_all(sent, "fsdp", 0, 0, tiled=True)
        whole = cube.gather(got[:, None], 1)
        return whole.reshape(n * depth, whole.shape[-1])

    def rows_of(grad):
        value = grad.reshape(n, cube.n, part, grad.shape[-1])
        value = cube.scatter(value, 1)[:, 0].astype(bf16)
        value = lax.all_to_all(value, "fsdp", 0, 0, tiled=True)
        value = cube.gather(value[:, None], 1)
        return value.reshape(n, depth, grad.shape[-1]).transpose(1, 0, 2).astype(f32)

    def own_rows(grad):
        value = grad.reshape(cube.n, grad.shape[0] // cube.n, grad.shape[1])
        value = cube.gather(cube.scatter(value, 0).astype(bf16), 0)
        return value.reshape(grad.shape).astype(f32)

    gains = jnp.stack([norm1_gain, norm1_bias, norm2_gain, norm2_bias])
    gains = lax.all_gather(gains, "fsdp", axis=1, tiled=True).astype(f32)
    x_all = jnp.concatenate(ring.gather(tokens))
    w_mix = columns_of(w_query, w_key, w_value, w_gate)
    dk = w_query.shape[1] // n
    dv = w_value.shape[1] // n
    ff = w_ffn_gate.shape[1] // n
    cot_all = jnp.concatenate(ring.gather(cotangent))
    w_ffn = columns_of(w_ffn_gate, w_ffn_up)

    head = lax.axis_index("fsdp")
    gamma_log = jnp.log(1.0 - 2.0 ** (-5.0 - head.astype(f32)))
    positions = (
        (ring.owners() * rows)[:, None] + jnp.arange(rows, dtype=jnp.int32)[None, :]
    ).reshape(-1).astype(f32)
    half = dk // 2
    freqs = jnp.exp(-jnp.arange(half, dtype=f32) * (math.log(10000.0) / half))
    angles = positions[:, None] * freqs[None, :]
    cosine, sine = jnp.cos(angles), jnp.sin(angles)
    differ = positions[:, None] - positions[None, :]
    decay = jnp.where(differ >= 0, jnp.exp(jnp.maximum(differ, 0.0) * gamma_log), 0.0)
    key_scale = dk ** (-0.5)

    z_first = layer_norm(x_all.astype(f32), gains[0], gains[1]).astype(bf16)
    pre = dot(z_first, w_mix)
    query = turn(pre[:, :dk], cosine, sine).astype(bf16)
    key = (turn(pre[:, dk : 2 * dk], cosine, sine) * key_scale).astype(bf16)
    value = pre[:, 2 * dk : 2 * dk + dv].astype(bf16)
    gate = pre[:, 2 * dk + dv :]
    scores = (dot(query, key, 1, 1) * decay).astype(bf16)
    retained = dot(scores, value)

    def mix(retained_in, gate_in):
        return head_norm(retained_in) * jax.nn.silu(gate_in)

    mixed, mix_pull = jax.vjp(mix, retained, gate)
    mixed = mixed.astype(bf16)
    out = dot(mixed, w_out)
    x_own = tokens.astype(f32)
    resid = x_own + ring.scatter(jnp.split(out, n))

    z_second_own, second_pull = jax.vjp(layer_norm, resid, gains[2], gains[3])
    z_second = jnp.concatenate(ring.gather(z_second_own.astype(bf16)))
    ab = dot(z_second, w_ffn)

    def unit(gate_in, up_in):
        return jax.nn.gelu(gate_in, approximate=False) * up_in

    hidden, unit_pull = jax.vjp(unit, ab[:, :ff], ab[:, ff:])
    hidden = hidden.astype(bf16)
    grad_hidden = dot(cot_all, w_ffn_down, 1, 1).astype(bf16).astype(f32)
    grad_ab = jnp.concatenate(unit_pull(grad_hidden), -1).astype(bf16)
    grad_z_second = ring.scatter(jnp.split(dot(grad_ab, w_ffn, 1, 1), n))
    grad_resid_norm, grad_gain_second, grad_bias_second = second_pull(grad_z_second)
    grad_resid = cotangent.astype(f32) + grad_resid_norm
    output = (resid + ring.scatter(jnp.split(dot(hidden, w_ffn_down), n))).astype(bf16)
    grad_down = own_rows(dot(hidden, cot_all, 0, 0))
    grad_ffn = rows_of(dot(z_second, grad_ab, 0, 0))

    grad_out = jnp.concatenate(ring.gather(grad_resid.astype(bf16)))
    grad_mixed = dot(grad_out, w_out, 1, 1).astype(bf16).astype(f32)
    grad_retained, grad_gate = mix_pull(grad_mixed)
    grad_retained = grad_retained.astype(bf16)
    grad_scores = (dot(grad_retained, value, 1, 1) * decay).astype(bf16)
    grad_query = turn_back(dot(grad_scores, key), cosine, sine)
    grad_key = turn_back(dot(grad_scores, query, 0, 0), cosine, sine) * key_scale
    grad_value = dot(scores, grad_retained, 0, 0)
    grad_pre = jnp.concatenate([grad_query, grad_key, grad_value, grad_gate], -1).astype(bf16)
    grad_z_first = ring.scatter(jnp.split(dot(grad_pre, w_mix, 1, 1), n))
    _, first_pull = jax.vjp(layer_norm, x_own, gains[0], gains[1])
    grad_input_norm, grad_gain_first, grad_bias_first = first_pull(grad_z_first)
    grad_tokens = grad_resid + grad_input_norm
    grad_w_out = own_rows(dot(mixed, grad_out, 0, 0))
    grad_mix = rows_of(dot(z_first, grad_pre, 0, 0))

    stack = jnp.stack([grad_gain_first, grad_bias_first, grad_gain_second, grad_bias_second])
    for bit in range(n.bit_length() - 1):
        stack = stack + lax.ppermute(stack, "fsdp", [(i, i ^ (1 << bit)) for i in range(n)])
    for bit in range(cube.bits):
        stack = stack + cube.swap(stack, bit)
    stack = lax.dynamic_slice_in_dim(stack, head * depth, depth, 1)

    def flat(grad, start, size):
        return grad[:, :, start : start + size].reshape(depth, n * size)

    return (
        output,
        grad_tokens,
        flat(grad_mix, 0, dk),
        flat(grad_mix, dk, dk),
        flat(grad_mix, 2 * dk, dv),
        flat(grad_mix, 2 * dk + dv, dv),
        grad_w_out,
        stack[0],
        stack[1],
        flat(grad_ffn, 0, ff),
        flat(grad_ffn, ff, ff),
        grad_down,
        stack[2],
        stack[3],
    )


def solution(mesh):
    tokens = P(("rep", "fsdp"), None)
    matrix = P("fsdp", None)
    vector = P("fsdp")
    in_specs = (tokens,) + (matrix,) * 5 + (vector,) * 2 + (matrix,) * 3 + (vector,) * 2 + (tokens,)
    out_specs = (
        (tokens,) * 2 + (matrix,) * 5 + (vector,) * 2 + (matrix,) * 3 + (vector,) * 2
    )
    return jax.shard_map(
        on_device, mesh=mesh, in_specs=in_specs, out_specs=out_specs, check_vma=False
    )
```

time: 4790 us -> 839 us (0.18)
  waiting for transfers between devices: 4090 us -> 352 us
  matrix products: 280 us -> 84.3 us
  blocking collectives: 170 us -> 26.1 us
  starting transfers between devices: 0.76 us -> 129 us
    all_gather x10 -> x0, waiting for transfers between devices: 2130 us -> none  [the longest x1 524 us: prefix(): everything = jax.tree.map(lambda part: lax.all_gather(part, axis), value)]
    unnamed x16 -> x0, waiting for transfers between devices: 1360 us -> none
    reduce_scatter x1 -> x0, waiting for transfers between devices: 350 us -> none  [on_device(): lax.psum_scatter(jnp.concatenate([contract_first(hidden_part, cotangent),...]
    ppermute x0 -> x89, waiting for transfers between devices: none -> 317 us  [the longest x64 267 us: send(): lax.ppermute(value, self.axis, self.forward if forward else self.backward)]
    psum x1 -> x0, waiting for transfers between devices: 249 us -> none  [on_device(): lax.psum(input_rows, 'rep').astype(jnp.float32)]
    dot_general x36 -> x18, matrix products: 280 us -> 84.3 us  [dot(): lax.dot_general(a, b, (((ca,), (cb,)), ((), ())), preferred_element_type=...]
    all_gather x6 -> x1, blocking collectives: 165 us -> 26.1 us  [on_device(): gains = lax.all_gather(gains, 'fsdp', axis=1, tiled=True).astype(f32)]
    ppermute x0 -> x89, starting transfers between devices: none -> 108 us  [the longest x64 75.8 us: send(): lax.ppermute(value, self.axis, self.forward if forward else self.backward)]
  transfers between devices with their start and end apart: 14 -> 93, of which waited for: 14 -> 48; matrix products, arithmetic and copies ran while one was open for 8% -> 21% of each run, Pallas kernels for 0% -> 0%
where the time goes in v1:
time: 839 us; the launch traced here: 825 us
  waiting for transfers between devices  352 us (42%)
  local copies, waits for them, and re-layouts  134 us (16%)
  starting transfers between devices  129 us (15%)
  other arithmetic  96.2 us (11%)
  matrix products  84.3 us (10%)
  blocking collectives  26.1 us (3%)
    ppermute x64, waiting for transfers between devices, send(): lax.ppermute(value, self.axis, self.forward if forward else self.backward)  267 us
    dot_general x18, matrix products, dot(): lax.dot_general(a, b, (((ca,), (cb,)), ((), ())), preferred_element_type=...  84.3 us
    ppermute x64, starting transfers between devices, send(): lax.ppermute(value, self.axis, self.forward if forward else self.backward)  75.8 us
    unnamed x158, local copies, waits for them, and re-layouts  48.9 us
    ppermute x22, waiting for transfers between devices, swap(): lax.ppermute(value, self.axis, [(i, i ^ 1 << bit) for i in range(self.n)])  46.4 us
    slice x9, local copies, waits for them, and re-layouts, flat(): return grad[:, :, start:start + size].reshape(depth, n * size)  42.8 us
    all_to_all x2, waiting for transfers between devices, columns_of(): got = lax.all_to_all(sent, 'fsdp', 0, 0, tiled=True)  35.7 us
    all_gather x1, blocking collectives, on_device(): gains = lax.all_gather(gains, 'fsdp', axis=1, tiled=True).astype(f32)  26.1 us
  transfers between devices with their start and end apart: 93, of which 48 were waited for; matrix products, arithmetic and copies ran while one was open for 21% of the time, Pallas kernels for 0%

profile of v1, /device:TPU:0, one launch (start us, length us, event | category | flops | bytes accessed | tf_op | source)
XLA Modules:
  0.0 824.6 jit_solution(11501050578288015221)
XLA Ops:
  5.5 7.3 all-to-all-start
  15.6 35.7 %all-to-all-done = bf16[8,64,1536]{2,1,0:T(8,128)(2,1)} async-done(((bf16[8,64,1536]{2,1,0:T(8,128)(2,1)}), bf16[8,64,1536]{2,1,0:T(8,128)(2,1)}, u32[]{:S(2)}, u32[]{:S(2)}) %all-to-all-start) | async-done | bytes 1572896 | tf_op jit(solution)/shard_map/all_to_all | solution.py:165
  54.3 26.1 %all_gather.3 = bf16[4,2048]{1,0:T(4,128)(2,1)S(1)} all-gather(bf16[4,256]{1,0:T(4,128)(2,1)S(1)} %pad_maximum_fusion.13), channel_id=1, replica_groups=mesh['rep'=4,'fsdp'=8] {'fsdp'}, dimensions={1}, use_global_device_ids=true | all-gather | bytes 18432 | tf_op jit(solution)/shard_map/all_gather | solution.py:182
  92.0 11.2 %collective-permute-done.4 = bf16[128,2048]{1,0:T(8,128)(2,1)S(1)} collective-permute-done((bf16[128,2048]{1,0:T(8,128)(2,1)S(1)}, bf16[128,2048]{1,0:T(8,128)(2,1)S(1)}, u32[]{:S(2)}, u32[]{:S(2)}) %collective-permute-start.4) | collective-permute-done | bytes 524320 | tf_op jit(solution)/shard_map/ppermute | solution.py:37
  105.5 5.7 collective-permute-done.6
  118.5 9.8 %fusion.130 = f32[1024,1536]{1,0:T(8,128)S(1)} fusion(bf16[2048,1536]{1,0:T(8,128)(2,1)} %bitcast.230, bf16[1024,2048]{1,0:T(8,128)(2,1)S(1)} %constant_dynamic-update-slice_fusion, f32[2048]{0:T(1024)S(1)} %bitcast.273, f32[2048]{0:T(1024)S(1)} %bitcast.252, f32[1024]{0:T(1024)S(1)} %add_rsqrt_fusion, f32[1024]{0:T(1024)S(1)} %broadcast_multiply_fusion.1), kind=kOutput, calls=%fused_computation.332 | convolution fusion | flops 6455033856 | bytes 16801792 | tf_op jit(solution)/shard_map/dot_general | solution.py:16
  157.0 10.8 %collective-permute-done.11 = bf16[128,2048]{1,0:T(8,128)(2,1)S(1)} collective-permute-done((bf16[128,2048]{1,0:T(8,128)(2,1)S(1)}, bf16[128,2048]{1,0:T(8,128)(2,1)S(1)}, u32[]{:S(2)}, u32[]{:S(2)}) %collective-permute-start.11) | collective-permute-done | bytes 524320 | tf_op jit(solution)/shard_map/ppermute | solution.py:37
  181.2 12.0 %collective-permute-done.12 = bf16[128,2048]{1,0:T(8,128)(2,1)} collective-permute-done((bf16[128,2048]{1,0:T(8,128)(2,1)}, bf16[128,2048]{1,0:T(8,128)(2,1)}, u32[]{:S(2)}, u32[]{:S(2)}) %collective-permute-start.12) | collective-permute-done | bytes 524320 | tf_op jit(solution)/shard_map/ppermute | solution.py:37
  198.8 15.9 %collective-permute-done.38 = bf16[128,2048]{1,0:T(8,128)(2,1)} collective-permute-done((bf16[128,2048]{1,0:T(8,128)(2,1)}, bf16[128,2048]{1,0:T(8,128)(2,1)}, u32[]{:S(2)}, u32[]{:S(2)}) %collective-permute-start.38) | collective-permute-done | bytes 524320 | tf_op jit(solution)/shard_map/ppermute | solution.py:37
  214.7 7.0 collective-permute-start.40
  240.4 8.1 collective-permute-done.16
  253.6 6.9 collective-permute-done.17
  268.6 7.0 collective-permute-done.18
  279.4 9.6 %collective-permute-done.20 = bf16[128,2048]{1,0:T(8,128)(2,1)S(1)} collective-permute-done((bf16[128,2048]{1,0:T(8,128)(2,1)S(1)}, bf16[128,2048]{1,0:T(8,128)(2,1)S(1)}, u32[]{:S(2)}, u32[]{:S(2)}) %collective-permute-start.20) | collective-permute-done | bytes 524320 | tf_op jit(solution)/shard_map/ppermute | solution.py:37
  291.4 9.7 %collective-permute-done.22 = bf16[128,2048]{1,0:T(8,128)(2,1)S(1)} collective-permute-done((bf16[128,2048]{1,0:T(8,128)(2,1)S(1)}, bf16[128,2048]{1,0:T(8,128)(2,1)S(1)}, u32[]{:S(2)}, u32[]{:S(2)}) %collective-permute-start.22) | collective-permute-done | bytes 524320 | tf_op jit(solution)/shard_map/ppermute | solution.py:37
  316.3 8.8 %add_convert_fusion.3 = (bf16[1024,512]{1,0:T(8,128)(2,1)S(1)}, f32[1024,512]{1,0:T(8,128)S(1)}, bf16[1024,512]{1,0:T(8,128)(2,1)S(1)}) fusion(f32[1024,1024]{1,0:T(8,128)S(1)} %fusion.153, bf16[1024,2048]{1,0:T(8,128)(2,1)} %constant_dynamic-update-slice_fusion.18, bf16[512,2048]{1,0:T(8,128)(2,1)S(1)} %copy-done), kind=kOutput, calls=%fused_computation.66 | convolution fusion | flops 2186805248 | bytes 14680064 | tf_op jit(solution)/shard_map/dot_general | solution.py:16
  327.1 6.1 fusion.150
  333.1 7.0 fusion.33
  358.9 11.5 %collective-permute-done.45 = bf16[128,2048]{1,0:T(8,128)(2,1)S(1)} collective-permute-done((bf16[128,2048]{1,0:T(8,128)(2,1)S(1)}, bf16[128,2048]{1,0:T(8,128)(2,1)S(1)}, u32[]{:S(2)}, u32[]{:S(2)}) %collective-permute-start.45) | collective-permute-done | bytes 524320 | tf_op jit(solution)/shard_map/ppermute | solution.py:37
  371.6 10.0 %collective-permute-done.29 = bf16[128,2048]{1,0:T(8,128)(2,1)S(1)} collective-permute-done((bf16[128,2048]{1,0:T(8,128)(2,1)S(1)}, bf16[128,2048]{1,0:T(8,128)(2,1)S(1)}, u32[]{:S(2)}, u32[]{:S(2)}) %collective-permute-start.29) | collective-permute-done | bytes 524320 | tf_op jit(solution)/shard_map/ppermute | solution.py:37
  382.1 7.8 collective-permute-done.46
  391.5 7.1 collective-permute-done.30
  404.0 10.7 %collective-permute-done.33 = bf16[128,2048]{1,0:T(8,128)(2,1)S(1)} collective-permute-done((bf16[128,2048]{1,0:T(8,128)(2,1)S(1)}, bf16[128,2048]{1,0:T(8,128)(2,1)S(1)}, u32[]{:S(2)}, u32[]{:S(2)}) %collective-permute-start.33) | collective-permute-done | bytes 524320 | tf_op jit(solution)/shard_map/ppermute | solution.py:37
  415.1 8.1 collective-permute-done.50
  424.2 13.9 %collective-permute-done.34 = bf16[128,2048]{1,0:T(8,128)(2,1)S(1)} collective-permute-done((bf16[128,2048]{1,0:T(8,128)(2,1)S(1)}, bf16[128,2048]{1,0:T(8,128)(2,1)S(1)}, u32[]{:S(2)}, u32[]{:S(2)}) %collective-permute-start.34) | collective-permute-done | bytes 524320 | tf_op jit(solution)/shard_map/ppermute | solution.py:37
  440.0 9.3 %collective-permute-done.51 = bf16[128,2048]{1,0:T(8,128)(2,1)S(1)} collective-permute-done((bf16[128,2048]{1,0:T(8,128)(2,1)S(1)}, bf16[128,2048]{1,0:T(8,128)(2,1)S(1)}, u32[]{:S(2)}, u32[]{:S(2)}) %collective-permute-start.51) | collective-permute-done | bytes 524320 | tf_op jit(solution)/shard_map/ppermute | solution.py:37
  449.8 6.5 collective-permute-done.35
  473.1 8.7 %collective-permute-done.54 = bf16[128,2048]{1,0:T(8,128)(2,1)S(1)} collective-permute-done((bf16[128,2048]{1,0:T(8,128)(2,1)S(1)}, bf16[128,2048]{1,0:T(8,128)(2,1)S(1)}, u32[]{:S(2)}, u32[]{:S(2)}) %collective-permute-start.54) | collective-permute-done | bytes 524320 | tf_op jit(solution)/shard_map/ppermute | solution.py:37
  484.3 9.5 %collective-permute-done.56 = bf16[128,2048]{1,0:T(8,128)(2,1)S(1)} collective-permute-done((bf16[128,2048]{1,0:T(8,128)(2,1)S(1)}, bf16[128,2048]{1,0:T(8,128)(2,1)S(1)}, u32[]{:S(2)}, u32[]{:S(2)}) %collective-permute-start.56) | collective-permute-done | bytes 524320 | tf_op jit(solution)/shard_map/ppermute | solution.py:37
  523.3 9.8 %fusion.128 = f32[2048,1536]{1,0:T(8,128)S(1)} fusion(bf16[1024,1536]{1,0:T(8,128)(2,1)} %fusion.74, bf16[1024,2048]{1,0:T(8,128)(2,1)S(1)} %copy-done.8, f32[2048]{0:T(1024)S(1)} %bitcast.274, f32[2048]{0:T(1024)S(1)} %bitcast.253, f32[1024]{0:T(1024)S(1)} %add_rsqrt_fusion, f32[1024]{0:T(1024)S(1)} %broadcast_multiply_fusion.1), kind=kOutput, calls=%fused_computation.331 | convolution fusion | flops 6455033856 | bytes 19947520 | tf_op jit(solution)/shard_map/dot_general | solution.py:16
  535.5 13.9 %fusion.152 = (bf16[1024,2048]{1,0:T(8,128)(2,1)}, f32[1024,2048]{1,0:T(8,128)}) fusion(bf16[1024,1536]{1,0:T(8,128)(2,1)} %fusion.74, bf16[2048,1536]{1,0:T(8,128)(2,1)S(1)} %bitcast.233), kind=kOutput, calls=%fused_computation.349 | convolution fusion | flops 6444548096 | bytes 22020096 | tf_op jit(solution)/shard_map/dot_general | solution.py:16
  566.0 19.2 %collective-permute-done.61 = bf16[128,2048]{1,0:T(8,128)(2,1)S(1)} collective-permute-done((bf16[128,2048]{1,0:T(8,128)(2,1)S(1)}, bf16[128,2048]{1,0:T(8,128)(2,1)S(1)}, u32[]{:S(2)}, u32[]{:S(2)}) %collective-permute-start.61) | collective-permute-done | bytes 524320 | tf_op jit(solution)/shard_map/ppermute | solution.py:37
  586.6 7.2 collective-permute-start.62
  622.9 12.9 %collective-permute-done.69 = bf16[8,1,64,1536]{3,2,0,1:T(8,128)(2,1)} collective-permute-done((bf16[8,1,64,1536]{3,2,0,1:T(8,128)(2,1)}, bf16[8,1,64,1536]{3,2,0,1:T(8,128)(2,1)}, u32[]{:S(2)}, u32[]{:S(2)}) %collective-permute-start.69) | collective-permute-done | bytes 1572896 | tf_op jit(solution)/shard_map/ppermute | solution.py:79
  639.8 5.5 all-to-all-start.2
  652.2 6.1 collective-permute-done.83
  660.0 6.6 collective-permute-done.73
  668.3 9.1 %collective-permute-done.63 = bf16[128,2048]{1,0:T(8,128)(2,1)S(1)} collective-permute-done((bf16[128,2048]{1,0:T(8,128)(2,1)}, bf16[128,2048]{1,0:T(8,128)(2,1)S(1)}, u32[]{:S(2)}, u32[]{:S(2)}) %collective-permute-start.63) | collective-permute-done | bytes 524320 | tf_op jit(solution)/shard_map/ppermute | solution.py:37
  684.9 11.3 %collective-permute-start.77 = (f32[4,2048]{1,0:T(4,128)S(1)}, f32[4,2048]{1,0:T(4,128)S(1)}, u32[]{:S(2)}, u32[]{:S(2)}) collective-permute-start(f32[4,2048]{1,0:T(4,128)S(1)} %fusion.126), channel_id=1, source_target_pairs={{0,2},{1,3},{2,0},{3,1},{4,6},{5,7},{6,4},{7,5},{8,10},{9,11},{10,... | collective-permute-start | bytes 98312 | tf_op jit(solution)/shard_map/ppermute | solution.py:258
  703.3 17.1 %collective-permute-done.70 = bf16[8,1,64,1536]{3,2,0,1:T(8,128)(2,1)S(1)} collective-permute-done((bf16[8,1,64,1536]{3,2,0,1:T(8,128)(2,1)}, bf16[8,1,64,1536]{3,2,0,1:T(8,128)(2,1)S(1)}, u32[]{:S(2)}, u32[]{:S(2)}) %collective-permute-start.70) | collective-permute-done | bytes 1572896 | tf_op jit(solution)/shard_map/ppermute | solution.py:79
  740.4 5.6 copy.127
  746.0 5.6 copy.135
  756.9 5.6 copy.136
  765.0 5.4 maximum_convert_fusion
  770.4 11.2 %copy.117 = f32[8,2,2,64,1536]{4,3,2,1,0:T(8,128)} copy(f32[8,2,2,64,1536]{4,3,1,0,2:T(8,128)} %maximum_convert_fusion) | data formatting | bytes 25165824 | tf_op jit(solution)/shard_map/convert_element_type | solution.py:174
  786.3 8.3 %fusion.139 = (f32[256,8,512]{2,0,1:T(8,128)}, f32[256,8,512]{2,0,1:T(8,128)}) fusion(f32[256,8,1536]{2,0,1:T(8,128)} %bitcast.212), kind=kLoop, calls=%fused_computation.336 | loop fusion | bytes 16777216 | tf_op jit(solution)/shard_map/slice | solution.py:264
  807.5 5.6 copy.133
  818.4 5.7 copy.134
  (469 shorter events, 342.0 us)
Async XLA Ops:
  5.5 45.9 %all-to-all-start = ((bf16[8,64,1536]{2,1,0:T(8,128)(2,1)}), bf16[8,64,1536]{2,1,0:T(8,128)(2,1)}, u32[]{:S(2)}, u32[]{:S(2)}) async-start(bf16[8,64,1536]{2,1,0:T(8,128)(2,1)} %copy.98), calls=%async_computation | async-start | bytes 3145728 | tf_op jit(solution)/shard_map/all_to_all | solution.py:165
  12.7 67.7 %collective-permute-start = (bf16[128,2048]{1,0:T(8,128)(2,1)S(1)}, bf16[128,2048]{1,0:T(8,128)(2,1)}, u32[]{:S(2)}, u32[]{:S(2)}) collective-permute-start(bf16[128,2048]{1,0:T(8,128)(2,1)S(1)} %copy-done.10), channel_id=1, source_target_pairs={{0,2},{2,4},{4,6},{6,7},{7,5},{5,3},{3,1},{1,0},{8,10},{10,12},{12... | collective-permute-start | bytes 1572872 | tf_op jit(solution)/shard_map/ppermute | solution.py:37
  14.8 65.9 %collective-permute-start.1 = (bf16[128,2048]{1,0:T(8,128)(2,1)S(1)}, bf16[128,2048]{1,0:T(8,128)(2,1)S(1)}, u32[]{:S(2)}, u32[]{:S(2)}) collective-permute-start(bf16[128,2048]{1,0:T(8,128)(2,1)S(1)} %copy-done.10), channel_id=1, source_target_pairs={{2,0},{4,2},{6,4},{7,6},{5,7},{3,5},{1,3},{0,1},{10,8},{12,10},{14... | collective-permute-start | bytes 1572872 | tf_op jit(solution)/shard_map/ppermute | solution.py:37
  51.3 33.9 %collective-permute-start.8 = (bf16[8,1,64,1536]{3,2,0,1:T(8,128)(2,1)}, bf16[8,1,64,1536]{3,2,0,1:T(8,128)(2,1)}, u32[]{:S(2)}, u32[]{:S(2)}) collective-permute-start(bf16[8,1,64,1536]{3,2,0,1:T(8,128)(2,1)} %bitcast.6), channel_id=1, source_target_pairs={{0,16},{8,24},{16,0},{24,8},{1,17},{9,25},{17,1},{25,9},{2,18},{10... | collective-permute-start | bytes 4718600 | tf_op jit(solution)/shard_map/ppermute | solution.py:79
  87.6 26.2 %collective-permute-start.9 = (bf16[8,2,64,1536]{3,2,1,0:T(8,128)(2,1)S(1)}, bf16[8,2,64,1536]{3,2,1,0:T(8,128)(2,1)S(1)}, u32[]{:S(2)}, u32[]{:S(2)}) collective-permute-start(bf16[8,2,64,1536]{3,2,1,0:T(8,128)(2,1)S(1)} %copy_bitcast_fusion), channel_id=1, source_target_pairs={{0,8},{8,0},{16,24},{24,16},{1,9},{9,1},{17,25},{25,17},{2,10},{10... | collective-permute-start | bytes 9437192 | tf_op jit(solution)/shard_map/ppermute | solution.py:79
  154.7 24.5 %collective-permute-start.36 = (bf16[128,2048]{1,0:T(8,128)(2,1)S(1)}, bf16[128,2048]{1,0:T(8,128)(2,1)}, u32[]{:S(2)}, u32[]{:S(2)}) collective-permute-start(bf16[128,2048]{1,0:T(8,128)(2,1)S(1)} %copy-done.25), channel_id=1, source_target_pairs={{0,2},{2,4},{4,6},{6,7},{7,5},{5,3},{3,1},{1,0},{8,10},{10,12},{12... | collective-permute-start | bytes 1572872 | tf_op jit(solution)/shard_map/ppermute | solution.py:37
  156.1 24.8 %collective-permute-start.37 = (bf16[128,2048]{1,0:T(8,128)(2,1)S(1)}, bf16[128,2048]{1,0:T(8,128)(2,1)}, u32[]{:S(2)}, u32[]{:S(2)}) collective-permute-start(bf16[128,2048]{1,0:T(8,128)(2,1)S(1)} %copy-done.25), channel_id=1, source_target_pairs={{2,0},{4,2},{6,4},{7,6},{5,7},{3,5},{1,3},{0,1},{10,8},{12,10},{14... | collective-permute-start | bytes 1572872 | tf_op jit(solution)/shard_map/ppermute | solution.py:37
  156.7 24.5 %collective-permute-start.14 = (bf16[64,2048]{1,0:T(8,128)(2,1)}, bf16[64,2048]{1,0:T(8,128)(2,1)S(1)}, u32[]{:S(2)}, u32[]{:S(2)}) collective-permute-start(bf16[64,2048]{1,0:T(8,128)(2,1)} %get-tuple-element.99), channel_id=1, source_target_pairs={{2,0},{4,2},{6,4},{7,6},{5,7},{3,5},{1,3},{0,1},{10,8},{12,10},{14... | collective-permute-start | bytes 786440 | tf_op jit(solution)/shard_map/ppermute | solution.py:37
  168.7 24.5 %collective-permute-start.12 = (bf16[128,2048]{1,0:T(8,128)(2,1)}, bf16[128,2048]{1,0:T(8,128)(2,1)}, u32[]{:S(2)}, u32[]{:S(2)}) collective-permute-start(bf16[128,2048]{1,0:T(8,128)(2,1)} %fusion.69), channel_id=1, source_target_pairs={{0,2},{2,4},{4,6},{6,7},{7,5},{5,3},{3,1},{1,0},{8,10},{10,12},{12... | collective-permute-start | bytes 1572872 | tf_op jit(solution)/shard_map/ppermute | solution.py:37
  174.1 53.5 %all-to-all-start.1 = ((bf16[8,64,1024]{2,1,0:T(8,128)(2,1)}), bf16[8,64,1024]{2,1,0:T(8,128)(2,1)}, u32[]{:S(2)}, u32[]{:S(2)}) async-start(bf16[8,64,1024]{2,1,0:T(8,128)(2,1)} %copy.102), calls=%async_computation.1 | async-start | bytes 2097152 | tf_op jit(solution)/shard_map/all_to_all | solution.py:165
  179.2 35.5 %collective-permute-start.38 = (bf16[128,2048]{1,0:T(8,128)(2,1)}, bf16[128,2048]{1,0:T(8,128)(2,1)}, u32[]{:S(2)}, u32[]{:S(2)}) collective-permute-start(bf16[128,2048]{1,0:T(8,128)(2,1)} %collective-permute-done.36), channel_id=1, source_target_pairs={{0,2},{2,4},{4,6},{6,7},{7,5},{5,3},{3,1},{1,0},{8,10},{10,12},{12... | collective-permute-start | bytes 1572872 | tf_op jit(solution)/shard_map/ppermute | solution.py:37
  180.9 40.8 %collective-permute-start.39 = (bf16[128,2048]{1,0:T(8,128)(2,1)}, bf16[128,2048]{1,0:T(8,128)(2,1)}, u32[]{:S(2)}, u32[]{:S(2)}) collective-permute-start(bf16[128,2048]{1,0:T(8,128)(2,1)} %collective-permute-done.37), channel_id=1, source_target_pairs={{2,0},{4,2},{6,4},{7,6},{5,7},{3,5},{1,3},{0,1},{10,8},{12,10},{14... | collective-permute-start | bytes 1572872 | tf_op jit(solution)/shard_map/ppermute | solution.py:37
  196.1 25.6 %collective-permute-start.15 = (bf16[128,2048]{1,0:T(8,128)(2,1)}, bf16[128,2048]{1,0:T(8,128)(2,1)}, u32[]{:S(2)}, u32[]{:S(2)}) collective-permute-start(bf16[128,2048]{1,0:T(8,128)(2,1)} %get-tuple-element.77), channel_id=1, source_target_pairs={{2,0},{4,2},{6,4},{7,6},{5,7},{3,5},{1,3},{0,1},{10,8},{12,10},{14... | collective-permute-start | bytes 1572872 | tf_op jit(solution)/shard_map/ppermute | solution.py:37
  223.9 24.6 %collective-permute-start.16 = (bf16[128,2048]{1,0:T(8,128)(2,1)}, bf16[128,2048]{1,0:T(8,128)(2,1)}, u32[]{:S(2)}, u32[]{:S(2)}) collective-permute-start(bf16[128,2048]{1,0:T(8,128)(2,1)} %fusion.66), channel_id=1, source_target_pairs={{2,0},{4,2},{6,4},{7,6},{5,7},{3,5},{1,3},{0,1},{10,8},{12,10},{14... | collective-permute-start | bytes 1572872 | tf_op jit(solution)/shard_map/ppermute | solution.py:37
  227.6 24.3 %collective-permute-start.26 = (bf16[8,1,64,1024]{3,2,0,1:T(8,128)(2,1)}, bf16[8,1,64,1024]{3,2,0,1:T(8,128)(2,1)S(1)}, u32[]{:S(2)}, u32[]{:S(2)}) collective-permute-start(bf16[8,1,64,1024]{3,2,0,1:T(8,128)(2,1)} %bitcast.20), channel_id=1, source_target_pairs={{0,16},{8,24},{16,0},{24,8},{1,17},{9,25},{17,1},{25,9},{2,18},{10... | collective-permute-start | bytes 3145736 | tf_op jit(solution)/shard_map/ppermute | solution.py:79
  233.9 33.3 %collective-permute-start.42 = (bf16[64,2048]{1,0:T(8,128)(2,1)S(1)}, bf16[64,2048]{1,0:T(8,128)(2,1)S(1)}, u32[]{:S(2)}, u32[]{:S(2)}) collective-permute-start(bf16[64,2048]{1,0:T(8,128)(2,1)S(1)} %slice.214), channel_id=1, source_target_pairs={{0,2},{2,4},{4,6},{6,7},{7,5},{5,3},{3,1},{1,0},{8,10},{10,12},{12... | collective-permute-start | bytes 786440 | tf_op jit(solution)/shard_map/ppermute | solution.py:37
  238.3 29.7 %collective-permute-start.43 = (bf16[64,2048]{1,0:T(8,128)(2,1)S(1)}, bf16[64,2048]{1,0:T(8,128)(2,1)S(1)}, u32[]{:S(2)}, u32[]{:S(2)}) collective-permute-start(bf16[64,2048]{1,0:T(8,128)(2,1)S(1)} %slice.215), channel_id=1, source_target_pairs={{2,0},{4,2},{6,4},{7,6},{5,7},{3,5},{1,3},{0,1},{10,8},{12,10},{14... | collective-permute-start | bytes 786440 | tf_op jit(solution)/shard_map/ppermute | solution.py:37
  253.6 24.1 %collective-permute-start.27 = (bf16[8,2,64,1024]{3,2,1,0:T(8,128)(2,1)S(1)}, bf16[8,2,64,1024]{3,2,1,0:T(8,128)(2,1)S(1)}, u32[]{:S(2)}, u32[]{:S(2)}) collective-permute-start(bf16[8,2,64,1024]{3,2,1,0:T(8,128)(2,1)S(1)} %copy_bitcast_fusion.1), channel_id=1, source_target_pairs={{0,8},{8,0},{16,24},{24,16},{1,9},{9,1},{17,25},{25,17},{2,10},{10... | collective-permute-start | bytes 6291464 | tf_op jit(solution)/shard_map/ppermute | solution.py:79
  348.2 33.6 %collective-permute-start.48 = (bf16[64,2048]{1,0:T(8,128)(2,1)S(1)}, bf16[64,2048]{1,0:T(8,128)(2,1)S(1)}, u32[]{:S(2)}, u32[]{:S(2)}) collective-permute-start(bf16[64,2048]{1,0:T(8,128)(2,1)S(1)} %get-tuple-element.93), channel_id=1, source_target_pairs={{2,0},{4,2},{6,4},{7,6},{5,7},{3,5},{1,3},{0,1},{10,8},{12,10},{14... | collective-permute-start | bytes 786440 | tf_op jit(solution)/shard_map/ppermute | solution.py:37
  351.0 40.5 %collective-permute-start.32 = (bf16[64,2048]{1,0:T(8,128)(2,1)}, bf16[64,2048]{1,0:T(8,128)(2,1)}, u32[]{:S(2)}, u32[]{:S(2)}) collective-permute-start(bf16[64,2048]{1,0:T(8,128)(2,1)} %get-tuple-element.95), channel_id=1, source_target_pairs={{2,0},{4,2},{6,4},{7,6},{5,7},{3,5},{1,3},{0,1},{10,8},{12,10},{14... | collective-permute-start | bytes 786440 | tf_op jit(solution)/shard_map/ppermute | solution.py:37
  356.2 35.1 %collective-permute-start.85 = (bf16[2,128,2048]{2,1,0:T(8,128)(2,1)S(1)}, bf16[2,128,2048]{2,1,0:T(8,128)(2,1)S(1)}, u32[]{:S(2)}, u32[]{:S(2)}) collective-permute-start(bf16[2,128,2048]{2,1,0:T(8,128)(2,1)S(1)} %fusion.41), channel_id=1, source_target_pairs={{0,8},{8,0},{16,24},{24,16},{1,9},{9,1},{17,25},{25,17},{2,10},{10... | collective-permute-start | bytes 3145736 | tf_op jit(solution)/shard_map/ppermute | solution.py:79
  358.5 23.1 %collective-permute-start.29 = (bf16[128,2048]{1,0:T(8,128)(2,1)S(1)}, bf16[128,2048]{1,0:T(8,128)(2,1)S(1)}, u32[]{:S(2)}, u32[]{:S(2)}) collective-permute-start(bf16[128,2048]{1,0:T(8,128)(2,1)S(1)} %fusion.59), channel_id=1, source_target_pairs={{0,2},{2,4},{4,6},{6,7},{7,5},{5,3},{3,1},{1,0},{8,10},{10,12},{12... | collective-permute-start | bytes 1572872 | tf_op jit(solution)/shard_map/ppermute | solution.py:37
  381.6 78.2 %collective-permute-start.81 = (bf16[8,2,64,1024]{3,2,0,1:T(8,128)(2,1)S(1)}, bf16[8,2,64,1024]{3,2,0,1:T(8,128)(2,1)}, u32[]{:S(2)}, u32[]{:S(2)}) collective-permute-start(bf16[8,2,64,1024]{3,2,0,1:T(8,128)(2,1)S(1)} %fusion.19), channel_id=1, source_target_pairs={{0,8},{8,0},{16,24},{24,16},{1,9},{9,1},{17,25},{25,17},{2,10},{10... | collective-permute-start | bytes 6291464 | tf_op jit(solution)/shard_map/ppermute | solution.py:79
  400.3 22.9 %collective-permute-start.50 = (bf16[128,2048]{1,0:T(8,128)(2,1)S(1)}, bf16[128,2048]{1,0:T(8,128)(2,1)S(1)}, u32[]{:S(2)}, u32[]{:S(2)}) collective-permute-start(bf16[128,2048]{1,0:T(8,128)(2,1)S(1)} %fusion.50), channel_id=1, source_target_pairs={{2,0},{4,2},{6,4},{7,6},{5,7},{3,5},{1,3},{0,1},{10,8},{12,10},{14... | collective-permute-start | bytes 1572872 | tf_op jit(solution)/shard_map/ppermute | solution.py:37
  400.8 22.8 %collective-permute-start.86 = (bf16[1,128,2048]{2,1,0:T(8,128)(2,1)S(1)}, bf16[1,128,2048]{2,1,0:T(8,128)(2,1)S(1)}, u32[]{:S(2)}, u32[]{:S(2)}) collective-permute-start(bf16[1,128,2048]{2,1,0:T(8,128)(2,1)S(1)} %dynamic-slice_convert_fusion.3), channel_id=1, source_target_pairs={{0,16},{8,24},{16,0},{24,8},{1,17},{9,25},{17,1},{25,9},{2,18},{10... | collective-permute-start | bytes 1572872 | tf_op jit(solution)/shard_map/ppermute | solution.py:79
  402.3 37.3 %collective-permute-start.47 = (bf16[128,2048]{1,0:T(8,128)(2,1)S(1)}, bf16[128,2048]{1,0:T(8,128)(2,1)S(1)}, u32[]{:S(2)}, u32[]{:S(2)}) collective-permute-start(bf16[128,2048]{1,0:T(8,128)(2,1)S(1)} %get-tuple-element.72), channel_id=1, source_target_pairs={{0,2},{2,4},{4,6},{6,7},{7,5},{5,3},{3,1},{1,0},{8,10},{10,12},{12... | collective-permute-start | bytes 1572872 | tf_op jit(solution)/shard_map/ppermute | solution.py:37
  414.7 35.1 %collective-permute-start.31 = (bf16[128,2048]{1,0:T(8,128)(2,1)S(1)}, bf16[128,2048]{1,0:T(8,128)(2,1)S(1)}, u32[]{:S(2)}, u32[]{:S(2)}) collective-permute-start(bf16[128,2048]{1,0:T(8,128)(2,1)S(1)} %get-tuple-element.74), channel_id=1, source_target_pairs={{0,2},{2,4},{4,6},{6,7},{7,5},{5,3},{3,1},{1,0},{8,10},{10,12},{12... | collective-permute-start | bytes 1572872 | tf_op jit(solution)/shard_map/ppermute | solution.py:37
  423.6 25.7 %collective-permute-start.51 = (bf16[128,2048]{1,0:T(8,128)(2,1)S(1)}, bf16[128,2048]{1,0:T(8,128)(2,1)S(1)}, u32[]{:S(2)}, u32[]{:S(2)}) collective-permute-start(bf16[128,2048]{1,0:T(8,128)(2,1)S(1)} %fusion.51), channel_id=1, source_target_pairs={{2,0},{4,2},{6,4},{7,6},{5,7},{3,5},{1,3},{0,1},{10,8},{12,10},{14... | collective-permute-start | bytes 1572872 | tf_op jit(solution)/shard_map/ppermute | solution.py:37
  438.1 33.9 %collective-permute-start.87 = (bf16[1,128,2048]{2,1,0:T(8,128)(2,1)S(1)}, bf16[1,128,2048]{2,1,0:T(8,128)(2,1)S(1)}, u32[]{:S(2)}, u32[]{:S(2)}) collective-permute-start(bf16[1,128,2048]{2,1,0:T(8,128)(2,1)S(1)} %add_convert_fusion.4), channel_id=1, source_target_pairs={{0,16},{8,24},{16,0},{24,8},{1,17},{9,25},{17,1},{25,9},{2,18},{10... | collective-permute-start | bytes 1572872 | tf_op jit(solution)/shard_map/ppermute | solution.py:79
  463.4 88.0 %collective-permute-start.82 = (bf16[8,1,64,1024]{3,2,0,1:T(8,128)(2,1)}, bf16[8,1,64,1024]{3,2,0,1:T(8,128)(2,1)}, u32[]{:S(2)}, u32[]{:S(2)}) collective-permute-start(bf16[8,1,64,1024]{3,2,0,1:T(8,128)(2,1)} %dynamic-slice_convert_fusion.1), channel_id=1, source_target_pairs={{0,16},{8,24},{16,0},{24,8},{1,17},{9,25},{17,1},{25,9},{2,18},{10... | collective-permute-start | bytes 3145736 | tf_op jit(solution)/shard_map/ppermute | solution.py:79
  473.1 88.8 %collective-permute-start.88 = (bf16[2,128,2048]{2,1,0:T(8,128)(2,1)}, bf16[2,128,2048]{2,1,0:T(8,128)(2,1)}, u32[]{:S(2)}, u32[]{:S(2)}) collective-permute-start(bf16[2,128,2048]{2,1,0:T(8,128)(2,1)} %maximum_bitcast_fusion.3), channel_id=1, source_target_pairs={{0,8},{8,0},{16,24},{24,16},{1,9},{9,1},{17,25},{25,17},{2,10},{10... | collective-permute-start | bytes 3145736 | tf_op jit(solution)/shard_map/ppermute | solution.py:79
  535.5 58.3 %collective-permute-start.68 = (bf16[8,2,64,1536]{3,2,0,1:T(8,128)(2,1)}, bf16[8,2,64,1536]{3,2,0,1:T(8,128)(2,1)}, u32[]{:S(2)}, u32[]{:S(2)}) collective-permute-start(bf16[8,2,64,1536]{3,2,0,1:T(8,128)(2,1)} %fusion.13), channel_id=1, source_target_pairs={{0,8},{8,0},{16,24},{24,16},{1,9},{9,1},{17,25},{25,17},{2,10},{10... | collective-permute-start | bytes 9437192 | tf_op jit(solution)/shard_map/ppermute | solution.py:79
  554.0 60.6 %all-to-all-start.3 = ((bf16[8,64,1024]{2,1,0:T(8,128)(2,1)}), bf16[8,64,1024]{2,1,0:T(8,128)(2,1)}, u32[]{:S(2)}, u32[]{:S(2)}) async-start(bf16[8,64,1024]{2,1,0:T(8,128)(2,1)} %fusion.40), calls=%async_computation.3 | async-start | bytes 2097152 | tf_op jit(solution)/shard_map/all_to_all | solution.py:172
  559.8 25.4 %collective-permute-start.61 = (bf16[128,2048]{1,0:T(8,128)(2,1)S(1)}, bf16[128,2048]{1,0:T(8,128)(2,1)S(1)}, u32[]{:S(2)}, u32[]{:S(2)}) collective-permute-start(bf16[128,2048]{1,0:T(8,128)(2,1)S(1)} %fusion.45), channel_id=1, source_target_pairs={{0,2},{2,4},{4,6},{6,7},{7,5},{5,3},{3,1},{1,0},{8,10},{10,12},{12... | collective-permute-start | bytes 1572872 | tf_op jit(solution)/shard_map/ppermute | solution.py:37
  565.9 33.7 %collective-permute-start.64 = (bf16[64,2048]{1,0:T(8,128)(2,1)S(1)}, bf16[64,2048]{1,0:T(8,128)(2,1)S(1)}, u32[]{:S(2)}, u32[]{:S(2)}) collective-permute-start(bf16[64,2048]{1,0:T(8,128)(2,1)S(1)} %copy-done.39), channel_id=1, source_target_pairs={{2,0},{4,2},{6,4},{7,6},{5,7},{3,5},{1,3},{0,1},{10,8},{12,10},{14... | collective-permute-start | bytes 786440 | tf_op jit(solution)/shard_map/ppermute | solution.py:37
  598.2 37.6 %collective-permute-start.69 = (bf16[8,1,64,1536]{3,2,0,1:T(8,128)(2,1)}, bf16[8,1,64,1536]{3,2,0,1:T(8,128)(2,1)}, u32[]{:S(2)}, u32[]{:S(2)}) collective-permute-start(bf16[8,1,64,1536]{3,2,0,1:T(8,128)(2,1)} %dynamic-slice_convert_fusion), channel_id=1, source_target_pairs={{0,16},{8,24},{16,0},{24,8},{1,17},{9,25},{17,1},{25,9},{2,18},{10... | collective-permute-start | bytes 4718600 | tf_op jit(solution)/shard_map/ppermute | solution.py:79
  614.5 30.7 %collective-permute-start.72 = (bf16[2,128,2048]{2,1,0:T(8,128)(2,1)S(1)}, bf16[2,128,2048]{2,1,0:T(8,128)(2,1)S(1)}, u32[]{:S(2)}, u32[]{:S(2)}) collective-permute-start(bf16[2,128,2048]{2,1,0:T(8,128)(2,1)S(1)} %fusion.39), channel_id=1, source_target_pairs={{0,8},{8,0},{16,24},{24,16},{1,9},{9,1},{17,25},{25,17},{2,10},{10... | collective-permute-start | bytes 3145736 | tf_op jit(solution)/shard_map/ppermute | solution.py:79
  614.6 43.7 %collective-permute-start.83 = (bf16[8,1,64,1024]{3,2,0,1:T(8,128)(2,1)}, bf16[8,1,64,1024]{3,2,0,1:T(8,128)(2,1)}, u32[]{:S(2)}, u32[]{:S(2)}) collective-permute-start(bf16[8,1,64,1024]{3,2,0,1:T(8,128)(2,1)} %bitcast.65), channel_id=1, source_target_pairs={{0,16},{8,24},{16,0},{24,8},{1,17},{9,25},{17,1},{25,9},{2,18},{10... | collective-permute-start | bytes 3145736 | tf_op jit(solution)/shard_map/ppermute | solution.py:79
  620.4 30.4 %collective-permute-start.66 = (bf16[128,2048]{1,0:T(8,128)(2,1)S(1)}, bf16[128,2048]{1,0:T(8,128)(2,1)S(1)}, u32[]{:S(2)}, u32[]{:S(2)}) collective-permute-start(bf16[128,2048]{1,0:T(8,128)(2,1)S(1)} %fusion.43), channel_id=1, source_target_pairs={{2,0},{4,2},{6,4},{7,6},{5,7},{3,5},{1,3},{0,1},{10,8},{12,10},{14... | collective-permute-start | bytes 1572872 | tf_op jit(solution)/shard_map/ppermute | solution.py:37
  639.8 43.6 %all-to-all-start.2 = ((bf16[8,64,1536]{2,1,0:T(8,128)(2,1)}), bf16[8,64,1536]{2,1,0:T(8,128)(2,1)}, u32[]{:S(2)}, u32[]{:S(2)}) async-start(bf16[8,64,1536]{2,1,0:T(8,128)(2,1)} %fusion.27), calls=%async_computation.2 | async-start | bytes 3145728 | tf_op jit(solution)/shard_map/all_to_all | solution.py:172
  648.8 28.6 %collective-permute-start.63 = (bf16[128,2048]{1,0:T(8,128)(2,1)}, bf16[128,2048]{1,0:T(8,128)(2,1)S(1)}, u32[]{:S(2)}, u32[]{:S(2)}) collective-permute-start(bf16[128,2048]{1,0:T(8,128)(2,1)} %get-tuple-element.70), channel_id=1, source_target_pairs={{0,2},{2,4},{4,6},{6,7},{7,5},{5,3},{3,1},{1,0},{8,10},{10,12},{12... | collective-permute-start | bytes 1572872 | tf_op jit(solution)/shard_map/ppermute | solution.py:37
  652.1 25.3 %collective-permute-start.67 = (bf16[128,2048]{1,0:T(8,128)(2,1)S(1)}, bf16[128,2048]{1,0:T(8,128)(2,1)S(1)}, u32[]{:S(2)}, u32[]{:S(2)}) collective-permute-start(bf16[128,2048]{1,0:T(8,128)(2,1)S(1)} %fusion.44), channel_id=1, source_target_pairs={{2,0},{4,2},{6,4},{7,6},{5,7},{3,5},{1,3},{0,1},{10,8},{12,10},{14... | collective-permute-start | bytes 1572872 | tf_op jit(solution)/shard_map/ppermute | solution.py:37
  666.7 29.5 %collective-permute-start.74 = (bf16[1,128,2048]{2,1,0:T(8,128)(2,1)S(1)}, bf16[1,128,2048]{2,1,0:T(8,128)(2,1)}, u32[]{:S(2)}, u32[]{:S(2)}) collective-permute-start(bf16[1,128,2048]{2,1,0:T(8,128)(2,1)S(1)} %add_convert_fusion.5), channel_id=1, source_target_pairs={{0,16},{8,24},{16,0},{24,8},{1,17},{9,25},{17,1},{25,9},{2,18},{10... | collective-permute-start | bytes 1572872 | tf_op jit(solution)/shard_map/ppermute | solution.py:79
  683.4 48.4 %collective-permute-start.84 = (bf16[8,2,64,1024]{3,2,1,0:T(8,128)(2,1)}, bf16[8,2,64,1024]{3,2,1,0:T(8,128)(2,1)}, u32[]{:S(2)}, u32[]{:S(2)}) collective-permute-start(bf16[8,2,64,1024]{3,2,1,0:T(8,128)(2,1)} %maximum_bitcast_fusion.1), channel_id=1, source_target_pairs={{0,8},{8,0},{16,24},{24,16},{1,9},{9,1},{17,25},{25,17},{2,10},{10... | collective-permute-start | bytes 6291464 | tf_op jit(solution)/shard_map/ppermute | solution.py:79
  683.4 37.0 %collective-permute-start.70 = (bf16[8,1,64,1536]{3,2,0,1:T(8,128)(2,1)}, bf16[8,1,64,1536]{3,2,0,1:T(8,128)(2,1)S(1)}, u32[]{:S(2)}, u32[]{:S(2)}) collective-permute-start(bf16[8,1,64,1536]{3,2,0,1:T(8,128)(2,1)} %bitcast.32), channel_id=1, source_target_pairs={{0,16},{8,24},{16,0},{24,8},{1,17},{9,25},{17,1},{25,9},{2,18},{10... | collective-permute-start | bytes 4718600 | tf_op jit(solution)/shard_map/ppermute | solution.py:79
  700.5 28.6 %collective-permute-start.75 = (bf16[2,128,2048]{2,1,0:T(8,128)(2,1)S(1)}, bf16[2,128,2048]{2,1,0:T(8,128)(2,1)S(1)}, u32[]{:S(2)}, u32[]{:S(2)}) collective-permute-start(bf16[2,128,2048]{2,1,0:T(8,128)(2,1)S(1)} %maximum_bitcast_fusion.2), channel_id=1, source_target_pairs={{0,8},{8,0},{16,24},{24,16},{1,9},{9,1},{17,25},{25,17},{2,10},{10... | collective-permute-start | bytes 3145736 | tf_op jit(solution)/shard_map/ppermute | solution.py:79
  703.2 21.2 %collective-permute-start.79 = (f32[4,2048]{1,0:T(4,128)S(1)}, f32[4,2048]{1,0:T(4,128)S(1)}, u32[]{:S(2)}, u32[]{:S(2)}) collective-permute-start(f32[4,2048]{1,0:T(4,128)S(1)} %add.399), channel_id=1, source_target_pairs={{0,8},{8,0},{16,24},{24,16},{1,9},{9,1},{17,25},{25,17},{2,10},{10... | collective-permute-start | bytes 98312 | tf_op jit(solution)/shard_map/ppermute | solution.py:79
  724.4 38.1 %collective-permute-start.71 = (bf16[8,2,64,1536]{3,2,1,0:T(8,128)(2,1)}, bf16[8,2,64,1536]{3,2,1,0:T(8,128)(2,1)}, u32[]{:S(2)}, u32[]{:S(2)}) collective-permute-start(bf16[8,2,64,1536]{3,2,1,0:T(8,128)(2,1)} %maximum_bitcast_fusion), channel_id=1, source_target_pairs={{0,8},{8,0},{16,24},{24,16},{1,9},{9,1},{17,25},{25,17},{2,10},{10... | collective-permute-start | bytes 9437192 | tf_op jit(solution)/shard_map/ppermute | solution.py:79
  (103 other events, 1466.8 us)

commit v2 on v1

v2 whole, which is shorter than its diff:
```python
import math

import jax
import jax.numpy as jnp
from jax import lax
from jax.experimental import pallas as pl
from jax.experimental.pallas import tpu as pltpu
from jax.sharding import PartitionSpec as P

HEADS = 8
epsilon = 1e-05
head_epsilon = 1.0
f32 = jnp.float32
bf16 = jnp.bfloat16
BOTH = ("rep", "fsdp")
CORE, X = 3, 4


def dot(a, b, ca=1, cb=0, kind=f32):
    return lax.dot_general(a, b, (((ca,), (cb,)), ((), ())), preferred_element_type=kind)


def after(*values):
    return lax.optimization_barrier(values)


def shape(dims, kind):
    return jax.ShapeDtypeStruct(tuple(dims), kind)


def block(dims, *index):
    return pl.BlockSpec(dims, lambda *_: index)


def kernel(body, outs, *ins, scalars=None, scratch=(), limit=48):
    whole = pl.BlockSpec(memory_space=pltpu.VMEM)
    grid = (1,) if any(isinstance(i, tuple) for i in ins) else ()
    specs = [i[1] if isinstance(i, tuple) else whole for i in ins]
    ins = [i[0] if isinstance(i, tuple) else i for i in ins]
    if scalars is not None:
        specs = [pl.BlockSpec(memory_space=pltpu.SMEM)] + specs
        ins = [scalars] + ins
    return pl.pallas_call(
        body,
        out_shape=list(outs),
        grid=grid,
        in_specs=specs,
        out_specs=[whole] * len(outs),
        scratch_shapes=list(scratch),
        compiler_params=pltpu.CompilerParams(vmem_limit_bytes=limit << 20),
        cost_estimate=pl.CostEstimate(flops=0, bytes_accessed=0, transcendentals=0),
    )(*ins)


def number():
    return lax.axis_index("rep") * lax.axis_size("fsdp") + lax.axis_index("fsdp")


def bit(place):
    return (number() >> place) & 1


def bits():
    return (lax.axis_size("rep") * lax.axis_size("fsdp")).bit_length() - 1


def swap(value, place):
    count = 1 << bits()
    return lax.ppermute(value, BOTH, [(i, i ^ (1 << place)) for i in range(count)])


def spread(value):
    for place in range(CORE):
        other = swap(value, place)
        first = bit(place) == 0
        value = jnp.concatenate(
            [jnp.where(first, value, other), jnp.where(first, other, value)], 1
        )
    return value


RING = (0, 2, 4, 6, 7, 5, 3, 1)
OFFSETS = (0, -1, -2, -3, 1, 2, 3, 4)


def owners():
    place = jnp.array([RING.index(i) for i in range(HEADS)], jnp.int32)[lax.axis_index("fsdp")]
    return jnp.array(RING, jnp.int32)[(place + jnp.array(OFFSETS, jnp.int32)) % HEADS]


def send(value, ahead):
    pairs = [(RING[i], RING[(i + 1) % HEADS]) for i in range(HEADS)]
    return lax.ppermute(value, "fsdp", pairs if ahead else [(b, a) for a, b in pairs])


class Gather:
    def __init__(self, own):
        self.own, self.ahead, self.behind = own, [own], [own]

    def step(self, *others):
        a, b = self.ahead[-1], self.behind[-1]
        if len(self.ahead) == 4:
            rows = a.shape[0] // 2
            a, b = a[:rows], b[rows:]
        a, b, *others = after(send(a, True), send(b, False), *others)
        self.ahead.append(a)
        self.behind.append(b)
        return others

    def hold(self, *others):
        self.ahead[-1], self.behind[-1], *others = after(self.ahead[-1], self.behind[-1], *others)
        return others

    def pieces(self):
        return (self.own, *self.ahead[1:4], *self.behind[1:4], self.ahead[4], self.behind[4])


def tile(refs, i):
    names = ((0, 1), (2, 3), (4, 5), (6, 7, 8))[i]
    return jnp.concatenate([refs[j][...] for j in names], 0)


def term_shapes(rows, width):
    return [shape((7 * rows, width), bf16)] + [shape((rows // 2, width), bf16)] * 2


def put_tile(refs, i, values):
    both = values.shape[0]
    rows = both // 2
    values = values.astype(bf16)
    if i < 3:
        refs[0][i * both : (i + 1) * both] = values
    else:
        refs[0][3 * both : 3 * both + rows] = values[:rows]
        refs[1][...] = values[rows : rows + rows // 2]
        refs[2][...] = values[rows + rows // 2 :]


class Scatter:
    def __init__(self, terms):
        self.terms, self.a, self.b = terms
        self.steps = 0

    def term(self, offset):
        rows, width = self.terms.shape[0] // 7, self.terms.shape[1]
        return self.terms, block((rows, width), OFFSETS.index(offset), 0)

    def step(self, *others):
        if self.steps:
            self.fold(4 - self.steps)
        self.a, self.b, *others = after(send(self.a, True), send(self.b, False), *others)
        self.steps += 1
        return others

    def hold(self, *others):
        self.a, self.b, *others = after(self.a, self.b, *others)
        return others

    def fold(self, offset):
        rows, width = self.terms.shape[0] // 7, self.terms.shape[1]
        half = rows // 2

        def body(term_a, term_b, a, b, out_a, out_b):
            if a.shape[0] == rows:
                out_a[...] = (term_a[...].astype(f32) + a[...].astype(f32)).astype(bf16)
                out_b[...] = (term_b[...].astype(f32) + b[...].astype(f32)).astype(bf16)
            else:
                out_a[:half] = (term_a[:half].astype(f32) + a[...].astype(f32)).astype(bf16)
                out_a[half:] = term_a[half:]
                out_b[:half] = term_b[:half]
                out_b[half:] = (term_b[half:].astype(f32) + b[...].astype(f32)).astype(bf16)

        self.a, self.b = kernel(
            body,
            [shape((rows, width), bf16)] * 2,
            self.term(offset), self.term(-offset), self.a, self.b,
            limit=16,
        )

    def pieces(self):
        return self.term(0), self.a, self.b


def total(refs):
    return refs[0][...].astype(f32) + refs[1][...].astype(f32) + refs[2][...].astype(f32)


def normalize(values):
    center = values - jnp.mean(values, axis=-1, keepdims=True)
    scale = lax.rsqrt(jnp.mean(center * center, axis=-1, keepdims=True) + epsilon)
    return center * scale, scale


def normalize_back(normed, scale, grad):
    return scale * (
        grad
        - jnp.mean(grad, axis=-1, keepdims=True)
        - normed * jnp.mean(grad * normed, axis=-1, keepdims=True)
    )


def head_norm(values):
    center = values - jnp.mean(values, axis=-1, keepdims=True)
    scale = lax.rsqrt(jnp.mean(center * center, axis=-1, keepdims=True) + head_epsilon)
    return center * scale, scale


def on_device(
    tokens,
    w_query,
    w_key,
    w_value,
    w_gate,
    w_out,
    norm1_gain,
    norm1_bias,
    w_ffn_gate,
    w_ffn_up,
    w_ffn_down,
    norm2_gain,
    norm2_bias,
    cotangent,
):
    n = lax.axis_size("fsdp")
    assert n == HEADS
    rows, width = tokens.shape
    depth = w_query.shape[0]
    half_depth = depth // 2
    dk = w_query.shape[1] // n
    dv = w_value.shape[1] // n
    ff = w_ffn_gate.shape[1] // n
    every = n * rows
    half_width = width // 2
    where = jnp.stack([bit(CORE), bit(X)])


    def fetch(*weights):
        sizes = [w.shape[1] // n // 2 for w in weights]
        whole = sum(sizes)

        def body(s, *refs):
            start = 0
            for ref, size in zip(refs, sizes):
                refs[-1][0, :, start : start + size] = ref[...]
                start += size

        packed = pl.pallas_call(
            body,
            out_shape=shape((n, half_depth, whole), bf16),
            grid_spec=pltpu.PrefetchScalarGridSpec(
                num_scalar_prefetch=1,
                grid=(n,),
                in_specs=[
                    pl.BlockSpec((half_depth, size), lambda k, s: (s[0], 2 * k + s[1]))
                    for size in sizes
                ],
                out_specs=pl.BlockSpec((1, half_depth, whole), lambda k, s: (k, 0, 0)),
            ),
            cost_estimate=pl.CostEstimate(flops=0, bytes_accessed=0, transcendentals=0),
        )(where, *weights)
        return packed

    def trade(packed):
        got = lax.all_to_all(packed, "fsdp", 0, 0, tiled=True)
        return got.reshape(n * half_depth, got.shape[-1])

    def more(value):
        for place in range(X + 1, bits()):
            value = value + swap(value.astype(bf16), place).astype(f32)
        return value

    def sum_cores(kept, given):
        size = n * half_depth
        kept = kept[:size].astype(f32) + swap(kept[size:], CORE).astype(f32)
        given = given[:size].astype(f32) + swap(given[size:], CORE).astype(f32)
        return kept, given.astype(bf16)

    def give(kept, got):
        grad = more(kept + got.astype(f32)).astype(bf16)
        grad = grad.reshape(n, half_depth, grad.shape[-1])
        return lax.all_to_all(grad, "fsdp", 0, 0, tiled=True)

    def everywhere(own):
        other = swap(own, X)
        return own, swap(own, CORE), other, swap(other, CORE)

    def flat(pieces, sizes):
        whole = sum(sizes) // 2

        def body(s, own, own_c, other, other_c, *outs):
            here = pl.ds(s[0] * half_depth, half_depth)
            there = pl.ds((1 - s[0]) * half_depth, half_depth)
            start = 0
            for out, size in zip(outs, sizes):
                half = size // 2
                columns = slice(start, start + half)
                for x, a, b in ((s[1], own, own_c), (1 - s[1], other, other_c)):
                    place = pl.ds(pl.multiple_of(x * half, half), half)
                    out[here, place] = a[0, :, columns].astype(f32)
                    out[there, place] = b[0, :, columns].astype(f32)
                start += half

        return pl.pallas_call(
            body,
            out_shape=[shape((depth, n * size), f32) for size in sizes],
            grid_spec=pltpu.PrefetchScalarGridSpec(
                num_scalar_prefetch=1,
                grid=(n,),
                in_specs=[pl.BlockSpec((1, half_depth, whole), lambda k, s: (k, 0, 0))] * 4,
                out_specs=[pl.BlockSpec((depth, size), lambda k, s: (0, k)) for size in sizes],
            ),
            cost_estimate=pl.CostEstimate(flops=0, bytes_accessed=0, transcendentals=0),
        )(where, *pieces)


    def sum_cores_rows(grad):
        size = grad.shape[0] // 4
        grad = grad.reshape(2, 2, size, grad.shape[1])
        core = bit(CORE)
        given = lax.dynamic_index_in_dim(grad, 1 - core, 1, False)
        kept = lax.dynamic_index_in_dim(grad, core, 1, False)
        grad = kept.astype(f32) + swap(given, CORE).astype(f32)
        return grad[0], grad[1].astype(bf16)

    def give_rows(kept, got):
        return more(kept + got.astype(f32)).astype(bf16)

    def flat_rows(pieces):
        size = pieces[0].shape[0]

        def body(s, own, own_c, other, other_c, out):
            for x, a, b in ((s[1], own, own_c), (1 - s[1], other, other_c)):
                out[pl.ds((2 * x + s[0]) * size, size), :] = a[...].astype(f32)
                out[pl.ds((2 * x + 1 - s[0]) * size, size), :] = b[...].astype(f32)

        (out,) = kernel(
            body, [shape((4 * size, pieces[0].shape[1]), f32)], *pieces, scalars=where, limit=24
        )
        return out


    def arranged(s):
        for i in range(2 * n):
            column = ((i % n) * 2 + (s[0] ^ (i // n))) * half_depth
            yield i * half_depth, pl.ds(pl.multiple_of(column, half_depth), half_depth)

    block_f32 = shape((rows, width), f32)
    block_bf16 = shape((rows, width), bf16)
    pair_f32 = shape((2, width), f32)
    room_of_block = [pltpu.VMEM((rows, width), f32)]

    def first_norm(s, *refs):
        parts, gains, z, room = refs[:-3], refs[-3], refs[-2], refs[-1]
        values = jnp.concatenate([part[...] for part in parts], 0).astype(f32)
        normed, _ = normalize(values)
        room[...] = normed * gains[0:1] + gains[1:2]
        for start, columns in arranged(s):
            z[:, start : start + half_depth] = room[:, columns].astype(bf16)

    def second_norm(s, *refs):
        sums, (tokens, gains, resid, z, room) = refs[:3], refs[3:]
        value = tokens[...].astype(f32) + total(sums)
        resid[...] = value
        normed, _ = normalize(value)
        room[...] = normed * gains[2:3] + gains[3:4]
        for start, columns in arranged(s):
            z[:, start : start + half_depth] = room[:, columns].astype(bf16)

    def norm_back(s, refs, inputs, gain, room, sums):
        grad = total(refs)
        for start, columns in arranged(s):
            room[:, columns] = grad[:, start : start + half_depth]
        grad = room[...]
        normed, scale = normalize(inputs)
        sums[0:1] = jnp.sum(grad * normed, axis=0, keepdims=True)
        sums[1:2] = jnp.sum(grad, axis=0, keepdims=True)
        return normalize_back(normed, scale, grad * gain)

    def second_back(s, *refs):
        parts, (resid, cot, gains, grad_resid, sums, out, room) = refs[:3], refs[3:]
        grad = norm_back(s, parts, resid[...], gains[2:3], room, sums)
        grad = grad + cot[...].astype(f32)
        grad_resid[...] = grad
        out[...] = grad.astype(bf16)

    def first_back(s, *refs):
        parts, (tokens, grad_resid, gains, out, sums, room) = refs[:3], refs[3:]
        grad = norm_back(s, parts, tokens[...].astype(f32), gains[0:1], room, sums)
        out[...] = grad_resid[...] + grad

    def last_sum(*refs):
        parts, resid, out = refs[:3], refs[3], refs[4]
        out[...] = (resid[...] + total(parts)).astype(bf16)


    tiles = range(4)
    halves = (slice(0, half_width), slice(half_width, width))

    def rows_of(i):
        return slice(2 * i * rows, 2 * (i + 1) * rows)

    def in_order(x, own, other):
        first = jnp.where(x == 0, own, other)
        second = jnp.where(x == 0, other, own)
        return first, second

    def project(s, *refs):
        zs, w, (cosine, sine, q, k, v, g) = refs[:4], refs[4:8], refs[8:]
        x = s[1]
        one = dk // 2
        for i in tiles:
            here = rows_of(i)
            own, other = (
                dot(zs[i][:, halves[0]], w[j][...]) + dot(zs[i][:, halves[1]], w[2 + j][...])
                for j in (0, 1)
            )
            c, sn = cosine[here], sine[here]
            a, b = in_order(x, own[:, :one], other[:, :one])
            q[here, :one] = (a * c - b * sn).astype(bf16)
            q[here, one:] = (b * c + a * sn).astype(bf16)
            a, b = in_order(x, own[:, one:dk], other[:, one:dk])
            k[here, :one] = ((a * c - b * sn) * dk**-0.5).astype(bf16)
            k[here, one:] = ((b * c + a * sn) * dk**-0.5).astype(bf16)
            middle = dk + dv // 2
            v[here, : dv // 2] = own[:, dk:middle].astype(bf16)
            v[here, dv // 2 :] = other[:, dk:middle].astype(bf16)
            g[here, : dv // 2] = own[:, middle:]
            g[here, dv // 2 :] = other[:, middle:]

    def of_x(ref, x, size):
        return [ref[pl.ds(pl.multiple_of(i * size, size), size), :] for i in (x, 1 - x)]

    def mix(s, q, k, v, decay, g, w, p, retained, mixed, *outs):
        for i in tiles:
            here = rows_of(i)
            scores = (dot(q[here], k[...], 1, 1) * decay[here]).astype(bf16)
            p[here] = scores
            value = dot(scores, v[...])
            retained[here] = value
            normed, _ = head_norm(value)
            gate = g[here]
            part = (normed * gate / (1.0 + jnp.exp(-gate))).astype(bf16)
            mixed[here] = part
            half = dv // 2
            own, other = of_x(w, s[1], half)
            put_tile(outs, i, dot(part[:, :half], own) + dot(part[:, half:], other))

    def hidden_back(s, *refs):
        pieces, (w, cot, d_hidden) = refs[:9], refs[9:]
        half = ff // 2
        for i in tiles:
            here = rows_of(i)
            part = tile(pieces, i)
            cot[here] = part
            own, other = of_x(w, s[1], half)
            d_hidden[here, :half] = dot(part, own, 1, 1).astype(bf16)
            d_hidden[here, half:] = dot(part, other, 1, 1).astype(bf16)

    def feed(*refs):
        pieces, d_hidden, w, (z, hidden, grad) = refs[:9], refs[9], refs[10:14], refs[14:17]
        outs = refs[17:]
        half = ff // 2
        for i in tiles:
            here = rows_of(i)
            part = tile(pieces, i)
            z[here] = part
            back = 0.0
            for j in (0, 1):
                ab = dot(part[:, halves[0]], w[j][...]) + dot(part[:, halves[1]], w[2 + j][...])
                a, b = ab[:, :half], ab[:, half:]
                below = 0.5 * (1.0 + lax.erf(a * math.sqrt(0.5)))
                gelu = a * below
                slope = below + a * jnp.exp(-0.5 * a * a) * (1.0 / math.sqrt(2.0 * math.pi))
                columns = slice(j * half, (j + 1) * half)
                hidden[here, columns] = (gelu * b).astype(bf16)
                d = d_hidden[here, columns].astype(f32)
                both = jnp.concatenate([d * b * slope, d * gelu], -1).astype(bf16)
                grad[j, here] = both
                back = back + jnp.concatenate(
                    [dot(both, w[j][...], 1, 1), dot(both, w[2 + j][...], 1, 1)], -1
                )
            put_tile(outs, i, back)

    def down(s, h, w, *outs):
        half = ff // 2
        for i in tiles:
            here = rows_of(i)
            own, other = of_x(w, s[1], half)
            put_tile(outs, i, dot(h[here, :half], own) + dot(h[here, half:], other))

    def mix_back(s, *refs):
        pieces, (w, r, g, d_out, d_retained, d_gate) = refs[:9], refs[9:]
        half = dv // 2
        for i in tiles:
            here = rows_of(i)
            part = tile(pieces, i)
            d_out[here] = part
            own, other = of_x(w, s[1], half)
            d_mixed = jnp.concatenate([dot(part, own, 1, 1), dot(part, other, 1, 1)], -1)
            d_mixed = d_mixed.astype(bf16).astype(f32)
            normed, scale = head_norm(r[here])
            gate = g[here]
            sigmoid = 1.0 / (1.0 + jnp.exp(-gate))
            d_gate[here] = (d_mixed * normed * sigmoid * (1.0 + gate * (1.0 - sigmoid))).astype(bf16)
            d_retained[here] = normalize_back(normed, scale, d_mixed * gate * sigmoid).astype(bf16)

    def within_back(s, d_r, d_g, q, k, v, p, decay, cosine, sine, *refs):
        w, wg, d_pre, outs, (d_k, d_v) = refs[:4], refs[4:8], refs[8], refs[9:12], refs[12:]
        one, half = dk // 2, dv // 2
        x = s[1]
        for i in tiles:
            here = rows_of(i)
            scores = (dot(d_r[here], v[...], 1, 1) * decay[here]).astype(bf16)
            c, sn = cosine[here], sine[here]
            grad = dot(scores, k[...])
            a, b = grad[:, :one], grad[:, one:]
            own, other = in_order(x, a * c + b * sn, b * c - a * sn)
            d_pre[0, here, :one] = own.astype(bf16)
            d_pre[1, here, :one] = other.astype(bf16)
            more_k, more_v = dot(scores, q[here], 0, 0), dot(p[here], d_r[here], 0, 0)
            if i == 0:
                d_k[...], d_v[...] = more_k, more_v
            else:
                d_k[...] += more_k
                d_v[...] += more_v
        for i in tiles:
            here = rows_of(i)
            c, sn = cosine[here] * dk**-0.5, sine[here] * dk**-0.5
            a, b = d_k[here, :one], d_k[here, one:]
            own, other = in_order(x, a * c + b * sn, b * c - a * sn)
            d_pre[0, here, one:dk] = own.astype(bf16)
            d_pre[1, here, one:dk] = other.astype(bf16)
            d_pre[0, here, dk:] = d_v[here, :half].astype(bf16)
            d_pre[1, here, dk:] = d_v[here, half:].astype(bf16)
            back = []
            for t in (0, 1):
                part = dot(d_g[here, :half], wg[2 * t][...], 1, 1)
                part = part + dot(d_g[here, half:], wg[2 * t + 1][...], 1, 1)
                for j in (0, 1):
                    part = part + dot(d_pre[j, here], w[2 * t + j][...], 1, 1)
                back.append(part)
            put_tile(outs, i, jnp.concatenate(back, -1))

    terms = term_shapes(rows, width)


    gains = jnp.stack([norm1_gain, norm1_bias, norm2_gain, norm2_bias])
    gains = spread(gains).astype(f32)
    packed, tokens_late = after(fetch(w_query, w_key, w_value, w_gate), tokens)
    mix_own = trade(packed)
    ring = Gather(tokens_late)

    head = lax.axis_index("fsdp")
    gamma_log = jnp.log(1.0 - 2.0 ** (-5.0 - head.astype(f32)))
    positions = (owners() * rows)[:, None] + jnp.arange(rows, dtype=jnp.int32)[None, :]
    positions = positions.reshape(-1).astype(f32)
    half = dk // 2
    freqs = jnp.exp(-jnp.arange(half, dtype=f32) * (math.log(10000.0) / half))
    angles = positions[:, None] * freqs[None, :]
    cosine, sine = jnp.cos(angles), jnp.sin(angles)
    differ = positions[:, None] - positions[None, :]
    decay = jnp.where(differ >= 0, jnp.exp(jnp.maximum(differ, 0.0) * gamma_log), 0.0)

    (mix_own,) = ring.step(mix_own)
    mix_other = swap(mix_own, X)
    mix_own_c = swap(mix_own, CORE)
    ring.step()
    ring.step()
    cosine, sine, decay = ring.step(cosine, sine, decay)
    pieces = ring.pieces()
    zs = []
    for i in tiles:
        names = ((0, 1), (2, 3), (4, 5), (6, 7, 8))[i]
        zs += kernel(
            first_norm,
            [shape((2 * rows, width), bf16)],
            *(pieces[j] for j in names), gains,
            scalars=where, scratch=[pltpu.VMEM((2 * rows, width), f32)], limit=16,
        )
    mix_other_c = swap(mix_other, CORE)
    w_mix = (mix_own, mix_other, mix_own_c, mix_other_c)
    *w_mix, z0, z1, z2, z3, ffn_gate_late, ffn_up_late = after(*w_mix, *zs, w_ffn_gate, w_ffn_up)
    zs = (z0, z1, z2, z3)
    ffn_own = trade(fetch(ffn_gate_late, ffn_up_late))
    query, key, value, gate = kernel(
        project,
        [shape((every, dk), bf16)] * 2 + [shape((every, dv), bf16), shape((every, dv), f32)],
        *zs, *w_mix, cosine, sine,
        scalars=where,
    )
    scores, retained, mixed, *parts = kernel(
        mix,
        [shape((every, every), bf16), shape((every, dv), f32), shape((every, dv), bf16)] + terms,
        query, key, value, decay, gate, w_out,
        scalars=where,
    )
    ring = Scatter(parts)
    cot_late, ffn_own = ring.hold(cotangent, ffn_own)
    ffn_other = swap(ffn_own, X)
    ffn_own_c = swap(ffn_own, CORE)
    cot_ring = Gather(cot_late)
    ring.step()
    cot_ring.step()
    ring.step()
    cot_ring.step()
    ring.step()
    cot_ring.step()
    ring.step()
    resid, second = kernel(
        second_norm, [block_f32, block_bf16], *ring.pieces(), tokens, gains,
        scalars=where, scratch=room_of_block, limit=16,
    )

    ring = Gather(second)
    (ffn_other,) = ring.step(ffn_other)
    ffn_other_c = swap(ffn_other, CORE)
    cot_ring.step()
    cot_all, d_hidden = kernel(
        hidden_back,
        [shape((every, width), bf16), shape((every, ff), bf16)],
        *cot_ring.pieces(), w_ffn_down,
        scalars=where,
    )
    ring.step()
    ring.step()
    w_ffn = (ffn_own, ffn_other, ffn_own_c, ffn_other_c)
    *w_ffn, d_hidden = ring.step(*w_ffn, d_hidden)
    z_second, hidden, d_ab, *parts = kernel(
        feed,
        [shape((every, width), bf16), shape((every, ff), bf16), shape((2, every, ff), bf16)]
        + terms,
        *ring.pieces(), d_hidden, *w_ffn,
    )
    ring = Scatter(parts)
    ring.step()
    grad_ffn = [dot(z_second, d_ab[j], 0, 0, bf16) for j in (0, 1)]
    grad_down = dot(hidden, cot_all, 0, 0, bf16)
    (grad_down, *grad_ffn) = ring.step(grad_down, *grad_ffn)
    down_kept, down_given = sum_cores_rows(grad_down)
    ffn_kept, ffn_given = sum_cores(*grad_ffn)
    ring.step()
    ring.step()
    grad_resid, second_sums, part = kernel(
        second_back, [block_f32, pair_f32, block_bf16],
        *ring.pieces(), resid, cotangent, gains,
        scalars=where, scratch=room_of_block, limit=16,
    )
    ring = Gather(part)
    ffn_given, ffn_kept, down_given, down_kept = ring.step(
        ffn_given, ffn_kept, down_given, down_kept
    )
    ffn_sent = swap(ffn_given, X)
    down_sent = swap(down_given, X)
    ring.step()
    ring.step()
    ffn_sent, down_sent, w_down_late = ring.step(ffn_sent, down_sent, w_ffn_down)

    ffn_owned = give(ffn_kept, ffn_sent)
    down_owned = give_rows(down_kept, down_sent)
    d_out, d_retained, d_gate = kernel(
        mix_back,
        [shape((every, width), bf16)] + [shape((every, dv), bf16)] * 2,
        *ring.pieces(), w_out, retained, gate,
        scalars=where,
    )
    z_first = jnp.concatenate(zs)
    w_qkv = [w[:, : dk + dv // 2] for w in w_mix]
    w_g = [w[:, dk + dv // 2 :] for w in w_mix]
    d_pre, *parts = kernel(
        within_back,
        [shape((2, every, dk + dv // 2), bf16)] + terms,
        d_retained, d_gate, query, key, value, scores, decay, cosine, sine, *w_qkv, *w_g,
        scalars=where, scratch=[pltpu.VMEM((every, dk), f32), pltpu.VMEM((every, dv), f32)],
    )
    grad_gate = [
        dot(z_first, d_gate[:, j * (dv // 2) : (j + 1) * (dv // 2)], 0, 0, bf16) for j in (0, 1)
    ]
    gate_kept, gate_given = sum_cores(*grad_gate)
    gate_owned = give(gate_kept, swap(gate_given, X))
    ring = Scatter(parts)
    grad_qkv = [dot(z_first, d_pre[j], 0, 0, bf16) for j in (0, 1)]
    qkv_kept, qkv_given = sum_cores(*grad_qkv)
    qkv_owned = give(qkv_kept, swap(qkv_given, X))
    out_kept, out_given = sum_cores_rows(dot(mixed, d_out, 0, 0, bf16))
    out_owned = give_rows(out_kept, swap(out_given, X))
    ring.step()
    ring.step()
    ring.step()
    ring.step()
    grad_tokens, first_sums = kernel(
        first_back, [block_f32, pair_f32], *ring.pieces(), tokens, grad_resid, gains,
        scalars=where, scratch=room_of_block, limit=16,
    )
    last = Scatter(
        kernel(down, terms, hidden, w_down_late, scalars=where)
    )
    last.hold(d_pre)
    for _ in range(4):
        last.step()
    (output,) = kernel(last_sum, [block_bf16], *last.pieces(), resid, limit=16)
    stack = jnp.concatenate([first_sums, second_sums])
    for place in range(bits()):
        stack = stack + swap(stack, place)
    stack = lax.dynamic_slice_in_dim(stack, lax.axis_index("fsdp") * depth, depth, 1)
    grad_ffn_gate, grad_ffn_up = flat(everywhere(ffn_owned), [ff, ff])
    grad_down = flat_rows(everywhere(down_owned))
    (grad_gate,) = flat(everywhere(gate_owned), [dv])
    grad_query, grad_key, grad_value = flat(everywhere(qkv_owned), [dk, dk, dv])
    grad_out = flat_rows(everywhere(out_owned))

    return (
        output,
        grad_tokens,
        grad_query,
        grad_key,
        grad_value,
        grad_gate,
        grad_out,
        stack[0],
        stack[1],
        grad_ffn_gate,
        grad_ffn_up,
        grad_down,
        stack[2],
        stack[3],
    )


def solution(mesh):
    tokens = P(("rep", "fsdp"), None)
    matrix = P("fsdp", None)
    vector = P("fsdp")
    in_specs = (tokens,) + (matrix,) * 5 + (vector,) * 2 + (matrix,) * 3 + (vector,) * 2 + (tokens,)
    out_specs = (tokens,) * 2 + (matrix,) * 5 + (vector,) * 2 + (matrix,) * 3 + (vector,) * 2
    return jax.shard_map(
        on_device, mesh=mesh, in_specs=in_specs, out_specs=out_specs, check_vma=False
    )
```

time: 839 us -> 732 us (0.87)
  Pallas kernels: 0 us -> 137 us
  local copies, waits for them, and re-layouts: 134 us -> 51.4 us
  other arithmetic: 96.2 us -> 21 us
  matrix products: 84.3 us -> 25.1 us
  blocking collectives: 26.1 us -> 0 us
  starting transfers between devices: 129 us -> 145 us
  waiting for transfers between devices: 352 us -> 339 us
    pallas_call x0 -> x34, Pallas kernels: none -> 137 us  [the longest x29 102 us: kernel(): pl.pallas_call(body, out_shape=list(outs), grid=grid, in_specs=specs, out...]
    dot_general x18 -> x8, matrix products: 84.3 us -> 25.1 us  [dot(): lax.dot_general(a, b, (((ca,), (cb,)), ((), ())), preferred_element_type=...]
    slice x22, local copies, waits for them, and re-layouts: 49.3 us -> 18.1 us  [the longest x4 9.06 us: on_device(): w_qkv = [w[:, :dk + dv // 2] for w in w_mix]]
    all_to_all x4 -> x5, waiting for transfers between devices: 35.7 us -> 7.96 us  [the longest x3 7.96 us: give(): return lax.all_to_all(grad, 'fsdp', 0, 0, tiled=True)]
    all_gather x1 -> x0, blocking collectives: 26.1 us -> none  [on_device(): gains = lax.all_gather(gains, 'fsdp', axis=1, tiled=True).astype(f32)]
    convert_element_type x30 -> x10, other arithmetic: 33.5 us -> 9.4 us  [the longest x3 5 us: give(): grad = more(kept + got.astype(f32)).astype(bf16)]
    convert_element_type x12 -> x2, local copies, waits for them, and re-layouts: 23.2 us -> 0.92 us  [sum_cores_rows(): return (grad[0], grad[1].astype(bf16))]
    unnamed x158 -> x179, local copies, waits for them, and re-layouts: 48.9 us -> 27 us
  transfers between devices with their start and end apart: 93 -> 111, of which waited for: 48 -> 51; matrix products, arithmetic and copies ran while one was open for 21% -> 9% of each run, Pallas kernels for 0% -> 10%
where the time goes in v2:
time: 732 us; the launch traced here: 722 us
  waiting for transfers between devices  339 us (46%)
  starting transfers between devices  145 us (20%)
  Pallas kernels  137 us (19%)
  local copies, waits for them, and re-layouts  51.4 us (7%)
  matrix products  25.1 us (3%)
  other arithmetic  21 us (3%)
    ppermute x64, waiting for transfers between devices, send(): lax.ppermute(value, 'fsdp', pairs if ahead else [(b, a) for a, b in pairs])  235 us
    pallas_call x29, Pallas kernels, kernel(): pl.pallas_call(body, out_shape=list(outs), grid=grid, in_specs=specs, out...  102 us
    ppermute x42, waiting for transfers between devices, swap(): lax.ppermute(value, BOTH, [(i, i ^ 1 << place) for i in range(count)])  96.6 us
    ppermute x64, starting transfers between devices, send(): lax.ppermute(value, 'fsdp', pairs if ahead else [(b, a) for a, b in pairs])  80.2 us
    ppermute x42, starting transfers between devices, swap(): lax.ppermute(value, BOTH, [(i, i ^ 1 << place) for i in range(count)])  39.6 us
    unnamed x179, local copies, waits for them, and re-layouts  27 us
    dot_general x8, matrix products, dot(): lax.dot_general(a, b, (((ca,), (cb,)), ((), ())), preferred_element_type=...  25.1 us
    pallas_call x3, Pallas kernels, flat(): pl.pallas_call(body, out_shape=[shape((depth, n * size), f32) for size in...  22.9 us
  transfers between devices with their start and end apart: 111, of which 51 were waited for; matrix products, arithmetic and copies ran while one was open for 9% of the time, Pallas kernels for 10%

profile of v2, /device:TPU:0, one launch (start us, length us, event | category | flops | bytes accessed | tf_op | source)
XLA Modules:
  0.0 721.7 jit_solution(2372373410870839057)
XLA Ops:
  1.2 6.1 shard_map.272
  7.4 7.4 %all-to-all-start = ((bf16[8,128,768]{2,1,0:T(8,128)(2,1)}), bf16[8,128,768]{2,1,0:T(8,128)(2,1)}, u32[]{:S(2)}, u32[]{:S(2)}) async-start(bf16[8,128,768]{2,1,0:T(8,128)(2,1)} %shard_map.272), calls=%async_computation | async-start | bytes 3145728 | tf_op jit(solution)/shard_map/all_to_all | solution.py:264
  16.9 35.4 %collective-permute-done.refs_1_ = bf16[128,2048]{1,0:T(8,128)(2,1)S(1)} collective-permute-done((bf16[128,2048]{1,0:T(8,128)(2,1)S(1)}, bf16[128,2048]{1,0:T(8,128)(2,1)S(1)}, u32[]{:S(2)}, u32[]{:S(2)}) %collective-permute-start) | collective-permute-done | bytes 524320 | tf_op jit(solution)/shard_map/ppermute | solution.py:93
  59.0 10.0 %collective-permute-start.8 = (bf16[128,2048]{1,0:T(8,128)(2,1)S(1)}, bf16[128,2048]{1,0:T(8,128)(2,1)S(1)}, u32[]{:S(2)}, u32[]{:S(2)}) collective-permute-start(bf16[128,2048]{1,0:T(8,128)(2,1)S(1)} %collective-permute-done.refs_1_), channel_id=1, source_target_pairs={{0,2},{2,4},{4,6},{6,7},{7,5},{5,3},{3,1},{1,0},{8,10},{10,12},{12... | collective-permute-start | bytes 1572872 | tf_op jit(solution)/shard_map/ppermute | solution.py:93
  69.0 19.2 %collective-permute-done.2.refs_5_ = bf16[1024,768]{1,0:T(8,128)(2,1)} collective-permute-done((bf16[1024,768]{1,0:T(8,128)(2,1)}, bf16[1024,768]{1,0:T(8,128)(2,1)}, u32[]{:S(2)}, u32[]{:S(2)}) %collective-permute-start.2) | collective-permute-done | bytes 1572896 | tf_op jit(solution)/shard_map/ppermute | solution.py:69
  91.2 10.9 %collective-permute-start.6 = (bf16[4,512]{1,0:T(4,128)(2,1)S(1)}, bf16[4,512]{1,0:T(4,128)(2,1)S(1)}, u32[]{:S(2)}, u32[]{:S(2)}) collective-permute-start(bf16[4,512]{1,0:T(4,128)(2,1)S(1)} %pad_maximum_fusion.2), channel_id=1, source_target_pairs={{0,2},{1,3},{2,0},{3,1},{4,6},{5,7},{6,4},{7,5},{8,10},{9,11},{10,... | collective-permute-start | bytes 12296 | tf_op jit(solution)/shard_map/ppermute | solution.py:69
  109.7 6.7 collective-permute-done.10.refs_1_
  130.5 5.7 shard_map.279
  136.2 4.9 all-to-all-start.1
  141.1 11.5 %shard_map.277 = (bf16[1024,256]{1,0:T(8,128)(2,1)S(1)}, bf16[1024,256]{1,0:T(8,128)(2,1)S(1)}, bf16[1024,512]{1,0:T(8,128)(2,1)S(1)}, f32[1024,512]{1,0:T(8,128)}) custom-call(s32[2]{0:T(128)S(1)} %copy-done.47, bf16[256,2048]{1,0:T(8,128)(2,1)S(1)} %shard_map.273.refs_0_, bf16[256,2048]{1,0:T(8,128)(2,1)S(1)} %shard_map.274.refs_1_, ...), custom_call_target="tpu_custom_call" | custom-call | tf_op jit(solution)/shard_map/pallas_call | solution.py:43
  152.6 10.6 %shard_map.278 = (bf16[1024,1024]{1,0:T(8,128)(2,1)S(1)}, f32[1024,512]{1,0:T(8,128)}, bf16[1024,512]{1,0:T(8,128)(2,1)S(1)}, bf16[896,2048]{1,0:T(8,128)(2,1)},...) custom-call(s32[2]{0:T(128)S(1)} %copy-done.47, bf16[1024,256]{1,0:T(8,128)(2,1)S(1)} %get-tuple-element.201.q, ...), custom_call_target="tpu_custom_call" | custom-call | tf_op jit(solution)/shard_map/pallas_call | solution.py:43
  170.9 5.4 collective-permute-done.14.a
  181.7 9.2 %collective-permute-done.16.a = bf16[128,2048]{1,0:T(8,128)(2,1)S(1)} collective-permute-done((bf16[128,2048]{1,0:T(8,128)(2,1)S(1)}, bf16[128,2048]{1,0:T(8,128)(2,1)S(1)}, u32[]{:S(2)}, u32[]{:S(2)}) %collective-permute-start.16) | collective-permute-done | bytes 524320 | tf_op jit(solution)/shard_map/ppermute | solution.py:93
  194.5 8.9 %collective-permute-done.18.a = bf16[128,2048]{1,0:T(8,128)(2,1)S(1)} collective-permute-done((bf16[128,2048]{1,0:T(8,128)(2,1)S(1)}, bf16[128,2048]{1,0:T(8,128)(2,1)S(1)}, u32[]{:S(2)}, u32[]{:S(2)}) %collective-permute-start.18) | collective-permute-done | bytes 524320 | tf_op jit(solution)/shard_map/ppermute | solution.py:93
  210.9 8.8 %collective-permute-done.20.refs_1_ = bf16[128,2048]{1,0:T(8,128)(2,1)S(1)} collective-permute-done((bf16[128,2048]{1,0:T(8,128)(2,1)S(1)}, bf16[128,2048]{1,0:T(8,128)(2,1)S(1)}, u32[]{:S(2)}, u32[]{:S(2)}) %collective-permute-start.20) | collective-permute-done | bytes 524320 | tf_op jit(solution)/shard_map/ppermute | solution.py:93
  225.7 5.2 collective-permute-done.33.refs_1_
  234.7 7.5 %collective-permute-done.22.refs_1_ = bf16[128,2048]{1,0:T(8,128)(2,1)S(1)} collective-permute-done((bf16[128,2048]{1,0:T(8,128)(2,1)S(1)}, bf16[128,2048]{1,0:T(8,128)(2,1)S(1)}, u32[]{:S(2)}, u32[]{:S(2)}) %collective-permute-start.22) | collective-permute-done | bytes 524320 | tf_op jit(solution)/shard_map/ppermute | solution.py:93
  245.9 7.5 %collective-permute-done.35.refs_2_ = bf16[128,2048]{1,0:T(8,128)(2,1)S(1)} collective-permute-done((bf16[128,2048]{1,0:T(8,128)(2,1)S(1)}, bf16[128,2048]{1,0:T(8,128)(2,1)S(1)}, u32[]{:S(2)}, u32[]{:S(2)}) %collective-permute-start.35) | collective-permute-done | bytes 524320 | tf_op jit(solution)/shard_map/ppermute | solution.py:93
  257.2 7.2 collective-permute-done.25.refs_2_
  267.0 5.4 collective-permute-done.37.refs_3_
  275.2 8.5 %collective-permute-done.27.refs_3_ = bf16[128,2048]{1,0:T(8,128)(2,1)S(1)} collective-permute-done((bf16[128,2048]{1,0:T(8,128)(2,1)S(1)}, bf16[128,2048]{1,0:T(8,128)(2,1)S(1)}, u32[]{:S(2)}, u32[]{:S(2)}) %collective-permute-start.27) | collective-permute-done | bytes 524320 | tf_op jit(solution)/shard_map/ppermute | solution.py:93
  292.7 5.8 shard_map.284
  300.9 14.9 %shard_map.285 = (bf16[1024,2048]{1,0:T(8,128)(2,1)}, bf16[1024,512]{1,0:T(8,128)(2,1)S(1)}, bf16[2,1024,512]{2,1,0:T(8,128)(2,1)}, bf16[896,2048]{1,0:T(8,128)(...) custom-call(bf16[128,2048]{1,0:T(8,128)(2,1)S(1)} %get-tuple-element.227.refs_0_, ...), custom_call_target="tpu_custom_call" | custom-call | tf_op jit(solution)/shard_map/pallas_call | solution.py:43
  317.9 5.0 fusion.11
  332.8 6.4 collective-permute-done.43.a
  361.2 6.0 collective-permute-done.47.refs_1_
  380.6 5.5 collective-permute-done.49.refs_1_
  391.0 10.3 %collective-permute-done.54.refs_2_ = bf16[128,2048]{1,0:T(8,128)(2,1)S(1)} collective-permute-done((bf16[128,2048]{1,0:T(8,128)(2,1)S(1)}, bf16[128,2048]{1,0:T(8,128)(2,1)S(1)}, u32[]{:S(2)}, u32[]{:S(2)}) %collective-permute-start.54) | collective-permute-done | bytes 524320 | tf_op jit(solution)/shard_map/ppermute | solution.py:93
  405.7 7.9 %collective-permute-done.56.refs_3_ = bf16[128,2048]{1,0:T(8,128)(2,1)S(1)} collective-permute-done((bf16[128,2048]{1,0:T(8,128)(2,1)S(1)}, bf16[128,2048]{1,0:T(8,128)(2,1)S(1)}, u32[]{:S(2)}, u32[]{:S(2)}) %collective-permute-start.56) | collective-permute-done | bytes 524320 | tf_op jit(solution)/shard_map/ppermute | solution.py:93
  432.2 8.5 %shard_map.291 = (bf16[1024,2048]{1,0:T(8,128)(2,1)}, bf16[1024,512]{1,0:T(8,128)(2,1)S(1)}, bf16[1024,512]{1,0:T(8,128)(2,1)}) custom-call(s32[2]{0:T(128)S(1)} %copy-done.47, bf16[128,2048]{1,0:T(8,128)(2,1)S(1)} %get-tuple-element.275.refs_0_, bf16[128,2048]{1,0:T(8,128)(2,1)S(1)} %collective-permute-done.49.refs_1_, ...), custom_call_target="tpu_custom_call" | custom-call | tf_op jit(solution)/shard_map/pallas_call | solution.py:43
  440.8 17.2 %shard_map.292 = (bf16[2,1024,512]{2,1,0:T(8,128)(2,1)}, bf16[896,2048]{1,0:T(8,128)(2,1)}, bf16[64,2048]{1,0:T(8,128)(2,1)S(1)}, bf16[64,2048]{1,0:T(8,128)(2,1)S(1)}) custom-call(s32[2]{0:T(128)S(1)} %copy-done.47, bf16[1024,512]{1,0:T(8,128)(2,1)S(1)} %get-tuple-element.294.d_r, bf16[1024,512]{1,0:T(8,128)(2,1)} %get-tuple-element.295.d_g, ...), custom_call_target="tpu_custom_call" | custom-call | tf_op jit(solution)/shard_map/pallas_call | solution.py:43
  465.5 4.7 shard_map.290
  476.7 4.9 all-to-all-start.4
  488.8 23.0 %collective-permute-done.72.a = bf16[128,2048]{1,0:T(8,128)(2,1)S(1)} collective-permute-done((bf16[128,2048]{1,0:T(8,128)(2,1)S(1)}, bf16[128,2048]{1,0:T(8,128)(2,1)S(1)}, u32[]{:S(2)}, u32[]{:S(2)}) %collective-permute-start.72) | collective-permute-done | bytes 524320 | tf_op jit(solution)/shard_map/ppermute | solution.py:93
  513.1 7.2 collective-permute-start.74
  526.7 5.9 collective-permute-done.74.a
  537.4 4.9 collective-permute-done.64.a
  549.0 6.3 collective-permute-done.76.refs_1_
  572.5 4.7 collective-permute-done.95
  580.1 19.9 %collective-permute-done.96 = f32[4,2048]{1,0:T(4,128)S(1)} collective-permute-done((f32[4,2048]{1,0:T(4,128)S(1)}, f32[4,2048]{1,0:T(4,128)S(1)}, u32[]{:S(2)}, u32[]{:S(2)}) %collective-permute-start.96) | collective-permute-done | bytes 32800 | tf_op jit(solution)/shard_map/ppermute | solution.py:69
  618.0 5.6 collective-permute-done.68.refs_1_
  625.6 8.0 %all-to-all-done.3.own = bf16[8,128,256]{2,1,0:T(8,128)(2,1)} async-done(((bf16[8,128,256]{2,1,0:T(8,128)(2,1)}), bf16[8,128,256]{2,1,0:T(8,128)(2,1)}, u32[]{:S(2)}, u32[]{:S(2)}) %all-to-all-start.3) | async-done | bytes 524320 | tf_op jit(solution)/shard_map/all_to_all | solution.py:281
  633.5 31.5 %collective-permute-done.99 = f32[4,2048]{1,0:T(4,128)S(1)} collective-permute-done((f32[4,2048]{1,0:T(4,128)S(1)}, f32[4,2048]{1,0:T(4,128)S(1)}, u32[]{:S(2)}, u32[]{:S(2)}) %collective-permute-start.99) | collective-permute-done | bytes 32800 | tf_op jit(solution)/shard_map/ppermute | solution.py:69
  665.4 11.0 %collective-permute-done.93.other = bf16[128,2048]{1,0:T(8,128)(2,1)} collective-permute-done((bf16[128,2048]{1,0:T(8,128)(2,1)S(1)}, bf16[128,2048]{1,0:T(8,128)(2,1)}, u32[]{:S(2)}, u32[]{:S(2)}) %collective-permute-start.93) | collective-permute-done | bytes 524320 | tf_op jit(solution)/shard_map/ppermute | solution.py:69
  677.0 10.2 %collective-permute-done.88.other = bf16[8,128,256]{2,1,0:T(8,128)(2,1)} collective-permute-done((bf16[8,128,256]{2,1,0:T(8,128)(2,1)}, bf16[8,128,256]{2,1,0:T(8,128)(2,1)}, u32[]{:S(2)}, u32[]{:S(2)}) %collective-permute-start.88) | collective-permute-done | bytes 524320 | tf_op jit(solution)/shard_map/ppermute | solution.py:69
  698.6 6.8 shard_map.302
  705.3 8.1 %shard_map.304 = (f32[256,4096]{1,0:T(8,128)}, f32[256,4096]{1,0:T(8,128)}) custom-call(s32[2]{0:T(128)} %pad_add_fusion.s, bf16[8,128,512]{2,1,0:T(8,128)(2,1)} %all-to-all-done.4.own, bf16[8,128,512]{2,1,0:T(8,128)(2,1)} %collective-permute-done.100.own_c, bf16[8,128,512]{2,1,0:T(8,128)(2,1)} %collective-permute-done.101.other, ...), custom_call_target="tpu_custom_call" | custom-call | tf_op jit(solution)/shard_map/pallas_call | solution.py:303
  713.4 8.1 %shard_map.301 = (f32[256,2048]{1,0:T(8,128)}, f32[256,2048]{1,0:T(8,128)}, f32[256,4096]{1,0:T(8,128)}) custom-call(s32[2]{0:T(128)} %pad_add_fusion.s, bf16[8,128,512]{2,1,0:T(8,128)(2,1)} %all-to-all-done.2.own, bf16[8,128,512]{2,1,0:T(8,128)(2,1)} %collective-permute-done.81.own_c, bf16[8,128,512]{2,1,0:T(8,128)(2,1)} %collective-permute-done.82.other, ...), custom_call_target="tpu_custom_call" | custom-call | tf_op jit(solution)/shard_map/pallas_call | solution.py:303
  (462 shorter events, 259.6 us)
Async XLA Ops:
  7.4 46.3 %all-to-all-start = ((bf16[8,128,768]{2,1,0:T(8,128)(2,1)}), bf16[8,128,768]{2,1,0:T(8,128)(2,1)}, u32[]{:S(2)}, u32[]{:S(2)}) async-start(bf16[8,128,768]{2,1,0:T(8,128)(2,1)} %shard_map.272), calls=%async_computation | async-start | bytes 3145728 | tf_op jit(solution)/shard_map/all_to_all | solution.py:264
  14.8 37.5 %collective-permute-start = (bf16[128,2048]{1,0:T(8,128)(2,1)S(1)}, bf16[128,2048]{1,0:T(8,128)(2,1)S(1)}, u32[]{:S(2)}, u32[]{:S(2)}) collective-permute-start(bf16[128,2048]{1,0:T(8,128)(2,1)S(1)} %copy-done.15), channel_id=1, source_target_pairs={{0,2},{2,4},{4,6},{6,7},{7,5},{5,3},{3,1},{1,0},{8,10},{10,12},{12... | collective-permute-start | bytes 1572872 | tf_op jit(solution)/shard_map/ppermute | solution.py:93
  16.8 36.9 %collective-permute-start.1 = (bf16[128,2048]{1,0:T(8,128)(2,1)S(1)}, bf16[128,2048]{1,0:T(8,128)(2,1)S(1)}, u32[]{:S(2)}, u32[]{:S(2)}) collective-permute-start(bf16[128,2048]{1,0:T(8,128)(2,1)S(1)} %copy-done.15), channel_id=1, source_target_pairs={{2,0},{4,2},{6,4},{7,6},{5,7},{3,5},{1,3},{0,1},{10,8},{12,10},{14... | collective-permute-start | bytes 1572872 | tf_op jit(solution)/shard_map/ppermute | solution.py:93
  53.7 34.4 %collective-permute-start.2 = (bf16[1024,768]{1,0:T(8,128)(2,1)}, bf16[1024,768]{1,0:T(8,128)(2,1)}, u32[]{:S(2)}, u32[]{:S(2)}) collective-permute-start(bf16[1024,768]{1,0:T(8,128)(2,1)} %bitcast.2.refs_4_), channel_id=1, source_target_pairs={{0,16},{1,17},{2,18},{3,19},{4,20},{5,21},{6,22},{7,23},{8,24},{9,... | collective-permute-start | bytes 4718600 | tf_op jit(solution)/shard_map/ppermute | solution.py:69
  55.3 35.9 %collective-permute-start.5 = (bf16[4,256]{1,0:T(4,128)(2,1)S(1)}, bf16[4,256]{1,0:T(4,128)(2,1)S(1)}, u32[]{:S(2)}, u32[]{:S(2)}) collective-permute-start(bf16[4,256]{1,0:T(4,128)(2,1)S(1)} %pad_maximum_fusion.3), channel_id=1, source_target_pairs={{0,1},{1,0},{2,3},{3,2},{4,5},{5,4},{6,7},{7,6},{8,9},{9,8},{10,11... | collective-permute-start | bytes 6152 | tf_op jit(solution)/shard_map/ppermute | solution.py:69
  58.9 71.5 %collective-permute-start.3 = (bf16[1024,768]{1,0:T(8,128)(2,1)}, bf16[1024,768]{1,0:T(8,128)(2,1)}, u32[]{:S(2)}, u32[]{:S(2)}) collective-permute-start(bf16[1024,768]{1,0:T(8,128)(2,1)} %bitcast.2.refs_4_), channel_id=1, source_target_pairs={{0,8},{1,9},{2,10},{3,11},{4,12},{5,13},{6,14},{7,15},{8,0},{9,1},... | collective-permute-start | bytes 4718600 | tf_op jit(solution)/shard_map/ppermute | solution.py:69
  59.0 43.2 %collective-permute-start.8 = (bf16[128,2048]{1,0:T(8,128)(2,1)S(1)}, bf16[128,2048]{1,0:T(8,128)(2,1)S(1)}, u32[]{:S(2)}, u32[]{:S(2)}) collective-permute-start(bf16[128,2048]{1,0:T(8,128)(2,1)S(1)} %collective-permute-done.refs_1_), channel_id=1, source_target_pairs={{0,2},{2,4},{4,6},{6,7},{7,5},{5,3},{3,1},{1,0},{8,10},{10,12},{12... | collective-permute-start | bytes 1572872 | tf_op jit(solution)/shard_map/ppermute | solution.py:93
  68.9 33.2 %collective-permute-start.9 = (bf16[128,2048]{1,0:T(8,128)(2,1)S(1)}, bf16[128,2048]{1,0:T(8,128)(2,1)}, u32[]{:S(2)}, u32[]{:S(2)}) collective-permute-start(bf16[128,2048]{1,0:T(8,128)(2,1)S(1)} %collective-permute-done.1.refs_0_), channel_id=1, source_target_pairs={{2,0},{4,2},{6,4},{7,6},{5,7},{3,5},{1,3},{0,1},{10,8},{12,10},{14... | collective-permute-start | bytes 1572872 | tf_op jit(solution)/shard_map/ppermute | solution.py:93
  88.1 42.3 %collective-permute-start.4 = (bf16[1024,768]{1,0:T(8,128)(2,1)}, bf16[1024,768]{1,0:T(8,128)(2,1)}, u32[]{:S(2)}, u32[]{:S(2)}) collective-permute-start(bf16[1024,768]{1,0:T(8,128)(2,1)} %collective-permute-done.2.refs_5_), channel_id=1, source_target_pairs={{0,8},{1,9},{2,10},{3,11},{4,12},{5,13},{6,14},{7,15},{8,0},{9,1},... | collective-permute-start | bytes 4718600 | tf_op jit(solution)/shard_map/ppermute | solution.py:69
  136.2 32.6 %all-to-all-start.1 = ((bf16[8,128,512]{2,1,0:T(8,128)(2,1)}), bf16[8,128,512]{2,1,0:T(8,128)(2,1)}, u32[]{:S(2)}, u32[]{:S(2)}) async-start(bf16[8,128,512]{2,1,0:T(8,128)(2,1)} %shard_map.279), calls=%async_computation.1 | async-start | bytes 2097152 | tf_op jit(solution)/shard_map/all_to_all | solution.py:264
  206.9 27.8 %collective-permute-start.24 = (bf16[1024,512]{1,0:T(8,128)(2,1)}, bf16[1024,512]{1,0:T(8,128)(2,1)S(1)}, u32[]{:S(2)}, u32[]{:S(2)}) collective-permute-start(bf16[1024,512]{1,0:T(8,128)(2,1)} %bitcast.5.refs_10_), channel_id=1, source_target_pairs={{0,16},{1,17},{2,18},{3,19},{4,20},{5,21},{6,22},{7,23},{8,24},{9,... | collective-permute-start | bytes 3145736 | tf_op jit(solution)/shard_map/ppermute | solution.py:69
  208.4 22.5 %collective-permute-start.33 = (bf16[128,2048]{1,0:T(8,128)(2,1)S(1)}, bf16[128,2048]{1,0:T(8,128)(2,1)S(1)}, u32[]{:S(2)}, u32[]{:S(2)}) collective-permute-start(bf16[128,2048]{1,0:T(8,128)(2,1)S(1)} %copy-done.23), channel_id=1, source_target_pairs={{0,2},{2,4},{4,6},{6,7},{7,5},{5,3},{3,1},{1,0},{8,10},{10,12},{12... | collective-permute-start | bytes 1572872 | tf_op jit(solution)/shard_map/ppermute | solution.py:93
  210.1 22.6 %collective-permute-start.34 = (bf16[128,2048]{1,0:T(8,128)(2,1)S(1)}, bf16[128,2048]{1,0:T(8,128)(2,1)S(1)}, u32[]{:S(2)}, u32[]{:S(2)}) collective-permute-start(bf16[128,2048]{1,0:T(8,128)(2,1)S(1)} %copy-done.23), channel_id=1, source_target_pairs={{2,0},{4,2},{6,4},{7,6},{5,7},{3,5},{1,3},{0,1},{10,8},{12,10},{14... | collective-permute-start | bytes 1572872 | tf_op jit(solution)/shard_map/ppermute | solution.py:93
  232.7 20.7 %collective-permute-start.35 = (bf16[128,2048]{1,0:T(8,128)(2,1)S(1)}, bf16[128,2048]{1,0:T(8,128)(2,1)S(1)}, u32[]{:S(2)}, u32[]{:S(2)}) collective-permute-start(bf16[128,2048]{1,0:T(8,128)(2,1)S(1)} %collective-permute-done.33.refs_1_), channel_id=1, source_target_pairs={{0,2},{2,4},{4,6},{6,7},{7,5},{5,3},{3,1},{1,0},{8,10},{10,12},{12... | collective-permute-start | bytes 1572872 | tf_op jit(solution)/shard_map/ppermute | solution.py:93
  233.9 21.2 %collective-permute-start.36 = (bf16[128,2048]{1,0:T(8,128)(2,1)S(1)}, bf16[128,2048]{1,0:T(8,128)(2,1)S(1)}, u32[]{:S(2)}, u32[]{:S(2)}) collective-permute-start(bf16[128,2048]{1,0:T(8,128)(2,1)S(1)} %collective-permute-done.34.refs_4_), channel_id=1, source_target_pairs={{2,0},{4,2},{6,4},{7,6},{5,7},{3,5},{1,3},{0,1},{10,8},{12,10},{14... | collective-permute-start | bytes 1572872 | tf_op jit(solution)/shard_map/ppermute | solution.py:93
  257.2 42.3 %collective-permute-start.31 = (bf16[1024,512]{1,0:T(8,128)(2,1)}, bf16[1024,512]{1,0:T(8,128)(2,1)S(1)}, u32[]{:S(2)}, u32[]{:S(2)}) collective-permute-start(bf16[1024,512]{1,0:T(8,128)(2,1)} %bitcast.5.refs_10_), channel_id=1, source_target_pairs={{0,8},{1,9},{2,10},{3,11},{4,12},{5,13},{6,14},{7,15},{8,0},{9,1},... | collective-permute-start | bytes 3145736 | tf_op jit(solution)/shard_map/ppermute | solution.py:69
  264.4 35.2 %collective-permute-start.32 = (bf16[1024,512]{1,0:T(8,128)(2,1)S(1)}, bf16[1024,512]{1,0:T(8,128)(2,1)S(1)}, u32[]{:S(2)}, u32[]{:S(2)}) collective-permute-start(bf16[1024,512]{1,0:T(8,128)(2,1)S(1)} %collective-permute-done.24.refs_11_), channel_id=1, source_target_pairs={{0,8},{1,9},{2,10},{3,11},{4,12},{5,13},{6,14},{7,15},{8,0},{9,1},... | collective-permute-start | bytes 3145736 | tf_op jit(solution)/shard_map/ppermute | solution.py:69
  345.0 30.7 %collective-permute-start.52 = (bf16[1024,512]{1,0:T(8,128)(2,1)}, bf16[1024,512]{1,0:T(8,128)(2,1)}, u32[]{:S(2)}, u32[]{:S(2)}) collective-permute-start(bf16[1024,512]{1,0:T(8,128)(2,1)} %slice.139), channel_id=1, source_target_pairs={{0,8},{1,9},{2,10},{3,11},{4,12},{5,13},{6,14},{7,15},{8,0},{9,1},... | collective-permute-start | bytes 3145736 | tf_op jit(solution)/shard_map/ppermute | solution.py:69
  347.4 30.0 %collective-permute-start.53 = (bf16[2,128,2048]{2,1,0:T(8,128)(2,1)}, bf16[2,128,2048]{2,1,0:T(8,128)(2,1)}, u32[]{:S(2)}, u32[]{:S(2)}) collective-permute-start(bf16[2,128,2048]{2,1,0:T(8,128)(2,1)} %dynamic-slice_bitcast_fusion.1), channel_id=1, source_target_pairs={{0,8},{1,9},{2,10},{3,11},{4,12},{5,13},{6,14},{7,15},{8,0},{9,1},... | collective-permute-start | bytes 3145736 | tf_op jit(solution)/shard_map/ppermute | solution.py:69
  389.3 40.4 %collective-permute-start.60 = (bf16[1024,512]{1,0:T(8,128)(2,1)S(1)}, bf16[1024,512]{1,0:T(8,128)(2,1)S(1)}, u32[]{:S(2)}, u32[]{:S(2)}) collective-permute-start(bf16[1024,512]{1,0:T(8,128)(2,1)S(1)} %add_convert_fusion.3), channel_id=1, source_target_pairs={{0,16},{1,17},{2,18},{3,19},{4,20},{5,21},{6,22},{7,23},{8,24},{9,... | collective-permute-start | bytes 3145736 | tf_op jit(solution)/shard_map/ppermute | solution.py:69
  403.8 26.0 %collective-permute-start.61 = (bf16[128,2048]{1,0:T(8,128)(2,1)S(1)}, bf16[128,2048]{1,0:T(8,128)(2,1)S(1)}, u32[]{:S(2)}, u32[]{:S(2)}) collective-permute-start(bf16[128,2048]{1,0:T(8,128)(2,1)S(1)} %fusion.17), channel_id=1, source_target_pairs={{0,16},{1,17},{2,18},{3,19},{4,20},{5,21},{6,22},{7,23},{8,24},{9,... | collective-permute-start | bytes 1572872 | tf_op jit(solution)/shard_map/ppermute | solution.py:69
  470.2 51.7 %collective-permute-start.62 = (bf16[64,2048]{1,0:T(8,128)(2,1)S(1)}, bf16[64,2048]{1,0:T(8,128)(2,1)S(1)}, u32[]{:S(2)}, u32[]{:S(2)}) collective-permute-start(bf16[64,2048]{1,0:T(8,128)(2,1)S(1)} %get-tuple-element.298), channel_id=1, source_target_pairs={{0,2},{2,4},{4,6},{6,7},{7,5},{5,3},{3,1},{1,0},{8,10},{10,12},{12... | collective-permute-start | bytes 786440 | tf_op jit(solution)/shard_map/ppermute | solution.py:93
  470.2 51.8 %collective-permute-start.63 = (bf16[64,2048]{1,0:T(8,128)(2,1)S(1)}, bf16[64,2048]{1,0:T(8,128)(2,1)S(1)}, u32[]{:S(2)}, u32[]{:S(2)}) collective-permute-start(bf16[64,2048]{1,0:T(8,128)(2,1)S(1)} %get-tuple-element.299), channel_id=1, source_target_pairs={{2,0},{4,2},{6,4},{7,6},{5,7},{3,5},{1,3},{0,1},{10,8},{12,10},{14... | collective-permute-start | bytes 786440 | tf_op jit(solution)/shard_map/ppermute | solution.py:93
  475.3 49.5 %collective-permute-start.79 = (bf16[1024,512]{1,0:T(8,128)(2,1)}, bf16[1024,512]{1,0:T(8,128)(2,1)}, u32[]{:S(2)}, u32[]{:S(2)}) collective-permute-start(bf16[1024,512]{1,0:T(8,128)(2,1)} %slice.177), channel_id=1, source_target_pairs={{0,8},{1,9},{2,10},{3,11},{4,12},{5,13},{6,14},{7,15},{8,0},{9,1},... | collective-permute-start | bytes 3145736 | tf_op jit(solution)/shard_map/ppermute | solution.py:69
  476.7 89.4 %all-to-all-start.4 = ((bf16[8,128,512]{2,1,0:T(8,128)(2,1)}), bf16[8,128,512]{2,1,0:T(8,128)(2,1)}, u32[]{:S(2)}, u32[]{:S(2)}) async-start(bf16[8,128,512]{2,1,0:T(8,128)(2,1)} %bitcast.64), calls=%async_computation.4 | async-start | bytes 2097152 | tf_op jit(solution)/shard_map/all_to_all | solution.py:281
  483.8 27.9 %collective-permute-start.72 = (bf16[128,2048]{1,0:T(8,128)(2,1)S(1)}, bf16[128,2048]{1,0:T(8,128)(2,1)S(1)}, u32[]{:S(2)}, u32[]{:S(2)}) collective-permute-start(bf16[128,2048]{1,0:T(8,128)(2,1)S(1)} %get-tuple-element.319), channel_id=1, source_target_pairs={{0,2},{2,4},{4,6},{6,7},{7,5},{5,3},{3,1},{1,0},{8,10},{10,12},{12... | collective-permute-start | bytes 1572872 | tf_op jit(solution)/shard_map/ppermute | solution.py:93
  485.9 26.9 %collective-permute-start.73 = (bf16[128,2048]{1,0:T(8,128)(2,1)S(1)}, bf16[128,2048]{1,0:T(8,128)(2,1)S(1)}, u32[]{:S(2)}, u32[]{:S(2)}) collective-permute-start(bf16[128,2048]{1,0:T(8,128)(2,1)S(1)} %get-tuple-element.320), channel_id=1, source_target_pairs={{2,0},{4,2},{6,4},{7,6},{5,7},{3,5},{1,3},{0,1},{10,8},{12,10},{14... | collective-permute-start | bytes 1572872 | tf_op jit(solution)/shard_map/ppermute | solution.py:93
  532.6 29.6 %collective-permute-start.78 = (bf16[1024,512]{1,0:T(8,128)(2,1)S(1)}, bf16[1024,512]{1,0:T(8,128)(2,1)S(1)}, u32[]{:S(2)}, u32[]{:S(2)}) collective-permute-start(bf16[1024,512]{1,0:T(8,128)(2,1)S(1)} %slice.175), channel_id=1, source_target_pairs={{0,8},{1,9},{2,10},{3,11},{4,12},{5,13},{6,14},{7,15},{8,0},{9,1},... | collective-permute-start | bytes 3145736 | tf_op jit(solution)/shard_map/ppermute | solution.py:69
  535.3 27.4 %collective-permute-start.80 = (bf16[1024,512]{1,0:T(8,128)(2,1)S(1)}, bf16[1024,512]{1,0:T(8,128)(2,1)S(1)}, u32[]{:S(2)}, u32[]{:S(2)}) collective-permute-start(bf16[1024,512]{1,0:T(8,128)(2,1)S(1)} %add_convert_fusion.2), channel_id=1, source_target_pairs={{0,16},{1,17},{2,18},{3,19},{4,20},{5,21},{6,22},{7,23},{8,24},{9,... | collective-permute-start | bytes 3145736 | tf_op jit(solution)/shard_map/ppermute | solution.py:69
  537.3 28.6 %collective-permute-start.90 = (bf16[2,128,2048]{2,1,0:T(8,128)(2,1)S(1)}, bf16[2,128,2048]{2,1,0:T(8,128)(2,1)}, u32[]{:S(2)}, u32[]{:S(2)}) collective-permute-start(bf16[2,128,2048]{2,1,0:T(8,128)(2,1)S(1)} %dynamic-slice_bitcast_fusion), channel_id=1, source_target_pairs={{0,8},{1,9},{2,10},{3,11},{4,12},{5,13},{6,14},{7,15},{8,0},{9,1},... | collective-permute-start | bytes 3145736 | tf_op jit(solution)/shard_map/ppermute | solution.py:69
  555.3 21.9 %collective-permute-start.84 = (bf16[1024,256]{1,0:T(8,128)(2,1)}, bf16[1024,256]{1,0:T(8,128)(2,1)}, u32[]{:S(2)}, u32[]{:S(2)}) collective-permute-start(bf16[1024,256]{1,0:T(8,128)(2,1)} %slice.179), channel_id=1, source_target_pairs={{0,8},{1,9},{2,10},{3,11},{4,12},{5,13},{6,14},{7,15},{8,0},{9,1},... | collective-permute-start | bytes 1572872 | tf_op jit(solution)/shard_map/ppermute | solution.py:69
  557.7 44.0 %collective-permute-start.104 = (bf16[128,2048]{1,0:T(8,128)(2,1)S(1)}, bf16[128,2048]{1,0:T(8,128)(2,1)S(1)}, u32[]{:S(2)}, u32[]{:S(2)}) collective-permute-start(bf16[128,2048]{1,0:T(8,128)(2,1)S(1)} %add_convert_fusion.4.own), channel_id=1, source_target_pairs={{0,16},{1,17},{2,18},{3,19},{4,20},{5,21},{6,22},{7,23},{8,24},{9,... | collective-permute-start | bytes 1572872 | tf_op jit(solution)/shard_map/ppermute | solution.py:69
  562.3 39.5 %collective-permute-start.86 = (bf16[1024,256]{1,0:T(8,128)(2,1)}, bf16[1024,256]{1,0:T(8,128)(2,1)}, u32[]{:S(2)}, u32[]{:S(2)}) collective-permute-start(bf16[1024,256]{1,0:T(8,128)(2,1)} %add_convert_fusion.6), channel_id=1, source_target_pairs={{0,16},{1,17},{2,18},{3,19},{4,20},{5,21},{6,22},{7,23},{8,24},{9,... | collective-permute-start | bytes 1572872 | tf_op jit(solution)/shard_map/ppermute | solution.py:69
  562.7 39.6 %collective-permute-start.66 = (bf16[128,2048]{1,0:T(8,128)(2,1)}, bf16[128,2048]{1,0:T(8,128)(2,1)S(1)}, u32[]{:S(2)}, u32[]{:S(2)}) collective-permute-start(bf16[128,2048]{1,0:T(8,128)(2,1)} %get-tuple-element.306), channel_id=1, source_target_pairs={{0,2},{2,4},{4,6},{6,7},{7,5},{5,3},{3,1},{1,0},{8,10},{10,12},{12... | collective-permute-start | bytes 1572872 | tf_op jit(solution)/shard_map/ppermute | solution.py:93
  566.1 43.7 %all-to-all-start.2 = ((bf16[8,128,512]{2,1,0:T(8,128)(2,1)}), bf16[8,128,512]{2,1,0:T(8,128)(2,1)}, u32[]{:S(2)}, u32[]{:S(2)}) async-start(bf16[8,128,512]{2,1,0:T(8,128)(2,1)} %bitcast.65), calls=%async_computation.2 | async-start | bytes 2097152 | tf_op jit(solution)/shard_map/all_to_all | solution.py:281
  577.1 29.5 %collective-permute-start.67 = (bf16[128,2048]{1,0:T(8,128)(2,1)S(1)}, bf16[128,2048]{1,0:T(8,128)(2,1)S(1)}, u32[]{:S(2)}, u32[]{:S(2)}) collective-permute-start(bf16[128,2048]{1,0:T(8,128)(2,1)S(1)} %get-tuple-element.307), channel_id=1, source_target_pairs={{2,0},{4,2},{6,4},{7,6},{5,7},{3,5},{1,3},{0,1},{10,8},{12,10},{14... | collective-permute-start | bytes 1572872 | tf_op jit(solution)/shard_map/ppermute | solution.py:93
  577.2 22.9 %collective-permute-start.96 = (f32[4,2048]{1,0:T(4,128)S(1)}, f32[4,2048]{1,0:T(4,128)S(1)}, u32[]{:S(2)}, u32[]{:S(2)}) collective-permute-start(f32[4,2048]{1,0:T(4,128)S(1)} %fusion.24), channel_id=1, source_target_pairs={{0,2},{1,3},{2,0},{3,1},{4,6},{5,7},{6,4},{7,5},{8,10},{9,11},{10,... | collective-permute-start | bytes 98312 | tf_op jit(solution)/shard_map/ppermute | solution.py:69
  609.9 23.6 %all-to-all-start.3 = ((bf16[8,128,256]{2,1,0:T(8,128)(2,1)}), bf16[8,128,256]{2,1,0:T(8,128)(2,1)}, u32[]{:S(2)}, u32[]{:S(2)}) async-start(bf16[8,128,256]{2,1,0:T(8,128)(2,1)} %bitcast.70), calls=%async_computation.3 | async-start | bytes 1048576 | tf_op jit(solution)/shard_map/all_to_all | solution.py:281
  615.6 61.3 %collective-permute-start.101 = (bf16[8,128,512]{2,1,0:T(8,128)(2,1)}, bf16[8,128,512]{2,1,0:T(8,128)(2,1)}, u32[]{:S(2)}, u32[]{:S(2)}) collective-permute-start(bf16[8,128,512]{2,1,0:T(8,128)(2,1)} %all-to-all-done.4.own), channel_id=1, source_target_pairs={{0,16},{1,17},{2,18},{3,19},{4,20},{5,21},{6,22},{7,23},{8,24},{9,... | collective-permute-start | bytes 3145736 | tf_op jit(solution)/shard_map/ppermute | solution.py:69
  616.1 49.0 %collective-permute-start.92 = (bf16[128,2048]{1,0:T(8,128)(2,1)S(1)}, bf16[128,2048]{1,0:T(8,128)(2,1)}, u32[]{:S(2)}, u32[]{:S(2)}) collective-permute-start(bf16[128,2048]{1,0:T(8,128)(2,1)S(1)} %fusion.4.own), channel_id=1, source_target_pairs={{0,8},{1,9},{2,10},{3,11},{4,12},{5,13},{6,14},{7,15},{8,0},{9,1},... | collective-permute-start | bytes 1572872 | tf_op jit(solution)/shard_map/ppermute | solution.py:69
  616.3 70.9 %collective-permute-start.82 = (bf16[8,128,512]{2,1,0:T(8,128)(2,1)}, bf16[8,128,512]{2,1,0:T(8,128)(2,1)}, u32[]{:S(2)}, u32[]{:S(2)}) collective-permute-start(bf16[8,128,512]{2,1,0:T(8,128)(2,1)} %all-to-all-done.2.own), channel_id=1, source_target_pairs={{0,16},{1,17},{2,18},{3,19},{4,20},{5,21},{6,22},{7,23},{8,24},{9,... | collective-permute-start | bytes 3145736 | tf_op jit(solution)/shard_map/ppermute | solution.py:69
  623.5 41.5 %collective-permute-start.99 = (f32[4,2048]{1,0:T(4,128)S(1)}, f32[4,2048]{1,0:T(4,128)S(1)}, u32[]{:S(2)}, u32[]{:S(2)}) collective-permute-start(f32[4,2048]{1,0:T(4,128)S(1)} %add.142), channel_id=1, source_target_pairs={{0,16},{1,17},{2,18},{3,19},{4,20},{5,21},{6,22},{7,23},{8,24},{9,... | collective-permute-start | bytes 98312 | tf_op jit(solution)/shard_map/ppermute | solution.py:69
  624.0 52.3 %collective-permute-start.93 = (bf16[128,2048]{1,0:T(8,128)(2,1)S(1)}, bf16[128,2048]{1,0:T(8,128)(2,1)}, u32[]{:S(2)}, u32[]{:S(2)}) collective-permute-start(bf16[128,2048]{1,0:T(8,128)(2,1)S(1)} %fusion.4.own), channel_id=1, source_target_pairs={{0,16},{1,17},{2,18},{3,19},{4,20},{5,21},{6,22},{7,23},{8,24},{9,... | collective-permute-start | bytes 1572872 | tf_op jit(solution)/shard_map/ppermute | solution.py:69
  665.0 22.2 %collective-permute-start.88 = (bf16[8,128,256]{2,1,0:T(8,128)(2,1)}, bf16[8,128,256]{2,1,0:T(8,128)(2,1)}, u32[]{:S(2)}, u32[]{:S(2)}) collective-permute-start(bf16[8,128,256]{2,1,0:T(8,128)(2,1)} %all-to-all-done.3.own), channel_id=1, source_target_pairs={{0,16},{1,17},{2,18},{3,19},{4,20},{5,21},{6,22},{7,23},{8,24},{9,... | collective-permute-start | bytes 1572872 | tf_op jit(solution)/shard_map/ppermute | solution.py:69
  676.4 29.0 %collective-permute-start.100 = (bf16[8,128,512]{2,1,0:T(8,128)(2,1)}, bf16[8,128,512]{2,1,0:T(8,128)(2,1)}, u32[]{:S(2)}, u32[]{:S(2)}) collective-permute-start(bf16[8,128,512]{2,1,0:T(8,128)(2,1)} %all-to-all-done.4.own), channel_id=1, source_target_pairs={{0,8},{1,9},{2,10},{3,11},{4,12},{5,13},{6,14},{7,15},{8,0},{9,1},... | collective-permute-start | bytes 3145736 | tf_op jit(solution)/shard_map/ppermute | solution.py:69
  676.9 28.5 %collective-permute-start.102 = (bf16[8,128,512]{2,1,0:T(8,128)(2,1)}, bf16[8,128,512]{2,1,0:T(8,128)(2,1)}, u32[]{:S(2)}, u32[]{:S(2)}) collective-permute-start(bf16[8,128,512]{2,1,0:T(8,128)(2,1)} %collective-permute-done.101.other), channel_id=1, source_target_pairs={{0,8},{1,9},{2,10},{3,11},{4,12},{5,13},{6,14},{7,15},{8,0},{9,1},... | collective-permute-start | bytes 3145736 | tf_op jit(solution)/shard_map/ppermute | solution.py:69
  687.2 26.2 %collective-permute-start.81 = (bf16[8,128,512]{2,1,0:T(8,128)(2,1)}, bf16[8,128,512]{2,1,0:T(8,128)(2,1)}, u32[]{:S(2)}, u32[]{:S(2)}) collective-permute-start(bf16[8,128,512]{2,1,0:T(8,128)(2,1)} %all-to-all-done.2.own), channel_id=1, source_target_pairs={{0,8},{1,9},{2,10},{3,11},{4,12},{5,13},{6,14},{7,15},{8,0},{9,1},... | collective-permute-start | bytes 3145736 | tf_op jit(solution)/shard_map/ppermute | solution.py:69
  687.2 26.2 %collective-permute-start.83 = (bf16[8,128,512]{2,1,0:T(8,128)(2,1)}, bf16[8,128,512]{2,1,0:T(8,128)(2,1)}, u32[]{:S(2)}, u32[]{:S(2)}) collective-permute-start(bf16[8,128,512]{2,1,0:T(8,128)(2,1)} %collective-permute-done.82.other), channel_id=1, source_target_pairs={{0,8},{1,9},{2,10},{3,11},{4,12},{5,13},{6,14},{7,15},{8,0},{9,1},... | collective-permute-start | bytes 3145736 | tf_op jit(solution)/shard_map/ppermute | solution.py:69
  (151 other events, 1955.3 us)

commit v3 on v2

--- a/solution.py
+++ b/solution.py
@@ -14,6 +14,7 @@
 bf16 = jnp.bfloat16
 BOTH = ("rep", "fsdp")
 CORE, X = 3, 4
+LIMITS = (26, 30, 38, 30, 38, 24)
 
 
 def dot(a, b, ca=1, cb=0, kind=f32):
@@ -32,7 +33,7 @@
     return pl.BlockSpec(dims, lambda *_: index)
 
 
-def kernel(body, outs, *ins, scalars=None, scratch=(), limit=48):
+def kernel(body, outs, *ins, scalars=None, scratch=(), limit=8):
     whole = pl.BlockSpec(memory_space=pltpu.VMEM)
     grid = (1,) if any(isinstance(i, tuple) for i in ins) else ()
     specs = [i[1] if isinstance(i, tuple) else whole for i in ins]
@@ -69,16 +70,6 @@
     return lax.ppermute(value, BOTH, [(i, i ^ (1 << place)) for i in range(count)])
 
 
-def spread(value):
-    for place in range(CORE):
-        other = swap(value, place)
-        first = bit(place) == 0
-        value = jnp.concatenate(
-            [jnp.where(first, value, other), jnp.where(first, other, value)], 1
-        )
-    return value
-
-
 RING = (0, 2, 4, 6, 7, 5, 3, 1)
 OFFSETS = (0, -1, -2, -3, 1, 2, 3, 4)
 
@@ -97,14 +88,20 @@
     def __init__(self, own):
         self.own, self.ahead, self.behind = own, [own], [own]
 
-    def step(self, *others):
+    def peek(self):
         a, b = self.ahead[-1], self.behind[-1]
         if len(self.ahead) == 4:
             rows = a.shape[0] // 2
             a, b = a[:rows], b[rows:]
-        a, b, *others = after(send(a, True), send(b, False), *others)
+        return send(a, True), send(b, False)
+
+    def put(self, a, b):
         self.ahead.append(a)
         self.behind.append(b)
+
+    def step(self, *others):
+        a, b, *others = after(*self.peek(), *others)
+        self.put(a, b)
         return others
 
     def hold(self, *others):
@@ -145,11 +142,18 @@
         rows, width = self.terms.shape[0] // 7, self.terms.shape[1]
         return self.terms, block((rows, width), OFFSETS.index(offset), 0)
 
-    def step(self, *others):
+    def peek(self):
         if self.steps:
             self.fold(4 - self.steps)
-        self.a, self.b, *others = after(send(self.a, True), send(self.b, False), *others)
         self.steps += 1
+        return send(self.a, True), send(self.b, False)
+
+    def put(self, a, b):
+        self.a, self.b = a, b
+
+    def step(self, *others):
+        a, b, *others = after(*self.peek(), *others)
+        self.put(a, b)
         return others
 
     def hold(self, *others):
@@ -174,7 +178,7 @@
             body,
             [shape((rows, width), bf16)] * 2,
             self.term(offset), self.term(-offset), self.a, self.b,
-            limit=16,
+            limit=8,
         )
 
     def pieces(self):
@@ -239,23 +243,25 @@
         whole = sum(sizes)
 
         def body(s, *refs):
-            start = 0
-            for ref, size in zip(refs, sizes):
-                refs[-1][0, :, start : start + size] = ref[...]
-                start += size
+            for h in range(4):
+                start = 0
+                for ref, size in zip(refs, sizes):
+                    place = pl.multiple_of((2 * h + s[1]) * size, size)
+                    refs[-1][h, :, start : start + size] = ref[:, pl.ds(place, size)]
+                    start += size
 
         packed = pl.pallas_call(
             body,
             out_shape=shape((n, half_depth, whole), bf16),
             grid_spec=pltpu.PrefetchScalarGridSpec(
                 num_scalar_prefetch=1,
-                grid=(n,),
+                grid=(n // 4,),
                 in_specs=[
-                    pl.BlockSpec((half_depth, size), lambda k, s: (s[0], 2 * k + s[1]))
-                    for size in sizes
+                    pl.BlockSpec((half_depth, 8 * size), lambda k, s: (s[0], k)) for size in sizes
                 ],
-                out_specs=pl.BlockSpec((1, half_depth, whole), lambda k, s: (k, 0, 0)),
+                out_specs=pl.BlockSpec((4, half_depth, whole), lambda k, s: (k, 0, 0)),
             ),
+            compiler_params=pltpu.CompilerParams(vmem_limit_bytes=60 << 20),
             cost_estimate=pl.CostEstimate(flops=0, bytes_accessed=0, transcendentals=0),
         )(where, *weights)
         return packed
@@ -269,10 +275,20 @@
             value = value + swap(value.astype(bf16), place).astype(f32)
         return value
 
-    def sum_cores(kept, given):
-        size = n * half_depth
-        kept = kept[:size].astype(f32) + swap(kept[size:], CORE).astype(f32)
-        given = given[:size].astype(f32) + swap(given[size:], CORE).astype(f32)
+    def columns_grad(z, own, other):
+        size = own.shape[-1]
+
+        def body(z, own, other, *outs):
+            for t in (0, 1):
+                rows_t = z[:, t * half_width : (t + 1) * half_width]
+                for out, part in ((outs[t], own), (outs[2 + t], other)):
+                    out[...] = dot(rows_t, part[...], 0, 0).astype(bf16)
+
+        return kernel(body, [shape((half_width, size), bf16)] * 4, z, own, other, limit=LIMITS[5])
+
+    def sum_cores(own, own_t, other, other_t):
+        kept = own.astype(f32) + swap(own_t, CORE).astype(f32)
+        given = other.astype(f32) + swap(other_t, CORE).astype(f32)
         return kept, given.astype(bf16)
 
     def give(kept, got):
@@ -290,35 +306,45 @@
         def body(s, own, own_c, other, other_c, *outs):
             here = pl.ds(s[0] * half_depth, half_depth)
             there = pl.ds((1 - s[0]) * half_depth, half_depth)
-            start = 0
-            for out, size in zip(outs, sizes):
-                half = size // 2
-                columns = slice(start, start + half)
-                for x, a, b in ((s[1], own, own_c), (1 - s[1], other, other_c)):
-                    place = pl.ds(pl.multiple_of(x * half, half), half)
-                    out[here, place] = a[0, :, columns].astype(f32)
-                    out[there, place] = b[0, :, columns].astype(f32)
-                start += half
+            for h in (0, 1):
+                start = 0
+                for out, size in zip(outs, sizes):
+                    half = size // 2
+                    columns = slice(start, start + half)
+                    for x, a, b in ((s[1], own, own_c), (1 - s[1], other, other_c)):
+                        place = pl.ds(pl.multiple_of(x * half, half) + h * size, half)
+                        out[here, place] = a[h, :, columns].astype(f32)
+                        out[there, place] = b[h, :, columns].astype(f32)
+                    start += half
 
         return pl.pallas_call(
             body,
             out_shape=[shape((depth, n * size), f32) for size in sizes],
             grid_spec=pltpu.PrefetchScalarGridSpec(
                 num_scalar_prefetch=1,
-                grid=(n,),
-                in_specs=[pl.BlockSpec((1, half_depth, whole), lambda k, s: (k, 0, 0))] * 4,
-                out_specs=[pl.BlockSpec((depth, size), lambda k, s: (0, k)) for size in sizes],
+                grid=(n // 2,),
+                in_specs=[pl.BlockSpec((2, half_depth, whole), lambda k, s: (k, 0, 0))] * 4,
+                out_specs=[pl.BlockSpec((depth, 2 * size), lambda k, s: (0, k)) for size in sizes],
             ),
+            compiler_params=pltpu.CompilerParams(vmem_limit_bytes=24 << 20),
             cost_estimate=pl.CostEstimate(flops=0, bytes_accessed=0, transcendentals=0),
         )(where, *pieces)
 
 
-    def sum_cores_rows(grad):
-        size = grad.shape[0] // 4
-        grad = grad.reshape(2, 2, size, grad.shape[1])
-        core = bit(CORE)
-        given = lax.dynamic_index_in_dim(grad, 1 - core, 1, False)
-        kept = lax.dynamic_index_in_dim(grad, core, 1, False)
+    def rows_products(s, left, right, kept, given):
+        size = left.shape[1] // 4
+        for out, c in ((kept, s[0]), (given, 1 - s[0])):
+            for i in (0, 1):
+                columns = pl.ds(pl.multiple_of((2 * i + c) * size, size), size)
+                out[i] = dot(left[:, columns], right[...], 0, 0).astype(bf16)
+
+    def rows_grad(left, right):
+        return kernel(
+            rows_products, [shape((2, left.shape[1] // 4, right.shape[1]), bf16)] * 2, left, right,
+            scalars=where, limit=14,
+        )
+
+    def sum_cores_rows(kept, given):
         grad = kept.astype(f32) + swap(given, CORE).astype(f32)
         return grad[0], grad[1].astype(bf16)
 
@@ -334,7 +360,7 @@
                 out[pl.ds((2 * x + 1 - s[0]) * size, size), :] = b[...].astype(f32)
 
         (out,) = kernel(
-            body, [shape((4 * size, pieces[0].shape[1]), f32)], *pieces, scalars=where, limit=24
+            body, [shape((4 * size, pieces[0].shape[1]), f32)], *pieces, scalars=where, limit=8
         )
         return out
 
@@ -366,14 +392,15 @@
         for start, columns in arranged(s):
             z[:, start : start + half_depth] = room[:, columns].astype(bf16)
 
-    def norm_back(s, refs, inputs, gain, room, sums):
+    def norm_back(s, refs, inputs, gain, room, sums=None):
         grad = total(refs)
         for start, columns in arranged(s):
             room[:, columns] = grad[:, start : start + half_depth]
         grad = room[...]
         normed, scale = normalize(inputs)
-        sums[0:1] = jnp.sum(grad * normed, axis=0, keepdims=True)
-        sums[1:2] = jnp.sum(grad, axis=0, keepdims=True)
+        if sums is not None:
+            sums[0:1] = jnp.sum(grad * normed, axis=0, keepdims=True)
+            sums[1:2] = jnp.sum(grad, axis=0, keepdims=True)
         return normalize_back(normed, scale, grad * gain)
 
     def second_back(s, *refs):
@@ -384,8 +411,8 @@
         out[...] = grad.astype(bf16)
 
     def first_back(s, *refs):
-        parts, (tokens, grad_resid, gains, out, sums, room) = refs[:3], refs[3:]
-        grad = norm_back(s, parts, tokens[...].astype(f32), gains[0:1], room, sums)
+        parts, (tokens, grad_resid, gains, out, room) = refs[:3], refs[3:]
+        grad = norm_back(s, parts, tokens[...].astype(f32), gains[0:1], room)
         out[...] = grad_resid[...] + grad
 
     def last_sum(*refs):
@@ -445,25 +472,20 @@
             own, other = of_x(w, s[1], half)
             put_tile(outs, i, dot(part[:, :half], own) + dot(part[:, half:], other))
 
-    def hidden_back(s, *refs):
-        pieces, (w, cot, d_hidden) = refs[:9], refs[9:]
-        half = ff // 2
+    def join_tiles(*refs):
         for i in tiles:
-            here = rows_of(i)
-            part = tile(pieces, i)
-            cot[here] = part
-            own, other = of_x(w, s[1], half)
-            d_hidden[here, :half] = dot(part, own, 1, 1).astype(bf16)
-            d_hidden[here, half:] = dot(part, other, 1, 1).astype(bf16)
-
-    def feed(*refs):
-        pieces, d_hidden, w, (z, hidden, grad) = refs[:9], refs[9], refs[10:14], refs[14:17]
-        outs = refs[17:]
+            refs[9][rows_of(i)] = tile(refs, i)
+
+    def feed(s, *refs):
+        pieces, cots, w_down, w = refs[:9], refs[9:18], refs[18], refs[19:23]
+        (z, hidden, grad), outs = refs[23:26], refs[26:]
         half = ff // 2
         for i in tiles:
             here = rows_of(i)
             part = tile(pieces, i)
             z[here] = part
+            cot = tile(cots, i)
+            downs = of_x(w_down, s[1], half)
             back = 0.0
             for j in (0, 1):
                 ab = dot(part[:, halves[0]], w[j][...]) + dot(part[:, halves[1]], w[2 + j][...])
@@ -473,7 +495,7 @@
                 slope = below + a * jnp.exp(-0.5 * a * a) * (1.0 / math.sqrt(2.0 * math.pi))
                 columns = slice(j * half, (j + 1) * half)
                 hidden[here, columns] = (gelu * b).astype(bf16)
-                d = d_hidden[here, columns].astype(f32)
+                d = dot(cot, downs[j], 1, 1).astype(bf16).astype(f32)
                 both = jnp.concatenate([d * b * slope, d * gelu], -1).astype(bf16)
                 grad[j, here] = both
                 back = back + jnp.concatenate(
@@ -489,7 +511,7 @@
             put_tile(outs, i, dot(h[here, :half], own) + dot(h[here, half:], other))
 
     def mix_back(s, *refs):
-        pieces, (w, r, g, d_out, d_retained, d_gate) = refs[:9], refs[9:]
+        pieces, (w, r, g, mixed, kept, given, d_retained, d_gate, d_out) = refs[:9], refs[9:]
         half = dv // 2
         for i in tiles:
             here = rows_of(i)
@@ -501,11 +523,15 @@
             normed, scale = head_norm(r[here])
             gate = g[here]
             sigmoid = 1.0 / (1.0 + jnp.exp(-gate))
-            d_gate[here] = (d_mixed * normed * sigmoid * (1.0 + gate * (1.0 - sigmoid))).astype(bf16)
+            both = (d_mixed * normed * sigmoid * (1.0 + gate * (1.0 - sigmoid))).astype(bf16)
+            d_gate[0, here], d_gate[1, here] = both[:, :half], both[:, half:]
             d_retained[here] = normalize_back(normed, scale, d_mixed * gate * sigmoid).astype(bf16)
+        rows_products(s, mixed, d_out, kept, given)
 
     def within_back(s, d_r, d_g, q, k, v, p, decay, cosine, sine, *refs):
-        w, wg, d_pre, outs, (d_k, d_v) = refs[:4], refs[4:8], refs[8], refs[9:12], refs[12:]
+        w, zs, (d_pre, sums), outs = refs[:4], refs[4:8], refs[8:10], refs[10:13]
+        d_k, d_v, room = refs[13:]
+        cut = dk + dv // 2
         one, half = dk // 2, dv // 2
         x = s[1]
         for i in tiles:
@@ -534,19 +560,34 @@
             d_pre[1, here, dk:] = d_v[here, half:].astype(bf16)
             back = []
             for t in (0, 1):
-                part = dot(d_g[here, :half], wg[2 * t][...], 1, 1)
-                part = part + dot(d_g[here, half:], wg[2 * t + 1][...], 1, 1)
+                part = dot(d_g[0, here], w[2 * t][:, cut:], 1, 1)
+                part = part + dot(d_g[1, here], w[2 * t + 1][:, cut:], 1, 1)
                 for j in (0, 1):
-                    part = part + dot(d_pre[j, here], w[2 * t + j][...], 1, 1)
+                    part = part + dot(d_pre[j, here], w[2 * t + j][:, :cut], 1, 1)
                 back.append(part)
-            put_tile(outs, i, jnp.concatenate(back, -1))
+            back = jnp.concatenate(back, -1)
+            put_tile(outs, i, back)
+            parts = jnp.concatenate(
+                [
+                    jnp.sum(back * zs[i][...].astype(f32), axis=0, keepdims=True),
+                    jnp.sum(back, axis=0, keepdims=True),
+                ],
+                0,
+            )
+            if i == 0:
+                room[...] = parts
+            else:
+                room[...] += parts
+        for start, columns in arranged(s):
+            sums[:, columns] = room[:, start : start + half_depth]
 
     terms = term_shapes(rows, width)
 
 
     gains = jnp.stack([norm1_gain, norm1_bias, norm2_gain, norm2_bias])
-    gains = spread(gains).astype(f32)
-    packed, tokens_late = after(fetch(w_query, w_key, w_value, w_gate), tokens)
+    packed, tokens_late, gains_late, ffn_gate_late, ffn_up_late = after(
+        fetch(w_query, w_key, w_value, w_gate), tokens, gains, w_ffn_gate, w_ffn_up
+    )
     mix_own = trade(packed)
     ring = Gather(tokens_late)
 
@@ -561,38 +602,49 @@
     differ = positions[:, None] - positions[None, :]
     decay = jnp.where(differ >= 0, jnp.exp(jnp.maximum(differ, 0.0) * gamma_log), 0.0)
 
-    (mix_own,) = ring.step(mix_own)
+    def widen(value, place):
+        other = swap(value, place)
+        first = bit(place) == 0
+        return jnp.concatenate([jnp.where(first, value, other), jnp.where(first, other, value)], 1)
+
+    cosine, sine, decay, ffn_packed, mix_own, gains = ring.step(
+        cosine, sine, decay, fetch(ffn_gate_late, ffn_up_late), mix_own, widen(gains_late, 0)
+    )
     mix_other = swap(mix_own, X)
     mix_own_c = swap(mix_own, CORE)
-    ring.step()
-    ring.step()
-    cosine, sine, decay = ring.step(cosine, sine, decay)
-    pieces = ring.pieces()
-    zs = []
-    for i in tiles:
-        names = ((0, 1), (2, 3), (4, 5), (6, 7, 8))[i]
-        zs += kernel(
+    (gains,) = ring.step(widen(gains, 1))
+    (gains,) = ring.step(widen(gains, 2))
+    gains = gains.astype(f32)
+
+    def norm_tile(*parts):
+        return kernel(
             first_norm,
             [shape((2 * rows, width), bf16)],
-            *(pieces[j] for j in names), gains,
-            scalars=where, scratch=[pltpu.VMEM((2 * rows, width), f32)], limit=16,
-        )
+            *parts, gains,
+            scalars=where, scratch=[pltpu.VMEM((2 * rows, width), f32)],
+        )[0]
+
+    z0 = norm_tile(ring.own, ring.ahead[1])
+    z2 = norm_tile(*ring.behind[1:3])
+    z1 = norm_tile(*ring.ahead[2:4])
+    z0, z1, z2, mix_other, mix_own_c = ring.step(z0, z1, z2, mix_other, mix_own_c)
     mix_other_c = swap(mix_other, CORE)
+    z3 = norm_tile(ring.behind[3], ring.ahead[4], ring.behind[4])
     w_mix = (mix_own, mix_other, mix_own_c, mix_other_c)
-    *w_mix, z0, z1, z2, z3, ffn_gate_late, ffn_up_late = after(*w_mix, *zs, w_ffn_gate, w_ffn_up)
+    *w_mix, z0, z1, z2, z3, ffn_packed = after(*w_mix, z0, z1, z2, z3, ffn_packed)
     zs = (z0, z1, z2, z3)
-    ffn_own = trade(fetch(ffn_gate_late, ffn_up_late))
+    ffn_own = trade(ffn_packed)
     query, key, value, gate = kernel(
         project,
         [shape((every, dk), bf16)] * 2 + [shape((every, dv), bf16), shape((every, dv), f32)],
         *zs, *w_mix, cosine, sine,
-        scalars=where,
+        scalars=where, limit=LIMITS[0],
     )
     scores, retained, mixed, *parts = kernel(
         mix,
         [shape((every, every), bf16), shape((every, dv), f32), shape((every, dv), bf16)] + terms,
         query, key, value, decay, gate, w_out,
-        scalars=where,
+        scalars=where, limit=LIMITS[1],
     )
     ring = Scatter(parts)
     cot_late, ffn_own = ring.hold(cotangent, ffn_own)
@@ -608,105 +660,120 @@
     ring.step()
     resid, second = kernel(
         second_norm, [block_f32, block_bf16], *ring.pieces(), tokens, gains,
-        scalars=where, scratch=room_of_block, limit=16,
+        scalars=where, scratch=room_of_block, limit=8,
     )
 
     ring = Gather(second)
     (ffn_other,) = ring.step(ffn_other)
     ffn_other_c = swap(ffn_other, CORE)
-    cot_ring.step()
-    cot_all, d_hidden = kernel(
-        hidden_back,
-        [shape((every, width), bf16), shape((every, ff), bf16)],
-        *cot_ring.pieces(), w_ffn_down,
-        scalars=where,
-    )
     ring.step()
     ring.step()
-    w_ffn = (ffn_own, ffn_other, ffn_own_c, ffn_other_c)
-    *w_ffn, d_hidden = ring.step(*w_ffn, d_hidden)
+    cot_ring.step()
+    w_ffn = ring.step(ffn_own, ffn_other, ffn_own_c, ffn_other_c)
     z_second, hidden, d_ab, *parts = kernel(
         feed,
         [shape((every, width), bf16), shape((every, ff), bf16), shape((2, every, ff), bf16)]
         + terms,
-        *ring.pieces(), d_hidden, *w_ffn,
+        *ring.pieces(), *cot_ring.pieces(), w_ffn_down, *w_ffn,
+        scalars=where, limit=LIMITS[2],
     )
     ring = Scatter(parts)
-    ring.step()
-    grad_ffn = [dot(z_second, d_ab[j], 0, 0, bf16) for j in (0, 1)]
-    grad_down = dot(hidden, cot_all, 0, 0, bf16)
-    (grad_down, *grad_ffn) = ring.step(grad_down, *grad_ffn)
-    down_kept, down_given = sum_cores_rows(grad_down)
+    (cot_all,) = ring.step(
+        *kernel(join_tiles, [shape((every, width), bf16)], *cot_ring.pieces(), limit=12)
+    )
+    grad_ffn = ring.step(*columns_grad(z_second, d_ab[0], d_ab[1]))
     ffn_kept, ffn_given = sum_cores(*grad_ffn)
-    ring.step()
-    ring.step()
+    ffn_kept, ffn_given, down_kept, down_given = ring.step(
+        ffn_kept, ffn_given, *rows_grad(hidden, cot_all)
+    )
+    ffn_sent = swap(ffn_given, X)
+    down_kept, down_given = ring.step(*sum_cores_rows(down_kept, down_given))
     grad_resid, second_sums, part = kernel(
         second_back, [block_f32, pair_f32, block_bf16],
         *ring.pieces(), resid, cotangent, gains,
-        scalars=where, scratch=room_of_block, limit=16,
+        scalars=where, scratch=room_of_block,
     )
     ring = Gather(part)
-    ffn_given, ffn_kept, down_given, down_kept = ring.step(
-        ffn_given, ffn_kept, down_given, down_kept
-    )
-    ffn_sent = swap(ffn_given, X)
+    ffn_kept, down_given = ring.step(ffn_kept, down_given)
+    ffn_kept, ffn_sent, hidden_late = ring.step(ffn_kept, ffn_sent, hidden)
     down_sent = swap(down_given, X)
-    ring.step()
-    ring.step()
-    ffn_sent, down_sent, w_down_late = ring.step(ffn_sent, down_sent, w_ffn_down)
-
-    ffn_owned = give(ffn_kept, ffn_sent)
+    last = Scatter(kernel(down, terms, hidden_late, w_ffn_down, scalars=where, limit=20))
+    ffn_sum = more(ffn_kept + ffn_sent.astype(f32)).astype(bf16)
+    (ffn_sum,) = ring.step(ffn_sum)
+    a, b, down_sent, z_first = ring.step(*last.peek(), down_sent, jnp.concatenate(zs))
+    last.put(a, b)
+
+    ffn_owned = lax.all_to_all(
+        ffn_sum.reshape(n, half_depth, ffn_sum.shape[-1]), "fsdp", 0, 0, tiled=True
+    )
+    out_kept, out_given, d_retained, d_gate = kernel(
+        mix_back,
+        [shape((2, dv // 4, width), bf16)] * 2
+        + [shape((every, dv), bf16), shape((2, every, dv // 2), bf16)],
+        *ring.pieces(), w_out, retained, gate, mixed,
+        scalars=where, limit=LIMITS[3], scratch=[pltpu.VMEM((every, width), bf16)],
+    )
+    d_pre, first_sums, *parts = kernel(
+        within_back,
+        [shape((2, every, dk + dv // 2), bf16), pair_f32] + terms,
+        d_retained, d_gate, query, key, value, scores, decay, cosine, sine, *w_mix, *zs,
+        scalars=where, limit=LIMITS[4],
+        scratch=[
+            pltpu.VMEM((every, dk), f32),
+            pltpu.VMEM((every, dv), f32),
+            pltpu.VMEM((2, width), f32),
+        ],
+    )
+    ring = Scatter(parts)
+    stack = jnp.concatenate([first_sums, second_sums])
+    *grad_gate, out_kept, out_given, stack_c, ffn_owned = ring.step(
+        *columns_grad(z_first, d_gate[0], d_gate[1]), out_kept, out_given,
+        swap(stack, CORE), ffn_owned,
+    )
+    stack = stack + stack_c
+    gate_kept, gate_given = sum_cores(*grad_gate)
+    grad_qkv = columns_grad(z_first, d_pre[0], d_pre[1])
+    gate_sent = swap(gate_given, X)
+    out_kept, out_given = sum_cores_rows(out_kept, out_given)
     down_owned = give_rows(down_kept, down_sent)
-    d_out, d_retained, d_gate = kernel(
-        mix_back,
-        [shape((every, width), bf16)] + [shape((every, dv), bf16)] * 2,
-        *ring.pieces(), w_out, retained, gate,
-        scalars=where,
-    )
-    z_first = jnp.concatenate(zs)
-    w_qkv = [w[:, : dk + dv // 2] for w in w_mix]
-    w_g = [w[:, dk + dv // 2 :] for w in w_mix]
-    d_pre, *parts = kernel(
-        within_back,
-        [shape((2, every, dk + dv // 2), bf16)] + terms,
-        d_retained, d_gate, query, key, value, scores, decay, cosine, sine, *w_qkv, *w_g,
-        scalars=where, scratch=[pltpu.VMEM((every, dk), f32), pltpu.VMEM((every, dv), f32)],
-    )
-    grad_gate = [
-        dot(z_first, d_gate[:, j * (dv // 2) : (j + 1) * (dv // 2)], 0, 0, bf16) for j in (0, 1)
-    ]
-    gate_kept, gate_given = sum_cores(*grad_gate)
-    gate_owned = give(gate_kept, swap(gate_given, X))
-    ring = Scatter(parts)
-    grad_qkv = [dot(z_first, d_pre[j], 0, 0, bf16) for j in (0, 1)]
+    a, b, gate_sent, *grad_qkv, out_given, stack_c = ring.step(
+        *last.peek(), gate_sent, *grad_qkv, out_given, swap(stack, X)
+    )
+    last.put(a, b)
+    stack = stack + stack_c
+    for place in range(X + 1, bits()):
+        stack = stack + swap(stack, place)
     qkv_kept, qkv_given = sum_cores(*grad_qkv)
-    qkv_owned = give(qkv_kept, swap(qkv_given, X))
-    out_kept, out_given = sum_cores_rows(dot(mixed, d_out, 0, 0, bf16))
-    out_owned = give_rows(out_kept, swap(out_given, X))
-    ring.step()
-    ring.step()
-    ring.step()
-    ring.step()
-    grad_tokens, first_sums = kernel(
-        first_back, [block_f32, pair_f32], *ring.pieces(), tokens, grad_resid, gains,
-        scalars=where, scratch=room_of_block, limit=16,
-    )
-    last = Scatter(
-        kernel(down, terms, hidden, w_down_late, scalars=where)
-    )
-    last.hold(d_pre)
-    for _ in range(4):
-        last.step()
-    (output,) = kernel(last_sum, [block_bf16], *last.pieces(), resid, limit=16)
-    stack = jnp.concatenate([first_sums, second_sums])
-    for place in range(bits()):
-        stack = stack + swap(stack, place)
-    stack = lax.dynamic_slice_in_dim(stack, lax.axis_index("fsdp") * depth, depth, 1)
-    grad_ffn_gate, grad_ffn_up = flat(everywhere(ffn_owned), [ff, ff])
-    grad_down = flat_rows(everywhere(down_owned))
-    (grad_gate,) = flat(everywhere(gate_owned), [dv])
-    grad_query, grad_key, grad_value = flat(everywhere(qkv_owned), [dk, dk, dv])
-    grad_out = flat_rows(everywhere(out_owned))
+    qkv_sent = swap(qkv_given, X)
+    gate_owned = give(gate_kept, gate_sent)
+    gate_owned, qkv_sent, stack_c = ring.step(gate_owned, qkv_sent, swap(stack, 0))
+    stack = stack + stack_c
+    qkv_owned = give(qkv_kept, qkv_sent)
+    out_sent = swap(out_given, X)
+    a, b, qkv_owned, out_sent, stack_c = ring.step(
+        *last.peek(), qkv_owned, out_sent, swap(stack, 1)
+    )
+    last.put(a, b)
+    stack = stack + stack_c
+    qkv_all = everywhere(qkv_owned)
+    grad_tokens = kernel(
+        first_back, [block_f32], *ring.pieces(), tokens, grad_resid, gains,
+        scalars=where, scratch=room_of_block,
+    )[0]
+    out_owned = give_rows(out_kept, out_sent)
+    gate_all = everywhere(gate_owned)
+    ffn_all = everywhere(ffn_owned)
+    down_all = everywhere(down_owned)
+    out_all = everywhere(out_owned)
+    (stack_c,) = last.step(swap(stack, 2))
+    stack = lax.dynamic_slice_in_dim(stack + stack_c, head * depth, depth, 1)
+    first_gain = (stack[0] - norm1_bias.astype(f32) * stack[1]) / norm1_gain.astype(f32)
+    (output,) = kernel(last_sum, [block_bf16], *last.pieces(), resid)
+    grad_ffn_gate, grad_ffn_up = flat(ffn_all, [ff, ff])
+    grad_down = flat_rows(down_all)
+    (grad_gate,) = flat(gate_all, [dv])
+    grad_query, grad_key, grad_value = flat(qkv_all, [dk, dk, dv])
+    grad_out = flat_rows(out_all)
 
     return (
         output,
@@ -716,7 +783,7 @@
         grad_value,
         grad_gate,
         grad_out,
-        stack[0],
+        first_gain,
         stack[1],
         grad_ffn_gate,
         grad_ffn_up,

time: 732 us -> 657 us (0.90)
  matrix products: 25.1 us -> 0 us
  waiting for transfers between devices: 339 us -> 314 us
  starting transfers between devices: 145 us -> 131 us
  Pallas kernels: 137 us -> 125 us
    ppermute x64, waiting for transfers between devices: 235 us -> 181 us  [send(): lax.ppermute(value, 'fsdp', pairs if ahead else [(b, a) for a, b in pairs])]
    ppermute x42, waiting for transfers between devices: 96.6 us -> 133 us  [swap(): lax.ppermute(value, BOTH, [(i, i ^ 1 << place) for i in range(count)])]
    dot_general x8 -> x0, matrix products: 25.1 us -> none  [dot(): lax.dot_general(a, b, (((ca,), (cb,)), ((), ())), preferred_element_type=...]
    unnamed x179 -> x232, local copies, waits for them, and re-layouts: 27 us -> 47.4 us
    slice x22 -> x8, local copies, waits for them, and re-layouts: 18.1 us -> 2.16 us  [peek(): a, b = (a[:rows], b[rows:])]
    ppermute x42, starting transfers between devices: 39.6 us -> 25.7 us  [swap(): lax.ppermute(value, BOTH, [(i, i ^ 1 << place) for i in range(count)])]
    all_to_all x3 -> x2, waiting for transfers between devices: 7.96 us -> 0.01 us  [give(): return lax.all_to_all(grad, 'fsdp', 0, 0, tiled=True)]
    pallas_call x29 -> x33, Pallas kernels: 102 us -> 101 us  [kernel(): pl.pallas_call(body, out_shape=list(outs), grid=grid, in_specs=specs, out...]
  transfers between devices with their start and end apart: 111 -> 111, of which waited for: 51 -> 60; matrix products, arithmetic and copies ran while one was open for 9% -> 3% of each run, Pallas kernels for 10% -> 15%
where the time goes in v3:
time: 657 us; the launch traced here: 650 us
  waiting for transfers between devices  314 us (48%)
  starting transfers between devices  131 us (20%)
  Pallas kernels  125 us (19%)
  local copies, waits for them, and re-layouts  57.2 us (9%)
  other arithmetic  18.9 us (3%)
    ppermute x64, waiting for transfers between devices, send(): lax.ppermute(value, 'fsdp', pairs if ahead else [(b, a) for a, b in pairs])  181 us
    ppermute x42, waiting for transfers between devices, swap(): lax.ppermute(value, BOTH, [(i, i ^ 1 << place) for i in range(count)])  133 us
    pallas_call x33, Pallas kernels, kernel(): pl.pallas_call(body, out_shape=list(outs), grid=grid, in_specs=specs, out...  101 us
    ppermute x64, starting transfers between devices, send(): lax.ppermute(value, 'fsdp', pairs if ahead else [(b, a) for a, b in pairs])  78.7 us
    unnamed x232, local copies, waits for them, and re-layouts  47.4 us
    ppermute x42, starting transfers between devices, swap(): lax.ppermute(value, BOTH, [(i, i ^ 1 << place) for i in range(count)])  25.7 us
    pallas_call x3, Pallas kernels, flat(): pl.pallas_call(body, out_shape=[shape((depth, n * size), f32) for size in...  17.3 us
  transfers between devices with their start and end apart: 111, of which 60 were waited for; matrix products, arithmetic and copies ran while one was open for 3% of the time, Pallas kernels for 15%

profile of v3, /device:TPU:0, one launch (start us, length us, event | category | flops | bytes accessed | tf_op | source)
XLA Modules:
  0.0 649.5 jit_solution(4604932192413957129)
XLA Ops:
  3.9 3.6 shard_map.272
  7.5 7.4 %all-to-all-start = ((bf16[8,128,768]{2,1,0:T(8,128)(2,1)}), bf16[8,128,768]{2,1,0:T(8,128)(2,1)}, u32[]{:S(2)}, u32[]{:S(2)}) async-start(bf16[8,128,768]{2,1,0:T(8,128)(2,1)} %shard_map.272), calls=%async_computation | async-start | bytes 3145728 | tf_op jit(solution)/shard_map/all_to_all | solution.py:270
  30.4 15.0 %collective-permute-done.2 = bf16[4,256]{1,0:T(4,128)(2,1)S(1)} collective-permute-done((bf16[4,256]{1,0:T(4,128)(2,1)S(1)}, bf16[4,256]{1,0:T(4,128)(2,1)S(1)}, u32[]{:S(2)}, u32[]{:S(2)}) %collective-permute-start.2) | collective-permute-done | bytes 2080 | tf_op jit(solution)/shard_map/ppermute | solution.py:70
  45.4 7.0 %collective-permute-done.refs_1_ = bf16[128,2048]{1,0:T(8,128)(2,1)S(1)} collective-permute-done((bf16[128,2048]{1,0:T(8,128)(2,1)S(1)}, bf16[128,2048]{1,0:T(8,128)(2,1)S(1)}, u32[]{:S(2)}, u32[]{:S(2)}) %collective-permute-start) | collective-permute-done | bytes 524320 | tf_op jit(solution)/shard_map/ppermute | solution.py:84
  55.3 9.9 %collective-permute-start.3 = (bf16[128,2048]{1,0:T(8,128)(2,1)S(1)}, bf16[128,2048]{1,0:T(8,128)(2,1)S(1)}, u32[]{:S(2)}, u32[]{:S(2)}) collective-permute-start(bf16[128,2048]{1,0:T(8,128)(2,1)S(1)} %collective-permute-done.refs_1_), channel_id=1, source_target_pairs={{0,2},{2,4},{4,6},{6,7},{7,5},{5,3},{3,1},{1,0},{8,10},{10,12},{12... | collective-permute-start | bytes 1572872 | tf_op jit(solution)/shard_map/ppermute | solution.py:84
  68.1 11.3 %collective-permute-done.5 = bf16[4,512]{1,0:T(4,128)(2,1)S(1)} collective-permute-done((bf16[4,512]{1,0:T(4,128)(2,1)S(1)}, bf16[4,512]{1,0:T(4,128)(2,1)S(1)}, u32[]{:S(2)}, u32[]{:S(2)}) %collective-permute-start.5) | collective-permute-done | bytes 4128 | tf_op jit(solution)/shard_map/ppermute | solution.py:70
  82.4 11.6 %collective-permute-done.8 = bf16[4,1024]{1,0:T(4,128)(2,1)S(1)} collective-permute-done((bf16[4,1024]{1,0:T(4,128)(2,1)S(1)}, bf16[4,1024]{1,0:T(4,128)(2,1)S(1)}, u32[]{:S(2)}, u32[]{:S(2)}) %collective-permute-start.8) | collective-permute-done | bytes 8224 | tf_op jit(solution)/shard_map/ppermute | solution.py:70
  106.0 4.4 all-to-all-start.1
  115.2 9.4 %shard_map.278 = (bf16[1024,256]{1,0:T(8,128)(2,1)S(1)}, bf16[1024,256]{1,0:T(8,128)(2,1)S(1)}, bf16[1024,512]{1,0:T(8,128)(2,1)S(1)}, f32[1024,512]{1,0:T(8,128)S(1)}) custom-call(s32[2]{0:T(128)S(1)} %copy-done.99, bf16[256,2048]{1,0:T(8,128)(2,1)S(1)} %shard_map.274.refs_0_.refs_4_, bf16[256,2048]{1,0:T(8,128)(2,1)S(1)} %shard_map.275.refs_1_.refs_5_, ...), custom_call_target="tpu_custom_call" | custom-call | tf_op jit(solution)/shard_map/pallas_call | solution.py:44
  124.6 5.9 shard_map.279
  142.6 6.5 %collective-permute-done.14.a = bf16[64,2048]{1,0:T(8,128)(2,1)S(1)} collective-permute-done((bf16[64,2048]{1,0:T(8,128)(2,1)}, bf16[64,2048]{1,0:T(8,128)(2,1)S(1)}, u32[]{:S(2)}, u32[]{:S(2)}) %collective-permute-start.14) | collective-permute-done | bytes 262176 | tf_op jit(solution)/shard_map/ppermute | solution.py:84
  154.6 10.5 %collective-permute-done.16.a = bf16[128,2048]{1,0:T(8,128)(2,1)S(1)} collective-permute-done((bf16[128,2048]{1,0:T(8,128)(2,1)S(1)}, bf16[128,2048]{1,0:T(8,128)(2,1)S(1)}, u32[]{:S(2)}, u32[]{:S(2)}) %collective-permute-start.16) | collective-permute-done | bytes 524320 | tf_op jit(solution)/shard_map/ppermute | solution.py:84
  168.6 9.3 %collective-permute-done.18.a = bf16[128,2048]{1,0:T(8,128)(2,1)S(1)} collective-permute-done((bf16[128,2048]{1,0:T(8,128)(2,1)S(1)}, bf16[128,2048]{1,0:T(8,128)(2,1)S(1)}, u32[]{:S(2)}, u32[]{:S(2)}) %collective-permute-start.18) | collective-permute-done | bytes 524320 | tf_op jit(solution)/shard_map/ppermute | solution.py:84
  184.3 9.9 %collective-permute-done.20.refs_1_ = bf16[128,2048]{1,0:T(8,128)(2,1)S(1)} collective-permute-done((bf16[128,2048]{1,0:T(8,128)(2,1)S(1)}, bf16[128,2048]{1,0:T(8,128)(2,1)S(1)}, u32[]{:S(2)}, u32[]{:S(2)}) %collective-permute-start.20) | collective-permute-done | bytes 524320 | tf_op jit(solution)/shard_map/ppermute | solution.py:84
  199.0 6.4 collective-permute-done.33.refs_10_.refs_1_
  208.9 7.7 %collective-permute-done.22.refs_1_ = bf16[128,2048]{1,0:T(8,128)(2,1)S(1)} collective-permute-done((bf16[128,2048]{1,0:T(8,128)(2,1)S(1)}, bf16[128,2048]{1,0:T(8,128)(2,1)S(1)}, u32[]{:S(2)}, u32[]{:S(2)}) %collective-permute-start.22) | collective-permute-done | bytes 524320 | tf_op jit(solution)/shard_map/ppermute | solution.py:84
  220.2 7.7 %collective-permute-done.35.refs_11_.refs_2_ = bf16[128,2048]{1,0:T(8,128)(2,1)S(1)} collective-permute-done((bf16[128,2048]{1,0:T(8,128)(2,1)S(1)}, bf16[128,2048]{1,0:T(8,128)(2,1)S(1)}, u32[]{:S(2)}, u32[]{:S(2)}) %collective-permute-start.35) | collective-permute-done | bytes 524320 | tf_op jit(solution)/shard_map/ppermute | solution.py:84
  231.4 7.7 %collective-permute-done.25.refs_2_ = bf16[128,2048]{1,0:T(8,128)(2,1)S(1)} collective-permute-done((bf16[128,2048]{1,0:T(8,128)(2,1)S(1)}, bf16[128,2048]{1,0:T(8,128)(2,1)S(1)}, u32[]{:S(2)}, u32[]{:S(2)}) %collective-permute-start.25) | collective-permute-done | bytes 524320 | tf_op jit(solution)/shard_map/ppermute | solution.py:84
  241.9 6.9 %collective-permute-done.37.refs_12_.refs_3_ = bf16[128,2048]{1,0:T(8,128)(2,1)S(1)} collective-permute-done((bf16[128,2048]{1,0:T(8,128)(2,1)S(1)}, bf16[128,2048]{1,0:T(8,128)(2,1)S(1)}, u32[]{:S(2)}, u32[]{:S(2)}) %collective-permute-start.37) | collective-permute-done | bytes 524320 | tf_op jit(solution)/shard_map/ppermute | solution.py:84
  251.3 8.8 %collective-permute-done.27.refs_3_ = bf16[128,2048]{1,0:T(8,128)(2,1)S(1)} collective-permute-done((bf16[128,2048]{1,0:T(8,128)(2,1)S(1)}, bf16[128,2048]{1,0:T(8,128)(2,1)S(1)}, u32[]{:S(2)}, u32[]{:S(2)}) %collective-permute-start.27) | collective-permute-done | bytes 524320 | tf_op jit(solution)/shard_map/ppermute | solution.py:84
  268.0 3.6 collective-permute-done.30.refs_8_
  271.6 17.7 %shard_map.284 = (bf16[1024,2048]{1,0:T(8,128)(2,1)}, bf16[1024,512]{1,0:T(8,128)(2,1)S(1)}, bf16[2,1024,512]{2,1,0:T(8,128)(2,1)S(1)}, bf16[896,2048]{1,0:T(8,1...) custom-call(s32[2]{0:T(128)S(1)} %copy-done.99, bf16[128,2048]{1,0:T(8,128)(2,1)S(1)} %get-tuple-element.289.refs_0_, ...), custom_call_target="tpu_custom_call" | custom-call | tf_op jit(solution)/shard_map/pallas_call | solution.py:44
  291.6 6.9 %collective-permute-done.41.a = bf16[64,2048]{1,0:T(8,128)(2,1)S(1)} collective-permute-done((bf16[64,2048]{1,0:T(8,128)(2,1)S(1)}, bf16[64,2048]{1,0:T(8,128)(2,1)S(1)}, u32[]{:S(2)}, u32[]{:S(2)}) %collective-permute-start.41) | collective-permute-done | bytes 262176 | tf_op jit(solution)/shard_map/ppermute | solution.py:84
  304.5 4.5 shard_map.287
  317.4 11.1 %collective-permute-done.45.a = bf16[128,2048]{1,0:T(8,128)(2,1)S(1)} collective-permute-done((bf16[128,2048]{1,0:T(8,128)(2,1)S(1)}, bf16[128,2048]{1,0:T(8,128)(2,1)S(1)}, u32[]{:S(2)}, u32[]{:S(2)}) %collective-permute-start.45) | collective-permute-done | bytes 524320 | tf_op jit(solution)/shard_map/ppermute | solution.py:84
  334.1 9.7 %collective-permute-done.49.refs_1_ = bf16[128,2048]{1,0:T(8,128)(2,1)S(1)} collective-permute-done((bf16[128,2048]{1,0:T(8,128)(2,1)S(1)}, bf16[128,2048]{1,0:T(8,128)(2,1)S(1)}, u32[]{:S(2)}, u32[]{:S(2)}) %collective-permute-start.49) | collective-permute-done | bytes 524320 | tf_op jit(solution)/shard_map/ppermute | solution.py:84
  349.3 10.8 %collective-permute-done.52.refs_1_ = bf16[128,2048]{1,0:T(8,128)(2,1)S(1)} collective-permute-done((bf16[128,2048]{1,0:T(8,128)(2,1)S(1)}, bf16[128,2048]{1,0:T(8,128)(2,1)S(1)}, u32[]{:S(2)}, u32[]{:S(2)}) %collective-permute-start.52) | collective-permute-done | bytes 524320 | tf_op jit(solution)/shard_map/ppermute | solution.py:84
  362.4 10.4 %collective-permute-done.56 = bf16[1024,512]{1,0:T(8,128)(2,1)S(1)} collective-permute-done((bf16[1024,512]{1,0:T(8,128)(2,1)S(1)}, bf16[1024,512]{1,0:T(8,128)(2,1)S(1)}, u32[]{:S(2)}, u32[]{:S(2)}) %collective-permute-start.56) | collective-permute-done | bytes 1048608 | tf_op jit(solution)/shard_map/ppermute | solution.py:70
  376.3 8.5 %collective-permute-done.57.refs_3_ = bf16[128,2048]{1,0:T(8,128)(2,1)} collective-permute-done((bf16[128,2048]{1,0:T(8,128)(2,1)S(1)}, bf16[128,2048]{1,0:T(8,128)(2,1)}, u32[]{:S(2)}, u32[]{:S(2)}) %collective-permute-start.57) | collective-permute-done | bytes 524320 | tf_op jit(solution)/shard_map/ppermute | solution.py:84
  385.1 4.3 all-to-all-start.2
  404.7 7.9 %collective-permute-done.61.a = bf16[64,2048]{1,0:T(8,128)(2,1)S(1)} collective-permute-done((bf16[64,2048]{1,0:T(8,128)(2,1)S(1)}, bf16[64,2048]{1,0:T(8,128)(2,1)S(1)}, u32[]{:S(2)}, u32[]{:S(2)}) %collective-permute-start.61) | collective-permute-done | bytes 262176 | tf_op jit(solution)/shard_map/ppermute | solution.py:84
  417.7 8.2 %shard_map.293 = (bf16[2,128,2048]{2,1,0:T(8,128)(2,1)S(1)}, bf16[2,128,2048]{2,1,0:T(8,128)(2,1)}, bf16[1024,512]{1,0:T(8,128)(2,1)S(1)}, bf16[2,1024,256]{2,1,0:T(8,128)(2,1)S(1)}) custom-call(s32[2]{0:T(128)S(1)} %copy-done.99, bf16[128,2048]{1,0:T(8,128)(2,1)S(1)} %copy-done.66, bf16[128,2048]{1,0:T(8,128)(2,1)S(1)} %copy-done.68, ...), custom_call_target="tpu_custom_call" | custom-call | tf_op jit(solution)/shard_map/pallas_call | solution.py:44
  426.0 17.6 %shard_map.294 = (bf16[2,1024,512]{2,1,0:T(8,128)(2,1)}, f32[2,2048]{1,0:T(2,128)S(1)}, bf16[896,2048]{1,0:T(8,128)(2,1)}, bf16[64,2048]{1,0:T(8,128)(2,1)S(1)}, bf16[64,2048]{1,0:T(8,128)(2,1)S(1)}) custom-call(s32[2]{0:T(128)S(1)} %copy-done.99, bf16[1024,512]{1,0:T(8,128)(2,1)S(1)} %get-tuple-element.369.d_r, ...), custom_call_target="tpu_custom_call" | custom-call | tf_op jit(solution)/shard_map/pallas_call | solution.py:44
  443.6 6.6 %collective-permute-start.64 = (bf16[64,2048]{1,0:T(8,128)(2,1)S(1)}, bf16[64,2048]{1,0:T(8,128)(2,1)S(1)}, u32[]{:S(2)}, u32[]{:S(2)}) collective-permute-start(bf16[64,2048]{1,0:T(8,128)(2,1)S(1)} %get-tuple-element.373), channel_id=1, source_target_pairs={{0,2},{2,4},{4,6},{6,7},{7,5},{5,3},{3,1},{1,0},{8,10},{10,12},{12... | collective-permute-start | bytes 786440 | tf_op jit(solution)/shard_map/ppermute | solution.py:84
  463.1 4.5 shard_map.298
  475.0 9.8 %collective-permute-done.74 = f32[4,2048]{1,0:T(4,128)S(1)} collective-permute-done((f32[4,2048]{1,0:T(4,128)S(1)}, f32[4,2048]{1,0:T(4,128)S(1)}, u32[]{:S(2)}, u32[]{:S(2)}) %collective-permute-start.74) | collective-permute-done | bytes 32800 | tf_op jit(solution)/shard_map/ppermute | solution.py:70
  490.2 4.3 all-to-all-start.3
  502.0 13.1 %collective-permute-done.80 = f32[4,2048]{1,0:T(4,128)S(1)} collective-permute-done((f32[4,2048]{1,0:T(4,128)S(1)}, f32[4,2048]{1,0:T(4,128)S(1)}, u32[]{:S(2)}, u32[]{:S(2)}) %collective-permute-start.80) | collective-permute-done | bytes 32800 | tf_op jit(solution)/shard_map/ppermute | solution.py:70
  520.1 6.6 %all-to-all-start.4 = ((bf16[8,128,512]{2,1,0:T(8,128)(2,1)}), bf16[8,128,512]{2,1,0:T(8,128)(2,1)S(1)}, u32[]{:S(2)}, u32[]{:S(2)}) async-start(bf16[8,128,512]{2,1,0:T(8,128)(2,1)} %bitcast.39), calls=%async_computation.4 | async-start | bytes 2097152 | tf_op jit(solution)/shard_map/all_to_all | solution.py:297
  536.5 27.8 %collective-permute-done.104.other = bf16[128,2048]{1,0:T(8,128)(2,1)} collective-permute-done((bf16[128,2048]{1,0:T(8,128)(2,1)S(1)}, bf16[128,2048]{1,0:T(8,128)(2,1)}, u32[]{:S(2)}, u32[]{:S(2)}) %collective-permute-start.104) | collective-permute-done | bytes 524320 | tf_op jit(solution)/shard_map/ppermute | solution.py:70
  570.1 4.0 collective-permute-done.86
  574.1 3.3 collective-permute-done.87
  581.6 12.9 %collective-permute-done.95.other = bf16[8,128,256]{2,1,0:T(8,128)(2,1)} collective-permute-done((bf16[8,128,256]{2,1,0:T(8,128)(2,1)S(1)}, bf16[8,128,256]{2,1,0:T(8,128)(2,1)}, u32[]{:S(2)}, u32[]{:S(2)}) %collective-permute-start.95) | collective-permute-done | bytes 524320 | tf_op jit(solution)/shard_map/ppermute | solution.py:70
  607.4 10.4 %collective-permute-done.90 = f32[4,2048]{1,0:T(4,128)S(1)} collective-permute-done((f32[4,2048]{1,0:T(4,128)S(1)}, f32[4,2048]{1,0:T(4,128)S(1)}, u32[]{:S(2)}, u32[]{:S(2)}) %collective-permute-start.90) | collective-permute-done | bytes 32800 | tf_op jit(solution)/shard_map/ppermute | solution.py:70
  618.3 3.7 shard_map.309
  622.0 6.3 shard_map.308
  628.4 4.7 shard_map.306
  643.0 6.2 shard_map.305
  (500 shorter events, 235.0 us)
Async XLA Ops:
  7.5 46.3 %all-to-all-start = ((bf16[8,128,768]{2,1,0:T(8,128)(2,1)}), bf16[8,128,768]{2,1,0:T(8,128)(2,1)}, u32[]{:S(2)}, u32[]{:S(2)}) async-start(bf16[8,128,768]{2,1,0:T(8,128)(2,1)} %shard_map.272), calls=%async_computation | async-start | bytes 3145728 | tf_op jit(solution)/shard_map/all_to_all | solution.py:270
  14.9 37.5 %collective-permute-start = (bf16[128,2048]{1,0:T(8,128)(2,1)S(1)}, bf16[128,2048]{1,0:T(8,128)(2,1)S(1)}, u32[]{:S(2)}, u32[]{:S(2)}) collective-permute-start(bf16[128,2048]{1,0:T(8,128)(2,1)S(1)} %copy-done.32), channel_id=1, source_target_pairs={{0,2},{2,4},{4,6},{6,7},{7,5},{5,3},{3,1},{1,0},{8,10},{10,12},{12... | collective-permute-start | bytes 1572872 | tf_op jit(solution)/shard_map/ppermute | solution.py:84
  16.9 36.9 %collective-permute-start.1 = (bf16[128,2048]{1,0:T(8,128)(2,1)S(1)}, bf16[128,2048]{1,0:T(8,128)(2,1)S(1)}, u32[]{:S(2)}, u32[]{:S(2)}) collective-permute-start(bf16[128,2048]{1,0:T(8,128)(2,1)S(1)} %copy-done.32), channel_id=1, source_target_pairs={{2,0},{4,2},{6,4},{7,6},{5,7},{3,5},{1,3},{0,1},{10,8},{12,10},{14... | collective-permute-start | bytes 1572872 | tf_op jit(solution)/shard_map/ppermute | solution.py:84
  17.0 28.4 %collective-permute-start.2 = (bf16[4,256]{1,0:T(4,128)(2,1)S(1)}, bf16[4,256]{1,0:T(4,128)(2,1)S(1)}, u32[]{:S(2)}, u32[]{:S(2)}) collective-permute-start(bf16[4,256]{1,0:T(4,128)(2,1)S(1)} %pad_maximum_fusion.5), channel_id=1, source_target_pairs={{0,1},{1,0},{2,3},{3,2},{4,5},{5,4},{6,7},{7,6},{8,9},{9,8},{10,11... | collective-permute-start | bytes 6152 | tf_op jit(solution)/shard_map/ppermute | solution.py:70
  53.8 47.4 %collective-permute-start.11 = (bf16[1024,768]{1,0:T(8,128)(2,1)}, bf16[1024,768]{1,0:T(8,128)(2,1)}, u32[]{:S(2)}, u32[]{:S(2)}) collective-permute-start(bf16[1024,768]{1,0:T(8,128)(2,1)} %bitcast.4.refs_4_.refs_0_), channel_id=1, source_target_pairs={{0,16},{1,17},{2,18},{3,19},{4,20},{5,21},{6,22},{7,23},{8,24},{9,... | collective-permute-start | bytes 4718600 | tf_op jit(solution)/shard_map/ppermute | solution.py:70
  55.3 45.9 %collective-permute-start.12 = (bf16[1024,768]{1,0:T(8,128)(2,1)}, bf16[1024,768]{1,0:T(8,128)(2,1)}, u32[]{:S(2)}, u32[]{:S(2)}) collective-permute-start(bf16[1024,768]{1,0:T(8,128)(2,1)} %bitcast.4.refs_4_.refs_0_), channel_id=1, source_target_pairs={{0,8},{1,9},{2,10},{3,11},{4,12},{5,13},{6,14},{7,15},{8,0},{9,1},... | collective-permute-start | bytes 4718600 | tf_op jit(solution)/shard_map/ppermute | solution.py:70
  55.3 24.1 %collective-permute-start.3 = (bf16[128,2048]{1,0:T(8,128)(2,1)S(1)}, bf16[128,2048]{1,0:T(8,128)(2,1)S(1)}, u32[]{:S(2)}, u32[]{:S(2)}) collective-permute-start(bf16[128,2048]{1,0:T(8,128)(2,1)S(1)} %collective-permute-done.refs_1_), channel_id=1, source_target_pairs={{0,2},{2,4},{4,6},{6,7},{7,5},{5,3},{3,1},{1,0},{8,10},{10,12},{12... | collective-permute-start | bytes 1572872 | tf_op jit(solution)/shard_map/ppermute | solution.py:84
  106.0 34.5 %all-to-all-start.1 = ((bf16[8,128,512]{2,1,0:T(8,128)(2,1)}), bf16[8,128,512]{2,1,0:T(8,128)(2,1)}, u32[]{:S(2)}, u32[]{:S(2)}) async-start(bf16[8,128,512]{2,1,0:T(8,128)(2,1)} %shard_map.273), calls=%async_computation.1 | async-start | bytes 2097152 | tf_op jit(solution)/shard_map/all_to_all | solution.py:270
  181.3 27.6 %collective-permute-start.24 = (bf16[1024,512]{1,0:T(8,128)(2,1)}, bf16[1024,512]{1,0:T(8,128)(2,1)S(1)}, u32[]{:S(2)}, u32[]{:S(2)}) collective-permute-start(bf16[1024,512]{1,0:T(8,128)(2,1)} %bitcast.5.refs_19_), channel_id=1, source_target_pairs={{0,16},{1,17},{2,18},{3,19},{4,20},{5,21},{6,22},{7,23},{8,24},{9,... | collective-permute-start | bytes 3145736 | tf_op jit(solution)/shard_map/ppermute | solution.py:70
  181.9 23.5 %collective-permute-start.33 = (bf16[128,2048]{1,0:T(8,128)(2,1)S(1)}, bf16[128,2048]{1,0:T(8,128)(2,1)S(1)}, u32[]{:S(2)}, u32[]{:S(2)}) collective-permute-start(bf16[128,2048]{1,0:T(8,128)(2,1)S(1)} %copy-done.27), channel_id=1, source_target_pairs={{0,2},{2,4},{4,6},{6,7},{7,5},{5,3},{3,1},{1,0},{8,10},{10,12},{12... | collective-permute-start | bytes 1572872 | tf_op jit(solution)/shard_map/ppermute | solution.py:84
  183.3 23.6 %collective-permute-start.34 = (bf16[128,2048]{1,0:T(8,128)(2,1)S(1)}, bf16[128,2048]{1,0:T(8,128)(2,1)S(1)}, u32[]{:S(2)}, u32[]{:S(2)}) collective-permute-start(bf16[128,2048]{1,0:T(8,128)(2,1)S(1)} %copy-done.27), channel_id=1, source_target_pairs={{2,0},{4,2},{6,4},{7,6},{5,7},{3,5},{1,3},{0,1},{10,8},{12,10},{14... | collective-permute-start | bytes 1572872 | tf_op jit(solution)/shard_map/ppermute | solution.py:84
  196.9 19.7 %collective-permute-start.22 = (bf16[128,2048]{1,0:T(8,128)(2,1)S(1)}, bf16[128,2048]{1,0:T(8,128)(2,1)S(1)}, u32[]{:S(2)}, u32[]{:S(2)}) collective-permute-start(bf16[128,2048]{1,0:T(8,128)(2,1)S(1)} %get-tuple-element.289.refs_0_), channel_id=1, source_target_pairs={{0,2},{2,4},{4,6},{6,7},{7,5},{5,3},{3,1},{1,0},{8,10},{10,12},{12... | collective-permute-start | bytes 1572872 | tf_op jit(solution)/shard_map/ppermute | solution.py:84
  198.3 19.8 %collective-permute-start.23 = (bf16[128,2048]{1,0:T(8,128)(2,1)S(1)}, bf16[128,2048]{1,0:T(8,128)(2,1)S(1)}, u32[]{:S(2)}, u32[]{:S(2)}) collective-permute-start(bf16[128,2048]{1,0:T(8,128)(2,1)S(1)} %get-tuple-element.289.refs_0_), channel_id=1, source_target_pairs={{2,0},{4,2},{6,4},{7,6},{5,7},{3,5},{1,3},{0,1},{10,8},{12,10},{14... | collective-permute-start | bytes 1572872 | tf_op jit(solution)/shard_map/ppermute | solution.py:84
  206.9 21.0 %collective-permute-start.35 = (bf16[128,2048]{1,0:T(8,128)(2,1)S(1)}, bf16[128,2048]{1,0:T(8,128)(2,1)S(1)}, u32[]{:S(2)}, u32[]{:S(2)}) collective-permute-start(bf16[128,2048]{1,0:T(8,128)(2,1)S(1)} %collective-permute-done.33.refs_10_.refs_1_), channel_id=1, source_target_pairs={{0,2},{2,4},{4,6},{6,7},{7,5},{5,3},{3,1},{1,0},{8,10},{10,12},{12... | collective-permute-start | bytes 1572872 | tf_op jit(solution)/shard_map/ppermute | solution.py:84
  208.2 21.2 %collective-permute-start.36 = (bf16[128,2048]{1,0:T(8,128)(2,1)S(1)}, bf16[128,2048]{1,0:T(8,128)(2,1)S(1)}, u32[]{:S(2)}, u32[]{:S(2)}) collective-permute-start(bf16[128,2048]{1,0:T(8,128)(2,1)S(1)} %collective-permute-done.34.refs_13_.refs_4_), channel_id=1, source_target_pairs={{2,0},{4,2},{6,4},{7,6},{5,7},{3,5},{1,3},{0,1},{10,8},{12,10},{14... | collective-permute-start | bytes 1572872 | tf_op jit(solution)/shard_map/ppermute | solution.py:84
  218.1 21.0 %collective-permute-start.25 = (bf16[128,2048]{1,0:T(8,128)(2,1)S(1)}, bf16[128,2048]{1,0:T(8,128)(2,1)S(1)}, u32[]{:S(2)}, u32[]{:S(2)}) collective-permute-start(bf16[128,2048]{1,0:T(8,128)(2,1)S(1)} %collective-permute-done.22.refs_1_), channel_id=1, source_target_pairs={{0,2},{2,4},{4,6},{6,7},{7,5},{5,3},{3,1},{1,0},{8,10},{10,12},{12... | collective-permute-start | bytes 1572872 | tf_op jit(solution)/shard_map/ppermute | solution.py:84
  219.4 21.2 %collective-permute-start.26 = (bf16[128,2048]{1,0:T(8,128)(2,1)S(1)}, bf16[128,2048]{1,0:T(8,128)(2,1)S(1)}, u32[]{:S(2)}, u32[]{:S(2)}) collective-permute-start(bf16[128,2048]{1,0:T(8,128)(2,1)S(1)} %collective-permute-done.23.refs_4_), channel_id=1, source_target_pairs={{2,0},{4,2},{6,4},{7,6},{5,7},{3,5},{1,3},{0,1},{10,8},{12,10},{14... | collective-permute-start | bytes 1572872 | tf_op jit(solution)/shard_map/ppermute | solution.py:84
  229.4 19.5 %collective-permute-start.37 = (bf16[128,2048]{1,0:T(8,128)(2,1)S(1)}, bf16[128,2048]{1,0:T(8,128)(2,1)S(1)}, u32[]{:S(2)}, u32[]{:S(2)}) collective-permute-start(bf16[128,2048]{1,0:T(8,128)(2,1)S(1)} %collective-permute-done.35.refs_11_.refs_2_), channel_id=1, source_target_pairs={{0,2},{2,4},{4,6},{6,7},{7,5},{5,3},{3,1},{1,0},{8,10},{10,12},{12... | collective-permute-start | bytes 1572872 | tf_op jit(solution)/shard_map/ppermute | solution.py:84
  230.7 19.4 %collective-permute-start.38 = (bf16[128,2048]{1,0:T(8,128)(2,1)S(1)}, bf16[128,2048]{1,0:T(8,128)(2,1)S(1)}, u32[]{:S(2)}, u32[]{:S(2)}) collective-permute-start(bf16[128,2048]{1,0:T(8,128)(2,1)S(1)} %collective-permute-done.36.refs_14_.refs_5_), channel_id=1, source_target_pairs={{2,0},{4,2},{6,4},{7,6},{5,7},{3,5},{1,3},{0,1},{10,8},{12,10},{14... | collective-permute-start | bytes 1572872 | tf_op jit(solution)/shard_map/ppermute | solution.py:84
  231.4 36.1 %collective-permute-start.31 = (bf16[1024,512]{1,0:T(8,128)(2,1)}, bf16[1024,512]{1,0:T(8,128)(2,1)S(1)}, u32[]{:S(2)}, u32[]{:S(2)}) collective-permute-start(bf16[1024,512]{1,0:T(8,128)(2,1)} %bitcast.5.refs_19_), channel_id=1, source_target_pairs={{0,8},{1,9},{2,10},{3,11},{4,12},{5,13},{6,14},{7,15},{8,0},{9,1},... | collective-permute-start | bytes 3145736 | tf_op jit(solution)/shard_map/ppermute | solution.py:70
  239.1 28.4 %collective-permute-start.32 = (bf16[1024,512]{1,0:T(8,128)(2,1)S(1)}, bf16[1024,512]{1,0:T(8,128)(2,1)S(1)}, u32[]{:S(2)}, u32[]{:S(2)}) collective-permute-start(bf16[1024,512]{1,0:T(8,128)(2,1)S(1)} %collective-permute-done.24.refs_20_), channel_id=1, source_target_pairs={{0,8},{1,9},{2,10},{3,11},{4,12},{5,13},{6,14},{7,15},{8,0},{9,1},... | collective-permute-start | bytes 3145736 | tf_op jit(solution)/shard_map/ppermute | solution.py:70
  240.6 19.5 %collective-permute-start.27 = (bf16[128,2048]{1,0:T(8,128)(2,1)S(1)}, bf16[128,2048]{1,0:T(8,128)(2,1)S(1)}, u32[]{:S(2)}, u32[]{:S(2)}) collective-permute-start(bf16[128,2048]{1,0:T(8,128)(2,1)S(1)} %collective-permute-done.25.refs_2_), channel_id=1, source_target_pairs={{0,2},{2,4},{4,6},{6,7},{7,5},{5,3},{3,1},{1,0},{8,10},{10,12},{12... | collective-permute-start | bytes 1572872 | tf_op jit(solution)/shard_map/ppermute | solution.py:84
  348.9 24.0 %collective-permute-start.56 = (bf16[1024,512]{1,0:T(8,128)(2,1)S(1)}, bf16[1024,512]{1,0:T(8,128)(2,1)S(1)}, u32[]{:S(2)}, u32[]{:S(2)}) collective-permute-start(bf16[1024,512]{1,0:T(8,128)(2,1)S(1)} %add_convert_fusion.3), channel_id=1, source_target_pairs={{0,16},{1,17},{2,18},{3,19},{4,20},{5,21},{6,22},{7,23},{8,24},{9,... | collective-permute-start | bytes 3145736 | tf_op jit(solution)/shard_map/ppermute | solution.py:70
  385.1 71.6 %all-to-all-start.2 = ((bf16[8,128,512]{2,1,0:T(8,128)(2,1)}), bf16[8,128,512]{2,1,0:T(8,128)(2,1)}, u32[]{:S(2)}, u32[]{:S(2)}) async-start(bf16[8,128,512]{2,1,0:T(8,128)(2,1)} %bitcast.38), calls=%async_computation.2 | async-start | bytes 2097152 | tf_op jit(solution)/shard_map/all_to_all | solution.py:706
  389.4 15.3 %collective-permute-start.63 = (bf16[128,2048]{1,0:T(8,128)(2,1)}, bf16[128,2048]{1,0:T(8,128)(2,1)S(1)}, u32[]{:S(2)}, u32[]{:S(2)}) collective-permute-start(bf16[128,2048]{1,0:T(8,128)(2,1)} %fusion.5), channel_id=1, source_target_pairs={{0,16},{1,17},{2,18},{3,19},{4,20},{5,21},{6,22},{7,23},{8,24},{9,... | collective-permute-start | bytes 1572872 | tf_op jit(solution)/shard_map/ppermute | solution.py:70
  459.4 15.5 %collective-permute-start.70 = (bf16[128,2048]{1,0:T(8,128)(2,1)S(1)}, bf16[128,2048]{1,0:T(8,128)(2,1)S(1)}, u32[]{:S(2)}, u32[]{:S(2)}) collective-permute-start(bf16[128,2048]{1,0:T(8,128)(2,1)S(1)} %get-tuple-element.392), channel_id=1, source_target_pairs={{2,0},{4,2},{6,4},{7,6},{5,7},{3,5},{1,3},{0,1},{10,8},{12,10},{14... | collective-permute-start | bytes 1572872 | tf_op jit(solution)/shard_map/ppermute | solution.py:84
  467.8 16.9 %collective-permute-start.67 = (bf16[128,2048]{1,0:T(8,128)(2,1)S(1)}, bf16[128,2048]{1,0:T(8,128)(2,1)S(1)}, u32[]{:S(2)}, u32[]{:S(2)}) collective-permute-start(bf16[128,2048]{1,0:T(8,128)(2,1)S(1)} %get-tuple-element.387), channel_id=1, source_target_pairs={{0,2},{2,4},{4,6},{6,7},{7,5},{5,3},{3,1},{1,0},{8,10},{10,12},{12... | collective-permute-start | bytes 1572872 | tf_op jit(solution)/shard_map/ppermute | solution.py:84
  468.4 16.3 %collective-permute-start.68 = (bf16[128,2048]{1,0:T(8,128)(2,1)S(1)}, bf16[128,2048]{1,0:T(8,128)(2,1)S(1)}, u32[]{:S(2)}, u32[]{:S(2)}) collective-permute-start(bf16[128,2048]{1,0:T(8,128)(2,1)S(1)} %get-tuple-element.388), channel_id=1, source_target_pairs={{2,0},{4,2},{6,4},{7,6},{5,7},{3,5},{1,3},{0,1},{10,8},{12,10},{14... | collective-permute-start | bytes 1572872 | tf_op jit(solution)/shard_map/ppermute | solution.py:84
  485.3 31.6 %collective-permute-start.85 = (bf16[1024,512]{1,0:T(8,128)(2,1)}, bf16[1024,512]{1,0:T(8,128)(2,1)}, u32[]{:S(2)}, u32[]{:S(2)}) collective-permute-start(bf16[1024,512]{1,0:T(8,128)(2,1)} %get-tuple-element.422), channel_id=1, source_target_pairs={{0,8},{1,9},{2,10},{3,11},{4,12},{5,13},{6,14},{7,15},{8,0},{9,1},... | collective-permute-start | bytes 3145736 | tf_op jit(solution)/shard_map/ppermute | solution.py:70
  488.7 28.1 %collective-permute-start.79 = (bf16[1024,512]{1,0:T(8,128)(2,1)}, bf16[1024,512]{1,0:T(8,128)(2,1)}, u32[]{:S(2)}, u32[]{:S(2)}) collective-permute-start(bf16[1024,512]{1,0:T(8,128)(2,1)} %add_convert_fusion.1), channel_id=1, source_target_pairs={{0,16},{1,17},{2,18},{3,19},{4,20},{5,21},{6,22},{7,23},{8,24},{9,... | collective-permute-start | bytes 3145736 | tf_op jit(solution)/shard_map/ppermute | solution.py:70
  490.2 26.7 %all-to-all-start.3 = ((bf16[8,128,256]{2,1,0:T(8,128)(2,1)}), bf16[8,128,256]{2,1,0:T(8,128)(2,1)S(1)}, u32[]{:S(2)}, u32[]{:S(2)}) async-start(bf16[8,128,256]{2,1,0:T(8,128)(2,1)} %bitcast.16), calls=%async_computation.3 | async-start | bytes 1048576 | tf_op jit(solution)/shard_map/all_to_all | solution.py:297
  497.8 17.3 %collective-permute-start.75 = (bf16[128,2048]{1,0:T(8,128)(2,1)S(1)}, bf16[128,2048]{1,0:T(8,128)(2,1)S(1)}, u32[]{:S(2)}, u32[]{:S(2)}) collective-permute-start(bf16[128,2048]{1,0:T(8,128)(2,1)S(1)} %get-tuple-element.405), channel_id=1, source_target_pairs={{0,2},{2,4},{4,6},{6,7},{7,5},{5,3},{3,1},{1,0},{8,10},{10,12},{12... | collective-permute-start | bytes 1572872 | tf_op jit(solution)/shard_map/ppermute | solution.py:84
  499.9 17.0 %collective-permute-start.76 = (bf16[128,2048]{1,0:T(8,128)(2,1)S(1)}, bf16[128,2048]{1,0:T(8,128)(2,1)S(1)}, u32[]{:S(2)}, u32[]{:S(2)}) collective-permute-start(bf16[128,2048]{1,0:T(8,128)(2,1)S(1)} %get-tuple-element.406), channel_id=1, source_target_pairs={{2,0},{4,2},{6,4},{7,6},{5,7},{3,5},{1,3},{0,1},{10,8},{12,10},{14... | collective-permute-start | bytes 1572872 | tf_op jit(solution)/shard_map/ppermute | solution.py:84
  520.1 61.0 %all-to-all-start.4 = ((bf16[8,128,512]{2,1,0:T(8,128)(2,1)}), bf16[8,128,512]{2,1,0:T(8,128)(2,1)S(1)}, u32[]{:S(2)}, u32[]{:S(2)}) async-start(bf16[8,128,512]{2,1,0:T(8,128)(2,1)} %bitcast.39), calls=%async_computation.4 | async-start | bytes 2097152 | tf_op jit(solution)/shard_map/all_to_all | solution.py:297
  526.7 39.7 %collective-permute-start.101 = (bf16[8,128,512]{2,1,0:T(8,128)(2,1)}, bf16[8,128,512]{2,1,0:T(8,128)(2,1)S(1)}, u32[]{:S(2)}, u32[]{:S(2)}) collective-permute-start(bf16[8,128,512]{2,1,0:T(8,128)(2,1)} %all-to-all-done.2.own), channel_id=1, source_target_pairs={{0,16},{1,17},{2,18},{3,19},{4,20},{5,21},{6,22},{7,23},{8,24},{9,... | collective-permute-start | bytes 3145736 | tf_op jit(solution)/shard_map/ppermute | solution.py:70
  529.8 34.6 %collective-permute-start.104 = (bf16[128,2048]{1,0:T(8,128)(2,1)S(1)}, bf16[128,2048]{1,0:T(8,128)(2,1)}, u32[]{:S(2)}, u32[]{:S(2)}) collective-permute-start(bf16[128,2048]{1,0:T(8,128)(2,1)S(1)} %add_convert_fusion.4.own), channel_id=1, source_target_pairs={{0,16},{1,17},{2,18},{3,19},{4,20},{5,21},{6,22},{7,23},{8,24},{9,... | collective-permute-start | bytes 1572872 | tf_op jit(solution)/shard_map/ppermute | solution.py:70
  532.6 33.9 %collective-permute-start.83 = (bf16[128,2048]{1,0:T(8,128)(2,1)S(1)}, bf16[128,2048]{1,0:T(8,128)(2,1)S(1)}, u32[]{:S(2)}, u32[]{:S(2)}) collective-permute-start(bf16[128,2048]{1,0:T(8,128)(2,1)S(1)} %get-tuple-element.419), channel_id=1, source_target_pairs={{0,2},{2,4},{4,6},{6,7},{7,5},{5,3},{3,1},{1,0},{8,10},{10,12},{12... | collective-permute-start | bytes 1572872 | tf_op jit(solution)/shard_map/ppermute | solution.py:84
  534.7 34.6 %collective-permute-start.84 = (bf16[128,2048]{1,0:T(8,128)(2,1)S(1)}, bf16[128,2048]{1,0:T(8,128)(2,1)S(1)}, u32[]{:S(2)}, u32[]{:S(2)}) collective-permute-start(bf16[128,2048]{1,0:T(8,128)(2,1)S(1)} %get-tuple-element.420), channel_id=1, source_target_pairs={{2,0},{4,2},{6,4},{7,6},{5,7},{3,5},{1,3},{0,1},{10,8},{12,10},{14... | collective-permute-start | bytes 1572872 | tf_op jit(solution)/shard_map/ppermute | solution.py:84
  534.8 39.3 %collective-permute-start.86 = (bf16[128,2048]{1,0:T(8,128)(2,1)S(1)}, bf16[128,2048]{1,0:T(8,128)(2,1)S(1)}, u32[]{:S(2)}, u32[]{:S(2)}) collective-permute-start(bf16[128,2048]{1,0:T(8,128)(2,1)S(1)} %copy-done.107), channel_id=1, source_target_pairs={{0,16},{1,17},{2,18},{3,19},{4,20},{5,21},{6,22},{7,23},{8,24},{9,... | collective-permute-start | bytes 1572872 | tf_op jit(solution)/shard_map/ppermute | solution.py:70
  570.1 29.6 %collective-permute-start.100 = (bf16[8,128,512]{2,1,0:T(8,128)(2,1)}, bf16[8,128,512]{2,1,0:T(8,128)(2,1)}, u32[]{:S(2)}, u32[]{:S(2)}) collective-permute-start(bf16[8,128,512]{2,1,0:T(8,128)(2,1)} %all-to-all-done.2.own), channel_id=1, source_target_pairs={{0,8},{1,9},{2,10},{3,11},{4,12},{5,13},{6,14},{7,15},{8,0},{9,1},... | collective-permute-start | bytes 3145736 | tf_op jit(solution)/shard_map/ppermute | solution.py:70
  574.1 25.9 %collective-permute-start.102 = (bf16[8,128,512]{2,1,0:T(8,128)(2,1)S(1)}, bf16[8,128,512]{2,1,0:T(8,128)(2,1)}, u32[]{:S(2)}, u32[]{:S(2)}) collective-permute-start(bf16[8,128,512]{2,1,0:T(8,128)(2,1)S(1)} %collective-permute-done.101.other), channel_id=1, source_target_pairs={{0,8},{1,9},{2,10},{3,11},{4,12},{5,13},{6,14},{7,15},{8,0},{9,1},... | collective-permute-start | bytes 3145736 | tf_op jit(solution)/shard_map/ppermute | solution.py:70
  581.1 36.7 %collective-permute-start.92 = (bf16[8,128,512]{2,1,0:T(8,128)(2,1)S(1)}, bf16[8,128,512]{2,1,0:T(8,128)(2,1)}, u32[]{:S(2)}, u32[]{:S(2)}) collective-permute-start(bf16[8,128,512]{2,1,0:T(8,128)(2,1)S(1)} %all-to-all-done.4.own), channel_id=1, source_target_pairs={{0,16},{1,17},{2,18},{3,19},{4,20},{5,21},{6,22},{7,23},{8,24},{9,... | collective-permute-start | bytes 3145736 | tf_op jit(solution)/shard_map/ppermute | solution.py:70
  581.6 20.3 %collective-permute-start.94 = (bf16[8,128,256]{2,1,0:T(8,128)(2,1)S(1)}, bf16[8,128,256]{2,1,0:T(8,128)(2,1)S(1)}, u32[]{:S(2)}, u32[]{:S(2)}) collective-permute-start(bf16[8,128,256]{2,1,0:T(8,128)(2,1)S(1)} %all-to-all-done.3.own), channel_id=1, source_target_pairs={{0,8},{1,9},{2,10},{3,11},{4,12},{5,13},{6,14},{7,15},{8,0},{9,1},... | collective-permute-start | bytes 1572872 | tf_op jit(solution)/shard_map/ppermute | solution.py:70
  599.7 36.1 %collective-permute-start.88 = (bf16[128,2048]{1,0:T(8,128)(2,1)}, bf16[128,2048]{1,0:T(8,128)(2,1)}, u32[]{:S(2)}, u32[]{:S(2)}) collective-permute-start(bf16[128,2048]{1,0:T(8,128)(2,1)} %get-tuple-element.428), channel_id=1, source_target_pairs={{0,2},{2,4},{4,6},{6,7},{7,5},{5,3},{3,1},{1,0},{8,10},{10,12},{12... | collective-permute-start | bytes 1572872 | tf_op jit(solution)/shard_map/ppermute | solution.py:84
  600.0 35.9 %collective-permute-start.89 = (bf16[128,2048]{1,0:T(8,128)(2,1)}, bf16[128,2048]{1,0:T(8,128)(2,1)}, u32[]{:S(2)}, u32[]{:S(2)}) collective-permute-start(bf16[128,2048]{1,0:T(8,128)(2,1)} %get-tuple-element.429), channel_id=1, source_target_pairs={{2,0},{4,2},{6,4},{7,6},{5,7},{3,5},{1,3},{0,1},{10,8},{12,10},{14... | collective-permute-start | bytes 1572872 | tf_op jit(solution)/shard_map/ppermute | solution.py:84
  602.7 35.5 %collective-permute-start.98 = (bf16[128,2048]{1,0:T(8,128)(2,1)S(1)}, bf16[128,2048]{1,0:T(8,128)(2,1)S(1)}, u32[]{:S(2)}, u32[]{:S(2)}) collective-permute-start(bf16[128,2048]{1,0:T(8,128)(2,1)S(1)} %fusion.4.own), channel_id=1, source_target_pairs={{0,16},{1,17},{2,18},{3,19},{4,20},{5,21},{6,22},{7,23},{8,24},{9,... | collective-permute-start | bytes 1572872 | tf_op jit(solution)/shard_map/ppermute | solution.py:70
  617.7 25.3 %collective-permute-start.91 = (bf16[8,128,512]{2,1,0:T(8,128)(2,1)S(1)}, bf16[8,128,512]{2,1,0:T(8,128)(2,1)}, u32[]{:S(2)}, u32[]{:S(2)}) collective-permute-start(bf16[8,128,512]{2,1,0:T(8,128)(2,1)S(1)} %all-to-all-done.4.own), channel_id=1, source_target_pairs={{0,8},{1,9},{2,10},{3,11},{4,12},{5,13},{6,14},{7,15},{8,0},{9,1},... | collective-permute-start | bytes 3145736 | tf_op jit(solution)/shard_map/ppermute | solution.py:70
  617.7 25.3 %collective-permute-start.93 = (bf16[8,128,512]{2,1,0:T(8,128)(2,1)}, bf16[8,128,512]{2,1,0:T(8,128)(2,1)}, u32[]{:S(2)}, u32[]{:S(2)}) collective-permute-start(bf16[8,128,512]{2,1,0:T(8,128)(2,1)} %collective-permute-done.92.other), channel_id=1, source_target_pairs={{0,8},{1,9},{2,10},{3,11},{4,12},{5,13},{6,14},{7,15},{8,0},{9,1},... | collective-permute-start | bytes 3145736 | tf_op jit(solution)/shard_map/ppermute | solution.py:70
  (179 other events, 1688.7 us)

commit v4 on v3

--- a/solution.py
+++ b/solution.py
@@ -14,7 +14,7 @@
 bf16 = jnp.bfloat16
 BOTH = ("rep", "fsdp")
 CORE, X = 3, 4
-LIMITS = (26, 30, 38, 30, 38, 24)
+LIMITS = (52, 30, 38, 30, 56, 24)
 
 
 def dot(a, b, ca=1, cb=0, kind=f32):
@@ -51,6 +51,69 @@
         compiler_params=pltpu.CompilerParams(vmem_limit_bytes=limit << 20),
         cost_estimate=pl.CostEstimate(flops=0, bytes_accessed=0, transcendentals=0),
     )(*ins)
+
+
+def streamed(body, outs, *ins, scalars=None, scratch=(), limit=8, late=(), stream=()):
+    whole = pl.BlockSpec(memory_space=pltpu.VMEM)
+    away = pl.BlockSpec(memory_space=pltpu.HBM)
+    first = 0 if scalars is None else 1
+    n_in, n_out, n_own = len(ins), len(outs), len(scratch)
+    late, stream = list(late), list(stream)
+    pushes = len(stream)
+
+    def run(*refs):
+        given, refs = refs[:first], refs[first:]
+        ins, refs = list(refs[:n_in]), refs[n_in:]
+        outs, refs = list(refs[:n_out]), refs[n_out:]
+        own, refs = refs[:n_own], refs[n_own:]
+        rooms, refs = refs[: len(late)], refs[len(late) :]
+        stages, refs = refs[: len(stream)], refs[len(stream) :]
+        comes, goes = refs
+        arrivals, departures = {}, []
+        for k, (i, room) in enumerate(zip(late, rooms)):
+            arrivals[i] = pltpu.make_async_copy(ins[i], room, comes.at[k])
+            arrivals[i].start()
+            ins[i] = room
+        targets = {}
+        for i, stage in zip(stream, stages):
+            targets[i], outs[i] = outs[i], stage
+
+        def ready(*numbers):
+            for i in numbers:
+                arrivals.pop(i).wait()
+
+        def push(i, *index):
+            source, target = outs[i], targets[i]
+            if index:
+                source, target = source.at[index], target.at[index]
+            copy = pltpu.make_async_copy(source, target, goes.at[len(departures)])
+            copy.start()
+            departures.append(copy)
+
+        more = {}
+        if late:
+            more["ready"] = ready
+        if stream:
+            more["push"] = push
+        body(*given, *ins, *outs, *own, **more)
+        for copy in departures:
+            copy.wait()
+
+    specs = [away if i in late else whole for i in range(n_in)]
+    if scalars is not None:
+        specs = [pl.BlockSpec(memory_space=pltpu.SMEM)] + specs
+    rooms = [pltpu.VMEM(ins[i].shape, ins[i].dtype) for i in late]
+    stages = [pltpu.VMEM(outs[i].shape, outs[i].dtype) for i in stream]
+    sems = [pltpu.SemaphoreType.DMA((max(len(late), 1),)), pltpu.SemaphoreType.DMA((pushes,))]
+    return pl.pallas_call(
+        run,
+        out_shape=list(outs),
+        in_specs=specs,
+        out_specs=[away if i in stream else whole for i in range(n_out)],
+        scratch_shapes=[*scratch, *rooms, *stages, *sems],
+        compiler_params=pltpu.CompilerParams(vmem_limit_bytes=limit << 20),
+        cost_estimate=pl.CostEstimate(flops=0, bytes_accessed=0, transcendentals=0),
+    )(*(() if scalars is None else (scalars,)), *ins)
 
 
 def number():
@@ -275,29 +338,29 @@
             value = value + swap(value.astype(bf16), place).astype(f32)
         return value
 
-    def columns_grad(z, own, other):
-        size = own.shape[-1]
-
-        def body(z, own, other, *outs):
-            for t in (0, 1):
-                rows_t = z[:, t * half_width : (t + 1) * half_width]
-                for out, part in ((outs[t], own), (outs[2 + t], other)):
-                    out[...] = dot(rows_t, part[...], 0, 0).astype(bf16)
-
-        return kernel(body, [shape((half_width, size), bf16)] * 4, z, own, other, limit=LIMITS[5])
+    def columns_grad(z, halves_of):
+        size = halves_of.shape[-1]
+
+        def body(z, parts, *outs):
+            for j in (1, 0):
+                for t in (1, 0):
+                    rows_t = z[:, t * half_width : (t + 1) * half_width]
+                    outs[2 * j + t][...] = dot(rows_t, parts[j], 0, 0).astype(bf16)
+
+        return kernel(body, [shape((half_width, size), bf16)] * 4, z, halves_of, limit=LIMITS[5])
 
     def sum_cores(own, own_t, other, other_t):
-        kept = own.astype(f32) + swap(own_t, CORE).astype(f32)
         given = other.astype(f32) + swap(other_t, CORE).astype(f32)
-        return kept, given.astype(bf16)
-
-    def give(kept, got):
-        grad = more(kept + got.astype(f32)).astype(bf16)
+        return own, swap(own_t, CORE), given.astype(bf16)
+
+    def sum_x(own, own_c, got):
+        return more(own.astype(f32) + own_c.astype(f32) + got.astype(f32)).astype(bf16)
+
+    def give(grad):
         grad = grad.reshape(n, half_depth, grad.shape[-1])
         return lax.all_to_all(grad, "fsdp", 0, 0, tiled=True)
 
-    def everywhere(own):
-        other = swap(own, X)
+    def everywhere(own, other):
         return own, swap(own, CORE), other, swap(other, CORE)
 
     def flat(pieces, sizes):
@@ -375,14 +438,6 @@
     pair_f32 = shape((2, width), f32)
     room_of_block = [pltpu.VMEM((rows, width), f32)]
 
-    def first_norm(s, *refs):
-        parts, gains, z, room = refs[:-3], refs[-3], refs[-2], refs[-1]
-        values = jnp.concatenate([part[...] for part in parts], 0).astype(f32)
-        normed, _ = normalize(values)
-        room[...] = normed * gains[0:1] + gains[1:2]
-        for start, columns in arranged(s):
-            z[:, start : start + half_depth] = room[:, columns].astype(bf16)
-
     def second_norm(s, *refs):
         sums, (tokens, gains, resid, z, room) = refs[:3], refs[3:]
         value = tokens[...].astype(f32) + total(sums)
@@ -431,14 +486,27 @@
         second = jnp.where(x == 0, other, own)
         return first, second
 
-    def project(s, *refs):
-        zs, w, (cosine, sine, q, k, v, g) = refs[:4], refs[4:8], refs[8:]
+    def of_x(ref, x, size):
+        return [ref[pl.ds(pl.multiple_of(i * size, size), size), :] for i in (x, 1 - x)]
+
+    def mixer(s, *refs, ready, push):
+        pieces, gains, w, (cosine, sine, decay, w_out), refs = (
+            refs[:9], refs[9], refs[10:14], refs[14:18], refs[18:]
+        )
+        z, q, k, v, g, p, retained, mixed, *outs, room = refs
         x = s[1]
-        one = dk // 2
+        one, half, middle = dk // 2, dv // 2, dk + dv // 2
+        for i in tiles:
+            normed, _ = normalize(tile(pieces, i).astype(f32))
+            room[...] = normed * gains[0:1] + gains[1:2]
+            for start, columns in arranged(s):
+                z[rows_of(i), start : start + half_depth] = room[:, columns].astype(bf16)
+        push(0)
+        ready(10, 11, 12, 13, 14, 15)
         for i in tiles:
             here = rows_of(i)
             own, other = (
-                dot(zs[i][:, halves[0]], w[j][...]) + dot(zs[i][:, halves[1]], w[2 + j][...])
+                dot(z[here, halves[0]], w[j][...]) + dot(z[here, halves[1]], w[2 + j][...])
                 for j in (0, 1)
             )
             c, sn = cosine[here], sine[here]
@@ -448,16 +516,13 @@
             a, b = in_order(x, own[:, one:dk], other[:, one:dk])
             k[here, :one] = ((a * c - b * sn) * dk**-0.5).astype(bf16)
             k[here, one:] = ((b * c + a * sn) * dk**-0.5).astype(bf16)
-            middle = dk + dv // 2
-            v[here, : dv // 2] = own[:, dk:middle].astype(bf16)
-            v[here, dv // 2 :] = other[:, dk:middle].astype(bf16)
-            g[here, : dv // 2] = own[:, middle:]
-            g[here, dv // 2 :] = other[:, middle:]
-
-    def of_x(ref, x, size):
-        return [ref[pl.ds(pl.multiple_of(i * size, size), size), :] for i in (x, 1 - x)]
-
-    def mix(s, q, k, v, decay, g, w, p, retained, mixed, *outs):
+            v[here, :half] = own[:, dk:middle].astype(bf16)
+            v[here, half:] = other[:, dk:middle].astype(bf16)
+            g[here, :half] = own[:, middle:]
+            g[here, half:] = other[:, middle:]
+        for i in (1, 2, 3, 4):
+            push(i)
+        ready(16, 17)
         for i in tiles:
             here = rows_of(i)
             scores = (dot(q[here], k[...], 1, 1) * decay[here]).astype(bf16)
@@ -468,9 +533,10 @@
             gate = g[here]
             part = (normed * gate / (1.0 + jnp.exp(-gate))).astype(bf16)
             mixed[here] = part
-            half = dv // 2
-            own, other = of_x(w, s[1], half)
+            own, other = of_x(w_out, x, half)
             put_tile(outs, i, dot(part[:, :half], own) + dot(part[:, half:], other))
+        for i in (9, 10, 8, 5, 6, 7):
+            push(i)
 
     def join_tiles(*refs):
         for i in tiles:
@@ -510,30 +576,34 @@
             own, other = of_x(w, s[1], half)
             put_tile(outs, i, dot(h[here, :half], own) + dot(h[here, half:], other))
 
-    def mix_back(s, *refs):
-        pieces, (w, r, g, mixed, kept, given, d_retained, d_gate, d_out) = refs[:9], refs[9:]
-        half = dv // 2
+    def mixer_back(s, *refs, ready, push):
+        pieces, (w_out, r, g, mixed, q, k, v, p, decay, cosine, sine), w, z = (
+            refs[:9], refs[9:20], refs[20:24], refs[24]
+        )
+        kept, given, sums, d_pre, *outs = refs[25:32]
+        d_out, d_r, d_k, d_v, room = refs[32:]
+        one, half = dk // 2, dv // 2
+        cut = dk + half
+        x = s[1]
+        ready(9, 10, 11)
         for i in tiles:
             here = rows_of(i)
             part = tile(pieces, i)
             d_out[here] = part
-            own, other = of_x(w, s[1], half)
+            own, other = of_x(w_out, x, half)
             d_mixed = jnp.concatenate([dot(part, own, 1, 1), dot(part, other, 1, 1)], -1)
             d_mixed = d_mixed.astype(bf16).astype(f32)
             normed, scale = head_norm(r[here])
             gate = g[here]
             sigmoid = 1.0 / (1.0 + jnp.exp(-gate))
             both = (d_mixed * normed * sigmoid * (1.0 + gate * (1.0 - sigmoid))).astype(bf16)
-            d_gate[0, here], d_gate[1, here] = both[:, :half], both[:, half:]
-            d_retained[here] = normalize_back(normed, scale, d_mixed * gate * sigmoid).astype(bf16)
+            d_pre[0, here, cut:], d_pre[1, here, cut:] = both[:, :half], both[:, half:]
+            d_r[here] = normalize_back(normed, scale, d_mixed * gate * sigmoid).astype(bf16)
+        ready(12)
         rows_products(s, mixed, d_out, kept, given)
-
-    def within_back(s, d_r, d_g, q, k, v, p, decay, cosine, sine, *refs):
-        w, zs, (d_pre, sums), outs = refs[:4], refs[4:8], refs[8:10], refs[10:13]
-        d_k, d_v, room = refs[13:]
-        cut = dk + dv // 2
-        one, half = dk // 2, dv // 2
-        x = s[1]
+        push(0)
+        push(1)
+        ready(13, 14, 15, 16, 17, 18, 19)
         for i in tiles:
             here = rows_of(i)
             scores = (dot(d_r[here], v[...], 1, 1) * decay[here]).astype(bf16)
@@ -556,20 +626,22 @@
             own, other = in_order(x, a * c + b * sn, b * c - a * sn)
             d_pre[0, here, one:dk] = own.astype(bf16)
             d_pre[1, here, one:dk] = other.astype(bf16)
-            d_pre[0, here, dk:] = d_v[here, :half].astype(bf16)
-            d_pre[1, here, dk:] = d_v[here, half:].astype(bf16)
-            back = []
-            for t in (0, 1):
-                part = dot(d_g[0, here], w[2 * t][:, cut:], 1, 1)
-                part = part + dot(d_g[1, here], w[2 * t + 1][:, cut:], 1, 1)
-                for j in (0, 1):
-                    part = part + dot(d_pre[j, here], w[2 * t + j][:, :cut], 1, 1)
-                back.append(part)
+            d_pre[0, here, dk:cut] = d_v[here, :half].astype(bf16)
+            d_pre[1, here, dk:cut] = d_v[here, half:].astype(bf16)
+        push(3)
+        ready(20, 21, 22, 23, 24)
+        for i in tiles:
+            here = rows_of(i)
+            back = [
+                dot(d_pre[0, here], w[2 * t][...], 1, 1)
+                + dot(d_pre[1, here], w[2 * t + 1][...], 1, 1)
+                for t in (0, 1)
+            ]
             back = jnp.concatenate(back, -1)
             put_tile(outs, i, back)
             parts = jnp.concatenate(
                 [
-                    jnp.sum(back * zs[i][...].astype(f32), axis=0, keepdims=True),
+                    jnp.sum(back * z[here].astype(f32), axis=0, keepdims=True),
                     jnp.sum(back, axis=0, keepdims=True),
                 ],
                 0,
@@ -578,16 +650,19 @@
                 room[...] = parts
             else:
                 room[...] += parts
+        for i in (5, 6, 4):
+            push(i)
         for start, columns in arranged(s):
             sums[:, columns] = room[:, start : start + half_depth]
 
     terms = term_shapes(rows, width)
 
 
-    gains = jnp.stack([norm1_gain, norm1_bias, norm2_gain, norm2_bias])
-    packed, tokens_late, gains_late, ffn_gate_late, ffn_up_late = after(
-        fetch(w_query, w_key, w_value, w_gate), tokens, gains, w_ffn_gate, w_ffn_up
-    )
+    packed, tokens_late, ffn_gate_late, ffn_up_late, *gains_late = after(
+        fetch(w_query, w_key, w_value, w_gate), tokens, w_ffn_gate, w_ffn_up,
+        norm1_gain, norm1_bias, norm2_gain, norm2_bias,
+    )
+    gains_late = jnp.stack(gains_late)
     mix_own = trade(packed)
     ring = Gather(tokens_late)
 
@@ -616,42 +691,27 @@
     (gains,) = ring.step(widen(gains, 2))
     gains = gains.astype(f32)
 
-    def norm_tile(*parts):
-        return kernel(
-            first_norm,
-            [shape((2 * rows, width), bf16)],
-            *parts, gains,
-            scalars=where, scratch=[pltpu.VMEM((2 * rows, width), f32)],
-        )[0]
-
-    z0 = norm_tile(ring.own, ring.ahead[1])
-    z2 = norm_tile(*ring.behind[1:3])
-    z1 = norm_tile(*ring.ahead[2:4])
-    z0, z1, z2, mix_other, mix_own_c = ring.step(z0, z1, z2, mix_other, mix_own_c)
+    mix_other, mix_own_c, ffn_packed = ring.step(mix_other, mix_own_c, ffn_packed)
     mix_other_c = swap(mix_other, CORE)
-    z3 = norm_tile(ring.behind[3], ring.ahead[4], ring.behind[4])
     w_mix = (mix_own, mix_other, mix_own_c, mix_other_c)
-    *w_mix, z0, z1, z2, z3, ffn_packed = after(*w_mix, z0, z1, z2, z3, ffn_packed)
-    zs = (z0, z1, z2, z3)
     ffn_own = trade(ffn_packed)
-    query, key, value, gate = kernel(
-        project,
-        [shape((every, dk), bf16)] * 2 + [shape((every, dv), bf16), shape((every, dv), f32)],
-        *zs, *w_mix, cosine, sine,
-        scalars=where, limit=LIMITS[0],
-    )
-    scores, retained, mixed, *parts = kernel(
-        mix,
-        [shape((every, every), bf16), shape((every, dv), f32), shape((every, dv), bf16)] + terms,
-        query, key, value, decay, gate, w_out,
-        scalars=where, limit=LIMITS[1],
+    z_first, query, key, value, gate, scores, retained, mixed, *parts = streamed(
+        mixer,
+        [shape((every, width), bf16)]
+        + [shape((every, dk), bf16)] * 2
+        + [shape((every, dv), bf16), shape((every, dv), f32), shape((every, every), bf16)]
+        + [shape((every, dv), f32), shape((every, dv), bf16)]
+        + terms,
+        *ring.pieces(), gains, *w_mix, cosine, sine, decay, w_out,
+        scalars=where, limit=LIMITS[0], late=range(10, 18), stream=range(11),
+        scratch=[pltpu.VMEM((2 * rows, width), f32)],
     )
     ring = Scatter(parts)
-    cot_late, ffn_own = ring.hold(cotangent, ffn_own)
+    cot_late = ring.hold(cotangent)[0]
+    cot_ring = Gather(cot_late)
+    (ffn_own,) = ring.step(ffn_own)
     ffn_other = swap(ffn_own, X)
     ffn_own_c = swap(ffn_own, CORE)
-    cot_ring = Gather(cot_late)
-    ring.step()
     cot_ring.step()
     ring.step()
     cot_ring.step()
@@ -681,10 +741,10 @@
     (cot_all,) = ring.step(
         *kernel(join_tiles, [shape((every, width), bf16)], *cot_ring.pieces(), limit=12)
     )
-    grad_ffn = ring.step(*columns_grad(z_second, d_ab[0], d_ab[1]))
-    ffn_kept, ffn_given = sum_cores(*grad_ffn)
-    ffn_kept, ffn_given, down_kept, down_given = ring.step(
-        ffn_kept, ffn_given, *rows_grad(hidden, cot_all)
+    grad_ffn = ring.step(*columns_grad(z_second, d_ab))
+    ffn_own, ffn_own_c, ffn_given = sum_cores(*grad_ffn)
+    ffn_own, ffn_own_c, ffn_given, down_kept, down_given = ring.step(
+        ffn_own, ffn_own_c, ffn_given, *rows_grad(hidden, cot_all)
     )
     ffn_sent = swap(ffn_given, X)
     down_kept, down_given = ring.step(*sum_cores_rows(down_kept, down_given))
@@ -694,86 +754,80 @@
         scalars=where, scratch=room_of_block,
     )
     ring = Gather(part)
-    ffn_kept, down_given = ring.step(ffn_kept, down_given)
-    ffn_kept, ffn_sent, hidden_late = ring.step(ffn_kept, ffn_sent, hidden)
+    ffn_own, ffn_sent, down_given = ring.step(ffn_own, ffn_sent, down_given)
     down_sent = swap(down_given, X)
-    last = Scatter(kernel(down, terms, hidden_late, w_ffn_down, scalars=where, limit=20))
-    ffn_sum = more(ffn_kept + ffn_sent.astype(f32)).astype(bf16)
-    (ffn_sum,) = ring.step(ffn_sum)
-    a, b, down_sent, z_first = ring.step(*last.peek(), down_sent, jnp.concatenate(zs))
+    ffn_sum = sum_x(ffn_own, ffn_own_c, ffn_sent)
+    ring.step()
+    last = Scatter(kernel(down, terms, hidden, w_ffn_down, scalars=where, limit=20))
+    (down_sent,) = ring.step(down_sent)
+    down_owned = give_rows(down_kept, down_sent)
+    a, b, down_owned, ffn_sum = ring.step(*last.peek(), down_owned, ffn_sum)
     last.put(a, b)
 
-    ffn_owned = lax.all_to_all(
-        ffn_sum.reshape(n, half_depth, ffn_sum.shape[-1]), "fsdp", 0, 0, tiled=True
-    )
-    out_kept, out_given, d_retained, d_gate = kernel(
-        mix_back,
+    ffn_owned = give(ffn_sum)
+    down_other = swap(down_owned, X)
+    out_kept, out_given, first_sums, d_pre, *parts = streamed(
+        mixer_back,
         [shape((2, dv // 4, width), bf16)] * 2
-        + [shape((every, dv), bf16), shape((2, every, dv // 2), bf16)],
+        + [pair_f32, shape((2, every, dk + dv), bf16)]
+        + terms,
         *ring.pieces(), w_out, retained, gate, mixed,
-        scalars=where, limit=LIMITS[3], scratch=[pltpu.VMEM((every, width), bf16)],
-    )
-    d_pre, first_sums, *parts = kernel(
-        within_back,
-        [shape((2, every, dk + dv // 2), bf16), pair_f32] + terms,
-        d_retained, d_gate, query, key, value, scores, decay, cosine, sine, *w_mix, *zs,
-        scalars=where, limit=LIMITS[4],
+        query, key, value, scores, decay, cosine, sine, *w_mix, z_first,
+        scalars=where, limit=LIMITS[4], late=range(9, 25), stream=(0, 1, 3, 4, 5, 6),
         scratch=[
+            pltpu.VMEM((every, width), bf16),
+            pltpu.VMEM((every, dv), bf16),
             pltpu.VMEM((every, dk), f32),
             pltpu.VMEM((every, dv), f32),
             pltpu.VMEM((2, width), f32),
         ],
     )
+    out_kept, out_given, first_sums, d_pre, ffn_owned, *parts = after(
+        out_kept, out_given, first_sums, d_pre, ffn_owned, *parts
+    )
     ring = Scatter(parts)
     stack = jnp.concatenate([first_sums, second_sums])
-    *grad_gate, out_kept, out_given, stack_c, ffn_owned = ring.step(
-        *columns_grad(z_first, d_gate[0], d_gate[1]), out_kept, out_given,
-        swap(stack, CORE), ffn_owned,
-    )
-    stack = stack + stack_c
-    gate_kept, gate_given = sum_cores(*grad_gate)
-    grad_qkv = columns_grad(z_first, d_pre[0], d_pre[1])
-    gate_sent = swap(gate_given, X)
+    mix_own, mix_own_c, mix_given = sum_cores(*columns_grad(z_first, d_pre))
     out_kept, out_given = sum_cores_rows(out_kept, out_given)
-    down_owned = give_rows(down_kept, down_sent)
-    a, b, gate_sent, *grad_qkv, out_given, stack_c = ring.step(
-        *last.peek(), gate_sent, *grad_qkv, out_given, swap(stack, X)
-    )
-    last.put(a, b)
+    mix_own, mix_own_c, mix_given, out_kept, out_given, stack_c = ring.step(
+        mix_own, mix_own_c, mix_given, out_kept, out_given, swap(stack, X)
+    )
     stack = stack + stack_c
     for place in range(X + 1, bits()):
         stack = stack + swap(stack, place)
-    qkv_kept, qkv_given = sum_cores(*grad_qkv)
-    qkv_sent = swap(qkv_given, X)
-    gate_owned = give(gate_kept, gate_sent)
-    gate_owned, qkv_sent, stack_c = ring.step(gate_owned, qkv_sent, swap(stack, 0))
+    mix_sent = swap(mix_given, X)
+    stack_c, down_other = ring.step(swap(stack, CORE), down_other)
     stack = stack + stack_c
-    qkv_owned = give(qkv_kept, qkv_sent)
     out_sent = swap(out_given, X)
-    a, b, qkv_owned, out_sent, stack_c = ring.step(
-        *last.peek(), qkv_owned, out_sent, swap(stack, 1)
-    )
-    last.put(a, b)
+    (stack_c,) = ring.step(swap(stack, 0))
     stack = stack + stack_c
-    qkv_all = everywhere(qkv_owned)
+    mix_sent, stack_c = ring.step(mix_sent, swap(stack, 1))
+    stack = stack + stack_c
+    mix_owned = give(sum_x(mix_own, mix_own_c, mix_sent))
+    out_owned = give_rows(out_kept, out_sent)
+    ffn_other, out_other = swap(ffn_owned, X), swap(out_owned, X)
     grad_tokens = kernel(
         first_back, [block_f32], *ring.pieces(), tokens, grad_resid, gains,
         scalars=where, scratch=room_of_block,
     )[0]
-    out_owned = give_rows(out_kept, out_sent)
-    gate_all = everywhere(gate_owned)
-    ffn_all = everywhere(ffn_owned)
-    down_all = everywhere(down_owned)
-    out_all = everywhere(out_owned)
-    (stack_c,) = last.step(swap(stack, 2))
+    grad_down = flat_rows(everywhere(down_owned, down_other))
+    a, b, mix_owned, stack_c, ffn_other, out_other, grad_tokens, grad_down = after(
+        *last.peek(), mix_owned, swap(stack, 2), ffn_other, out_other, grad_tokens, grad_down
+    )
+    last.put(a, b)
     stack = lax.dynamic_slice_in_dim(stack + stack_c, head * depth, depth, 1)
     first_gain = (stack[0] - norm1_bias.astype(f32) * stack[1]) / norm1_gain.astype(f32)
+    mix_other = swap(mix_owned, X)
+    grad_ffn_gate, grad_ffn_up = flat(everywhere(ffn_owned, ffn_other), [ff, ff])
+    grad_out = flat_rows(everywhere(out_owned, out_other))
+    last.put(*last.peek())
+    a, b, mix_other, grad_ffn_gate, grad_ffn_up, grad_out = after(
+        last.a, last.b, mix_other, grad_ffn_gate, grad_ffn_up, grad_out
+    )
+    last.put(a, b)
+    mix_grads = last.step(*flat(everywhere(mix_owned, mix_other), [dk, dk, dv, dv]))
+    grad_query, grad_key, grad_value, grad_gate = mix_grads
     (output,) = kernel(last_sum, [block_bf16], *last.pieces(), resid)
-    grad_ffn_gate, grad_ffn_up = flat(ffn_all, [ff, ff])
-    grad_down = flat_rows(down_all)
-    (grad_gate,) = flat(gate_all, [dv])
-    grad_query, grad_key, grad_value = flat(qkv_all, [dk, dk, dv])
-    grad_out = flat_rows(out_all)
 
     return (
         output,

time: 657 us -> 593 us (0.903)
  local copies, waits for them, and re-layouts: 57.2 us -> 30.3 us
  starting transfers between devices: 131 us -> 116 us
  Pallas kernels: 125 us -> 115 us
    pallas_call x33 -> x24, Pallas kernels: 101 us -> 49.2 us  [kernel(): pl.pallas_call(body, out_shape=list(outs), grid=grid, in_specs=specs, out...]
    pallas_call x0 -> x2, Pallas kernels: none -> 47.6 us  [streamed(): pl.pallas_call(run, out_shape=list(outs), in_specs=specs, out_specs=[away...]
    ppermute x42 -> x36, waiting for transfers between devices: 133 us -> 94.8 us  [swap(): lax.ppermute(value, BOTH, [(i, i ^ 1 << place) for i in range(count)])]
    ppermute x64, waiting for transfers between devices: 181 us -> 216 us  [send(): lax.ppermute(value, 'fsdp', pairs if ahead else [(b, a) for a, b in pairs])]
    unnamed x232 -> x152, local copies, waits for them, and re-layouts: 47.4 us -> 26.3 us
    pallas_call x3 -> x2, Pallas kernels: 17.3 us -> 12.1 us  [flat(): pl.pallas_call(body, out_shape=[shape((depth, n * size), f32) for size in...]
    ppermute x42 -> x36, starting transfers between devices: 25.7 us -> 20.8 us  [swap(): lax.ppermute(value, BOTH, [(i, i ^ 1 << place) for i in range(count)])]
  transfers between devices with their start and end apart: 111 -> 104, of which waited for: 60 -> 66; matrix products, arithmetic and copies ran while one was open for 3% -> 3% of each run, Pallas kernels for 15% -> 16%
where the time goes in v4:
time: 593 us; the launch traced here: 588 us
  waiting for transfers between devices  311 us (52%)
  starting transfers between devices  116 us (20%)
  Pallas kernels  115 us (19%)
  local copies, waits for them, and re-layouts  30.3 us (5%)
  other arithmetic  13 us (2%)
    ppermute x64, waiting for transfers between devices, send(): lax.ppermute(value, 'fsdp', pairs if ahead else [(b, a) for a, b in pairs])  216 us
    ppermute x36, waiting for transfers between devices, swap(): lax.ppermute(value, BOTH, [(i, i ^ 1 << place) for i in range(count)])  94.8 us
    ppermute x64, starting transfers between devices, send(): lax.ppermute(value, 'fsdp', pairs if ahead else [(b, a) for a, b in pairs])  75 us
    pallas_call x24, Pallas kernels, kernel(): pl.pallas_call(body, out_shape=list(outs), grid=grid, in_specs=specs, out...  49.2 us
    pallas_call x2, Pallas kernels, streamed(): pl.pallas_call(run, out_shape=list(outs), in_specs=specs, out_specs=[away...  47.6 us
    unnamed x152, local copies, waits for them, and re-layouts  26.3 us
    ppermute x36, starting transfers between devices, swap(): lax.ppermute(value, BOTH, [(i, i ^ 1 << place) for i in range(count)])  20.8 us
    pallas_call x2, Pallas kernels, flat(): pl.pallas_call(body, out_shape=[shape((depth, n * size), f32) for size in...  12.1 us
  transfers between devices with their start and end apart: 104, of which 66 were waited for; matrix products, arithmetic and copies ran while one was open for 3% of the time, Pallas kernels for 16%

profile of v4, /device:TPU:0, one launch (start us, length us, event | category | flops | bytes accessed | tf_op | source)
XLA Modules:
  0.0 588.2 jit_solution(9957959160113268213)
XLA Ops:
  1.2 3.5 shard_map.272
  4.9 7.4 %all-to-all-start = ((bf16[8,128,768]{2,1,0:T(8,128)(2,1)}), bf16[8,128,768]{2,1,0:T(8,128)(2,1)}, u32[]{:S(2)}, u32[]{:S(2)}) async-start(bf16[8,128,768]{2,1,0:T(8,128)(2,1)} %shard_map.272), calls=%async_computation | async-start | bytes 3145728 | tf_op jit(solution)/shard_map/all_to_all | solution.py:333
  24.7 3.1 shard_map.273
  27.7 15.0 %collective-permute-done.2 = bf16[4,256]{1,0:T(4,128)(2,1)S(1)} collective-permute-done((bf16[4,256]{1,0:T(4,128)(2,1)S(1)}, bf16[4,256]{1,0:T(4,128)(2,1)S(1)}, u32[]{:S(2)}, u32[]{:S(2)}) %collective-permute-start.2) | collective-permute-done | bytes 2080 | tf_op jit(solution)/shard_map/ppermute | solution.py:133
  42.8 8.4 %collective-permute-done.1.refs_5_ = bf16[128,2048]{1,0:T(8,128)(2,1)S(1)} collective-permute-done((bf16[128,2048]{1,0:T(8,128)(2,1)S(1)}, bf16[128,2048]{1,0:T(8,128)(2,1)S(1)}, u32[]{:S(2)}, u32[]{:S(2)}) %collective-permute-start.1) | collective-permute-done | bytes 524320 | tf_op jit(solution)/shard_map/ppermute | solution.py:147
  52.9 9.9 %collective-permute-start.3 = (bf16[128,2048]{1,0:T(8,128)(2,1)S(1)}, bf16[128,2048]{1,0:T(8,128)(2,1)S(1)}, u32[]{:S(2)}, u32[]{:S(2)}) collective-permute-start(bf16[128,2048]{1,0:T(8,128)(2,1)S(1)} %collective-permute-done.refs_2_), channel_id=1, source_target_pairs={{0,2},{2,4},{4,6},{6,7},{7,5},{5,3},{3,1},{1,0},{8,10},{10,12},{12... | collective-permute-start | bytes 1572872 | tf_op jit(solution)/shard_map/ppermute | solution.py:147
  64.8 11.8 %collective-permute-done.5 = bf16[4,512]{1,0:T(4,128)(2,1)S(1)} collective-permute-done((bf16[4,512]{1,0:T(4,128)(2,1)S(1)}, bf16[4,512]{1,0:T(4,128)(2,1)S(1)}, u32[]{:S(2)}, u32[]{:S(2)}) %collective-permute-start.5) | collective-permute-done | bytes 4128 | tf_op jit(solution)/shard_map/ppermute | solution.py:133
  79.5 11.2 %collective-permute-done.8 = bf16[4,1024]{1,0:T(4,128)(2,1)S(1)} collective-permute-done((bf16[4,1024]{1,0:T(4,128)(2,1)S(1)}, bf16[4,1024]{1,0:T(4,128)(2,1)S(1)}, u32[]{:S(2)}, u32[]{:S(2)}) %collective-permute-start.8) | collective-permute-done | bytes 8224 | tf_op jit(solution)/shard_map/ppermute | solution.py:133
  92.9 4.3 collective-permute-done.10.refs_9_
  98.0 4.5 all-to-all-start.1
  102.5 23.3 %shard_map.274 = (bf16[1024,2048]{1,0:T(8,128)(2,1)}, bf16[1024,256]{1,0:T(8,128)(2,1)S(1)}, bf16[1024,256]{1,0:T(8,128)(2,1)}, bf16[1024,512]{1,0:T(8,128)(2,1)...) custom-call(s32[2]{0:T(128)S(1)} %copy-done.47, ...), custom_call_target="tpu_custom_call" | custom-call | tf_op jit(solution)/shard_map/pallas_call | solution.py:108
  128.8 6.2 %collective-permute-done.14.a = bf16[64,2048]{1,0:T(8,128)(2,1)S(1)} collective-permute-done((bf16[64,2048]{1,0:T(8,128)(2,1)S(1)}, bf16[64,2048]{1,0:T(8,128)(2,1)S(1)}, u32[]{:S(2)}, u32[]{:S(2)}) %collective-permute-start.14) | collective-permute-done | bytes 262176 | tf_op jit(solution)/shard_map/ppermute | solution.py:147
  140.7 10.5 %collective-permute-done.16.a = bf16[128,2048]{1,0:T(8,128)(2,1)S(1)} collective-permute-done((bf16[128,2048]{1,0:T(8,128)(2,1)S(1)}, bf16[128,2048]{1,0:T(8,128)(2,1)S(1)}, u32[]{:S(2)}, u32[]{:S(2)}) %collective-permute-start.16) | collective-permute-done | bytes 524320 | tf_op jit(solution)/shard_map/ppermute | solution.py:147
  154.8 9.4 %collective-permute-done.18.a = bf16[128,2048]{1,0:T(8,128)(2,1)S(1)} collective-permute-done((bf16[128,2048]{1,0:T(8,128)(2,1)S(1)}, bf16[128,2048]{1,0:T(8,128)(2,1)S(1)}, u32[]{:S(2)}, u32[]{:S(2)}) %collective-permute-start.18) | collective-permute-done | bytes 524320 | tf_op jit(solution)/shard_map/ppermute | solution.py:147
  170.1 10.3 %collective-permute-done.20.refs_1_ = bf16[128,2048]{1,0:T(8,128)(2,1)S(1)} collective-permute-done((bf16[128,2048]{1,0:T(8,128)(2,1)S(1)}, bf16[128,2048]{1,0:T(8,128)(2,1)S(1)}, u32[]{:S(2)}, u32[]{:S(2)}) %collective-permute-start.20) | collective-permute-done | bytes 524320 | tf_op jit(solution)/shard_map/ppermute | solution.py:147
  185.6 7.9 %collective-permute-done.34.refs_13_.refs_4_ = bf16[128,2048]{1,0:T(8,128)(2,1)S(1)} collective-permute-done((bf16[128,2048]{1,0:T(8,128)(2,1)S(1)}, bf16[128,2048]{1,0:T(8,128)(2,1)S(1)}, u32[]{:S(2)}, u32[]{:S(2)}) %collective-permute-start.34) | collective-permute-done | bytes 524320 | tf_op jit(solution)/shard_map/ppermute | solution.py:147
  195.5 9.2 %collective-permute-done.23.refs_4_ = bf16[128,2048]{1,0:T(8,128)(2,1)S(1)} collective-permute-done((bf16[128,2048]{1,0:T(8,128)(2,1)S(1)}, bf16[128,2048]{1,0:T(8,128)(2,1)S(1)}, u32[]{:S(2)}, u32[]{:S(2)}) %collective-permute-start.23) | collective-permute-done | bytes 524320 | tf_op jit(solution)/shard_map/ppermute | solution.py:147
  206.7 7.3 %collective-permute-done.35.refs_11_.refs_2_ = bf16[128,2048]{1,0:T(8,128)(2,1)S(1)} collective-permute-done((bf16[128,2048]{1,0:T(8,128)(2,1)S(1)}, bf16[128,2048]{1,0:T(8,128)(2,1)S(1)}, u32[]{:S(2)}, u32[]{:S(2)}) %collective-permute-start.35) | collective-permute-done | bytes 524320 | tf_op jit(solution)/shard_map/ppermute | solution.py:147
  218.0 7.3 %collective-permute-done.25.refs_2_ = bf16[128,2048]{1,0:T(8,128)(2,1)S(1)} collective-permute-done((bf16[128,2048]{1,0:T(8,128)(2,1)S(1)}, bf16[128,2048]{1,0:T(8,128)(2,1)S(1)}, u32[]{:S(2)}, u32[]{:S(2)}) %collective-permute-start.25) | collective-permute-done | bytes 524320 | tf_op jit(solution)/shard_map/ppermute | solution.py:147
  227.9 7.3 %collective-permute-done.37.refs_12_.refs_3_ = bf16[128,2048]{1,0:T(8,128)(2,1)S(1)} collective-permute-done((bf16[128,2048]{1,0:T(8,128)(2,1)S(1)}, bf16[128,2048]{1,0:T(8,128)(2,1)S(1)}, u32[]{:S(2)}, u32[]{:S(2)}) %collective-permute-start.37) | collective-permute-done | bytes 524320 | tf_op jit(solution)/shard_map/ppermute | solution.py:147
  236.5 7.1 %collective-permute-done.27.refs_3_ = bf16[128,2048]{1,0:T(8,128)(2,1)S(1)} collective-permute-done((bf16[128,2048]{1,0:T(8,128)(2,1)S(1)}, bf16[128,2048]{1,0:T(8,128)(2,1)S(1)}, u32[]{:S(2)}, u32[]{:S(2)}) %collective-permute-start.27) | collective-permute-done | bytes 524320 | tf_op jit(solution)/shard_map/ppermute | solution.py:147
  245.0 5.0 collective-permute-done.28.refs_6_
  259.4 17.0 %shard_map.279 = (bf16[1024,2048]{1,0:T(8,128)(2,1)}, bf16[1024,512]{1,0:T(8,128)(2,1)S(1)}, bf16[2,1024,512]{2,1,0:T(8,128)(2,1)S(1)}, bf16[896,2048]{1,0:T(8,1...) custom-call(s32[2]{0:T(128)S(1)} %copy-done.47, bf16[128,2048]{1,0:T(8,128)(2,1)S(1)} %get-tuple-element.275.refs_0_, ...), custom_call_target="tpu_custom_call" | custom-call | tf_op jit(solution)/shard_map/pallas_call | solution.py:44
  278.7 6.9 %collective-permute-done.41.a = bf16[64,2048]{1,0:T(8,128)(2,1)S(1)} collective-permute-done((bf16[64,2048]{1,0:T(8,128)(2,1)S(1)}, bf16[64,2048]{1,0:T(8,128)(2,1)S(1)}, u32[]{:S(2)}, u32[]{:S(2)}) %collective-permute-start.41) | collective-permute-done | bytes 262176 | tf_op jit(solution)/shard_map/ppermute | solution.py:147
  289.3 4.5 shard_map.283
  303.0 8.5 %collective-permute-done.45.a = bf16[128,2048]{1,0:T(8,128)(2,1)S(1)} collective-permute-done((bf16[128,2048]{1,0:T(8,128)(2,1)S(1)}, bf16[128,2048]{1,0:T(8,128)(2,1)S(1)}, u32[]{:S(2)}, u32[]{:S(2)}) %collective-permute-start.45) | collective-permute-done | bytes 524320 | tf_op jit(solution)/shard_map/ppermute | solution.py:147
  315.4 11.2 %collective-permute-done.49.refs_1_ = bf16[128,2048]{1,0:T(8,128)(2,1)S(1)} collective-permute-done((bf16[128,2048]{1,0:T(8,128)(2,1)S(1)}, bf16[128,2048]{1,0:T(8,128)(2,1)S(1)}, u32[]{:S(2)}, u32[]{:S(2)}) %collective-permute-start.49) | collective-permute-done | bytes 524320 | tf_op jit(solution)/shard_map/ppermute | solution.py:147
  331.8 7.6 %collective-permute-done.54 = bf16[1024,512]{1,0:T(8,128)(2,1)S(1)} collective-permute-done((bf16[1024,512]{1,0:T(8,128)(2,1)S(1)}, bf16[1024,512]{1,0:T(8,128)(2,1)S(1)}, u32[]{:S(2)}, u32[]{:S(2)}) %collective-permute-start.54) | collective-permute-done | bytes 1048608 | tf_op jit(solution)/shard_map/ppermute | solution.py:133
  339.4 3.6 collective-permute-done.53.refs_5_
  346.7 9.5 %collective-permute-done.55.refs_3_ = bf16[128,2048]{1,0:T(8,128)(2,1)S(1)} collective-permute-done((bf16[128,2048]{1,0:T(8,128)(2,1)S(1)}, bf16[128,2048]{1,0:T(8,128)(2,1)S(1)}, u32[]{:S(2)}, u32[]{:S(2)}) %collective-permute-start.55) | collective-permute-done | bytes 524320 | tf_op jit(solution)/shard_map/ppermute | solution.py:147
  365.0 6.4 %collective-permute-done.57.refs_4_ = bf16[128,2048]{1,0:T(8,128)(2,1)S(1)} collective-permute-done((bf16[128,2048]{1,0:T(8,128)(2,1)S(1)}, bf16[128,2048]{1,0:T(8,128)(2,1)S(1)}, u32[]{:S(2)}, u32[]{:S(2)}) %collective-permute-start.57) | collective-permute-done | bytes 524320 | tf_op jit(solution)/shard_map/ppermute | solution.py:147
  380.6 4.9 all-to-all-start.2
  385.5 24.3 %shard_map.289 = (bf16[2,128,2048]{2,1,0:T(8,128)(2,1)}, bf16[2,128,2048]{2,1,0:T(8,128)(2,1)}, f32[2,2048]{1,0:T(2,128)}, bf16[2,1024,768]{2,1,0:T(8,128)(2,1)}...) custom-call(s32[2]{0:T(128)} %pad_add_fusion.s.refs_0_, ...), custom_call_target="tpu_custom_call" | custom-call | tf_op jit(solution)/shard_map/pallas_call | solution.py:108
  414.7 6.7 %shard_map.290 = (bf16[1024,768]{1,0:T(8,128)(2,1)S(1)}, bf16[1024,768]{1,0:T(8,128)(2,1)S(1)}, bf16[1024,768]{1,0:T(8,128)(2,1)S(1)}, bf16[1024,768]{1,0:T(8,128)(2,1)S(1)}) custom-call(bf16[1024,2048]{1,0:T(8,128)(2,1)S(1)} %copy-done.10, bf16[2,1024,768]{2,1,0:T(8,128)(2,1)S(1)} %copy-done.18), custom_call_target="tpu_custom_call" | custom-call | tf_op jit(solution)/shard_map/pallas_call | solution.py:44
  428.2 3.6 collective-permute-done.66.a
  431.7 4.5 collective-permute-done.67.b
  440.3 9.7 %collective-permute-done.72.a = bf16[128,2048]{1,0:T(8,128)(2,1)S(1)} collective-permute-done((bf16[128,2048]{1,0:T(8,128)(2,1)S(1)}, bf16[128,2048]{1,0:T(8,128)(2,1)S(1)}, u32[]{:S(2)}, u32[]{:S(2)}) %collective-permute-start.72) | collective-permute-done | bytes 524320 | tf_op jit(solution)/shard_map/ppermute | solution.py:147
  454.1 10.4 %collective-permute-done.78 = f32[4,2048]{1,0:T(4,128)S(1)} collective-permute-done((f32[4,2048]{1,0:T(4,128)S(1)}, f32[4,2048]{1,0:T(4,128)S(1)}, u32[]{:S(2)}, u32[]{:S(2)}) %collective-permute-start.78) | collective-permute-done | bytes 32800 | tf_op jit(solution)/shard_map/ppermute | solution.py:133
  468.9 9.5 %collective-permute-done.82 = f32[4,2048]{1,0:T(4,128)S(1)} collective-permute-done((f32[4,2048]{1,0:T(4,128)S(1)}, f32[4,2048]{1,0:T(4,128)S(1)}, u32[]{:S(2)}, u32[]{:S(2)}) %collective-permute-start.82) | collective-permute-done | bytes 32800 | tf_op jit(solution)/shard_map/ppermute | solution.py:133
  481.7 3.6 all-to-all-start.3
  492.8 7.6 %collective-permute-done.85 = bf16[128,2048]{1,0:T(8,128)(2,1)S(1)} collective-permute-done((bf16[128,2048]{1,0:T(8,128)(2,1)}, bf16[128,2048]{1,0:T(8,128)(2,1)S(1)}, u32[]{:S(2)}, u32[]{:S(2)}) %collective-permute-start.85) | collective-permute-done | bytes 524320 | tf_op jit(solution)/shard_map/ppermute | solution.py:133
  510.6 9.2 %collective-permute-done.64.a = bf16[128,2048]{1,0:T(8,128)(2,1)S(1)} collective-permute-done((bf16[128,2048]{1,0:T(8,128)(2,1)S(1)}, bf16[128,2048]{1,0:T(8,128)(2,1)S(1)}, u32[]{:S(2)}, u32[]{:S(2)}) %collective-permute-start.64) | collective-permute-done | bytes 524320 | tf_op jit(solution)/shard_map/ppermute | solution.py:147
  522.9 6.3 %collective-permute-done.86.other = bf16[128,2048]{1,0:T(8,128)(2,1)S(1)} collective-permute-done((bf16[128,2048]{1,0:T(8,128)(2,1)S(1)}, bf16[128,2048]{1,0:T(8,128)(2,1)S(1)}, u32[]{:S(2)}, u32[]{:S(2)}) %collective-permute-start.86) | collective-permute-done | bytes 524320 | tf_op jit(solution)/shard_map/ppermute | solution.py:133
  543.3 4.1 shard_map.297
  547.4 4.3 collective-permute-done.89.a
  554.7 9.9 %collective-permute-done.91.other = bf16[8,128,768]{2,1,0:T(8,128)(2,1)} collective-permute-done((bf16[8,128,768]{2,1,0:T(8,128)(2,1)S(1)}, bf16[8,128,768]{2,1,0:T(8,128)(2,1)}, u32[]{:S(2)}, u32[]{:S(2)}) %collective-permute-start.91) | collective-permute-done | bytes 1572896 | tf_op jit(solution)/shard_map/ppermute | solution.py:133
  569.0 3.1 collective-permute-start.96
  573.3 7.9 %shard_map.300 = (f32[256,2048]{1,0:T(8,128)}, f32[256,2048]{1,0:T(8,128)}, f32[256,4096]{1,0:T(8,128)}, f32[256,4096]{1,0:T(8,128)}) custom-call(s32[2]{0:T(128)S(1)} %copy-done.48, bf16[8,128,768]{2,1,0:T(8,128)(2,1)S(1)} %all-to-all-done.3.own, bf16[8,128,768]{2,1,0:T(8,128)(2,1)} %collective-permute-done.98.own_c, ...), custom_call_target="tpu_custom_call" | custom-call | tf_op jit(solution)/shard_map/pallas_call | solution.py:383
  (392 shorter events, 191.5 us)
Async XLA Ops:
  4.9 46.3 %all-to-all-start = ((bf16[8,128,768]{2,1,0:T(8,128)(2,1)}), bf16[8,128,768]{2,1,0:T(8,128)(2,1)}, u32[]{:S(2)}, u32[]{:S(2)}) async-start(bf16[8,128,768]{2,1,0:T(8,128)(2,1)} %shard_map.272), calls=%async_computation | async-start | bytes 3145728 | tf_op jit(solution)/shard_map/all_to_all | solution.py:333
  12.3 38.9 %collective-permute-start.1 = (bf16[128,2048]{1,0:T(8,128)(2,1)S(1)}, bf16[128,2048]{1,0:T(8,128)(2,1)S(1)}, u32[]{:S(2)}, u32[]{:S(2)}) collective-permute-start(bf16[128,2048]{1,0:T(8,128)(2,1)S(1)} %copy-done.13), channel_id=1, source_target_pairs={{2,0},{4,2},{6,4},{7,6},{5,7},{3,5},{1,3},{0,1},{10,8},{12,10},{14... | collective-permute-start | bytes 1572872 | tf_op jit(solution)/shard_map/ppermute | solution.py:147
  14.3 36.9 %collective-permute-start = (bf16[128,2048]{1,0:T(8,128)(2,1)S(1)}, bf16[128,2048]{1,0:T(8,128)(2,1)S(1)}, u32[]{:S(2)}, u32[]{:S(2)}) collective-permute-start(bf16[128,2048]{1,0:T(8,128)(2,1)S(1)} %copy-done.13), channel_id=1, source_target_pairs={{0,2},{2,4},{4,6},{6,7},{7,5},{5,3},{3,1},{1,0},{8,10},{10,12},{12... | collective-permute-start | bytes 1572872 | tf_op jit(solution)/shard_map/ppermute | solution.py:147
  14.5 28.3 %collective-permute-start.2 = (bf16[4,256]{1,0:T(4,128)(2,1)S(1)}, bf16[4,256]{1,0:T(4,128)(2,1)S(1)}, u32[]{:S(2)}, u32[]{:S(2)}) collective-permute-start(bf16[4,256]{1,0:T(4,128)(2,1)S(1)} %pad_maximum_fusion.4), channel_id=1, source_target_pairs={{0,1},{1,0},{2,3},{3,2},{4,5},{5,4},{6,7},{7,6},{8,9},{9,8},{10,11... | collective-permute-start | bytes 6152 | tf_op jit(solution)/shard_map/ppermute | solution.py:133
  51.2 46.7 %collective-permute-start.12 = (bf16[1024,768]{1,0:T(8,128)(2,1)}, bf16[1024,768]{1,0:T(8,128)(2,1)}, u32[]{:S(2)}, u32[]{:S(2)}) collective-permute-start(bf16[1024,768]{1,0:T(8,128)(2,1)} %bitcast.4.refs_11_.refs_21_), channel_id=1, source_target_pairs={{0,8},{1,9},{2,10},{3,11},{4,12},{5,13},{6,14},{7,15},{8,0},{9,1},... | collective-permute-start | bytes 4718600 | tf_op jit(solution)/shard_map/ppermute | solution.py:133
  51.3 46.6 %collective-permute-start.11 = (bf16[1024,768]{1,0:T(8,128)(2,1)}, bf16[1024,768]{1,0:T(8,128)(2,1)}, u32[]{:S(2)}, u32[]{:S(2)}) collective-permute-start(bf16[1024,768]{1,0:T(8,128)(2,1)} %bitcast.4.refs_11_.refs_21_), channel_id=1, source_target_pairs={{0,16},{1,17},{2,18},{3,19},{4,20},{5,21},{6,22},{7,23},{8,24},{9,... | collective-permute-start | bytes 4718600 | tf_op jit(solution)/shard_map/ppermute | solution.py:133
  52.9 23.8 %collective-permute-start.3 = (bf16[128,2048]{1,0:T(8,128)(2,1)S(1)}, bf16[128,2048]{1,0:T(8,128)(2,1)S(1)}, u32[]{:S(2)}, u32[]{:S(2)}) collective-permute-start(bf16[128,2048]{1,0:T(8,128)(2,1)S(1)} %collective-permute-done.refs_2_), channel_id=1, source_target_pairs={{0,2},{2,4},{4,6},{6,7},{7,5},{5,3},{3,1},{1,0},{8,10},{10,12},{12... | collective-permute-start | bytes 1572872 | tf_op jit(solution)/shard_map/ppermute | solution.py:147
  98.0 30.9 %all-to-all-start.1 = ((bf16[8,128,512]{2,1,0:T(8,128)(2,1)}), bf16[8,128,512]{2,1,0:T(8,128)(2,1)S(1)}, u32[]{:S(2)}, u32[]{:S(2)}) async-start(bf16[8,128,512]{2,1,0:T(8,128)(2,1)} %shard_map.273), calls=%async_computation.1 | async-start | bytes 2097152 | tf_op jit(solution)/shard_map/all_to_all | solution.py:333
  165.4 14.9 %collective-permute-start.20 = (bf16[128,2048]{1,0:T(8,128)(2,1)S(1)}, bf16[128,2048]{1,0:T(8,128)(2,1)S(1)}, u32[]{:S(2)}, u32[]{:S(2)}) collective-permute-start(bf16[128,2048]{1,0:T(8,128)(2,1)S(1)} %get-tuple-element.271), channel_id=1, source_target_pairs={{0,2},{2,4},{4,6},{6,7},{7,5},{5,3},{3,1},{1,0},{8,10},{10,12},{12... | collective-permute-start | bytes 1572872 | tf_op jit(solution)/shard_map/ppermute | solution.py:147
  167.4 14.9 %collective-permute-start.21 = (bf16[128,2048]{1,0:T(8,128)(2,1)S(1)}, bf16[128,2048]{1,0:T(8,128)(2,1)S(1)}, u32[]{:S(2)}, u32[]{:S(2)}) collective-permute-start(bf16[128,2048]{1,0:T(8,128)(2,1)S(1)} %get-tuple-element.272), channel_id=1, source_target_pairs={{2,0},{4,2},{6,4},{7,6},{5,7},{3,5},{1,3},{0,1},{10,8},{12,10},{14... | collective-permute-start | bytes 1572872 | tf_op jit(solution)/shard_map/ppermute | solution.py:147
  167.5 28.0 %collective-permute-start.24 = (bf16[1024,512]{1,0:T(8,128)(2,1)S(1)}, bf16[1024,512]{1,0:T(8,128)(2,1)S(1)}, u32[]{:S(2)}, u32[]{:S(2)}) collective-permute-start(bf16[1024,512]{1,0:T(8,128)(2,1)S(1)} %bitcast.21), channel_id=1, source_target_pairs={{0,16},{1,17},{2,18},{3,19},{4,20},{5,21},{6,22},{7,23},{8,24},{9,... | collective-permute-start | bytes 3145736 | tf_op jit(solution)/shard_map/ppermute | solution.py:133
  168.1 25.4 %collective-permute-start.34 = (bf16[128,2048]{1,0:T(8,128)(2,1)S(1)}, bf16[128,2048]{1,0:T(8,128)(2,1)S(1)}, u32[]{:S(2)}, u32[]{:S(2)}) collective-permute-start(bf16[128,2048]{1,0:T(8,128)(2,1)S(1)} %copy-done.12), channel_id=1, source_target_pairs={{2,0},{4,2},{6,4},{7,6},{5,7},{3,5},{1,3},{0,1},{10,8},{12,10},{14... | collective-permute-start | bytes 1572872 | tf_op jit(solution)/shard_map/ppermute | solution.py:147
  168.8 24.7 %collective-permute-start.33 = (bf16[128,2048]{1,0:T(8,128)(2,1)S(1)}, bf16[128,2048]{1,0:T(8,128)(2,1)S(1)}, u32[]{:S(2)}, u32[]{:S(2)}) collective-permute-start(bf16[128,2048]{1,0:T(8,128)(2,1)S(1)} %copy-done.12), channel_id=1, source_target_pairs={{0,2},{2,4},{4,6},{6,7},{7,5},{5,3},{3,1},{1,0},{8,10},{10,12},{12... | collective-permute-start | bytes 1572872 | tf_op jit(solution)/shard_map/ppermute | solution.py:147
  183.5 21.2 %collective-permute-start.23 = (bf16[128,2048]{1,0:T(8,128)(2,1)S(1)}, bf16[128,2048]{1,0:T(8,128)(2,1)S(1)}, u32[]{:S(2)}, u32[]{:S(2)}) collective-permute-start(bf16[128,2048]{1,0:T(8,128)(2,1)S(1)} %get-tuple-element.275.refs_0_), channel_id=1, source_target_pairs={{2,0},{4,2},{6,4},{7,6},{5,7},{3,5},{1,3},{0,1},{10,8},{12,10},{14... | collective-permute-start | bytes 1572872 | tf_op jit(solution)/shard_map/ppermute | solution.py:147
  183.7 21.0 %collective-permute-start.22 = (bf16[128,2048]{1,0:T(8,128)(2,1)S(1)}, bf16[128,2048]{1,0:T(8,128)(2,1)S(1)}, u32[]{:S(2)}, u32[]{:S(2)}) collective-permute-start(bf16[128,2048]{1,0:T(8,128)(2,1)S(1)} %get-tuple-element.275.refs_0_), channel_id=1, source_target_pairs={{0,2},{2,4},{4,6},{6,7},{7,5},{5,3},{3,1},{1,0},{8,10},{10,12},{12... | collective-permute-start | bytes 1572872 | tf_op jit(solution)/shard_map/ppermute | solution.py:147
  193.5 20.6 %collective-permute-start.35 = (bf16[128,2048]{1,0:T(8,128)(2,1)S(1)}, bf16[128,2048]{1,0:T(8,128)(2,1)S(1)}, u32[]{:S(2)}, u32[]{:S(2)}) collective-permute-start(bf16[128,2048]{1,0:T(8,128)(2,1)S(1)} %collective-permute-done.33.refs_10_.refs_1_), channel_id=1, source_target_pairs={{0,2},{2,4},{4,6},{6,7},{7,5},{5,3},{3,1},{1,0},{8,10},{10,12},{12... | collective-permute-start | bytes 1572872 | tf_op jit(solution)/shard_map/ppermute | solution.py:147
  194.2 21.8 %collective-permute-start.36 = (bf16[128,2048]{1,0:T(8,128)(2,1)S(1)}, bf16[128,2048]{1,0:T(8,128)(2,1)S(1)}, u32[]{:S(2)}, u32[]{:S(2)}) collective-permute-start(bf16[128,2048]{1,0:T(8,128)(2,1)S(1)} %collective-permute-done.34.refs_13_.refs_4_), channel_id=1, source_target_pairs={{2,0},{4,2},{6,4},{7,6},{5,7},{3,5},{1,3},{0,1},{10,8},{12,10},{14... | collective-permute-start | bytes 1572872 | tf_op jit(solution)/shard_map/ppermute | solution.py:147
  204.7 20.6 %collective-permute-start.25 = (bf16[128,2048]{1,0:T(8,128)(2,1)S(1)}, bf16[128,2048]{1,0:T(8,128)(2,1)S(1)}, u32[]{:S(2)}, u32[]{:S(2)}) collective-permute-start(bf16[128,2048]{1,0:T(8,128)(2,1)S(1)} %collective-permute-done.22.refs_1_), channel_id=1, source_target_pairs={{0,2},{2,4},{4,6},{6,7},{7,5},{5,3},{3,1},{1,0},{8,10},{10,12},{12... | collective-permute-start | bytes 1572872 | tf_op jit(solution)/shard_map/ppermute | solution.py:147
  205.4 21.8 %collective-permute-start.26 = (bf16[128,2048]{1,0:T(8,128)(2,1)S(1)}, bf16[128,2048]{1,0:T(8,128)(2,1)S(1)}, u32[]{:S(2)}, u32[]{:S(2)}) collective-permute-start(bf16[128,2048]{1,0:T(8,128)(2,1)S(1)} %collective-permute-done.23.refs_4_), channel_id=1, source_target_pairs={{2,0},{4,2},{6,4},{7,6},{5,7},{3,5},{1,3},{0,1},{10,8},{12,10},{14... | collective-permute-start | bytes 1572872 | tf_op jit(solution)/shard_map/ppermute | solution.py:147
  215.9 19.2 %collective-permute-start.37 = (bf16[128,2048]{1,0:T(8,128)(2,1)S(1)}, bf16[128,2048]{1,0:T(8,128)(2,1)S(1)}, u32[]{:S(2)}, u32[]{:S(2)}) collective-permute-start(bf16[128,2048]{1,0:T(8,128)(2,1)S(1)} %collective-permute-done.35.refs_11_.refs_2_), channel_id=1, source_target_pairs={{0,2},{2,4},{4,6},{6,7},{7,5},{5,3},{3,1},{1,0},{8,10},{10,12},{12... | collective-permute-start | bytes 1572872 | tf_op jit(solution)/shard_map/ppermute | solution.py:147
  216.6 19.6 %collective-permute-start.38 = (bf16[128,2048]{1,0:T(8,128)(2,1)S(1)}, bf16[128,2048]{1,0:T(8,128)(2,1)S(1)}, u32[]{:S(2)}, u32[]{:S(2)}) collective-permute-start(bf16[128,2048]{1,0:T(8,128)(2,1)S(1)} %collective-permute-done.36.refs_14_.refs_5_), channel_id=1, source_target_pairs={{2,0},{4,2},{6,4},{7,6},{5,7},{3,5},{1,3},{0,1},{10,8},{12,10},{14... | collective-permute-start | bytes 1572872 | tf_op jit(solution)/shard_map/ppermute | solution.py:147
  218.0 36.1 %collective-permute-start.31 = (bf16[1024,512]{1,0:T(8,128)(2,1)S(1)}, bf16[1024,512]{1,0:T(8,128)(2,1)S(1)}, u32[]{:S(2)}, u32[]{:S(2)}) collective-permute-start(bf16[1024,512]{1,0:T(8,128)(2,1)S(1)} %bitcast.22), channel_id=1, source_target_pairs={{0,8},{1,9},{2,10},{3,11},{4,12},{5,13},{6,14},{7,15},{8,0},{9,1},... | collective-permute-start | bytes 3145736 | tf_op jit(solution)/shard_map/ppermute | solution.py:133
  225.3 28.8 %collective-permute-start.32 = (bf16[1024,512]{1,0:T(8,128)(2,1)S(1)}, bf16[1024,512]{1,0:T(8,128)(2,1)S(1)}, u32[]{:S(2)}, u32[]{:S(2)}) collective-permute-start(bf16[1024,512]{1,0:T(8,128)(2,1)S(1)} %collective-permute-done.24.refs_20_), channel_id=1, source_target_pairs={{0,8},{1,9},{2,10},{3,11},{4,12},{5,13},{6,14},{7,15},{8,0},{9,1},... | collective-permute-start | bytes 3145736 | tf_op jit(solution)/shard_map/ppermute | solution.py:133
  227.2 16.4 %collective-permute-start.27 = (bf16[128,2048]{1,0:T(8,128)(2,1)S(1)}, bf16[128,2048]{1,0:T(8,128)(2,1)S(1)}, u32[]{:S(2)}, u32[]{:S(2)}) collective-permute-start(bf16[128,2048]{1,0:T(8,128)(2,1)S(1)} %collective-permute-done.25.refs_2_), channel_id=1, source_target_pairs={{0,2},{2,4},{4,6},{6,7},{7,5},{5,3},{3,1},{1,0},{8,10},{10,12},{12... | collective-permute-start | bytes 1572872 | tf_op jit(solution)/shard_map/ppermute | solution.py:147
  235.1 14.9 %collective-permute-start.28 = (bf16[128,2048]{1,0:T(8,128)(2,1)S(1)}, bf16[128,2048]{1,0:T(8,128)(2,1)S(1)}, u32[]{:S(2)}, u32[]{:S(2)}) collective-permute-start(bf16[128,2048]{1,0:T(8,128)(2,1)S(1)} %collective-permute-done.26.refs_5_), channel_id=1, source_target_pairs={{2,0},{4,2},{6,4},{7,6},{5,7},{3,5},{1,3},{0,1},{10,8},{12,10},{14... | collective-permute-start | bytes 1572872 | tf_op jit(solution)/shard_map/ppermute | solution.py:147
  236.3 16.5 %collective-permute-start.40 = (bf16[64,2048]{1,0:T(8,128)(2,1)S(1)}, bf16[64,2048]{1,0:T(8,128)(2,1)S(1)}, u32[]{:S(2)}, u32[]{:S(2)}) collective-permute-start(bf16[64,2048]{1,0:T(8,128)(2,1)S(1)} %slice.56), channel_id=1, source_target_pairs={{2,0},{4,2},{6,4},{7,6},{5,7},{3,5},{1,3},{0,1},{10,8},{12,10},{14... | collective-permute-start | bytes 786440 | tf_op jit(solution)/shard_map/ppermute | solution.py:147
  296.9 15.2 %collective-permute-start.47 = (bf16[1024,512]{1,0:T(8,128)(2,1)S(1)}, bf16[1024,512]{1,0:T(8,128)(2,1)S(1)}, u32[]{:S(2)}, u32[]{:S(2)}) collective-permute-start(bf16[1024,512]{1,0:T(8,128)(2,1)S(1)} %get-tuple-element.319), channel_id=1, source_target_pairs={{0,8},{1,9},{2,10},{3,11},{4,12},{5,13},{6,14},{7,15},{8,0},{9,1},... | collective-permute-start | bytes 3145736 | tf_op jit(solution)/shard_map/ppermute | solution.py:133
  312.3 14.4 %collective-permute-start.49 = (bf16[128,2048]{1,0:T(8,128)(2,1)S(1)}, bf16[128,2048]{1,0:T(8,128)(2,1)S(1)}, u32[]{:S(2)}, u32[]{:S(2)}) collective-permute-start(bf16[128,2048]{1,0:T(8,128)(2,1)S(1)} %get-tuple-element.327), channel_id=1, source_target_pairs={{0,2},{2,4},{4,6},{6,7},{7,5},{5,3},{3,1},{1,0},{8,10},{10,12},{12... | collective-permute-start | bytes 1572872 | tf_op jit(solution)/shard_map/ppermute | solution.py:147
  314.3 25.0 %collective-permute-start.54 = (bf16[1024,512]{1,0:T(8,128)(2,1)S(1)}, bf16[1024,512]{1,0:T(8,128)(2,1)S(1)}, u32[]{:S(2)}, u32[]{:S(2)}) collective-permute-start(bf16[1024,512]{1,0:T(8,128)(2,1)S(1)} %add_convert_fusion.3), channel_id=1, source_target_pairs={{0,16},{1,17},{2,18},{3,19},{4,20},{5,21},{6,22},{7,23},{8,24},{9,... | collective-permute-start | bytes 3145736 | tf_op jit(solution)/shard_map/ppermute | solution.py:133
  346.1 18.8 %collective-permute-start.59 = (bf16[128,2048]{1,0:T(8,128)(2,1)S(1)}, bf16[128,2048]{1,0:T(8,128)(2,1)S(1)}, u32[]{:S(2)}, u32[]{:S(2)}) collective-permute-start(bf16[128,2048]{1,0:T(8,128)(2,1)S(1)} %fusion.3), channel_id=1, source_target_pairs={{0,16},{1,17},{2,18},{3,19},{4,20},{5,21},{6,22},{7,23},{8,24},{9,... | collective-permute-start | bytes 1572872 | tf_op jit(solution)/shard_map/ppermute | solution.py:133
  356.5 14.9 %collective-permute-start.57 = (bf16[128,2048]{1,0:T(8,128)(2,1)S(1)}, bf16[128,2048]{1,0:T(8,128)(2,1)S(1)}, u32[]{:S(2)}, u32[]{:S(2)}) collective-permute-start(bf16[128,2048]{1,0:T(8,128)(2,1)S(1)} %collective-permute-done.55.refs_3_), channel_id=1, source_target_pairs={{0,2},{2,4},{4,6},{6,7},{7,5},{5,3},{3,1},{1,0},{8,10},{10,12},{12... | collective-permute-start | bytes 1572872 | tf_op jit(solution)/shard_map/ppermute | solution.py:147
  357.4 14.9 %collective-permute-start.58 = (bf16[128,2048]{1,0:T(8,128)(2,1)S(1)}, bf16[128,2048]{1,0:T(8,128)(2,1)S(1)}, u32[]{:S(2)}, u32[]{:S(2)}) collective-permute-start(bf16[128,2048]{1,0:T(8,128)(2,1)S(1)} %collective-permute-done.56.refs_6_), channel_id=1, source_target_pairs={{2,0},{4,2},{6,4},{7,6},{5,7},{3,5},{1,3},{0,1},{10,8},{12,10},{14... | collective-permute-start | bytes 1572872 | tf_op jit(solution)/shard_map/ppermute | solution.py:147
  380.6 29.3 %all-to-all-start.2 = ((bf16[8,128,512]{2,1,0:T(8,128)(2,1)}), bf16[8,128,512]{2,1,0:T(8,128)(2,1)S(1)}, u32[]{:S(2)}, u32[]{:S(2)}) async-start(bf16[8,128,512]{2,1,0:T(8,128)(2,1)} %bitcast.25), calls=%async_computation.2 | async-start | bytes 2097152 | tf_op jit(solution)/shard_map/all_to_all | solution.py:361
  409.9 15.3 %collective-permute-start.70 = (bf16[2,128,2048]{2,1,0:T(8,128)(2,1)}, bf16[2,128,2048]{2,1,0:T(8,128)(2,1)S(1)}, u32[]{:S(2)}, u32[]{:S(2)}) collective-permute-start(bf16[2,128,2048]{2,1,0:T(8,128)(2,1)} %get-tuple-element.382), channel_id=1, source_target_pairs={{0,8},{1,9},{2,10},{3,11},{4,12},{5,13},{6,14},{7,15},{8,0},{9,1},... | collective-permute-start | bytes 3145736 | tf_op jit(solution)/shard_map/ppermute | solution.py:133
  410.0 29.1 %collective-permute-start.75 = (bf16[128,2048]{1,0:T(8,128)(2,1)S(1)}, bf16[128,2048]{1,0:T(8,128)(2,1)S(1)}, u32[]{:S(2)}, u32[]{:S(2)}) collective-permute-start(bf16[128,2048]{1,0:T(8,128)(2,1)S(1)} %add_convert_fusion.5.own), channel_id=1, source_target_pairs={{0,16},{1,17},{2,18},{3,19},{4,20},{5,21},{6,22},{7,23},{8,24},{9,... | collective-permute-start | bytes 1572872 | tf_op jit(solution)/shard_map/ppermute | solution.py:133
  438.5 41.5 %collective-permute-start.81 = (bf16[1024,768]{1,0:T(8,128)(2,1)S(1)}, bf16[1024,768]{1,0:T(8,128)(2,1)S(1)}, u32[]{:S(2)}, u32[]{:S(2)}) collective-permute-start(bf16[1024,768]{1,0:T(8,128)(2,1)S(1)} %add_convert_fusion.1), channel_id=1, source_target_pairs={{0,16},{1,17},{2,18},{3,19},{4,20},{5,21},{6,22},{7,23},{8,24},{9,... | collective-permute-start | bytes 4718600 | tf_op jit(solution)/shard_map/ppermute | solution.py:133
  481.7 49.9 %all-to-all-start.3 = ((bf16[8,128,768]{2,1,0:T(8,128)(2,1)}), bf16[8,128,768]{2,1,0:T(8,128)(2,1)S(1)}, u32[]{:S(2)}, u32[]{:S(2)}) async-start(bf16[8,128,768]{2,1,0:T(8,128)(2,1)} %bitcast.24), calls=%async_computation.3 | async-start | bytes 3145728 | tf_op jit(solution)/shard_map/all_to_all | solution.py:361
  485.3 15.1 %collective-permute-start.85 = (bf16[128,2048]{1,0:T(8,128)(2,1)}, bf16[128,2048]{1,0:T(8,128)(2,1)S(1)}, u32[]{:S(2)}, u32[]{:S(2)}) collective-permute-start(bf16[128,2048]{1,0:T(8,128)(2,1)} %fusion.4), channel_id=1, source_target_pairs={{0,16},{1,17},{2,18},{3,19},{4,20},{5,21},{6,22},{7,23},{8,24},{9,... | collective-permute-start | bytes 1572872 | tf_op jit(solution)/shard_map/ppermute | solution.py:133
  485.9 14.7 %collective-permute-start.87 = (bf16[128,2048]{1,0:T(8,128)(2,1)}, bf16[128,2048]{1,0:T(8,128)(2,1)S(1)}, u32[]{:S(2)}, u32[]{:S(2)}) collective-permute-start(bf16[128,2048]{1,0:T(8,128)(2,1)} %copy-done.19), channel_id=1, source_target_pairs={{0,8},{1,9},{2,10},{3,11},{4,12},{5,13},{6,14},{7,15},{8,0},{9,1},... | collective-permute-start | bytes 1572872 | tf_op jit(solution)/shard_map/ppermute | solution.py:133
  485.9 37.0 %collective-permute-start.84 = (bf16[8,128,512]{2,1,0:T(8,128)(2,1)S(1)}, bf16[8,128,512]{2,1,0:T(8,128)(2,1)S(1)}, u32[]{:S(2)}, u32[]{:S(2)}) collective-permute-start(bf16[8,128,512]{2,1,0:T(8,128)(2,1)S(1)} %all-to-all-done.2.own), channel_id=1, source_target_pairs={{0,16},{1,17},{2,18},{3,19},{4,20},{5,21},{6,22},{7,23},{8,24},{9,... | collective-permute-start | bytes 3145736 | tf_op jit(solution)/shard_map/ppermute | solution.py:133
  490.5 29.2 %collective-permute-start.64 = (bf16[128,2048]{1,0:T(8,128)(2,1)S(1)}, bf16[128,2048]{1,0:T(8,128)(2,1)S(1)}, u32[]{:S(2)}, u32[]{:S(2)}) collective-permute-start(bf16[128,2048]{1,0:T(8,128)(2,1)S(1)} %get-tuple-element.354), channel_id=1, source_target_pairs={{0,2},{2,4},{4,6},{6,7},{7,5},{5,3},{3,1},{1,0},{8,10},{10,12},{12... | collective-permute-start | bytes 1572872 | tf_op jit(solution)/shard_map/ppermute | solution.py:147
  492.4 28.1 %collective-permute-start.65 = (bf16[128,2048]{1,0:T(8,128)(2,1)S(1)}, bf16[128,2048]{1,0:T(8,128)(2,1)S(1)}, u32[]{:S(2)}, u32[]{:S(2)}) collective-permute-start(bf16[128,2048]{1,0:T(8,128)(2,1)S(1)} %get-tuple-element.355), channel_id=1, source_target_pairs={{2,0},{4,2},{6,4},{7,6},{5,7},{3,5},{1,3},{0,1},{10,8},{12,10},{14... | collective-permute-start | bytes 1572872 | tf_op jit(solution)/shard_map/ppermute | solution.py:147
  500.6 28.6 %collective-permute-start.86 = (bf16[128,2048]{1,0:T(8,128)(2,1)S(1)}, bf16[128,2048]{1,0:T(8,128)(2,1)S(1)}, u32[]{:S(2)}, u32[]{:S(2)}) collective-permute-start(bf16[128,2048]{1,0:T(8,128)(2,1)S(1)} %add_convert_fusion.4.own), channel_id=1, source_target_pairs={{0,16},{1,17},{2,18},{3,19},{4,20},{5,21},{6,22},{7,23},{8,24},{9,... | collective-permute-start | bytes 1572872 | tf_op jit(solution)/shard_map/ppermute | solution.py:133
  502.3 29.3 %collective-permute-start.83 = (f32[4,2048]{1,0:T(4,128)S(1)}, f32[4,2048]{1,0:T(4,128)S(1)}, u32[]{:S(2)}, u32[]{:S(2)}) collective-permute-start(f32[4,2048]{1,0:T(4,128)S(1)} %add.117), channel_id=1, source_target_pairs={{0,4},{1,5},{2,6},{3,7},{4,0},{5,1},{6,2},{7,3},{8,12},{9,13},{10,... | collective-permute-start | bytes 98312 | tf_op jit(solution)/shard_map/ppermute | solution.py:133
  531.6 33.1 %collective-permute-start.91 = (bf16[8,128,768]{2,1,0:T(8,128)(2,1)S(1)}, bf16[8,128,768]{2,1,0:T(8,128)(2,1)}, u32[]{:S(2)}, u32[]{:S(2)}) collective-permute-start(bf16[8,128,768]{2,1,0:T(8,128)(2,1)S(1)} %all-to-all-done.3.own), channel_id=1, source_target_pairs={{0,16},{1,17},{2,18},{3,19},{4,20},{5,21},{6,22},{7,23},{8,24},{9,... | collective-permute-start | bytes 4718600 | tf_op jit(solution)/shard_map/ppermute | solution.py:133
  543.2 30.0 %collective-permute-start.98 = (bf16[8,128,768]{2,1,0:T(8,128)(2,1)S(1)}, bf16[8,128,768]{2,1,0:T(8,128)(2,1)}, u32[]{:S(2)}, u32[]{:S(2)}) collective-permute-start(bf16[8,128,768]{2,1,0:T(8,128)(2,1)S(1)} %all-to-all-done.3.own), channel_id=1, source_target_pairs={{0,8},{1,9},{2,10},{3,11},{4,12},{5,13},{6,14},{7,15},{8,0},{9,1},... | collective-permute-start | bytes 4718600 | tf_op jit(solution)/shard_map/ppermute | solution.py:133
  569.0 14.9 %collective-permute-start.96 = (bf16[128,2048]{1,0:T(8,128)(2,1)S(1)}, bf16[128,2048]{1,0:T(8,128)(2,1)S(1)}, u32[]{:S(2)}, u32[]{:S(2)}) collective-permute-start(bf16[128,2048]{1,0:T(8,128)(2,1)S(1)} %get-tuple-element.425), channel_id=1, source_target_pairs={{0,2},{2,4},{4,6},{6,7},{7,5},{5,3},{3,1},{1,0},{8,10},{10,12},{12... | collective-permute-start | bytes 1572872 | tf_op jit(solution)/shard_map/ppermute | solution.py:147
  572.1 14.8 %collective-permute-start.97 = (bf16[128,2048]{1,0:T(8,128)(2,1)S(1)}, bf16[128,2048]{1,0:T(8,128)(2,1)S(1)}, u32[]{:S(2)}, u32[]{:S(2)}) collective-permute-start(bf16[128,2048]{1,0:T(8,128)(2,1)S(1)} %get-tuple-element.426), channel_id=1, source_target_pairs={{2,0},{4,2},{6,4},{7,6},{5,7},{3,5},{1,3},{0,1},{10,8},{12,10},{14... | collective-permute-start | bytes 1572872 | tf_op jit(solution)/shard_map/ppermute | solution.py:147
  (132 other events, 1452.6 us)

commit v5 on v4

--- a/solution.py
+++ b/solution.py
@@ -180,30 +180,53 @@
     return jnp.concatenate([refs[j][...] for j in names], 0)
 
 
-def term_shapes(rows, width):
-    return [shape((7 * rows, width), bf16)] + [shape((rows // 2, width), bf16)] * 2
-
-
-def put_tile(refs, i, values):
+def term_shapes(rows, width, tiles=(0, 1, 2, 3)):
+    full = 2 * len(tiles) - (3 in tiles)
+    return [shape((full * rows, width), bf16)] + [shape((rows // 2, width), bf16)] * 2 * (3 in tiles)
+
+
+def put_tile(refs, i, values, first=0):
     both = values.shape[0]
-    rows = both // 2
+    rows, start = both // 2, (i - first) * both
     values = values.astype(bf16)
     if i < 3:
-        refs[0][i * both : (i + 1) * both] = values
+        refs[0][start : start + both] = values
     else:
-        refs[0][3 * both : 3 * both + rows] = values[:rows]
+        refs[0][start : start + rows] = values[:rows]
         refs[1][...] = values[rows : rows + rows // 2]
         refs[2][...] = values[rows + rows // 2 :]
 
 
+def fold(term_a, term_b, a, b):
+    rows, width = term_a[1].block_shape
+    half = rows // 2
+
+    def body(term_a, term_b, a, b, out_a, out_b):
+        if a.shape[0] == rows:
+            out_a[...] = (term_a[...].astype(f32) + a[...].astype(f32)).astype(bf16)
+            out_b[...] = (term_b[...].astype(f32) + b[...].astype(f32)).astype(bf16)
+        else:
+            out_a[:half] = (term_a[:half].astype(f32) + a[...].astype(f32)).astype(bf16)
+            out_a[half:] = term_a[half:]
+            out_b[:half] = term_b[:half]
+            out_b[half:] = (term_b[half:].astype(f32) + b[...].astype(f32)).astype(bf16)
+
+    return kernel(body, [shape((rows, width), bf16)] * 2, term_a, term_b, a, b)
+
+
 class Scatter:
     def __init__(self, terms):
-        self.terms, self.a, self.b = terms
+        *self.terms, self.a, self.b = terms
+        self.rows = 2 * self.a.shape[0]
         self.steps = 0
 
     def term(self, offset):
-        rows, width = self.terms.shape[0] // 7, self.terms.shape[1]
-        return self.terms, block((rows, width), OFFSETS.index(offset), 0)
+        slot = OFFSETS.index(offset)
+        rows, width = self.rows, self.terms[0].shape[1]
+        for terms in self.terms:
+            if slot < terms.shape[0] // rows:
+                return terms, block((rows, width), slot, 0)
+            slot -= terms.shape[0] // rows
 
     def peek(self):
         if self.steps:
@@ -224,32 +247,52 @@
         return others
 
     def fold(self, offset):
-        rows, width = self.terms.shape[0] // 7, self.terms.shape[1]
-        half = rows // 2
-
-        def body(term_a, term_b, a, b, out_a, out_b):
-            if a.shape[0] == rows:
-                out_a[...] = (term_a[...].astype(f32) + a[...].astype(f32)).astype(bf16)
-                out_b[...] = (term_b[...].astype(f32) + b[...].astype(f32)).astype(bf16)
-            else:
-                out_a[:half] = (term_a[:half].astype(f32) + a[...].astype(f32)).astype(bf16)
-                out_a[half:] = term_a[half:]
-                out_b[:half] = term_b[:half]
-                out_b[half:] = (term_b[half:].astype(f32) + b[...].astype(f32)).astype(bf16)
-
-        self.a, self.b = kernel(
-            body,
-            [shape((rows, width), bf16)] * 2,
-            self.term(offset), self.term(-offset), self.a, self.b,
-            limit=8,
-        )
+        self.a, self.b = fold(self.term(offset), self.term(-offset), self.a, self.b)
 
     def pieces(self):
         return self.term(0), self.a, self.b
 
 
+class Pair:
+    def __init__(self, terms):
+        *self.terms, a, b = terms
+        self.rows, self.width = 2 * a.shape[0], a.shape[1] // 2
+        self.a = [a[:, : self.width], a[:, self.width :]]
+        self.b = [b[:, : self.width], b[:, self.width :]]
+        self.steps = [0, 0]
+
+    def term(self, offset, c):
+        slot = OFFSETS.index(offset)
+        for terms in self.terms:
+            if slot < terms.shape[0] // self.rows:
+                return terms, block((self.rows, self.width), slot, c)
+            slot -= terms.shape[0] // self.rows
+
+    def step(self, c):
+        if self.steps[c]:
+            offset = 4 - self.steps[c]
+            self.a[c], self.b[c] = fold(
+                self.term(offset, c), self.term(-offset, c), self.a[c], self.b[c]
+            )
+        self.steps[c] += 1
+        self.a[c], self.b[c] = after(send(self.a[c], True), send(self.b[c], False))
+
+    def run(self):
+        for _ in range(4):
+            for c in (0, 1):
+                self.step(c)
+
+    def pieces(self):
+        whole = block((self.rows, 2 * self.width), 0, 0)
+        return ((self.terms[0], whole), *self.a, *self.b)
+
+
 def total(refs):
-    return refs[0][...].astype(f32) + refs[1][...].astype(f32) + refs[2][...].astype(f32)
+    if len(refs) == 5:
+        a, b = (jnp.concatenate([refs[i][...], refs[i + 1][...]], -1) for i in (1, 3))
+    else:
+        a, b = refs[1][...], refs[2][...]
+    return refs[0][...].astype(f32) + a.astype(f32) + b.astype(f32)
 
 
 def normalize(values):
@@ -335,19 +378,24 @@
 
     def more(value):
         for place in range(X + 1, bits()):
-            value = value + swap(value.astype(bf16), place).astype(f32)
+            low = value.astype(bf16)
+            value = low.astype(f32) + swap(low, place).astype(f32)
         return value
 
-    def columns_grad(z, halves_of):
-        size = halves_of.shape[-1]
-
-        def body(z, parts, *outs):
+    def columns_grad(zs, parts):
+        count, size = len(zs), parts[0].shape[-1]
+
+        def body(*refs):
+            zs, parts, outs = refs[:count], refs[count : 2 * count], refs[2 * count :]
             for j in (1, 0):
                 for t in (1, 0):
-                    rows_t = z[:, t * half_width : (t + 1) * half_width]
-                    outs[2 * j + t][...] = dot(rows_t, parts[j], 0, 0).astype(bf16)
-
-        return kernel(body, [shape((half_width, size), bf16)] * 4, z, halves_of, limit=LIMITS[5])
+                    columns = slice(t * half_width, (t + 1) * half_width)
+                    value = sum(dot(z[:, columns], part[j], 0, 0) for z, part in zip(zs, parts))
+                    outs[2 * j + t][...] = value.astype(bf16)
+
+        return kernel(
+            body, [shape((half_width, size), bf16)] * 4, *zs, *parts, limit=LIMITS[5]
+        )
 
     def sum_cores(own, own_t, other, other_t):
         given = other.astype(f32) + swap(other_t, CORE).astype(f32)
@@ -394,36 +442,45 @@
         )(where, *pieces)
 
 
-    def rows_products(s, left, right, kept, given):
-        size = left.shape[1] // 4
+    def rows_products(s, lefts, right, kept, given):
+        size = lefts[0].shape[1] // 4
         for out, c in ((kept, s[0]), (given, 1 - s[0])):
             for i in (0, 1):
                 columns = pl.ds(pl.multiple_of((2 * i + c) * size, size), size)
-                out[i] = dot(left[:, columns], right[...], 0, 0).astype(bf16)
-
-    def rows_grad(left, right):
+                total, start = 0.0, 0
+                for left in lefts:
+                    rows_here = slice(start, start + left.shape[0])
+                    total = total + dot(left[:, columns], right[rows_here], 0, 0)
+                    start += left.shape[0]
+                out[i] = total.astype(bf16)
+
+    def rows_grad(lefts, right):
+        count = len(lefts)
+
+        def body(s, *refs):
+            rows_products(s, refs[:count], *refs[count:])
+
         return kernel(
-            rows_products, [shape((2, left.shape[1] // 4, right.shape[1]), bf16)] * 2, left, right,
+            body, [shape((2, lefts[0].shape[1] // 4, right.shape[1]), bf16)] * 2, *lefts, right,
             scalars=where, limit=14,
         )
 
     def sum_cores_rows(kept, given):
-        grad = kept.astype(f32) + swap(given, CORE).astype(f32)
-        return grad[0], grad[1].astype(bf16)
-
-    def give_rows(kept, got):
-        return more(kept + got.astype(f32)).astype(bf16)
-
-    def flat_rows(pieces):
-        size = pieces[0].shape[0]
-
-        def body(s, own, own_c, other, other_c, out):
-            for x, a, b in ((s[1], own, own_c), (1 - s[1], other, other_c)):
-                out[pl.ds((2 * x + s[0]) * size, size), :] = a[...].astype(f32)
-                out[pl.ds((2 * x + 1 - s[0]) * size, size), :] = b[...].astype(f32)
+        return (kept.astype(f32) + swap(given, CORE).astype(f32)).astype(bf16)
+
+    def sum_x_rows(mine, got):
+        return more(mine.astype(f32) + got[::-1].astype(f32)).astype(bf16)
+
+    def flat_rows(grad):
+        size = grad.shape[1]
+
+        def body(s, own, own_c, out):
+            for i, x in enumerate((s[1], 1 - s[1])):
+                out[pl.ds((2 * x + s[0]) * size, size), :] = own[i].astype(f32)
+                out[pl.ds((2 * x + 1 - s[0]) * size, size), :] = own_c[i].astype(f32)
 
         (out,) = kernel(
-            body, [shape((4 * size, pieces[0].shape[1]), f32)], *pieces, scalars=where, limit=8
+            body, [shape((4 * size, grad.shape[2]), f32)], grad, swap(grad, CORE), scalars=where
         )
         return out
 
@@ -439,7 +496,7 @@
     room_of_block = [pltpu.VMEM((rows, width), f32)]
 
     def second_norm(s, *refs):
-        sums, (tokens, gains, resid, z, room) = refs[:3], refs[3:]
+        sums, (tokens, gains, resid, z, room) = refs[:-5], refs[-5:]
         value = tokens[...].astype(f32) + total(sums)
         resid[...] = value
         normed, _ = normalize(value)
@@ -542,39 +599,53 @@
         for i in tiles:
             refs[9][rows_of(i)] = tile(refs, i)
 
-    def feed(s, *refs):
-        pieces, cots, w_down, w = refs[:9], refs[9:18], refs[18], refs[19:23]
-        (z, hidden, grad), outs = refs[23:26], refs[26:]
+    def feed(which, count):
+        def body(s, *refs):
+            pieces, cots, w_down, w = (
+                refs[:count], refs[count : 2 * count], refs[2 * count],
+                refs[2 * count + 1 : 2 * count + 5],
+            )
+            (z, hidden, grad), outs = refs[2 * count + 5 : 2 * count + 8], refs[2 * count + 8 :]
+            half = ff // 2
+            for i in which:
+                here = rows_of(i - which[0])
+                part, cot = (
+                    tile(p, i) if count > 3 else jnp.concatenate([r[...] for r in p], 0)
+                    for p in (pieces, cots)
+                )
+                z[here] = part
+                downs = of_x(w_down, s[1], half)
+                back = 0.0
+                for j in (0, 1):
+                    ab = dot(part[:, halves[0]], w[j][...]) + dot(part[:, halves[1]], w[2 + j][...])
+                    a, b = ab[:, :half], ab[:, half:]
+                    below = 0.5 * (1.0 + lax.erf(a * math.sqrt(0.5)))
+                    gelu = a * below
+                    slope = below + a * jnp.exp(-0.5 * a * a) * (1.0 / math.sqrt(2.0 * math.pi))
+                    columns = slice(j * half, (j + 1) * half)
+                    hidden[here, columns] = (gelu * b).astype(bf16)
+                    d = dot(cot, downs[j], 1, 1).astype(bf16).astype(f32)
+                    both = jnp.concatenate([d * b * slope, d * gelu], -1).astype(bf16)
+                    grad[j, here] = both
+                    back = back + jnp.concatenate(
+                        [dot(both, w[j][...], 1, 1), dot(both, w[2 + j][...], 1, 1)], -1
+                    )
+                put_tile(outs, i, back, which[0])
+
+        return body
+
+    def feed_shapes(which):
+        count = 2 * rows * len(which)
+        return [
+            shape((count, width), bf16), shape((count, ff), bf16), shape((2, count, ff), bf16)
+        ] + term_shapes(rows, width, which)
+
+    def down(s, h, last_h, w, *outs):
         half = ff // 2
         for i in tiles:
-            here = rows_of(i)
-            part = tile(pieces, i)
-            z[here] = part
-            cot = tile(cots, i)
-            downs = of_x(w_down, s[1], half)
-            back = 0.0
-            for j in (0, 1):
-                ab = dot(part[:, halves[0]], w[j][...]) + dot(part[:, halves[1]], w[2 + j][...])
-                a, b = ab[:, :half], ab[:, half:]
-                below = 0.5 * (1.0 + lax.erf(a * math.sqrt(0.5)))
-                gelu = a * below
-                slope = below + a * jnp.exp(-0.5 * a * a) * (1.0 / math.sqrt(2.0 * math.pi))
-                columns = slice(j * half, (j + 1) * half)
-                hidden[here, columns] = (gelu * b).astype(bf16)
-                d = dot(cot, downs[j], 1, 1).astype(bf16).astype(f32)
-                both = jnp.concatenate([d * b * slope, d * gelu], -1).astype(bf16)
-                grad[j, here] = both
-                back = back + jnp.concatenate(
-                    [dot(both, w[j][...], 1, 1), dot(both, w[2 + j][...], 1, 1)], -1
-                )
-            put_tile(outs, i, back)
-
-    def down(s, h, w, *outs):
-        half = ff // 2
-        for i in tiles:
-            here = rows_of(i)
+            here = h[rows_of(i)] if i < 3 else last_h[...]
             own, other = of_x(w, s[1], half)
-            put_tile(outs, i, dot(h[here, :half], own) + dot(h[here, half:], other))
+            put_tile(outs, i, dot(here[:, :half], own) + dot(here[:, half:], other))
 
     def mixer_back(s, *refs, ready, push):
         pieces, (w_out, r, g, mixed, q, k, v, p, decay, cosine, sine), w, z = (
@@ -600,7 +671,7 @@
             d_pre[0, here, cut:], d_pre[1, here, cut:] = both[:, :half], both[:, half:]
             d_r[here] = normalize_back(normed, scale, d_mixed * gate * sigmoid).astype(bf16)
         ready(12)
-        rows_products(s, mixed, d_out, kept, given)
+        rows_products(s, [mixed], d_out, kept, given)
         push(0)
         push(1)
         ready(13, 14, 15, 16, 17, 18, 19)
@@ -706,18 +777,18 @@
         scalars=where, limit=LIMITS[0], late=range(10, 18), stream=range(11),
         scratch=[pltpu.VMEM((2 * rows, width), f32)],
     )
-    ring = Scatter(parts)
-    cot_late = ring.hold(cotangent)[0]
+    *parts, cot_late = after(*parts, cotangent)
+    ring = Pair(parts)
     cot_ring = Gather(cot_late)
-    (ffn_own,) = ring.step(ffn_own)
+    ring.step(0)
+    ring.a[0], ffn_own = after(ring.a[0], ffn_own)
     ffn_other = swap(ffn_own, X)
     ffn_own_c = swap(ffn_own, CORE)
-    cot_ring.step()
-    ring.step()
-    cot_ring.step()
-    ring.step()
-    cot_ring.step()
-    ring.step()
+    ring.step(1)
+    for _ in range(3):
+        ring.step(0)
+        ring.step(1)
+        cot_ring.step()
     resid, second = kernel(
         second_norm, [block_f32, block_bf16], *ring.pieces(), tokens, gains,
         scalars=where, scratch=room_of_block, limit=8,
@@ -727,45 +798,51 @@
     (ffn_other,) = ring.step(ffn_other)
     ffn_other_c = swap(ffn_other, CORE)
     ring.step()
-    ring.step()
-    cot_ring.step()
     w_ffn = ring.step(ffn_own, ffn_other, ffn_own_c, ffn_other_c)
-    z_second, hidden, d_ab, *parts = kernel(
-        feed,
-        [shape((every, width), bf16), shape((every, ff), bf16), shape((2, every, ff), bf16)]
-        + terms,
-        *ring.pieces(), *cot_ring.pieces(), w_ffn_down, *w_ffn,
+    early = (ring.own, *ring.ahead[1:4], *ring.behind[1:3])
+    early_cots = (cot_ring.own, *cot_ring.ahead[1:4], *cot_ring.behind[1:3])
+    done = kernel(
+        feed((0, 1, 2), 6), feed_shapes((0, 1, 2)),
+        *early, *early_cots, w_ffn_down, *w_ffn,
         scalars=where, limit=LIMITS[2],
     )
-    ring = Scatter(parts)
+    a, b, *done = after(*cot_ring.peek(), *done)
+    cot_ring.put(a, b)
+    done = ring.step(*done)
+    z_second, hidden, d_ab, terms_early = done
+    z_last, hidden_last, d_ab_last, *parts = kernel(
+        feed((3,), 3), feed_shapes((3,)),
+        ring.behind[3], ring.ahead[4], ring.behind[4],
+        cot_ring.behind[3], cot_ring.ahead[4], cot_ring.behind[4], w_ffn_down, *w_ffn,
+        scalars=where, limit=18,
+    )
+    ring = Scatter([terms_early, *parts])
     (cot_all,) = ring.step(
-        *kernel(join_tiles, [shape((every, width), bf16)], *cot_ring.pieces(), limit=12)
-    )
-    grad_ffn = ring.step(*columns_grad(z_second, d_ab))
+        *kernel(join_tiles, [shape((every, width), bf16)], *cot_ring.pieces(), limit=24)
+    )
+    grad_ffn = ring.step(*columns_grad([z_second, z_last], [d_ab, d_ab_last]))
     ffn_own, ffn_own_c, ffn_given = sum_cores(*grad_ffn)
     ffn_own, ffn_own_c, ffn_given, down_kept, down_given = ring.step(
-        ffn_own, ffn_own_c, ffn_given, *rows_grad(hidden, cot_all)
+        ffn_own, ffn_own_c, ffn_given, *rows_grad([hidden, hidden_last], cot_all)
     )
     ffn_sent = swap(ffn_given, X)
-    down_kept, down_given = ring.step(*sum_cores_rows(down_kept, down_given))
+    (down_sum,) = ring.step(sum_cores_rows(down_kept, down_given))
     grad_resid, second_sums, part = kernel(
         second_back, [block_f32, pair_f32, block_bf16],
         *ring.pieces(), resid, cotangent, gains,
         scalars=where, scratch=room_of_block,
     )
     ring = Gather(part)
-    ffn_own, ffn_sent, down_given = ring.step(ffn_own, ffn_sent, down_given)
-    down_sent = swap(down_given, X)
+    ffn_own, ffn_sent, down_sum = ring.step(ffn_own, ffn_sent, down_sum)
+    down_got = swap(down_sum, X)
     ffn_sum = sum_x(ffn_own, ffn_own_c, ffn_sent)
     ring.step()
-    last = Scatter(kernel(down, terms, hidden, w_ffn_down, scalars=where, limit=20))
-    (down_sent,) = ring.step(down_sent)
-    down_owned = give_rows(down_kept, down_sent)
-    a, b, down_owned, ffn_sum = ring.step(*last.peek(), down_owned, ffn_sum)
+    last = Scatter(kernel(down, terms, hidden, hidden_last, w_ffn_down, scalars=where, limit=20))
+    ring.step()
+    a, b, down_got, ffn_sum = ring.step(*last.peek(), down_got, ffn_sum)
     last.put(a, b)
 
     ffn_owned = give(ffn_sum)
-    down_other = swap(down_owned, X)
     out_kept, out_given, first_sums, d_pre, *parts = streamed(
         mixer_back,
         [shape((2, dv // 4, width), bf16)] * 2
@@ -787,47 +864,46 @@
     )
     ring = Scatter(parts)
     stack = jnp.concatenate([first_sums, second_sums])
-    mix_own, mix_own_c, mix_given = sum_cores(*columns_grad(z_first, d_pre))
-    out_kept, out_given = sum_cores_rows(out_kept, out_given)
-    mix_own, mix_own_c, mix_given, out_kept, out_given, stack_c = ring.step(
-        mix_own, mix_own_c, mix_given, out_kept, out_given, swap(stack, X)
+    mix_own, mix_own_c, mix_given = sum_cores(*columns_grad([z_first], [d_pre]))
+    out_sum = sum_cores_rows(out_kept, out_given)
+    mix_own, mix_own_c, mix_given, out_sum, stack_c = ring.step(
+        mix_own, mix_own_c, mix_given, out_sum, swap(stack, X)
     )
     stack = stack + stack_c
     for place in range(X + 1, bits()):
         stack = stack + swap(stack, place)
     mix_sent = swap(mix_given, X)
-    stack_c, down_other = ring.step(swap(stack, CORE), down_other)
+    (stack_c,) = ring.step(swap(stack, CORE))
     stack = stack + stack_c
-    out_sent = swap(out_given, X)
     (stack_c,) = ring.step(swap(stack, 0))
     stack = stack + stack_c
-    mix_sent, stack_c = ring.step(mix_sent, swap(stack, 1))
+    mix_sent, stack_c, out_sum = ring.step(mix_sent, swap(stack, 1), out_sum)
     stack = stack + stack_c
     mix_owned = give(sum_x(mix_own, mix_own_c, mix_sent))
-    out_owned = give_rows(out_kept, out_sent)
-    ffn_other, out_other = swap(ffn_owned, X), swap(out_owned, X)
+    out_got, ffn_other = swap(out_sum, X), swap(ffn_owned, X)
     grad_tokens = kernel(
         first_back, [block_f32], *ring.pieces(), tokens, grad_resid, gains,
         scalars=where, scratch=room_of_block,
     )[0]
-    grad_down = flat_rows(everywhere(down_owned, down_other))
-    a, b, mix_owned, stack_c, ffn_other, out_other, grad_tokens, grad_down = after(
-        *last.peek(), mix_owned, swap(stack, 2), ffn_other, out_other, grad_tokens, grad_down
+    grad_down = flat_rows(sum_x_rows(down_sum, down_got))
+    a, b, mix_owned, ffn_other, out_got, grad_tokens, grad_down = after(
+        *last.peek(), mix_owned, ffn_other, out_got, grad_tokens, grad_down
     )
     last.put(a, b)
+    mix_other = swap(mix_owned, X)
+    grad_ffn_gate, grad_ffn_up = flat(everywhere(ffn_owned, ffn_other), [ff, ff])
+    grad_out = flat_rows(sum_x_rows(out_sum, out_got))
+    grad_ffn_gate, grad_ffn_up, grad_out, stack_c = last.step(
+        grad_ffn_gate, grad_ffn_up, grad_out, swap(stack, 2)
+    )
     stack = lax.dynamic_slice_in_dim(stack + stack_c, head * depth, depth, 1)
     first_gain = (stack[0] - norm1_bias.astype(f32) * stack[1]) / norm1_gain.astype(f32)
-    mix_other = swap(mix_owned, X)
-    grad_ffn_gate, grad_ffn_up = flat(everywhere(ffn_owned, ffn_other), [ff, ff])
-    grad_out = flat_rows(everywhere(out_owned, out_other))
-    last.put(*last.peek())
-    a, b, mix_other, grad_ffn_gate, grad_ffn_up, grad_out = after(
-        last.a, last.b, mix_other, grad_ffn_gate, grad_ffn_up, grad_out
-    )
-    last.put(a, b)
-    mix_grads = last.step(*flat(everywhere(mix_owned, mix_other), [dk, dk, dv, dv]))
-    grad_query, grad_key, grad_value, grad_gate = mix_grads
+    last.step()
     (output,) = kernel(last_sum, [block_bf16], *last.pieces(), resid)
+    mix_other, output, first_gain = after(mix_other, output, first_gain)
+    grad_query, grad_key, grad_value, grad_gate = flat(
+        everywhere(mix_owned, mix_other), [dk, dk, dv, dv]
+    )
 
     return (
         output,

time: 593 us -> 575 us (0.970)
  waiting for transfers between devices: 311 us -> 289 us
  local copies, waits for them, and re-layouts: 30.3 us -> 20.9 us
  starting transfers between devices: 116 us -> 123 us
    ppermute x64 -> x72, waiting for transfers between devices: 216 us -> 203 us  [send(): lax.ppermute(value, 'fsdp', pairs if ahead else [(b, a) for a, b in pairs])]
    ppermute x36 -> x32, waiting for transfers between devices: 94.8 us -> 86 us  [swap(): lax.ppermute(value, BOTH, [(i, i ^ 1 << place) for i in range(count)])]
    unnamed x152 -> x126, local copies, waits for them, and re-layouts: 26.3 us -> 18.9 us
    ppermute x64 -> x72, starting transfers between devices: 75 us -> 82.1 us  [send(): lax.ppermute(value, 'fsdp', pairs if ahead else [(b, a) for a, b in pairs])]
    pallas_call x24 -> x28, Pallas kernels: 49.2 us -> 51.3 us  [kernel(): pl.pallas_call(body, out_shape=list(outs), grid=grid, in_specs=specs, out...]
    ppermute x36 -> x32, starting transfers between devices: 20.8 us -> 20.7 us  [swap(): lax.ppermute(value, BOTH, [(i, i ^ 1 << place) for i in range(count)])]
  transfers between devices with their start and end apart: 104 -> 108, of which waited for: 66 -> 62; matrix products, arithmetic and copies ran while one was open for 3% -> 3% of each run, Pallas kernels for 16% -> 18%
where the time goes in v5:
time: 575 us; the launch traced here: 571 us
  waiting for transfers between devices  289 us (50%)
  starting transfers between devices  123 us (21%)
  Pallas kernels  119 us (21%)
  local copies, waits for them, and re-layouts  20.9 us (4%)
  other arithmetic  17.9 us (3%)
    ppermute x72, waiting for transfers between devices, send(): lax.ppermute(value, 'fsdp', pairs if ahead else [(b, a) for a, b in pairs])  203 us
    ppermute x32, waiting for transfers between devices, swap(): lax.ppermute(value, BOTH, [(i, i ^ 1 << place) for i in range(count)])  86 us
    ppermute x72, starting transfers between devices, send(): lax.ppermute(value, 'fsdp', pairs if ahead else [(b, a) for a, b in pairs])  82.1 us
    pallas_call x28, Pallas kernels, kernel(): pl.pallas_call(body, out_shape=list(outs), grid=grid, in_specs=specs, out...  51.3 us
    pallas_call x2, Pallas kernels, streamed(): pl.pallas_call(run, out_shape=list(outs), in_specs=specs, out_specs=[away...  47.6 us
    ppermute x32, starting transfers between devices, swap(): lax.ppermute(value, BOTH, [(i, i ^ 1 << place) for i in range(count)])  20.7 us
    unnamed x126, local copies, waits for them, and re-layouts  18.9 us
    pallas_call x2, Pallas kernels, flat(): pl.pallas_call(body, out_shape=[shape((depth, n * size), f32) for size in...  13.2 us
  transfers between devices with their start and end apart: 108, of which 62 were waited for; matrix products, arithmetic and copies ran while one was open for 3% of the time, Pallas kernels for 18%

profile of v5, /device:TPU:0, one launch (start us, length us, event | category | flops | bytes accessed | tf_op | source)
XLA Modules:
  0.0 570.9 jit_solution(6711265158827207263)
XLA Ops:
  1.2 3.5 shard_map.272
  4.9 7.4 %all-to-all-start = ((bf16[8,128,768]{2,1,0:T(8,128)(2,1)}), bf16[8,128,768]{2,1,0:T(8,128)(2,1)}, u32[]{:S(2)}, u32[]{:S(2)}) async-start(bf16[8,128,768]{2,1,0:T(8,128)(2,1)} %shard_map.272), calls=%async_computation | async-start | bytes 3145728 | tf_op jit(solution)/shard_map/all_to_all | solution.py:376
  18.6 3.0 fusion.2.refs_17_.refs_18_
  21.6 3.1 multiply_sine_fusion
  24.7 3.1 shard_map.273
  27.8 15.0 %collective-permute-done.2 = bf16[4,256]{1,0:T(4,128)(2,1)S(1)} collective-permute-done((bf16[4,256]{1,0:T(4,128)(2,1)S(1)}, bf16[4,256]{1,0:T(4,128)(2,1)S(1)}, u32[]{:S(2)}, u32[]{:S(2)}) %collective-permute-start.2) | collective-permute-done | bytes 2080 | tf_op jit(solution)/shard_map/ppermute | solution.py:133
  42.8 8.4 %collective-permute-done.1.refs_5_ = bf16[128,2048]{1,0:T(8,128)(2,1)S(1)} collective-permute-done((bf16[128,2048]{1,0:T(8,128)(2,1)S(1)}, bf16[128,2048]{1,0:T(8,128)(2,1)S(1)}, u32[]{:S(2)}, u32[]{:S(2)}) %collective-permute-start.1) | collective-permute-done | bytes 524320 | tf_op jit(solution)/shard_map/ppermute | solution.py:147
  52.8 9.9 %collective-permute-start.3 = (bf16[128,2048]{1,0:T(8,128)(2,1)S(1)}, bf16[128,2048]{1,0:T(8,128)(2,1)}, u32[]{:S(2)}, u32[]{:S(2)}) collective-permute-start(bf16[128,2048]{1,0:T(8,128)(2,1)S(1)} %collective-permute-done.refs_2_), channel_id=1, source_target_pairs={{0,2},{2,4},{4,6},{6,7},{7,5},{5,3},{3,1},{1,0},{8,10},{10,12},{12... | collective-permute-start | bytes 1572872 | tf_op jit(solution)/shard_map/ppermute | solution.py:147
  64.8 11.8 %collective-permute-done.5 = bf16[4,512]{1,0:T(4,128)(2,1)S(1)} collective-permute-done((bf16[4,512]{1,0:T(4,128)(2,1)S(1)}, bf16[4,512]{1,0:T(4,128)(2,1)S(1)}, u32[]{:S(2)}, u32[]{:S(2)}) %collective-permute-start.5) | collective-permute-done | bytes 4128 | tf_op jit(solution)/shard_map/ppermute | solution.py:133
  79.5 11.4 %collective-permute-done.8 = bf16[4,1024]{1,0:T(4,128)(2,1)S(1)} collective-permute-done((bf16[4,1024]{1,0:T(4,128)(2,1)S(1)}, bf16[4,1024]{1,0:T(4,128)(2,1)S(1)}, u32[]{:S(2)}, u32[]{:S(2)}) %collective-permute-start.8) | collective-permute-done | bytes 8224 | tf_op jit(solution)/shard_map/ppermute | solution.py:133
  93.1 4.3 collective-permute-done.10.refs_9_
  98.2 4.5 all-to-all-start.1
  102.8 23.3 %shard_map.274 = (bf16[1024,2048]{1,0:T(8,128)(2,1)}, bf16[1024,256]{1,0:T(8,128)(2,1)S(1)}, bf16[1024,256]{1,0:T(8,128)(2,1)}, bf16[1024,512]{1,0:T(8,128)(2,1)...) custom-call(s32[2]{0:T(128)S(1)} %copy-done.33, ...), custom_call_target="tpu_custom_call" | custom-call | tf_op jit(solution)/shard_map/pallas_call | solution.py:108
  143.0 2.8 collective-permute-done.24.a
  170.5 12.0 %collective-permute-done.20.refs_1_ = bf16[128,1024]{1,0:T(8,128)(2,1)S(1)} collective-permute-done((bf16[128,1024]{1,0:T(8,128)(2,1)S(1)}, bf16[128,1024]{1,0:T(8,128)(2,1)S(1)}, u32[]{:S(2)}, u32[]{:S(2)}) %collective-permute-start.20) | collective-permute-done | bytes 262176 | tf_op jit(solution)/shard_map/ppermute | solution.py:147
  189.2 10.8 %collective-permute-done.31.refs_4_ = bf16[128,2048]{1,0:T(8,128)(2,1)S(1)} collective-permute-done((bf16[128,2048]{1,0:T(8,128)(2,1)S(1)}, bf16[128,2048]{1,0:T(8,128)(2,1)S(1)}, u32[]{:S(2)}, u32[]{:S(2)}) %collective-permute-start.31) | collective-permute-done | bytes 524320 | tf_op jit(solution)/shard_map/ppermute | solution.py:147
  202.0 9.8 %collective-permute-done.43.refs_8_.refs_2_ = bf16[128,2048]{1,0:T(8,128)(2,1)S(1)} collective-permute-done((bf16[128,2048]{1,0:T(8,128)(2,1)S(1)}, bf16[128,2048]{1,0:T(8,128)(2,1)S(1)}, u32[]{:S(2)}, u32[]{:S(2)}) %collective-permute-start.43) | collective-permute-done | bytes 524320 | tf_op jit(solution)/shard_map/ppermute | solution.py:147
  213.9 9.2 %collective-permute-done.33.refs_2_ = bf16[128,2048]{1,0:T(8,128)(2,1)S(1)} collective-permute-done((bf16[128,2048]{1,0:T(8,128)(2,1)S(1)}, bf16[128,2048]{1,0:T(8,128)(2,1)S(1)}, u32[]{:S(2)}, u32[]{:S(2)}) %collective-permute-start.33) | collective-permute-done | bytes 524320 | tf_op jit(solution)/shard_map/ppermute | solution.py:147
  226.1 8.3 %collective-permute-done.45.refs_9_.refs_3_ = bf16[128,2048]{1,0:T(8,128)(2,1)S(1)} collective-permute-done((bf16[128,2048]{1,0:T(8,128)(2,1)S(1)}, bf16[128,2048]{1,0:T(8,128)(2,1)S(1)}, u32[]{:S(2)}, u32[]{:S(2)}) %collective-permute-start.45) | collective-permute-done | bytes 524320 | tf_op jit(solution)/shard_map/ppermute | solution.py:147
  237.9 7.6 %collective-permute-done.35.refs_3_ = bf16[128,2048]{1,0:T(8,128)(2,1)S(1)} collective-permute-done((bf16[128,2048]{1,0:T(8,128)(2,1)S(1)}, bf16[128,2048]{1,0:T(8,128)(2,1)S(1)}, u32[]{:S(2)}, u32[]{:S(2)}) %collective-permute-start.35) | collective-permute-done | bytes 524320 | tf_op jit(solution)/shard_map/ppermute | solution.py:147
  245.6 3.6 collective-permute-done.36.refs_0_
  251.4 12.8 %shard_map.282 = (bf16[768,2048]{1,0:T(8,128)(2,1)}, bf16[768,512]{1,0:T(8,128)(2,1)S(1)}, bf16[2,768,512]{2,1,0:T(8,128)(2,1)S(1)}, bf16[768,2048]{1,0:T(8,128)(2,1)}) custom-call(s32[2]{0:T(128)S(1)} %copy-done.33, bf16[128,2048]{1,0:T(8,128)(2,1)S(1)} %get-tuple-element.314.refs_0_, bf16[128,2048]{1,0:T(8,128)(2,1)S(1)} %collective-permute-done.30.refs_1_, ...), custom_call_target="tpu_custom_call" | custom-call | tf_op jit(solution)/shard_map/pallas_call | solution.py:44
  264.2 4.3 shard_map.283
  270.9 4.1 collective-permute-done.49.a
  279.0 4.5 shard_map.287
  290.5 3.0 shard_map.289
  293.8 8.5 %collective-permute-done.53.a = bf16[128,2048]{1,0:T(8,128)(2,1)S(1)} collective-permute-done((bf16[128,2048]{1,0:T(8,128)(2,1)S(1)}, bf16[128,2048]{1,0:T(8,128)(2,1)S(1)}, u32[]{:S(2)}, u32[]{:S(2)}) %collective-permute-start.53) | collective-permute-done | bytes 524320 | tf_op jit(solution)/shard_map/ppermute | solution.py:147
  306.7 11.3 %collective-permute-done.57.refs_1_ = bf16[128,2048]{1,0:T(8,128)(2,1)S(1)} collective-permute-done((bf16[128,2048]{1,0:T(8,128)(2,1)S(1)}, bf16[128,2048]{1,0:T(8,128)(2,1)S(1)}, u32[]{:S(2)}, u32[]{:S(2)}) %collective-permute-start.57) | collective-permute-done | bytes 524320 | tf_op jit(solution)/shard_map/ppermute | solution.py:147
  322.3 8.5 %collective-permute-done.62 = bf16[1024,512]{1,0:T(8,128)(2,1)S(1)} collective-permute-done((bf16[1024,512]{1,0:T(8,128)(2,1)S(1)}, bf16[1024,512]{1,0:T(8,128)(2,1)S(1)}, u32[]{:S(2)}, u32[]{:S(2)}) %collective-permute-start.62) | collective-permute-done | bytes 1048608 | tf_op jit(solution)/shard_map/ppermute | solution.py:133
  337.2 9.4 %collective-permute-done.63.refs_3_ = bf16[128,2048]{1,0:T(8,128)(2,1)S(1)} collective-permute-done((bf16[128,2048]{1,0:T(8,128)(2,1)S(1)}, bf16[128,2048]{1,0:T(8,128)(2,1)S(1)}, u32[]{:S(2)}, u32[]{:S(2)}) %collective-permute-start.63) | collective-permute-done | bytes 524320 | tf_op jit(solution)/shard_map/ppermute | solution.py:147
  349.0 2.9 shard_map.284
  354.0 7.9 %collective-permute-done.65.refs_4_ = bf16[128,2048]{1,0:T(8,128)(2,1)S(1)} collective-permute-done((bf16[128,2048]{1,0:T(8,128)(2,1)S(1)}, bf16[128,2048]{1,0:T(8,128)(2,1)S(1)}, u32[]{:S(2)}, u32[]{:S(2)}) %collective-permute-start.65) | collective-permute-done | bytes 524320 | tf_op jit(solution)/shard_map/ppermute | solution.py:147
  370.4 4.4 all-to-all-start.2
  374.9 24.3 %shard_map.293 = (bf16[2,128,2048]{2,1,0:T(8,128)(2,1)}, bf16[2,128,2048]{2,1,0:T(8,128)(2,1)}, f32[2,2048]{1,0:T(2,128)}, bf16[2,1024,768]{2,1,0:T(8,128)(2,1)}...) custom-call(s32[2]{0:T(128)} %pad_add_fusion.s.refs_0_, ...), custom_call_target="tpu_custom_call" | custom-call | tf_op jit(solution)/shard_map/pallas_call | solution.py:108
  403.4 6.7 %shard_map.294 = (bf16[1024,768]{1,0:T(8,128)(2,1)S(1)}, bf16[1024,768]{1,0:T(8,128)(2,1)S(1)}, bf16[1024,768]{1,0:T(8,128)(2,1)S(1)}, bf16[1024,768]{1,0:T(8,128)(2,1)S(1)}) custom-call(bf16[1024,2048]{1,0:T(8,128)(2,1)S(1)} %copy-done.11, bf16[2,1024,768]{2,1,0:T(8,128)(2,1)S(1)} %copy-done.17), custom_call_target="tpu_custom_call" | custom-call | tf_op jit(solution)/shard_map/pallas_call | solution.py:44
  415.2 4.6 collective-permute-done.74.a
  426.4 8.0 %collective-permute-done.80.a = bf16[128,2048]{1,0:T(8,128)(2,1)S(1)} collective-permute-done((bf16[128,2048]{1,0:T(8,128)(2,1)S(1)}, bf16[128,2048]{1,0:T(8,128)(2,1)S(1)}, u32[]{:S(2)}, u32[]{:S(2)}) %collective-permute-start.80) | collective-permute-done | bytes 524320 | tf_op jit(solution)/shard_map/ppermute | solution.py:147
  438.5 9.7 %collective-permute-done.85 = f32[4,2048]{1,0:T(4,128)S(1)} collective-permute-done((f32[4,2048]{1,0:T(4,128)S(1)}, f32[4,2048]{1,0:T(4,128)S(1)}, u32[]{:S(2)}, u32[]{:S(2)}) %collective-permute-start.85) | collective-permute-done | bytes 32800 | tf_op jit(solution)/shard_map/ppermute | solution.py:133
  452.6 8.8 %collective-permute-done.89 = f32[4,2048]{1,0:T(4,128)S(1)} collective-permute-done((f32[4,2048]{1,0:T(4,128)S(1)}, f32[4,2048]{1,0:T(4,128)S(1)}, u32[]{:S(2)}, u32[]{:S(2)}) %collective-permute-start.89) | collective-permute-done | bytes 32800 | tf_op jit(solution)/shard_map/ppermute | solution.py:133
  464.7 3.6 all-to-all-start.3
  477.1 2.8 shard_map.299
  482.5 19.5 %collective-permute-done.72.a = bf16[128,2048]{1,0:T(8,128)(2,1)S(1)} collective-permute-done((bf16[128,2048]{1,0:T(8,128)(2,1)S(1)}, bf16[128,2048]{1,0:T(8,128)(2,1)S(1)}, u32[]{:S(2)}, u32[]{:S(2)}) %collective-permute-start.72) | collective-permute-done | bytes 524320 | tf_op jit(solution)/shard_map/ppermute | solution.py:147
  503.7 15.2 %collective-permute-done.91 = bf16[2,128,2048]{2,1,0:T(8,128)(2,1)} collective-permute-done((bf16[2,128,2048]{2,1,0:T(8,128)(2,1)S(1)}, bf16[2,128,2048]{2,1,0:T(8,128)(2,1)}, u32[]{:S(2)}, u32[]{:S(2)}) %collective-permute-start.91) | collective-permute-done | bytes 1048608 | tf_op jit(solution)/shard_map/ppermute | solution.py:133
  533.1 2.8 shard_map.302
  536.0 6.7 %shard_map.301 = (f32[256,4096]{1,0:T(8,128)}, f32[256,4096]{1,0:T(8,128)}) custom-call(s32[2]{0:T(128)S(1)} %copy-done.34, bf16[8,128,512]{2,1,0:T(8,128)(2,1)} %all-to-all-done.2.own, bf16[8,128,512]{2,1,0:T(8,128)(2,1)} %collective-permute-done.96.own_c, bf16[8,128,512]{2,1,0:T(8,128)(2,1)} %collective-permute-done.90.other, ...), custom_call_target="tpu_custom_call" | custom-call | tf_op jit(solution)/shard_map/pallas_call | solution.py:431
  548.1 10.1 %collective-permute-done.100.refs_1_ = bf16[128,2048]{1,0:T(8,128)(2,1)S(1)} collective-permute-done((bf16[128,2048]{1,0:T(8,128)(2,1)S(1)}, bf16[128,2048]{1,0:T(8,128)(2,1)S(1)}, u32[]{:S(2)}, u32[]{:S(2)}) %collective-permute-start.100) | collective-permute-done | bytes 524320 | tf_op jit(solution)/shard_map/ppermute | solution.py:147
  560.4 3.6 collective-permute-done.103.other_c
  564.0 6.5 %shard_map.305 = (f32[256,2048]{1,0:T(8,128)}, f32[256,2048]{1,0:T(8,128)}, f32[256,4096]{1,0:T(8,128)}, f32[256,4096]{1,0:T(8,128)}) custom-call(s32[2]{0:T(128)S(1)} %copy-done.34, bf16[8,128,768]{2,1,0:T(8,128)(2,1)S(1)} %all-to-all-done.3.own, bf16[8,128,768]{2,1,0:T(8,128)(2,1)S(1)} %collective-permute-done.102.own_c, ...), custom_call_target="tpu_custom_call" | custom-call | tf_op jit(solution)/shard_map/pallas_call | solution.py:431
  (376 shorter events, 181.4 us)
Async XLA Ops:
  4.9 46.3 %all-to-all-start = ((bf16[8,128,768]{2,1,0:T(8,128)(2,1)}), bf16[8,128,768]{2,1,0:T(8,128)(2,1)}, u32[]{:S(2)}, u32[]{:S(2)}) async-start(bf16[8,128,768]{2,1,0:T(8,128)(2,1)} %shard_map.272), calls=%async_computation | async-start | bytes 3145728 | tf_op jit(solution)/shard_map/all_to_all | solution.py:376
  12.3 38.9 %collective-permute-start.1 = (bf16[128,2048]{1,0:T(8,128)(2,1)S(1)}, bf16[128,2048]{1,0:T(8,128)(2,1)S(1)}, u32[]{:S(2)}, u32[]{:S(2)}) collective-permute-start(bf16[128,2048]{1,0:T(8,128)(2,1)S(1)} %copy-done.13), channel_id=1, source_target_pairs={{2,0},{4,2},{6,4},{7,6},{5,7},{3,5},{1,3},{0,1},{10,8},{12,10},{14... | collective-permute-start | bytes 1572872 | tf_op jit(solution)/shard_map/ppermute | solution.py:147
  14.3 36.9 %collective-permute-start = (bf16[128,2048]{1,0:T(8,128)(2,1)S(1)}, bf16[128,2048]{1,0:T(8,128)(2,1)S(1)}, u32[]{:S(2)}, u32[]{:S(2)}) collective-permute-start(bf16[128,2048]{1,0:T(8,128)(2,1)S(1)} %copy-done.13), channel_id=1, source_target_pairs={{0,2},{2,4},{4,6},{6,7},{7,5},{5,3},{3,1},{1,0},{8,10},{10,12},{12... | collective-permute-start | bytes 1572872 | tf_op jit(solution)/shard_map/ppermute | solution.py:147
  14.5 28.3 %collective-permute-start.2 = (bf16[4,256]{1,0:T(4,128)(2,1)S(1)}, bf16[4,256]{1,0:T(4,128)(2,1)S(1)}, u32[]{:S(2)}, u32[]{:S(2)}) collective-permute-start(bf16[4,256]{1,0:T(4,128)(2,1)S(1)} %pad_maximum_fusion.4), channel_id=1, source_target_pairs={{0,1},{1,0},{2,3},{3,2},{4,5},{5,4},{6,7},{7,6},{8,9},{9,8},{10,11... | collective-permute-start | bytes 6152 | tf_op jit(solution)/shard_map/ppermute | solution.py:133
  51.2 46.9 %collective-permute-start.12 = (bf16[1024,768]{1,0:T(8,128)(2,1)}, bf16[1024,768]{1,0:T(8,128)(2,1)S(1)}, u32[]{:S(2)}, u32[]{:S(2)}) collective-permute-start(bf16[1024,768]{1,0:T(8,128)(2,1)} %bitcast.4.refs_11_.refs_21_), channel_id=1, source_target_pairs={{0,8},{1,9},{2,10},{3,11},{4,12},{5,13},{6,14},{7,15},{8,0},{9,1},... | collective-permute-start | bytes 4718600 | tf_op jit(solution)/shard_map/ppermute | solution.py:133
  51.3 46.8 %collective-permute-start.11 = (bf16[1024,768]{1,0:T(8,128)(2,1)}, bf16[1024,768]{1,0:T(8,128)(2,1)}, u32[]{:S(2)}, u32[]{:S(2)}) collective-permute-start(bf16[1024,768]{1,0:T(8,128)(2,1)} %bitcast.4.refs_11_.refs_21_), channel_id=1, source_target_pairs={{0,16},{1,17},{2,18},{3,19},{4,20},{5,21},{6,22},{7,23},{8,24},{9,... | collective-permute-start | bytes 4718600 | tf_op jit(solution)/shard_map/ppermute | solution.py:133
  52.8 23.8 %collective-permute-start.3 = (bf16[128,2048]{1,0:T(8,128)(2,1)S(1)}, bf16[128,2048]{1,0:T(8,128)(2,1)}, u32[]{:S(2)}, u32[]{:S(2)}) collective-permute-start(bf16[128,2048]{1,0:T(8,128)(2,1)S(1)} %collective-permute-done.refs_2_), channel_id=1, source_target_pairs={{0,2},{2,4},{4,6},{6,7},{7,5},{5,3},{3,1},{1,0},{8,10},{10,12},{12... | collective-permute-start | bytes 1572872 | tf_op jit(solution)/shard_map/ppermute | solution.py:147
  76.7 14.2 %collective-permute-start.6 = (bf16[128,2048]{1,0:T(8,128)(2,1)}, bf16[128,2048]{1,0:T(8,128)(2,1)S(1)}, u32[]{:S(2)}, u32[]{:S(2)}) collective-permute-start(bf16[128,2048]{1,0:T(8,128)(2,1)} %collective-permute-done.3.refs_3_), channel_id=1, source_target_pairs={{0,2},{2,4},{4,6},{6,7},{7,5},{5,3},{3,1},{1,0},{8,10},{10,12},{12... | collective-permute-start | bytes 1572872 | tf_op jit(solution)/shard_map/ppermute | solution.py:147
  98.2 40.6 %all-to-all-start.1 = ((bf16[8,128,512]{2,1,0:T(8,128)(2,1)}), bf16[8,128,512]{2,1,0:T(8,128)(2,1)S(1)}, u32[]{:S(2)}, u32[]{:S(2)}) async-start(bf16[8,128,512]{2,1,0:T(8,128)(2,1)} %shard_map.273), calls=%async_computation.1 | async-start | bytes 2097152 | tf_op jit(solution)/shard_map/all_to_all | solution.py:376
  160.9 28.3 %collective-permute-start.32 = (bf16[1024,512]{1,0:T(8,128)(2,1)S(1)}, bf16[1024,512]{1,0:T(8,128)(2,1)S(1)}, u32[]{:S(2)}, u32[]{:S(2)}) collective-permute-start(bf16[1024,512]{1,0:T(8,128)(2,1)S(1)} %bitcast.13), channel_id=1, source_target_pairs={{0,16},{1,17},{2,18},{3,19},{4,20},{5,21},{6,22},{7,23},{8,24},{9,... | collective-permute-start | bytes 3145736 | tf_op jit(solution)/shard_map/ppermute | solution.py:133
  162.7 24.5 %collective-permute-start.42 = (bf16[128,2048]{1,0:T(8,128)(2,1)S(1)}, bf16[128,2048]{1,0:T(8,128)(2,1)S(1)}, u32[]{:S(2)}, u32[]{:S(2)}) collective-permute-start(bf16[128,2048]{1,0:T(8,128)(2,1)S(1)} %copy-done.12), channel_id=1, source_target_pairs={{2,0},{4,2},{6,4},{7,6},{5,7},{3,5},{1,3},{0,1},{10,8},{12,10},{14... | collective-permute-start | bytes 1572872 | tf_op jit(solution)/shard_map/ppermute | solution.py:147
  164.3 22.9 %collective-permute-start.41 = (bf16[128,2048]{1,0:T(8,128)(2,1)S(1)}, bf16[128,2048]{1,0:T(8,128)(2,1)S(1)}, u32[]{:S(2)}, u32[]{:S(2)}) collective-permute-start(bf16[128,2048]{1,0:T(8,128)(2,1)S(1)} %copy-done.12), channel_id=1, source_target_pairs={{0,2},{2,4},{4,6},{6,7},{7,5},{5,3},{3,1},{1,0},{8,10},{10,12},{12... | collective-permute-start | bytes 1572872 | tf_op jit(solution)/shard_map/ppermute | solution.py:147
  168.3 14.2 %collective-permute-start.20 = (bf16[128,1024]{1,0:T(8,128)(2,1)S(1)}, bf16[128,1024]{1,0:T(8,128)(2,1)S(1)}, u32[]{:S(2)}, u32[]{:S(2)}) collective-permute-start(bf16[128,1024]{1,0:T(8,128)(2,1)S(1)} %get-tuple-element.296), channel_id=1, source_target_pairs={{0,2},{2,4},{4,6},{6,7},{7,5},{5,3},{3,1},{1,0},{8,10},{10,12},{12... | collective-permute-start | bytes 786440 | tf_op jit(solution)/shard_map/ppermute | solution.py:147
  185.1 14.9 %collective-permute-start.31 = (bf16[128,2048]{1,0:T(8,128)(2,1)S(1)}, bf16[128,2048]{1,0:T(8,128)(2,1)S(1)}, u32[]{:S(2)}, u32[]{:S(2)}) collective-permute-start(bf16[128,2048]{1,0:T(8,128)(2,1)S(1)} %get-tuple-element.314.refs_0_), channel_id=1, source_target_pairs={{2,0},{4,2},{6,4},{7,6},{5,7},{3,5},{1,3},{0,1},{10,8},{12,10},{14... | collective-permute-start | bytes 1572872 | tf_op jit(solution)/shard_map/ppermute | solution.py:147
  185.8 14.9 %collective-permute-start.30 = (bf16[128,2048]{1,0:T(8,128)(2,1)S(1)}, bf16[128,2048]{1,0:T(8,128)(2,1)S(1)}, u32[]{:S(2)}, u32[]{:S(2)}) collective-permute-start(bf16[128,2048]{1,0:T(8,128)(2,1)S(1)} %get-tuple-element.314.refs_0_), channel_id=1, source_target_pairs={{0,2},{2,4},{4,6},{6,7},{7,5},{5,3},{3,1},{1,0},{8,10},{10,12},{12... | collective-permute-start | bytes 1572872 | tf_op jit(solution)/shard_map/ppermute | solution.py:147
  187.2 24.7 %collective-permute-start.43 = (bf16[128,2048]{1,0:T(8,128)(2,1)S(1)}, bf16[128,2048]{1,0:T(8,128)(2,1)S(1)}, u32[]{:S(2)}, u32[]{:S(2)}) collective-permute-start(bf16[128,2048]{1,0:T(8,128)(2,1)S(1)} %collective-permute-done.41.refs_7_.refs_1_), channel_id=1, source_target_pairs={{0,2},{2,4},{4,6},{6,7},{7,5},{5,3},{3,1},{1,0},{8,10},{10,12},{12... | collective-permute-start | bytes 1572872 | tf_op jit(solution)/shard_map/ppermute | solution.py:147
  188.7 23.2 %collective-permute-start.44 = (bf16[128,2048]{1,0:T(8,128)(2,1)S(1)}, bf16[128,2048]{1,0:T(8,128)(2,1)S(1)}, u32[]{:S(2)}, u32[]{:S(2)}) collective-permute-start(bf16[128,2048]{1,0:T(8,128)(2,1)S(1)} %collective-permute-done.42.refs_10_.refs_4_), channel_id=1, source_target_pairs={{2,0},{4,2},{6,4},{7,6},{5,7},{3,5},{1,3},{0,1},{10,8},{12,10},{14... | collective-permute-start | bytes 1572872 | tf_op jit(solution)/shard_map/ppermute | solution.py:147
  200.6 22.5 %collective-permute-start.33 = (bf16[128,2048]{1,0:T(8,128)(2,1)S(1)}, bf16[128,2048]{1,0:T(8,128)(2,1)S(1)}, u32[]{:S(2)}, u32[]{:S(2)}) collective-permute-start(bf16[128,2048]{1,0:T(8,128)(2,1)S(1)} %collective-permute-done.30.refs_1_), channel_id=1, source_target_pairs={{0,2},{2,4},{4,6},{6,7},{7,5},{5,3},{3,1},{1,0},{8,10},{10,12},{12... | collective-permute-start | bytes 1572872 | tf_op jit(solution)/shard_map/ppermute | solution.py:147
  202.0 34.4 %collective-permute-start.37 = (bf16[1024,512]{1,0:T(8,128)(2,1)S(1)}, bf16[1024,512]{1,0:T(8,128)(2,1)S(1)}, u32[]{:S(2)}, u32[]{:S(2)}) collective-permute-start(bf16[1024,512]{1,0:T(8,128)(2,1)S(1)} %bitcast.14), channel_id=1, source_target_pairs={{0,8},{1,9},{2,10},{3,11},{4,12},{5,13},{6,14},{7,15},{8,0},{9,1},... | collective-permute-start | bytes 3145736 | tf_op jit(solution)/shard_map/ppermute | solution.py:133
  212.1 22.2 %collective-permute-start.45 = (bf16[128,2048]{1,0:T(8,128)(2,1)S(1)}, bf16[128,2048]{1,0:T(8,128)(2,1)S(1)}, u32[]{:S(2)}, u32[]{:S(2)}) collective-permute-start(bf16[128,2048]{1,0:T(8,128)(2,1)S(1)} %collective-permute-done.43.refs_8_.refs_2_), channel_id=1, source_target_pairs={{0,2},{2,4},{4,6},{6,7},{7,5},{5,3},{3,1},{1,0},{8,10},{10,12},{12... | collective-permute-start | bytes 1572872 | tf_op jit(solution)/shard_map/ppermute | solution.py:147
  213.9 24.1 %collective-permute-start.38 = (bf16[1024,512]{1,0:T(8,128)(2,1)S(1)}, bf16[1024,512]{1,0:T(8,128)(2,1)S(1)}, u32[]{:S(2)}, u32[]{:S(2)}) collective-permute-start(bf16[1024,512]{1,0:T(8,128)(2,1)S(1)} %collective-permute-done.32.refs_14_.refs_8_), channel_id=1, source_target_pairs={{0,8},{1,9},{2,10},{3,11},{4,12},{5,13},{6,14},{7,15},{8,0},{9,1},... | collective-permute-start | bytes 3145736 | tf_op jit(solution)/shard_map/ppermute | solution.py:133
  224.6 21.0 %collective-permute-start.35 = (bf16[128,2048]{1,0:T(8,128)(2,1)S(1)}, bf16[128,2048]{1,0:T(8,128)(2,1)S(1)}, u32[]{:S(2)}, u32[]{:S(2)}) collective-permute-start(bf16[128,2048]{1,0:T(8,128)(2,1)S(1)} %collective-permute-done.33.refs_2_), channel_id=1, source_target_pairs={{0,2},{2,4},{4,6},{6,7},{7,5},{5,3},{3,1},{1,0},{8,10},{10,12},{12... | collective-permute-start | bytes 1572872 | tf_op jit(solution)/shard_map/ppermute | solution.py:147
  234.3 14.8 %collective-permute-start.36 = (bf16[128,2048]{1,0:T(8,128)(2,1)S(1)}, bf16[128,2048]{1,0:T(8,128)(2,1)S(1)}, u32[]{:S(2)}, u32[]{:S(2)}) collective-permute-start(bf16[128,2048]{1,0:T(8,128)(2,1)S(1)} %collective-permute-done.34.refs_5_), channel_id=1, source_target_pairs={{2,0},{4,2},{6,4},{7,6},{5,7},{3,5},{1,3},{0,1},{10,8},{12,10},{14... | collective-permute-start | bytes 1572872 | tf_op jit(solution)/shard_map/ppermute | solution.py:147
  235.9 28.4 %collective-permute-start.48 = (bf16[64,2048]{1,0:T(8,128)(2,1)S(1)}, bf16[64,2048]{1,0:T(8,128)(2,1)S(1)}, u32[]{:S(2)}, u32[]{:S(2)}) collective-permute-start(bf16[64,2048]{1,0:T(8,128)(2,1)S(1)} %slice.58), channel_id=1, source_target_pairs={{2,0},{4,2},{6,4},{7,6},{5,7},{3,5},{1,3},{0,1},{10,8},{12,10},{14... | collective-permute-start | bytes 786440 | tf_op jit(solution)/shard_map/ppermute | solution.py:147
  236.4 27.8 %collective-permute-start.47 = (bf16[64,2048]{1,0:T(8,128)(2,1)S(1)}, bf16[64,2048]{1,0:T(8,128)(2,1)S(1)}, u32[]{:S(2)}, u32[]{:S(2)}) collective-permute-start(bf16[64,2048]{1,0:T(8,128)(2,1)S(1)} %slice.57), channel_id=1, source_target_pairs={{0,2},{2,4},{4,6},{6,7},{7,5},{5,3},{3,1},{1,0},{8,10},{10,12},{12... | collective-permute-start | bytes 786440 | tf_op jit(solution)/shard_map/ppermute | solution.py:147
  249.2 15.1 %collective-permute-start.40 = (bf16[64,2048]{1,0:T(8,128)(2,1)S(1)}, bf16[64,2048]{1,0:T(8,128)(2,1)S(1)}, u32[]{:S(2)}, u32[]{:S(2)}) collective-permute-start(bf16[64,2048]{1,0:T(8,128)(2,1)S(1)} %slice.56), channel_id=1, source_target_pairs={{2,0},{4,2},{6,4},{7,6},{5,7},{3,5},{1,3},{0,1},{10,8},{12,10},{14... | collective-permute-start | bytes 786440 | tf_op jit(solution)/shard_map/ppermute | solution.py:147
  249.5 14.8 %collective-permute-start.39 = (bf16[64,2048]{1,0:T(8,128)(2,1)S(1)}, bf16[64,2048]{1,0:T(8,128)(2,1)S(1)}, u32[]{:S(2)}, u32[]{:S(2)}) collective-permute-start(bf16[64,2048]{1,0:T(8,128)(2,1)S(1)} %slice.55), channel_id=1, source_target_pairs={{0,2},{2,4},{4,6},{6,7},{7,5},{5,3},{3,1},{1,0},{8,10},{10,12},{12... | collective-permute-start | bytes 786440 | tf_op jit(solution)/shard_map/ppermute | solution.py:147
  287.7 15.7 %collective-permute-start.55 = (bf16[1024,512]{1,0:T(8,128)(2,1)S(1)}, bf16[1024,512]{1,0:T(8,128)(2,1)S(1)}, u32[]{:S(2)}, u32[]{:S(2)}) collective-permute-start(bf16[1024,512]{1,0:T(8,128)(2,1)S(1)} %get-tuple-element.370), channel_id=1, source_target_pairs={{0,8},{1,9},{2,10},{3,11},{4,12},{5,13},{6,14},{7,15},{8,0},{9,1},... | collective-permute-start | bytes 3145736 | tf_op jit(solution)/shard_map/ppermute | solution.py:133
  303.7 14.4 %collective-permute-start.57 = (bf16[128,2048]{1,0:T(8,128)(2,1)S(1)}, bf16[128,2048]{1,0:T(8,128)(2,1)S(1)}, u32[]{:S(2)}, u32[]{:S(2)}) collective-permute-start(bf16[128,2048]{1,0:T(8,128)(2,1)S(1)} %get-tuple-element.378), channel_id=1, source_target_pairs={{0,2},{2,4},{4,6},{6,7},{7,5},{5,3},{3,1},{1,0},{8,10},{10,12},{12... | collective-permute-start | bytes 1572872 | tf_op jit(solution)/shard_map/ppermute | solution.py:147
  305.8 25.0 %collective-permute-start.62 = (bf16[1024,512]{1,0:T(8,128)(2,1)S(1)}, bf16[1024,512]{1,0:T(8,128)(2,1)S(1)}, u32[]{:S(2)}, u32[]{:S(2)}) collective-permute-start(bf16[1024,512]{1,0:T(8,128)(2,1)S(1)} %add_convert_fusion.7), channel_id=1, source_target_pairs={{0,16},{1,17},{2,18},{3,19},{4,20},{5,21},{6,22},{7,23},{8,24},{9,... | collective-permute-start | bytes 3145736 | tf_op jit(solution)/shard_map/ppermute | solution.py:133
  336.7 30.1 %collective-permute-start.71 = (bf16[2,128,2048]{2,1,0:T(8,128)(2,1)S(1)}, bf16[2,128,2048]{2,1,0:T(8,128)(2,1)S(1)}, u32[]{:S(2)}, u32[]{:S(2)}) collective-permute-start(bf16[2,128,2048]{2,1,0:T(8,128)(2,1)S(1)} %add_convert_fusion.6), channel_id=1, source_target_pairs={{0,16},{1,17},{2,18},{3,19},{4,20},{5,21},{6,22},{7,23},{8,24},{9,... | collective-permute-start | bytes 3145736 | tf_op jit(solution)/shard_map/ppermute | solution.py:133
  347.0 14.9 %collective-permute-start.65 = (bf16[128,2048]{1,0:T(8,128)(2,1)S(1)}, bf16[128,2048]{1,0:T(8,128)(2,1)S(1)}, u32[]{:S(2)}, u32[]{:S(2)}) collective-permute-start(bf16[128,2048]{1,0:T(8,128)(2,1)S(1)} %collective-permute-done.63.refs_3_), channel_id=1, source_target_pairs={{0,2},{2,4},{4,6},{6,7},{7,5},{5,3},{3,1},{1,0},{8,10},{10,12},{12... | collective-permute-start | bytes 1572872 | tf_op jit(solution)/shard_map/ppermute | solution.py:147
  347.7 14.9 %collective-permute-start.66 = (bf16[128,2048]{1,0:T(8,128)(2,1)S(1)}, bf16[128,2048]{1,0:T(8,128)(2,1)S(1)}, u32[]{:S(2)}, u32[]{:S(2)}) collective-permute-start(bf16[128,2048]{1,0:T(8,128)(2,1)S(1)} %collective-permute-done.64.refs_6_), channel_id=1, source_target_pairs={{2,0},{4,2},{6,4},{7,6},{5,7},{3,5},{1,3},{0,1},{10,8},{12,10},{14... | collective-permute-start | bytes 1572872 | tf_op jit(solution)/shard_map/ppermute | solution.py:147
  351.9 14.4 %collective-permute-start.69 = (bf16[64,2048]{1,0:T(8,128)(2,1)S(1)}, bf16[64,2048]{1,0:T(8,128)(2,1)S(1)}, u32[]{:S(2)}, u32[]{:S(2)}) collective-permute-start(bf16[64,2048]{1,0:T(8,128)(2,1)S(1)} %get-tuple-element.395), channel_id=1, source_target_pairs={{0,2},{2,4},{4,6},{6,7},{7,5},{5,3},{3,1},{1,0},{8,10},{10,12},{12... | collective-permute-start | bytes 786440 | tf_op jit(solution)/shard_map/ppermute | solution.py:147
  370.4 28.8 %all-to-all-start.2 = ((bf16[8,128,512]{2,1,0:T(8,128)(2,1)}), bf16[8,128,512]{2,1,0:T(8,128)(2,1)}, u32[]{:S(2)}, u32[]{:S(2)}) async-start(bf16[8,128,512]{2,1,0:T(8,128)(2,1)} %bitcast.18), calls=%async_computation.2 | async-start | bytes 2097152 | tf_op jit(solution)/shard_map/all_to_all | solution.py:409
  423.6 39.4 %collective-permute-start.88 = (bf16[1024,768]{1,0:T(8,128)(2,1)S(1)}, bf16[1024,768]{1,0:T(8,128)(2,1)S(1)}, u32[]{:S(2)}, u32[]{:S(2)}) collective-permute-start(bf16[1024,768]{1,0:T(8,128)(2,1)S(1)} %add_convert_fusion.1), channel_id=1, source_target_pairs={{0,16},{1,17},{2,18},{3,19},{4,20},{5,21},{6,22},{7,23},{8,24},{9,... | collective-permute-start | bytes 4718600 | tf_op jit(solution)/shard_map/ppermute | solution.py:133
  464.7 54.1 %all-to-all-start.3 = ((bf16[8,128,768]{2,1,0:T(8,128)(2,1)}), bf16[8,128,768]{2,1,0:T(8,128)(2,1)S(1)}, u32[]{:S(2)}, u32[]{:S(2)}) async-start(bf16[8,128,768]{2,1,0:T(8,128)(2,1)} %bitcast.17), calls=%async_computation.3 | async-start | bytes 3145728 | tf_op jit(solution)/shard_map/all_to_all | solution.py:409
  470.5 33.2 %collective-permute-start.90 = (bf16[8,128,512]{2,1,0:T(8,128)(2,1)}, bf16[8,128,512]{2,1,0:T(8,128)(2,1)}, u32[]{:S(2)}, u32[]{:S(2)}) collective-permute-start(bf16[8,128,512]{2,1,0:T(8,128)(2,1)} %all-to-all-done.2.own), channel_id=1, source_target_pairs={{0,16},{1,17},{2,18},{3,19},{4,20},{5,21},{6,22},{7,23},{8,24},{9,... | collective-permute-start | bytes 3145736 | tf_op jit(solution)/shard_map/ppermute | solution.py:133
  472.0 46.8 %collective-permute-start.91 = (bf16[2,128,2048]{2,1,0:T(8,128)(2,1)S(1)}, bf16[2,128,2048]{2,1,0:T(8,128)(2,1)}, u32[]{:S(2)}, u32[]{:S(2)}) collective-permute-start(bf16[2,128,2048]{2,1,0:T(8,128)(2,1)S(1)} %copy-done.38), channel_id=1, source_target_pairs={{0,16},{1,17},{2,18},{3,19},{4,20},{5,21},{6,22},{7,23},{8,24},{9,... | collective-permute-start | bytes 3145736 | tf_op jit(solution)/shard_map/ppermute | solution.py:133
  474.7 27.3 %collective-permute-start.72 = (bf16[128,2048]{1,0:T(8,128)(2,1)S(1)}, bf16[128,2048]{1,0:T(8,128)(2,1)S(1)}, u32[]{:S(2)}, u32[]{:S(2)}) collective-permute-start(bf16[128,2048]{1,0:T(8,128)(2,1)S(1)} %get-tuple-element.403), channel_id=1, source_target_pairs={{0,2},{2,4},{4,6},{6,7},{7,5},{5,3},{3,1},{1,0},{8,10},{10,12},{12... | collective-permute-start | bytes 1572872 | tf_op jit(solution)/shard_map/ppermute | solution.py:147
  476.7 26.2 %collective-permute-start.73 = (bf16[128,2048]{1,0:T(8,128)(2,1)S(1)}, bf16[128,2048]{1,0:T(8,128)(2,1)S(1)}, u32[]{:S(2)}, u32[]{:S(2)}) collective-permute-start(bf16[128,2048]{1,0:T(8,128)(2,1)S(1)} %get-tuple-element.404), channel_id=1, source_target_pairs={{2,0},{4,2},{6,4},{7,6},{5,7},{3,5},{1,3},{0,1},{10,8},{12,10},{14... | collective-permute-start | bytes 1572872 | tf_op jit(solution)/shard_map/ppermute | solution.py:147
  479.9 48.1 %collective-permute-start.96 = (bf16[8,128,512]{2,1,0:T(8,128)(2,1)}, bf16[8,128,512]{2,1,0:T(8,128)(2,1)}, u32[]{:S(2)}, u32[]{:S(2)}) collective-permute-start(bf16[8,128,512]{2,1,0:T(8,128)(2,1)} %all-to-all-done.2.own), channel_id=1, source_target_pairs={{0,8},{1,9},{2,10},{3,11},{4,12},{5,13},{6,14},{7,15},{8,0},{9,1},... | collective-permute-start | bytes 3145736 | tf_op jit(solution)/shard_map/ppermute | solution.py:133
  520.9 15.1 %collective-permute-start.97 = (bf16[8,128,512]{2,1,0:T(8,128)(2,1)}, bf16[8,128,512]{2,1,0:T(8,128)(2,1)}, u32[]{:S(2)}, u32[]{:S(2)}) collective-permute-start(bf16[8,128,512]{2,1,0:T(8,128)(2,1)} %collective-permute-done.90.other), channel_id=1, source_target_pairs={{0,8},{1,9},{2,10},{3,11},{4,12},{5,13},{6,14},{7,15},{8,0},{9,1},... | collective-permute-start | bytes 3145736 | tf_op jit(solution)/shard_map/ppermute | solution.py:133
  521.4 39.0 %collective-permute-start.93 = (bf16[8,128,768]{2,1,0:T(8,128)(2,1)S(1)}, bf16[8,128,768]{2,1,0:T(8,128)(2,1)}, u32[]{:S(2)}, u32[]{:S(2)}) collective-permute-start(bf16[8,128,768]{2,1,0:T(8,128)(2,1)S(1)} %all-to-all-done.3.own), channel_id=1, source_target_pairs={{0,16},{1,17},{2,18},{3,19},{4,20},{5,21},{6,22},{7,23},{8,24},{9,... | collective-permute-start | bytes 4718600 | tf_op jit(solution)/shard_map/ppermute | solution.py:133
  526.1 17.4 %collective-permute-start.94 = (bf16[128,2048]{1,0:T(8,128)(2,1)}, bf16[128,2048]{1,0:T(8,128)(2,1)S(1)}, u32[]{:S(2)}, u32[]{:S(2)}) collective-permute-start(bf16[128,2048]{1,0:T(8,128)(2,1)} %get-tuple-element.464), channel_id=1, source_target_pairs={{0,2},{2,4},{4,6},{6,7},{7,5},{5,3},{3,1},{1,0},{8,10},{10,12},{12... | collective-permute-start | bytes 1572872 | tf_op jit(solution)/shard_map/ppermute | solution.py:147
  528.0 15.5 %collective-permute-start.95 = (bf16[128,2048]{1,0:T(8,128)(2,1)}, bf16[128,2048]{1,0:T(8,128)(2,1)}, u32[]{:S(2)}, u32[]{:S(2)}) collective-permute-start(bf16[128,2048]{1,0:T(8,128)(2,1)} %get-tuple-element.465), channel_id=1, source_target_pairs={{2,0},{4,2},{6,4},{7,6},{5,7},{3,5},{1,3},{0,1},{10,8},{12,10},{14... | collective-permute-start | bytes 1572872 | tf_op jit(solution)/shard_map/ppermute | solution.py:147
  529.1 14.4 %collective-permute-start.99 = (f32[4,2048]{1,0:T(4,128)S(1)}, f32[4,2048]{1,0:T(4,128)S(1)}, u32[]{:S(2)}, u32[]{:S(2)}) collective-permute-start(f32[4,2048]{1,0:T(4,128)S(1)} %add.118), channel_id=1, source_target_pairs={{0,4},{1,5},{2,6},{3,7},{4,0},{5,1},{6,2},{7,3},{8,12},{9,13},{10,... | collective-permute-start | bytes 98312 | tf_op jit(solution)/shard_map/ppermute | solution.py:133
  536.0 24.5 %collective-permute-start.102 = (bf16[8,128,768]{2,1,0:T(8,128)(2,1)S(1)}, bf16[8,128,768]{2,1,0:T(8,128)(2,1)S(1)}, u32[]{:S(2)}, u32[]{:S(2)}) collective-permute-start(bf16[8,128,768]{2,1,0:T(8,128)(2,1)S(1)} %all-to-all-done.3.own), channel_id=1, source_target_pairs={{0,8},{1,9},{2,10},{3,11},{4,12},{5,13},{6,14},{7,15},{8,0},{9,1},... | collective-permute-start | bytes 4718600 | tf_op jit(solution)/shard_map/ppermute | solution.py:133
  (123 other events, 1468.8 us)

commit v6 on v5

--- a/solution.py
+++ b/solution.py
@@ -185,16 +185,17 @@
     return [shape((full * rows, width), bf16)] + [shape((rows // 2, width), bf16)] * 2 * (3 in tiles)
 
 
-def put_tile(refs, i, values, first=0):
-    both = values.shape[0]
+def put_tile(refs, i, values, first=0, part=None):
+    both, width = values.shape
     rows, start = both // 2, (i - first) * both
     values = values.astype(bf16)
+    columns = slice(0, width) if part is None else slice(part * width, (part + 1) * width)
     if i < 3:
-        refs[0][start : start + both] = values
+        refs[0][start : start + both, columns] = values
     else:
-        refs[0][start : start + rows] = values[:rows]
-        refs[1][...] = values[rows : rows + rows // 2]
-        refs[2][...] = values[rows + rows // 2 :]
+        refs[0][start : start + rows, columns] = values[:rows]
+        refs[1][:, columns] = values[rows : rows + rows // 2]
+        refs[2][:, columns] = values[rows + rows // 2 :]
 
 
 def fold(term_a, term_b, a, b):
@@ -615,7 +616,6 @@
                 )
                 z[here] = part
                 downs = of_x(w_down, s[1], half)
-                back = 0.0
                 for j in (0, 1):
                     ab = dot(part[:, halves[0]], w[j][...]) + dot(part[:, halves[1]], w[2 + j][...])
                     a, b = ab[:, :half], ab[:, half:]
@@ -627,10 +627,10 @@
                     d = dot(cot, downs[j], 1, 1).astype(bf16).astype(f32)
                     both = jnp.concatenate([d * b * slope, d * gelu], -1).astype(bf16)
                     grad[j, here] = both
-                    back = back + jnp.concatenate(
-                        [dot(both, w[j][...], 1, 1), dot(both, w[2 + j][...], 1, 1)], -1
-                    )
-                put_tile(outs, i, back, which[0])
+                for t in (0, 1):
+                    back = dot(grad[0, here], w[2 * t][...], 1, 1)
+                    back = back + dot(grad[1, here], w[2 * t + 1][...], 1, 1)
+                    put_tile(outs, i, back, which[0], t)
 
         return body
 
@@ -656,7 +656,6 @@
         one, half = dk // 2, dv // 2
         cut = dk + half
         x = s[1]
-        ready(9, 10, 11)
         for i in tiles:
             here = rows_of(i)
             part = tile(pieces, i)
@@ -703,24 +702,21 @@
         ready(20, 21, 22, 23, 24)
         for i in tiles:
             here = rows_of(i)
-            back = [
-                dot(d_pre[0, here], w[2 * t][...], 1, 1)
-                + dot(d_pre[1, here], w[2 * t + 1][...], 1, 1)
-                for t in (0, 1)
-            ]
-            back = jnp.concatenate(back, -1)
-            put_tile(outs, i, back)
-            parts = jnp.concatenate(
-                [
-                    jnp.sum(back * z[here].astype(f32), axis=0, keepdims=True),
-                    jnp.sum(back, axis=0, keepdims=True),
-                ],
-                0,
-            )
-            if i == 0:
-                room[...] = parts
-            else:
-                room[...] += parts
+            for t in (0, 1):
+                back = dot(d_pre[0, here], w[2 * t][...], 1, 1)
+                back = back + dot(d_pre[1, here], w[2 * t + 1][...], 1, 1)
+                put_tile(outs, i, back, part=t)
+                parts = jnp.concatenate(
+                    [
+                        jnp.sum(back * z[here, halves[t]].astype(f32), axis=0, keepdims=True),
+                        jnp.sum(back, axis=0, keepdims=True),
+                    ],
+                    0,
+                )
+                if i == 0:
+                    room[:, halves[t]] = parts
+                else:
+                    room[:, halves[t]] += parts
         for i in (5, 6, 4):
             push(i)
         for start, columns in arranged(s):
@@ -850,7 +846,7 @@
         + terms,
         *ring.pieces(), w_out, retained, gate, mixed,
         query, key, value, scores, decay, cosine, sine, *w_mix, z_first,
-        scalars=where, limit=LIMITS[4], late=range(9, 25), stream=(0, 1, 3, 4, 5, 6),
+        scalars=where, limit=LIMITS[4], late=range(12, 25), stream=(0, 1, 3, 4, 5, 6),
         scratch=[
             pltpu.VMEM((every, width), bf16),
             pltpu.VMEM((every, dv), bf16),

time: 575 us -> 572 us (level)
  no operation moved by 1% of the time
where the time goes in v6:
time: 572 us; the launch traced here: 568 us
  waiting for transfers between devices  288 us (50%)
  starting transfers between devices  123 us (22%)
  Pallas kernels  116 us (20%)
  local copies, waits for them, and re-layouts  20.9 us (4%)
  other arithmetic  17.9 us (3%)
    ppermute x72, waiting for transfers between devices, send(): lax.ppermute(value, 'fsdp', pairs if ahead else [(b, a) for a, b in pairs])  203 us
    ppermute x32, waiting for transfers between devices, swap(): lax.ppermute(value, BOTH, [(i, i ^ 1 << place) for i in range(count)])  85.9 us
    ppermute x72, starting transfers between devices, send(): lax.ppermute(value, 'fsdp', pairs if ahead else [(b, a) for a, b in pairs])  82.1 us
    pallas_call x28, Pallas kernels, kernel(): pl.pallas_call(body, out_shape=list(outs), grid=grid, in_specs=specs, out...  49.1 us
    pallas_call x2, Pallas kernels, streamed(): pl.pallas_call(run, out_shape=list(outs), in_specs=specs, out_specs=[away...  46.7 us
    ppermute x32, starting transfers between devices, swap(): lax.ppermute(value, BOTH, [(i, i ^ 1 << place) for i in range(count)])  20.8 us
    unnamed x126, local copies, waits for them, and re-layouts  18.9 us
    pallas_call x2, Pallas kernels, flat(): pl.pallas_call(body, out_shape=[shape((depth, n * size), f32) for size in...  13.2 us
  transfers between devices with their start and end apart: 108, of which 62 were waited for; matrix products, arithmetic and copies ran while one was open for 3% of the time, Pallas kernels for 18%

profile of v6, /device:TPU:0, one launch (start us, length us, event | category | flops | bytes accessed | tf_op | source)
XLA Modules:
  0.0 567.7 jit_solution(1075413766195506610)
XLA Ops:
  1.2 3.5 shard_map.272
  4.9 7.4 %all-to-all-start = ((bf16[8,128,768]{2,1,0:T(8,128)(2,1)}), bf16[8,128,768]{2,1,0:T(8,128)(2,1)}, u32[]{:S(2)}, u32[]{:S(2)}) async-start(bf16[8,128,768]{2,1,0:T(8,128)(2,1)} %shard_map.272), calls=%async_computation | async-start | bytes 3145728 | tf_op jit(solution)/shard_map/all_to_all | solution.py:377
  18.6 3.0 fusion.2.refs_17_.refs_18_
  21.6 3.1 multiply_sine_fusion
  24.7 3.1 shard_map.273
  27.8 15.0 %collective-permute-done.2 = bf16[4,256]{1,0:T(4,128)(2,1)S(1)} collective-permute-done((bf16[4,256]{1,0:T(4,128)(2,1)S(1)}, bf16[4,256]{1,0:T(4,128)(2,1)S(1)}, u32[]{:S(2)}, u32[]{:S(2)}) %collective-permute-start.2) | collective-permute-done | bytes 2080 | tf_op jit(solution)/shard_map/ppermute | solution.py:133
  42.8 8.4 %collective-permute-done.1.refs_5_ = bf16[128,2048]{1,0:T(8,128)(2,1)S(1)} collective-permute-done((bf16[128,2048]{1,0:T(8,128)(2,1)S(1)}, bf16[128,2048]{1,0:T(8,128)(2,1)S(1)}, u32[]{:S(2)}, u32[]{:S(2)}) %collective-permute-start.1) | collective-permute-done | bytes 524320 | tf_op jit(solution)/shard_map/ppermute | solution.py:147
  52.8 9.9 %collective-permute-start.3 = (bf16[128,2048]{1,0:T(8,128)(2,1)S(1)}, bf16[128,2048]{1,0:T(8,128)(2,1)}, u32[]{:S(2)}, u32[]{:S(2)}) collective-permute-start(bf16[128,2048]{1,0:T(8,128)(2,1)S(1)} %collective-permute-done.refs_2_), channel_id=1, source_target_pairs={{0,2},{2,4},{4,6},{6,7},{7,5},{5,3},{3,1},{1,0},{8,10},{10,12},{12... | collective-permute-start | bytes 1572872 | tf_op jit(solution)/shard_map/ppermute | solution.py:147
  64.8 11.8 %collective-permute-done.5 = bf16[4,512]{1,0:T(4,128)(2,1)S(1)} collective-permute-done((bf16[4,512]{1,0:T(4,128)(2,1)S(1)}, bf16[4,512]{1,0:T(4,128)(2,1)S(1)}, u32[]{:S(2)}, u32[]{:S(2)}) %collective-permute-start.5) | collective-permute-done | bytes 4128 | tf_op jit(solution)/shard_map/ppermute | solution.py:133
  79.5 11.4 %collective-permute-done.8 = bf16[4,1024]{1,0:T(4,128)(2,1)S(1)} collective-permute-done((bf16[4,1024]{1,0:T(4,128)(2,1)S(1)}, bf16[4,1024]{1,0:T(4,128)(2,1)S(1)}, u32[]{:S(2)}, u32[]{:S(2)}) %collective-permute-start.8) | collective-permute-done | bytes 8224 | tf_op jit(solution)/shard_map/ppermute | solution.py:133
  93.1 4.3 collective-permute-done.10.refs_9_
  98.2 4.5 all-to-all-start.1
  102.8 23.3 %shard_map.274 = (bf16[1024,2048]{1,0:T(8,128)(2,1)}, bf16[1024,256]{1,0:T(8,128)(2,1)S(1)}, bf16[1024,256]{1,0:T(8,128)(2,1)}, bf16[1024,512]{1,0:T(8,128)(2,1)...) custom-call(s32[2]{0:T(128)S(1)} %copy-done.33, ...), custom_call_target="tpu_custom_call" | custom-call | tf_op jit(solution)/shard_map/pallas_call | solution.py:108
  143.0 2.8 collective-permute-done.24.a
  170.5 12.0 %collective-permute-done.20.refs_1_ = bf16[128,1024]{1,0:T(8,128)(2,1)S(1)} collective-permute-done((bf16[128,1024]{1,0:T(8,128)(2,1)S(1)}, bf16[128,1024]{1,0:T(8,128)(2,1)S(1)}, u32[]{:S(2)}, u32[]{:S(2)}) %collective-permute-start.20) | collective-permute-done | bytes 262176 | tf_op jit(solution)/shard_map/ppermute | solution.py:147
  189.2 10.8 %collective-permute-done.31.refs_4_ = bf16[128,2048]{1,0:T(8,128)(2,1)S(1)} collective-permute-done((bf16[128,2048]{1,0:T(8,128)(2,1)S(1)}, bf16[128,2048]{1,0:T(8,128)(2,1)S(1)}, u32[]{:S(2)}, u32[]{:S(2)}) %collective-permute-start.31) | collective-permute-done | bytes 524320 | tf_op jit(solution)/shard_map/ppermute | solution.py:147
  202.0 9.8 %collective-permute-done.43.refs_8_.refs_2_ = bf16[128,2048]{1,0:T(8,128)(2,1)S(1)} collective-permute-done((bf16[128,2048]{1,0:T(8,128)(2,1)S(1)}, bf16[128,2048]{1,0:T(8,128)(2,1)S(1)}, u32[]{:S(2)}, u32[]{:S(2)}) %collective-permute-start.43) | collective-permute-done | bytes 524320 | tf_op jit(solution)/shard_map/ppermute | solution.py:147
  213.9 9.2 %collective-permute-done.33.refs_2_ = bf16[128,2048]{1,0:T(8,128)(2,1)S(1)} collective-permute-done((bf16[128,2048]{1,0:T(8,128)(2,1)S(1)}, bf16[128,2048]{1,0:T(8,128)(2,1)S(1)}, u32[]{:S(2)}, u32[]{:S(2)}) %collective-permute-start.33) | collective-permute-done | bytes 524320 | tf_op jit(solution)/shard_map/ppermute | solution.py:147
  226.1 8.3 %collective-permute-done.45.refs_9_.refs_3_ = bf16[128,2048]{1,0:T(8,128)(2,1)S(1)} collective-permute-done((bf16[128,2048]{1,0:T(8,128)(2,1)S(1)}, bf16[128,2048]{1,0:T(8,128)(2,1)S(1)}, u32[]{:S(2)}, u32[]{:S(2)}) %collective-permute-start.45) | collective-permute-done | bytes 524320 | tf_op jit(solution)/shard_map/ppermute | solution.py:147
  237.9 7.6 %collective-permute-done.35.refs_3_ = bf16[128,2048]{1,0:T(8,128)(2,1)S(1)} collective-permute-done((bf16[128,2048]{1,0:T(8,128)(2,1)S(1)}, bf16[128,2048]{1,0:T(8,128)(2,1)S(1)}, u32[]{:S(2)}, u32[]{:S(2)}) %collective-permute-start.35) | collective-permute-done | bytes 524320 | tf_op jit(solution)/shard_map/ppermute | solution.py:147
  245.6 3.6 collective-permute-done.36.refs_0_
  251.4 11.1 %shard_map.282 = (bf16[768,2048]{1,0:T(8,128)(2,1)}, bf16[768,512]{1,0:T(8,128)(2,1)S(1)}, bf16[2,768,512]{2,1,0:T(8,128)(2,1)S(1)}, bf16[768,2048]{1,0:T(8,128)(2,1)}) custom-call(s32[2]{0:T(128)S(1)} %copy-done.33, bf16[128,2048]{1,0:T(8,128)(2,1)S(1)} %get-tuple-element.314.refs_0_, bf16[128,2048]{1,0:T(8,128)(2,1)S(1)} %collective-permute-done.30.refs_1_, ...), custom_call_target="tpu_custom_call" | custom-call | tf_op jit(solution)/shard_map/pallas_call | solution.py:44
  262.6 3.6 shard_map.283
  268.6 4.1 collective-permute-done.49.a
  276.8 4.5 shard_map.287
  288.3 3.0 shard_map.289
  291.5 8.5 %collective-permute-done.53.a = bf16[128,2048]{1,0:T(8,128)(2,1)S(1)} collective-permute-done((bf16[128,2048]{1,0:T(8,128)(2,1)S(1)}, bf16[128,2048]{1,0:T(8,128)(2,1)S(1)}, u32[]{:S(2)}, u32[]{:S(2)}) %collective-permute-start.53) | collective-permute-done | bytes 524320 | tf_op jit(solution)/shard_map/ppermute | solution.py:147
  304.5 11.3 %collective-permute-done.57.refs_1_ = bf16[128,2048]{1,0:T(8,128)(2,1)S(1)} collective-permute-done((bf16[128,2048]{1,0:T(8,128)(2,1)S(1)}, bf16[128,2048]{1,0:T(8,128)(2,1)S(1)}, u32[]{:S(2)}, u32[]{:S(2)}) %collective-permute-start.57) | collective-permute-done | bytes 524320 | tf_op jit(solution)/shard_map/ppermute | solution.py:147
  320.0 8.5 %collective-permute-done.62 = bf16[1024,512]{1,0:T(8,128)(2,1)S(1)} collective-permute-done((bf16[1024,512]{1,0:T(8,128)(2,1)S(1)}, bf16[1024,512]{1,0:T(8,128)(2,1)S(1)}, u32[]{:S(2)}, u32[]{:S(2)}) %collective-permute-start.62) | collective-permute-done | bytes 1048608 | tf_op jit(solution)/shard_map/ppermute | solution.py:133
  335.0 9.4 %collective-permute-done.63.refs_3_ = bf16[128,2048]{1,0:T(8,128)(2,1)S(1)} collective-permute-done((bf16[128,2048]{1,0:T(8,128)(2,1)S(1)}, bf16[128,2048]{1,0:T(8,128)(2,1)S(1)}, u32[]{:S(2)}, u32[]{:S(2)}) %collective-permute-start.63) | collective-permute-done | bytes 524320 | tf_op jit(solution)/shard_map/ppermute | solution.py:147
  346.8 2.9 shard_map.284
  351.8 7.9 %collective-permute-done.65.refs_4_ = bf16[128,2048]{1,0:T(8,128)(2,1)S(1)} collective-permute-done((bf16[128,2048]{1,0:T(8,128)(2,1)S(1)}, bf16[128,2048]{1,0:T(8,128)(2,1)S(1)}, u32[]{:S(2)}, u32[]{:S(2)}) %collective-permute-start.65) | collective-permute-done | bytes 524320 | tf_op jit(solution)/shard_map/ppermute | solution.py:147
  368.1 4.4 all-to-all-start.2
  372.6 23.4 %shard_map.293 = (bf16[2,128,2048]{2,1,0:T(8,128)(2,1)}, bf16[2,128,2048]{2,1,0:T(8,128)(2,1)}, f32[2,2048]{1,0:T(2,128)}, bf16[2,1024,768]{2,1,0:T(8,128)(2,1)}...) custom-call(s32[2]{0:T(128)} %pad_add_fusion.s.refs_0_, ...), custom_call_target="tpu_custom_call" | custom-call | tf_op jit(solution)/shard_map/pallas_call | solution.py:108
  400.2 6.7 %shard_map.294 = (bf16[1024,768]{1,0:T(8,128)(2,1)S(1)}, bf16[1024,768]{1,0:T(8,128)(2,1)S(1)}, bf16[1024,768]{1,0:T(8,128)(2,1)S(1)}, bf16[1024,768]{1,0:T(8,128)(2,1)S(1)}) custom-call(bf16[1024,2048]{1,0:T(8,128)(2,1)S(1)} %copy-done.11, bf16[2,1024,768]{2,1,0:T(8,128)(2,1)S(1)} %copy-done.17), custom_call_target="tpu_custom_call" | custom-call | tf_op jit(solution)/shard_map/pallas_call | solution.py:44
  412.1 4.6 collective-permute-done.74.a
  423.2 8.1 %collective-permute-done.80.a = bf16[128,2048]{1,0:T(8,128)(2,1)S(1)} collective-permute-done((bf16[128,2048]{1,0:T(8,128)(2,1)S(1)}, bf16[128,2048]{1,0:T(8,128)(2,1)S(1)}, u32[]{:S(2)}, u32[]{:S(2)}) %collective-permute-start.80) | collective-permute-done | bytes 524320 | tf_op jit(solution)/shard_map/ppermute | solution.py:147
  435.4 9.7 %collective-permute-done.85 = f32[4,2048]{1,0:T(4,128)S(1)} collective-permute-done((f32[4,2048]{1,0:T(4,128)S(1)}, f32[4,2048]{1,0:T(4,128)S(1)}, u32[]{:S(2)}, u32[]{:S(2)}) %collective-permute-start.85) | collective-permute-done | bytes 32800 | tf_op jit(solution)/shard_map/ppermute | solution.py:133
  449.4 8.8 %collective-permute-done.89 = f32[4,2048]{1,0:T(4,128)S(1)} collective-permute-done((f32[4,2048]{1,0:T(4,128)S(1)}, f32[4,2048]{1,0:T(4,128)S(1)}, u32[]{:S(2)}, u32[]{:S(2)}) %collective-permute-start.89) | collective-permute-done | bytes 32800 | tf_op jit(solution)/shard_map/ppermute | solution.py:133
  461.5 3.6 all-to-all-start.3
  473.9 2.8 shard_map.299
  479.3 19.5 %collective-permute-done.72.a = bf16[128,2048]{1,0:T(8,128)(2,1)S(1)} collective-permute-done((bf16[128,2048]{1,0:T(8,128)(2,1)S(1)}, bf16[128,2048]{1,0:T(8,128)(2,1)S(1)}, u32[]{:S(2)}, u32[]{:S(2)}) %collective-permute-start.72) | collective-permute-done | bytes 524320 | tf_op jit(solution)/shard_map/ppermute | solution.py:147
  500.5 15.2 %collective-permute-done.91 = bf16[2,128,2048]{2,1,0:T(8,128)(2,1)} collective-permute-done((bf16[2,128,2048]{2,1,0:T(8,128)(2,1)S(1)}, bf16[2,128,2048]{2,1,0:T(8,128)(2,1)}, u32[]{:S(2)}, u32[]{:S(2)}) %collective-permute-start.91) | collective-permute-done | bytes 1048608 | tf_op jit(solution)/shard_map/ppermute | solution.py:133
  530.0 2.8 shard_map.302
  532.8 6.7 %shard_map.301 = (f32[256,4096]{1,0:T(8,128)}, f32[256,4096]{1,0:T(8,128)}) custom-call(s32[2]{0:T(128)S(1)} %copy-done.34, bf16[8,128,512]{2,1,0:T(8,128)(2,1)} %all-to-all-done.2.own, bf16[8,128,512]{2,1,0:T(8,128)(2,1)} %collective-permute-done.96.own_c, bf16[8,128,512]{2,1,0:T(8,128)(2,1)} %collective-permute-done.90.other, ...), custom_call_target="tpu_custom_call" | custom-call | tf_op jit(solution)/shard_map/pallas_call | solution.py:432
  544.9 10.1 %collective-permute-done.100.refs_1_ = bf16[128,2048]{1,0:T(8,128)(2,1)S(1)} collective-permute-done((bf16[128,2048]{1,0:T(8,128)(2,1)S(1)}, bf16[128,2048]{1,0:T(8,128)(2,1)S(1)}, u32[]{:S(2)}, u32[]{:S(2)}) %collective-permute-start.100) | collective-permute-done | bytes 524320 | tf_op jit(solution)/shard_map/ppermute | solution.py:147
  557.3 3.6 collective-permute-done.103.other_c
  560.9 6.5 %shard_map.305 = (f32[256,2048]{1,0:T(8,128)}, f32[256,2048]{1,0:T(8,128)}, f32[256,4096]{1,0:T(8,128)}, f32[256,4096]{1,0:T(8,128)}) custom-call(s32[2]{0:T(128)S(1)} %copy-done.34, bf16[8,128,768]{2,1,0:T(8,128)(2,1)S(1)} %all-to-all-done.3.own, bf16[8,128,768]{2,1,0:T(8,128)(2,1)S(1)} %collective-permute-done.102.own_c, ...), custom_call_target="tpu_custom_call" | custom-call | tf_op jit(solution)/shard_map/pallas_call | solution.py:432
  (376 shorter events, 181.5 us)
Async XLA Ops:
  4.9 46.3 %all-to-all-start = ((bf16[8,128,768]{2,1,0:T(8,128)(2,1)}), bf16[8,128,768]{2,1,0:T(8,128)(2,1)}, u32[]{:S(2)}, u32[]{:S(2)}) async-start(bf16[8,128,768]{2,1,0:T(8,128)(2,1)} %shard_map.272), calls=%async_computation | async-start | bytes 3145728 | tf_op jit(solution)/shard_map/all_to_all | solution.py:377
  12.3 38.9 %collective-permute-start.1 = (bf16[128,2048]{1,0:T(8,128)(2,1)S(1)}, bf16[128,2048]{1,0:T(8,128)(2,1)S(1)}, u32[]{:S(2)}, u32[]{:S(2)}) collective-permute-start(bf16[128,2048]{1,0:T(8,128)(2,1)S(1)} %copy-done.13), channel_id=1, source_target_pairs={{2,0},{4,2},{6,4},{7,6},{5,7},{3,5},{1,3},{0,1},{10,8},{12,10},{14... | collective-permute-start | bytes 1572872 | tf_op jit(solution)/shard_map/ppermute | solution.py:147
  14.3 36.9 %collective-permute-start = (bf16[128,2048]{1,0:T(8,128)(2,1)S(1)}, bf16[128,2048]{1,0:T(8,128)(2,1)S(1)}, u32[]{:S(2)}, u32[]{:S(2)}) collective-permute-start(bf16[128,2048]{1,0:T(8,128)(2,1)S(1)} %copy-done.13), channel_id=1, source_target_pairs={{0,2},{2,4},{4,6},{6,7},{7,5},{5,3},{3,1},{1,0},{8,10},{10,12},{12... | collective-permute-start | bytes 1572872 | tf_op jit(solution)/shard_map/ppermute | solution.py:147
  14.5 28.3 %collective-permute-start.2 = (bf16[4,256]{1,0:T(4,128)(2,1)S(1)}, bf16[4,256]{1,0:T(4,128)(2,1)S(1)}, u32[]{:S(2)}, u32[]{:S(2)}) collective-permute-start(bf16[4,256]{1,0:T(4,128)(2,1)S(1)} %pad_maximum_fusion.4), channel_id=1, source_target_pairs={{0,1},{1,0},{2,3},{3,2},{4,5},{5,4},{6,7},{7,6},{8,9},{9,8},{10,11... | collective-permute-start | bytes 6152 | tf_op jit(solution)/shard_map/ppermute | solution.py:133
  51.2 46.9 %collective-permute-start.12 = (bf16[1024,768]{1,0:T(8,128)(2,1)}, bf16[1024,768]{1,0:T(8,128)(2,1)S(1)}, u32[]{:S(2)}, u32[]{:S(2)}) collective-permute-start(bf16[1024,768]{1,0:T(8,128)(2,1)} %bitcast.4.refs_11_.refs_21_), channel_id=1, source_target_pairs={{0,8},{1,9},{2,10},{3,11},{4,12},{5,13},{6,14},{7,15},{8,0},{9,1},... | collective-permute-start | bytes 4718600 | tf_op jit(solution)/shard_map/ppermute | solution.py:133
  51.3 46.8 %collective-permute-start.11 = (bf16[1024,768]{1,0:T(8,128)(2,1)}, bf16[1024,768]{1,0:T(8,128)(2,1)}, u32[]{:S(2)}, u32[]{:S(2)}) collective-permute-start(bf16[1024,768]{1,0:T(8,128)(2,1)} %bitcast.4.refs_11_.refs_21_), channel_id=1, source_target_pairs={{0,16},{1,17},{2,18},{3,19},{4,20},{5,21},{6,22},{7,23},{8,24},{9,... | collective-permute-start | bytes 4718600 | tf_op jit(solution)/shard_map/ppermute | solution.py:133
  52.8 23.8 %collective-permute-start.3 = (bf16[128,2048]{1,0:T(8,128)(2,1)S(1)}, bf16[128,2048]{1,0:T(8,128)(2,1)}, u32[]{:S(2)}, u32[]{:S(2)}) collective-permute-start(bf16[128,2048]{1,0:T(8,128)(2,1)S(1)} %collective-permute-done.refs_2_), channel_id=1, source_target_pairs={{0,2},{2,4},{4,6},{6,7},{7,5},{5,3},{3,1},{1,0},{8,10},{10,12},{12... | collective-permute-start | bytes 1572872 | tf_op jit(solution)/shard_map/ppermute | solution.py:147
  76.7 14.2 %collective-permute-start.6 = (bf16[128,2048]{1,0:T(8,128)(2,1)}, bf16[128,2048]{1,0:T(8,128)(2,1)S(1)}, u32[]{:S(2)}, u32[]{:S(2)}) collective-permute-start(bf16[128,2048]{1,0:T(8,128)(2,1)} %collective-permute-done.3.refs_3_), channel_id=1, source_target_pairs={{0,2},{2,4},{4,6},{6,7},{7,5},{5,3},{3,1},{1,0},{8,10},{10,12},{12... | collective-permute-start | bytes 1572872 | tf_op jit(solution)/shard_map/ppermute | solution.py:147
  98.2 40.6 %all-to-all-start.1 = ((bf16[8,128,512]{2,1,0:T(8,128)(2,1)}), bf16[8,128,512]{2,1,0:T(8,128)(2,1)S(1)}, u32[]{:S(2)}, u32[]{:S(2)}) async-start(bf16[8,128,512]{2,1,0:T(8,128)(2,1)} %shard_map.273), calls=%async_computation.1 | async-start | bytes 2097152 | tf_op jit(solution)/shard_map/all_to_all | solution.py:377
  160.9 28.3 %collective-permute-start.32 = (bf16[1024,512]{1,0:T(8,128)(2,1)S(1)}, bf16[1024,512]{1,0:T(8,128)(2,1)S(1)}, u32[]{:S(2)}, u32[]{:S(2)}) collective-permute-start(bf16[1024,512]{1,0:T(8,128)(2,1)S(1)} %bitcast.13), channel_id=1, source_target_pairs={{0,16},{1,17},{2,18},{3,19},{4,20},{5,21},{6,22},{7,23},{8,24},{9,... | collective-permute-start | bytes 3145736 | tf_op jit(solution)/shard_map/ppermute | solution.py:133
  162.7 24.5 %collective-permute-start.42 = (bf16[128,2048]{1,0:T(8,128)(2,1)S(1)}, bf16[128,2048]{1,0:T(8,128)(2,1)S(1)}, u32[]{:S(2)}, u32[]{:S(2)}) collective-permute-start(bf16[128,2048]{1,0:T(8,128)(2,1)S(1)} %copy-done.12), channel_id=1, source_target_pairs={{2,0},{4,2},{6,4},{7,6},{5,7},{3,5},{1,3},{0,1},{10,8},{12,10},{14... | collective-permute-start | bytes 1572872 | tf_op jit(solution)/shard_map/ppermute | solution.py:147
  164.3 22.9 %collective-permute-start.41 = (bf16[128,2048]{1,0:T(8,128)(2,1)S(1)}, bf16[128,2048]{1,0:T(8,128)(2,1)S(1)}, u32[]{:S(2)}, u32[]{:S(2)}) collective-permute-start(bf16[128,2048]{1,0:T(8,128)(2,1)S(1)} %copy-done.12), channel_id=1, source_target_pairs={{0,2},{2,4},{4,6},{6,7},{7,5},{5,3},{3,1},{1,0},{8,10},{10,12},{12... | collective-permute-start | bytes 1572872 | tf_op jit(solution)/shard_map/ppermute | solution.py:147
  168.3 14.2 %collective-permute-start.20 = (bf16[128,1024]{1,0:T(8,128)(2,1)S(1)}, bf16[128,1024]{1,0:T(8,128)(2,1)S(1)}, u32[]{:S(2)}, u32[]{:S(2)}) collective-permute-start(bf16[128,1024]{1,0:T(8,128)(2,1)S(1)} %get-tuple-element.296), channel_id=1, source_target_pairs={{0,2},{2,4},{4,6},{6,7},{7,5},{5,3},{3,1},{1,0},{8,10},{10,12},{12... | collective-permute-start | bytes 786440 | tf_op jit(solution)/shard_map/ppermute | solution.py:147
  185.1 14.9 %collective-permute-start.31 = (bf16[128,2048]{1,0:T(8,128)(2,1)S(1)}, bf16[128,2048]{1,0:T(8,128)(2,1)S(1)}, u32[]{:S(2)}, u32[]{:S(2)}) collective-permute-start(bf16[128,2048]{1,0:T(8,128)(2,1)S(1)} %get-tuple-element.314.refs_0_), channel_id=1, source_target_pairs={{2,0},{4,2},{6,4},{7,6},{5,7},{3,5},{1,3},{0,1},{10,8},{12,10},{14... | collective-permute-start | bytes 1572872 | tf_op jit(solution)/shard_map/ppermute | solution.py:147
  185.8 14.9 %collective-permute-start.30 = (bf16[128,2048]{1,0:T(8,128)(2,1)S(1)}, bf16[128,2048]{1,0:T(8,128)(2,1)S(1)}, u32[]{:S(2)}, u32[]{:S(2)}) collective-permute-start(bf16[128,2048]{1,0:T(8,128)(2,1)S(1)} %get-tuple-element.314.refs_0_), channel_id=1, source_target_pairs={{0,2},{2,4},{4,6},{6,7},{7,5},{5,3},{3,1},{1,0},{8,10},{10,12},{12... | collective-permute-start | bytes 1572872 | tf_op jit(solution)/shard_map/ppermute | solution.py:147
  187.2 24.7 %collective-permute-start.43 = (bf16[128,2048]{1,0:T(8,128)(2,1)S(1)}, bf16[128,2048]{1,0:T(8,128)(2,1)S(1)}, u32[]{:S(2)}, u32[]{:S(2)}) collective-permute-start(bf16[128,2048]{1,0:T(8,128)(2,1)S(1)} %collective-permute-done.41.refs_7_.refs_1_), channel_id=1, source_target_pairs={{0,2},{2,4},{4,6},{6,7},{7,5},{5,3},{3,1},{1,0},{8,10},{10,12},{12... | collective-permute-start | bytes 1572872 | tf_op jit(solution)/shard_map/ppermute | solution.py:147
  188.7 23.2 %collective-permute-start.44 = (bf16[128,2048]{1,0:T(8,128)(2,1)S(1)}, bf16[128,2048]{1,0:T(8,128)(2,1)S(1)}, u32[]{:S(2)}, u32[]{:S(2)}) collective-permute-start(bf16[128,2048]{1,0:T(8,128)(2,1)S(1)} %collective-permute-done.42.refs_10_.refs_4_), channel_id=1, source_target_pairs={{2,0},{4,2},{6,4},{7,6},{5,7},{3,5},{1,3},{0,1},{10,8},{12,10},{14... | collective-permute-start | bytes 1572872 | tf_op jit(solution)/shard_map/ppermute | solution.py:147
  200.6 22.5 %collective-permute-start.33 = (bf16[128,2048]{1,0:T(8,128)(2,1)S(1)}, bf16[128,2048]{1,0:T(8,128)(2,1)S(1)}, u32[]{:S(2)}, u32[]{:S(2)}) collective-permute-start(bf16[128,2048]{1,0:T(8,128)(2,1)S(1)} %collective-permute-done.30.refs_1_), channel_id=1, source_target_pairs={{0,2},{2,4},{4,6},{6,7},{7,5},{5,3},{3,1},{1,0},{8,10},{10,12},{12... | collective-permute-start | bytes 1572872 | tf_op jit(solution)/shard_map/ppermute | solution.py:147
  202.0 34.4 %collective-permute-start.37 = (bf16[1024,512]{1,0:T(8,128)(2,1)S(1)}, bf16[1024,512]{1,0:T(8,128)(2,1)S(1)}, u32[]{:S(2)}, u32[]{:S(2)}) collective-permute-start(bf16[1024,512]{1,0:T(8,128)(2,1)S(1)} %bitcast.14), channel_id=1, source_target_pairs={{0,8},{1,9},{2,10},{3,11},{4,12},{5,13},{6,14},{7,15},{8,0},{9,1},... | collective-permute-start | bytes 3145736 | tf_op jit(solution)/shard_map/ppermute | solution.py:133
  212.1 22.2 %collective-permute-start.45 = (bf16[128,2048]{1,0:T(8,128)(2,1)S(1)}, bf16[128,2048]{1,0:T(8,128)(2,1)S(1)}, u32[]{:S(2)}, u32[]{:S(2)}) collective-permute-start(bf16[128,2048]{1,0:T(8,128)(2,1)S(1)} %collective-permute-done.43.refs_8_.refs_2_), channel_id=1, source_target_pairs={{0,2},{2,4},{4,6},{6,7},{7,5},{5,3},{3,1},{1,0},{8,10},{10,12},{12... | collective-permute-start | bytes 1572872 | tf_op jit(solution)/shard_map/ppermute | solution.py:147
  213.9 24.1 %collective-permute-start.38 = (bf16[1024,512]{1,0:T(8,128)(2,1)S(1)}, bf16[1024,512]{1,0:T(8,128)(2,1)S(1)}, u32[]{:S(2)}, u32[]{:S(2)}) collective-permute-start(bf16[1024,512]{1,0:T(8,128)(2,1)S(1)} %collective-permute-done.32.refs_14_.refs_8_), channel_id=1, source_target_pairs={{0,8},{1,9},{2,10},{3,11},{4,12},{5,13},{6,14},{7,15},{8,0},{9,1},... | collective-permute-start | bytes 3145736 | tf_op jit(solution)/shard_map/ppermute | solution.py:133
  224.6 21.0 %collective-permute-start.35 = (bf16[128,2048]{1,0:T(8,128)(2,1)S(1)}, bf16[128,2048]{1,0:T(8,128)(2,1)S(1)}, u32[]{:S(2)}, u32[]{:S(2)}) collective-permute-start(bf16[128,2048]{1,0:T(8,128)(2,1)S(1)} %collective-permute-done.33.refs_2_), channel_id=1, source_target_pairs={{0,2},{2,4},{4,6},{6,7},{7,5},{5,3},{3,1},{1,0},{8,10},{10,12},{12... | collective-permute-start | bytes 1572872 | tf_op jit(solution)/shard_map/ppermute | solution.py:147
  234.3 14.8 %collective-permute-start.36 = (bf16[128,2048]{1,0:T(8,128)(2,1)S(1)}, bf16[128,2048]{1,0:T(8,128)(2,1)S(1)}, u32[]{:S(2)}, u32[]{:S(2)}) collective-permute-start(bf16[128,2048]{1,0:T(8,128)(2,1)S(1)} %collective-permute-done.34.refs_5_), channel_id=1, source_target_pairs={{2,0},{4,2},{6,4},{7,6},{5,7},{3,5},{1,3},{0,1},{10,8},{12,10},{14... | collective-permute-start | bytes 1572872 | tf_op jit(solution)/shard_map/ppermute | solution.py:147
  235.9 26.7 %collective-permute-start.48 = (bf16[64,2048]{1,0:T(8,128)(2,1)S(1)}, bf16[64,2048]{1,0:T(8,128)(2,1)S(1)}, u32[]{:S(2)}, u32[]{:S(2)}) collective-permute-start(bf16[64,2048]{1,0:T(8,128)(2,1)S(1)} %slice.58), channel_id=1, source_target_pairs={{2,0},{4,2},{6,4},{7,6},{5,7},{3,5},{1,3},{0,1},{10,8},{12,10},{14... | collective-permute-start | bytes 786440 | tf_op jit(solution)/shard_map/ppermute | solution.py:147
  236.4 26.2 %collective-permute-start.47 = (bf16[64,2048]{1,0:T(8,128)(2,1)S(1)}, bf16[64,2048]{1,0:T(8,128)(2,1)S(1)}, u32[]{:S(2)}, u32[]{:S(2)}) collective-permute-start(bf16[64,2048]{1,0:T(8,128)(2,1)S(1)} %slice.57), channel_id=1, source_target_pairs={{0,2},{2,4},{4,6},{6,7},{7,5},{5,3},{3,1},{1,0},{8,10},{10,12},{12... | collective-permute-start | bytes 786440 | tf_op jit(solution)/shard_map/ppermute | solution.py:147
  285.4 15.7 %collective-permute-start.55 = (bf16[1024,512]{1,0:T(8,128)(2,1)S(1)}, bf16[1024,512]{1,0:T(8,128)(2,1)S(1)}, u32[]{:S(2)}, u32[]{:S(2)}) collective-permute-start(bf16[1024,512]{1,0:T(8,128)(2,1)S(1)} %get-tuple-element.370), channel_id=1, source_target_pairs={{0,8},{1,9},{2,10},{3,11},{4,12},{5,13},{6,14},{7,15},{8,0},{9,1},... | collective-permute-start | bytes 3145736 | tf_op jit(solution)/shard_map/ppermute | solution.py:133
  301.4 14.4 %collective-permute-start.57 = (bf16[128,2048]{1,0:T(8,128)(2,1)S(1)}, bf16[128,2048]{1,0:T(8,128)(2,1)S(1)}, u32[]{:S(2)}, u32[]{:S(2)}) collective-permute-start(bf16[128,2048]{1,0:T(8,128)(2,1)S(1)} %get-tuple-element.378), channel_id=1, source_target_pairs={{0,2},{2,4},{4,6},{6,7},{7,5},{5,3},{3,1},{1,0},{8,10},{10,12},{12... | collective-permute-start | bytes 1572872 | tf_op jit(solution)/shard_map/ppermute | solution.py:147
  302.1 14.1 %collective-permute-start.58 = (bf16[128,2048]{1,0:T(8,128)(2,1)S(1)}, bf16[128,2048]{1,0:T(8,128)(2,1)S(1)}, u32[]{:S(2)}, u32[]{:S(2)}) collective-permute-start(bf16[128,2048]{1,0:T(8,128)(2,1)S(1)} %get-tuple-element.379), channel_id=1, source_target_pairs={{2,0},{4,2},{6,4},{7,6},{5,7},{3,5},{1,3},{0,1},{10,8},{12,10},{14... | collective-permute-start | bytes 1572872 | tf_op jit(solution)/shard_map/ppermute | solution.py:147
  303.5 25.0 %collective-permute-start.62 = (bf16[1024,512]{1,0:T(8,128)(2,1)S(1)}, bf16[1024,512]{1,0:T(8,128)(2,1)S(1)}, u32[]{:S(2)}, u32[]{:S(2)}) collective-permute-start(bf16[1024,512]{1,0:T(8,128)(2,1)S(1)} %add_convert_fusion.7), channel_id=1, source_target_pairs={{0,16},{1,17},{2,18},{3,19},{4,20},{5,21},{6,22},{7,23},{8,24},{9,... | collective-permute-start | bytes 3145736 | tf_op jit(solution)/shard_map/ppermute | solution.py:133
  334.4 30.1 %collective-permute-start.71 = (bf16[2,128,2048]{2,1,0:T(8,128)(2,1)S(1)}, bf16[2,128,2048]{2,1,0:T(8,128)(2,1)S(1)}, u32[]{:S(2)}, u32[]{:S(2)}) collective-permute-start(bf16[2,128,2048]{2,1,0:T(8,128)(2,1)S(1)} %add_convert_fusion.6), channel_id=1, source_target_pairs={{0,16},{1,17},{2,18},{3,19},{4,20},{5,21},{6,22},{7,23},{8,24},{9,... | collective-permute-start | bytes 3145736 | tf_op jit(solution)/shard_map/ppermute | solution.py:133
  344.7 14.9 %collective-permute-start.65 = (bf16[128,2048]{1,0:T(8,128)(2,1)S(1)}, bf16[128,2048]{1,0:T(8,128)(2,1)S(1)}, u32[]{:S(2)}, u32[]{:S(2)}) collective-permute-start(bf16[128,2048]{1,0:T(8,128)(2,1)S(1)} %collective-permute-done.63.refs_3_), channel_id=1, source_target_pairs={{0,2},{2,4},{4,6},{6,7},{7,5},{5,3},{3,1},{1,0},{8,10},{10,12},{12... | collective-permute-start | bytes 1572872 | tf_op jit(solution)/shard_map/ppermute | solution.py:147
  345.4 14.9 %collective-permute-start.66 = (bf16[128,2048]{1,0:T(8,128)(2,1)S(1)}, bf16[128,2048]{1,0:T(8,128)(2,1)S(1)}, u32[]{:S(2)}, u32[]{:S(2)}) collective-permute-start(bf16[128,2048]{1,0:T(8,128)(2,1)S(1)} %collective-permute-done.64.refs_6_), channel_id=1, source_target_pairs={{2,0},{4,2},{6,4},{7,6},{5,7},{3,5},{1,3},{0,1},{10,8},{12,10},{14... | collective-permute-start | bytes 1572872 | tf_op jit(solution)/shard_map/ppermute | solution.py:147
  349.7 14.4 %collective-permute-start.69 = (bf16[64,2048]{1,0:T(8,128)(2,1)S(1)}, bf16[64,2048]{1,0:T(8,128)(2,1)S(1)}, u32[]{:S(2)}, u32[]{:S(2)}) collective-permute-start(bf16[64,2048]{1,0:T(8,128)(2,1)S(1)} %get-tuple-element.395), channel_id=1, source_target_pairs={{0,2},{2,4},{4,6},{6,7},{7,5},{5,3},{3,1},{1,0},{8,10},{10,12},{12... | collective-permute-start | bytes 786440 | tf_op jit(solution)/shard_map/ppermute | solution.py:147
  350.4 14.1 %collective-permute-start.70 = (bf16[64,2048]{1,0:T(8,128)(2,1)S(1)}, bf16[64,2048]{1,0:T(8,128)(2,1)S(1)}, u32[]{:S(2)}, u32[]{:S(2)}) collective-permute-start(bf16[64,2048]{1,0:T(8,128)(2,1)S(1)} %get-tuple-element.396), channel_id=1, source_target_pairs={{2,0},{4,2},{6,4},{7,6},{5,7},{3,5},{1,3},{0,1},{10,8},{12,10},{14... | collective-permute-start | bytes 786440 | tf_op jit(solution)/shard_map/ppermute | solution.py:147
  368.1 27.9 %all-to-all-start.2 = ((bf16[8,128,512]{2,1,0:T(8,128)(2,1)}), bf16[8,128,512]{2,1,0:T(8,128)(2,1)}, u32[]{:S(2)}, u32[]{:S(2)}) async-start(bf16[8,128,512]{2,1,0:T(8,128)(2,1)} %bitcast.18), calls=%async_computation.2 | async-start | bytes 2097152 | tf_op jit(solution)/shard_map/all_to_all | solution.py:410
  420.4 39.4 %collective-permute-start.88 = (bf16[1024,768]{1,0:T(8,128)(2,1)S(1)}, bf16[1024,768]{1,0:T(8,128)(2,1)S(1)}, u32[]{:S(2)}, u32[]{:S(2)}) collective-permute-start(bf16[1024,768]{1,0:T(8,128)(2,1)S(1)} %add_convert_fusion.1), channel_id=1, source_target_pairs={{0,16},{1,17},{2,18},{3,19},{4,20},{5,21},{6,22},{7,23},{8,24},{9,... | collective-permute-start | bytes 4718600 | tf_op jit(solution)/shard_map/ppermute | solution.py:133
  461.5 54.1 %all-to-all-start.3 = ((bf16[8,128,768]{2,1,0:T(8,128)(2,1)}), bf16[8,128,768]{2,1,0:T(8,128)(2,1)S(1)}, u32[]{:S(2)}, u32[]{:S(2)}) async-start(bf16[8,128,768]{2,1,0:T(8,128)(2,1)} %bitcast.17), calls=%async_computation.3 | async-start | bytes 3145728 | tf_op jit(solution)/shard_map/all_to_all | solution.py:410
  467.3 33.2 %collective-permute-start.90 = (bf16[8,128,512]{2,1,0:T(8,128)(2,1)}, bf16[8,128,512]{2,1,0:T(8,128)(2,1)}, u32[]{:S(2)}, u32[]{:S(2)}) collective-permute-start(bf16[8,128,512]{2,1,0:T(8,128)(2,1)} %all-to-all-done.2.own), channel_id=1, source_target_pairs={{0,16},{1,17},{2,18},{3,19},{4,20},{5,21},{6,22},{7,23},{8,24},{9,... | collective-permute-start | bytes 3145736 | tf_op jit(solution)/shard_map/ppermute | solution.py:133
  468.8 46.8 %collective-permute-start.91 = (bf16[2,128,2048]{2,1,0:T(8,128)(2,1)S(1)}, bf16[2,128,2048]{2,1,0:T(8,128)(2,1)}, u32[]{:S(2)}, u32[]{:S(2)}) collective-permute-start(bf16[2,128,2048]{2,1,0:T(8,128)(2,1)S(1)} %copy-done.38), channel_id=1, source_target_pairs={{0,16},{1,17},{2,18},{3,19},{4,20},{5,21},{6,22},{7,23},{8,24},{9,... | collective-permute-start | bytes 3145736 | tf_op jit(solution)/shard_map/ppermute | solution.py:133
  471.6 27.3 %collective-permute-start.72 = (bf16[128,2048]{1,0:T(8,128)(2,1)S(1)}, bf16[128,2048]{1,0:T(8,128)(2,1)S(1)}, u32[]{:S(2)}, u32[]{:S(2)}) collective-permute-start(bf16[128,2048]{1,0:T(8,128)(2,1)S(1)} %get-tuple-element.403), channel_id=1, source_target_pairs={{0,2},{2,4},{4,6},{6,7},{7,5},{5,3},{3,1},{1,0},{8,10},{10,12},{12... | collective-permute-start | bytes 1572872 | tf_op jit(solution)/shard_map/ppermute | solution.py:147
  473.5 26.2 %collective-permute-start.73 = (bf16[128,2048]{1,0:T(8,128)(2,1)S(1)}, bf16[128,2048]{1,0:T(8,128)(2,1)S(1)}, u32[]{:S(2)}, u32[]{:S(2)}) collective-permute-start(bf16[128,2048]{1,0:T(8,128)(2,1)S(1)} %get-tuple-element.404), channel_id=1, source_target_pairs={{2,0},{4,2},{6,4},{7,6},{5,7},{3,5},{1,3},{0,1},{10,8},{12,10},{14... | collective-permute-start | bytes 1572872 | tf_op jit(solution)/shard_map/ppermute | solution.py:147
  476.7 48.1 %collective-permute-start.96 = (bf16[8,128,512]{2,1,0:T(8,128)(2,1)}, bf16[8,128,512]{2,1,0:T(8,128)(2,1)}, u32[]{:S(2)}, u32[]{:S(2)}) collective-permute-start(bf16[8,128,512]{2,1,0:T(8,128)(2,1)} %all-to-all-done.2.own), channel_id=1, source_target_pairs={{0,8},{1,9},{2,10},{3,11},{4,12},{5,13},{6,14},{7,15},{8,0},{9,1},... | collective-permute-start | bytes 3145736 | tf_op jit(solution)/shard_map/ppermute | solution.py:133
  517.7 15.1 %collective-permute-start.97 = (bf16[8,128,512]{2,1,0:T(8,128)(2,1)}, bf16[8,128,512]{2,1,0:T(8,128)(2,1)}, u32[]{:S(2)}, u32[]{:S(2)}) collective-permute-start(bf16[8,128,512]{2,1,0:T(8,128)(2,1)} %collective-permute-done.90.other), channel_id=1, source_target_pairs={{0,8},{1,9},{2,10},{3,11},{4,12},{5,13},{6,14},{7,15},{8,0},{9,1},... | collective-permute-start | bytes 3145736 | tf_op jit(solution)/shard_map/ppermute | solution.py:133
  518.2 39.0 %collective-permute-start.93 = (bf16[8,128,768]{2,1,0:T(8,128)(2,1)S(1)}, bf16[8,128,768]{2,1,0:T(8,128)(2,1)}, u32[]{:S(2)}, u32[]{:S(2)}) collective-permute-start(bf16[8,128,768]{2,1,0:T(8,128)(2,1)S(1)} %all-to-all-done.3.own), channel_id=1, source_target_pairs={{0,16},{1,17},{2,18},{3,19},{4,20},{5,21},{6,22},{7,23},{8,24},{9,... | collective-permute-start | bytes 4718600 | tf_op jit(solution)/shard_map/ppermute | solution.py:133
  522.9 17.4 %collective-permute-start.94 = (bf16[128,2048]{1,0:T(8,128)(2,1)}, bf16[128,2048]{1,0:T(8,128)(2,1)S(1)}, u32[]{:S(2)}, u32[]{:S(2)}) collective-permute-start(bf16[128,2048]{1,0:T(8,128)(2,1)} %get-tuple-element.464), channel_id=1, source_target_pairs={{0,2},{2,4},{4,6},{6,7},{7,5},{5,3},{3,1},{1,0},{8,10},{10,12},{12... | collective-permute-start | bytes 1572872 | tf_op jit(solution)/shard_map/ppermute | solution.py:147
  524.8 15.5 %collective-permute-start.95 = (bf16[128,2048]{1,0:T(8,128)(2,1)}, bf16[128,2048]{1,0:T(8,128)(2,1)}, u32[]{:S(2)}, u32[]{:S(2)}) collective-permute-start(bf16[128,2048]{1,0:T(8,128)(2,1)} %get-tuple-element.465), channel_id=1, source_target_pairs={{2,0},{4,2},{6,4},{7,6},{5,7},{3,5},{1,3},{0,1},{10,8},{12,10},{14... | collective-permute-start | bytes 1572872 | tf_op jit(solution)/shard_map/ppermute | solution.py:147
  525.9 14.4 %collective-permute-start.99 = (f32[4,2048]{1,0:T(4,128)S(1)}, f32[4,2048]{1,0:T(4,128)S(1)}, u32[]{:S(2)}, u32[]{:S(2)}) collective-permute-start(f32[4,2048]{1,0:T(4,128)S(1)} %add.118), channel_id=1, source_target_pairs={{0,4},{1,5},{2,6},{3,7},{4,0},{5,1},{6,2},{7,3},{8,12},{9,13},{10,... | collective-permute-start | bytes 98312 | tf_op jit(solution)/shard_map/ppermute | solution.py:133
  532.8 24.5 %collective-permute-start.102 = (bf16[8,128,768]{2,1,0:T(8,128)(2,1)S(1)}, bf16[8,128,768]{2,1,0:T(8,128)(2,1)S(1)}, u32[]{:S(2)}, u32[]{:S(2)}) collective-permute-start(bf16[8,128,768]{2,1,0:T(8,128)(2,1)S(1)} %all-to-all-done.3.own), channel_id=1, source_target_pairs={{0,8},{1,9},{2,10},{3,11},{4,12},{5,13},{6,14},{7,15},{8,0},{9,1},... | collective-permute-start | bytes 4718600 | tf_op jit(solution)/shard_map/ppermute | solution.py:133
  (123 other events, 1464.2 us)

commit v7 on v6

--- a/solution.py
+++ b/solution.py
@@ -896,7 +896,7 @@
     first_gain = (stack[0] - norm1_bias.astype(f32) * stack[1]) / norm1_gain.astype(f32)
     last.step()
     (output,) = kernel(last_sum, [block_bf16], *last.pieces(), resid)
-    mix_other, output, first_gain = after(mix_other, output, first_gain)
+    mix_other, first_gain = after(mix_other, first_gain)
     grad_query, grad_key, grad_value, grad_gate = flat(
         everywhere(mix_owned, mix_other), [dk, dk, dv, dv]
     )

time: 572 us -> 584 us (1.021)
  waiting for transfers between devices: 288 us -> 301 us
    ppermute x32, waiting for transfers between devices: 85.9 us -> 95.5 us  [swap(): lax.ppermute(value, BOTH, [(i, i ^ 1 << place) for i in range(count)])]
  transfers between devices with their start and end apart: 108 -> 108, of which waited for: 62 -> 62; matrix products, arithmetic and copies ran while one was open for 3% -> 3% of each run, Pallas kernels for 18% -> 17%
where the time goes in v7:
time: 584 us; the launch traced here: 580 us
  waiting for transfers between devices  301 us (52%)
  starting transfers between devices  123 us (21%)
  Pallas kernels  116 us (20%)
  local copies, waits for them, and re-layouts  20.9 us (4%)
  other arithmetic  17.9 us (3%)
    ppermute x72, waiting for transfers between devices, send(): lax.ppermute(value, 'fsdp', pairs if ahead else [(b, a) for a, b in pairs])  205 us
    ppermute x32, waiting for transfers between devices, swap(): lax.ppermute(value, BOTH, [(i, i ^ 1 << place) for i in range(count)])  95.5 us
    ppermute x72, starting transfers between devices, send(): lax.ppermute(value, 'fsdp', pairs if ahead else [(b, a) for a, b in pairs])  82.1 us
    pallas_call x28, Pallas kernels, kernel(): pl.pallas_call(body, out_shape=list(outs), grid=grid, in_specs=specs, out...  49 us
    pallas_call x2, Pallas kernels, streamed(): pl.pallas_call(run, out_shape=list(outs), in_specs=specs, out_specs=[away...  46.7 us
    ppermute x32, starting transfers between devices, swap(): lax.ppermute(value, BOTH, [(i, i ^ 1 << place) for i in range(count)])  20.8 us
    unnamed x126, local copies, waits for them, and re-layouts  18.9 us
    pallas_call x2, Pallas kernels, flat(): pl.pallas_call(body, out_shape=[shape((depth, n * size), f32) for size in...  13.2 us
  transfers between devices with their start and end apart: 108, of which 62 were waited for; matrix products, arithmetic and copies ran while one was open for 3% of the time, Pallas kernels for 17%

profile of v7, /device:TPU:0, one launch (start us, length us, event | category | flops | bytes accessed | tf_op | source)
XLA Modules:
  0.0 579.9 jit_solution(13312783240200835039)
XLA Ops:
  1.2 3.5 shard_map.272
  4.9 7.4 %all-to-all-start = ((bf16[8,128,768]{2,1,0:T(8,128)(2,1)}), bf16[8,128,768]{2,1,0:T(8,128)(2,1)}, u32[]{:S(2)}, u32[]{:S(2)}) async-start(bf16[8,128,768]{2,1,0:T(8,128)(2,1)} %shard_map.272), calls=%async_computation | async-start | bytes 3145728 | tf_op jit(solution)/shard_map/all_to_all | solution.py:377
  18.6 3.0 fusion.2.refs_17_.refs_18_
  21.6 3.1 multiply_sine_fusion
  24.7 3.1 shard_map.273
  27.8 15.0 %collective-permute-done.2 = bf16[4,256]{1,0:T(4,128)(2,1)S(1)} collective-permute-done((bf16[4,256]{1,0:T(4,128)(2,1)S(1)}, bf16[4,256]{1,0:T(4,128)(2,1)S(1)}, u32[]{:S(2)}, u32[]{:S(2)}) %collective-permute-start.2) | collective-permute-done | bytes 2080 | tf_op jit(solution)/shard_map/ppermute | solution.py:133
  42.8 8.4 %collective-permute-done.1.refs_5_ = bf16[128,2048]{1,0:T(8,128)(2,1)S(1)} collective-permute-done((bf16[128,2048]{1,0:T(8,128)(2,1)S(1)}, bf16[128,2048]{1,0:T(8,128)(2,1)S(1)}, u32[]{:S(2)}, u32[]{:S(2)}) %collective-permute-start.1) | collective-permute-done | bytes 524320 | tf_op jit(solution)/shard_map/ppermute | solution.py:147
  52.8 9.9 %collective-permute-start.3 = (bf16[128,2048]{1,0:T(8,128)(2,1)S(1)}, bf16[128,2048]{1,0:T(8,128)(2,1)}, u32[]{:S(2)}, u32[]{:S(2)}) collective-permute-start(bf16[128,2048]{1,0:T(8,128)(2,1)S(1)} %collective-permute-done.refs_2_), channel_id=1, source_target_pairs={{0,2},{2,4},{4,6},{6,7},{7,5},{5,3},{3,1},{1,0},{8,10},{10,12},{12... | collective-permute-start | bytes 1572872 | tf_op jit(solution)/shard_map/ppermute | solution.py:147
  64.8 11.8 %collective-permute-done.5 = bf16[4,512]{1,0:T(4,128)(2,1)S(1)} collective-permute-done((bf16[4,512]{1,0:T(4,128)(2,1)S(1)}, bf16[4,512]{1,0:T(4,128)(2,1)S(1)}, u32[]{:S(2)}, u32[]{:S(2)}) %collective-permute-start.5) | collective-permute-done | bytes 4128 | tf_op jit(solution)/shard_map/ppermute | solution.py:133
  79.5 11.4 %collective-permute-done.8 = bf16[4,1024]{1,0:T(4,128)(2,1)S(1)} collective-permute-done((bf16[4,1024]{1,0:T(4,128)(2,1)S(1)}, bf16[4,1024]{1,0:T(4,128)(2,1)S(1)}, u32[]{:S(2)}, u32[]{:S(2)}) %collective-permute-start.8) | collective-permute-done | bytes 8224 | tf_op jit(solution)/shard_map/ppermute | solution.py:133
  93.1 4.3 collective-permute-done.10.refs_9_
  98.2 4.5 all-to-all-start.1
  102.8 23.3 %shard_map.274 = (bf16[1024,2048]{1,0:T(8,128)(2,1)}, bf16[1024,256]{1,0:T(8,128)(2,1)S(1)}, bf16[1024,256]{1,0:T(8,128)(2,1)}, bf16[1024,512]{1,0:T(8,128)(2,1)...) custom-call(s32[2]{0:T(128)S(1)} %copy-done.33, ...), custom_call_target="tpu_custom_call" | custom-call | tf_op jit(solution)/shard_map/pallas_call | solution.py:108
  143.0 2.8 collective-permute-done.24.a
  170.5 12.0 %collective-permute-done.20.refs_1_ = bf16[128,1024]{1,0:T(8,128)(2,1)S(1)} collective-permute-done((bf16[128,1024]{1,0:T(8,128)(2,1)S(1)}, bf16[128,1024]{1,0:T(8,128)(2,1)S(1)}, u32[]{:S(2)}, u32[]{:S(2)}) %collective-permute-start.20) | collective-permute-done | bytes 262176 | tf_op jit(solution)/shard_map/ppermute | solution.py:147
  189.2 10.8 %collective-permute-done.31.refs_4_ = bf16[128,2048]{1,0:T(8,128)(2,1)S(1)} collective-permute-done((bf16[128,2048]{1,0:T(8,128)(2,1)S(1)}, bf16[128,2048]{1,0:T(8,128)(2,1)S(1)}, u32[]{:S(2)}, u32[]{:S(2)}) %collective-permute-start.31) | collective-permute-done | bytes 524320 | tf_op jit(solution)/shard_map/ppermute | solution.py:147
  202.0 9.8 %collective-permute-done.43.refs_8_.refs_2_ = bf16[128,2048]{1,0:T(8,128)(2,1)S(1)} collective-permute-done((bf16[128,2048]{1,0:T(8,128)(2,1)S(1)}, bf16[128,2048]{1,0:T(8,128)(2,1)S(1)}, u32[]{:S(2)}, u32[]{:S(2)}) %collective-permute-start.43) | collective-permute-done | bytes 524320 | tf_op jit(solution)/shard_map/ppermute | solution.py:147
  213.9 9.2 %collective-permute-done.33.refs_2_ = bf16[128,2048]{1,0:T(8,128)(2,1)S(1)} collective-permute-done((bf16[128,2048]{1,0:T(8,128)(2,1)S(1)}, bf16[128,2048]{1,0:T(8,128)(2,1)S(1)}, u32[]{:S(2)}, u32[]{:S(2)}) %collective-permute-start.33) | collective-permute-done | bytes 524320 | tf_op jit(solution)/shard_map/ppermute | solution.py:147
  226.1 8.3 %collective-permute-done.45.refs_9_.refs_3_ = bf16[128,2048]{1,0:T(8,128)(2,1)S(1)} collective-permute-done((bf16[128,2048]{1,0:T(8,128)(2,1)S(1)}, bf16[128,2048]{1,0:T(8,128)(2,1)S(1)}, u32[]{:S(2)}, u32[]{:S(2)}) %collective-permute-start.45) | collective-permute-done | bytes 524320 | tf_op jit(solution)/shard_map/ppermute | solution.py:147
  237.9 7.6 %collective-permute-done.35.refs_3_ = bf16[128,2048]{1,0:T(8,128)(2,1)S(1)} collective-permute-done((bf16[128,2048]{1,0:T(8,128)(2,1)S(1)}, bf16[128,2048]{1,0:T(8,128)(2,1)S(1)}, u32[]{:S(2)}, u32[]{:S(2)}) %collective-permute-start.35) | collective-permute-done | bytes 524320 | tf_op jit(solution)/shard_map/ppermute | solution.py:147
  245.6 3.6 collective-permute-done.36.refs_0_
  251.4 11.1 %shard_map.282 = (bf16[768,2048]{1,0:T(8,128)(2,1)}, bf16[768,512]{1,0:T(8,128)(2,1)S(1)}, bf16[2,768,512]{2,1,0:T(8,128)(2,1)S(1)}, bf16[768,2048]{1,0:T(8,128)(2,1)}) custom-call(s32[2]{0:T(128)S(1)} %copy-done.33, bf16[128,2048]{1,0:T(8,128)(2,1)S(1)} %get-tuple-element.313.refs_0_, bf16[128,2048]{1,0:T(8,128)(2,1)S(1)} %collective-permute-done.30.refs_1_, ...), custom_call_target="tpu_custom_call" | custom-call | tf_op jit(solution)/shard_map/pallas_call | solution.py:44
  262.6 3.6 shard_map.283
  268.6 4.1 collective-permute-done.49.a
  276.8 4.5 shard_map.287
  288.3 3.0 shard_map.289
  291.5 8.5 %collective-permute-done.53.a = bf16[128,2048]{1,0:T(8,128)(2,1)S(1)} collective-permute-done((bf16[128,2048]{1,0:T(8,128)(2,1)S(1)}, bf16[128,2048]{1,0:T(8,128)(2,1)S(1)}, u32[]{:S(2)}, u32[]{:S(2)}) %collective-permute-start.53) | collective-permute-done | bytes 524320 | tf_op jit(solution)/shard_map/ppermute | solution.py:147
  304.5 11.3 %collective-permute-done.57.refs_1_ = bf16[128,2048]{1,0:T(8,128)(2,1)S(1)} collective-permute-done((bf16[128,2048]{1,0:T(8,128)(2,1)S(1)}, bf16[128,2048]{1,0:T(8,128)(2,1)S(1)}, u32[]{:S(2)}, u32[]{:S(2)}) %collective-permute-start.57) | collective-permute-done | bytes 524320 | tf_op jit(solution)/shard_map/ppermute | solution.py:147
  320.0 8.5 %collective-permute-done.62 = bf16[1024,512]{1,0:T(8,128)(2,1)S(1)} collective-permute-done((bf16[1024,512]{1,0:T(8,128)(2,1)S(1)}, bf16[1024,512]{1,0:T(8,128)(2,1)S(1)}, u32[]{:S(2)}, u32[]{:S(2)}) %collective-permute-start.62) | collective-permute-done | bytes 1048608 | tf_op jit(solution)/shard_map/ppermute | solution.py:133
  335.0 9.4 %collective-permute-done.63.refs_3_ = bf16[128,2048]{1,0:T(8,128)(2,1)S(1)} collective-permute-done((bf16[128,2048]{1,0:T(8,128)(2,1)S(1)}, bf16[128,2048]{1,0:T(8,128)(2,1)S(1)}, u32[]{:S(2)}, u32[]{:S(2)}) %collective-permute-start.63) | collective-permute-done | bytes 524320 | tf_op jit(solution)/shard_map/ppermute | solution.py:147
  346.8 2.9 shard_map.284
  351.8 7.9 %collective-permute-done.65.refs_4_ = bf16[128,2048]{1,0:T(8,128)(2,1)S(1)} collective-permute-done((bf16[128,2048]{1,0:T(8,128)(2,1)S(1)}, bf16[128,2048]{1,0:T(8,128)(2,1)S(1)}, u32[]{:S(2)}, u32[]{:S(2)}) %collective-permute-start.65) | collective-permute-done | bytes 524320 | tf_op jit(solution)/shard_map/ppermute | solution.py:147
  368.1 4.4 all-to-all-start.2
  372.6 23.4 %shard_map.293 = (bf16[2,128,2048]{2,1,0:T(8,128)(2,1)}, bf16[2,128,2048]{2,1,0:T(8,128)(2,1)}, f32[2,2048]{1,0:T(2,128)}, bf16[2,1024,768]{2,1,0:T(8,128)(2,1)}...) custom-call(s32[2]{0:T(128)} %pad_add_fusion.s.refs_0_, ...), custom_call_target="tpu_custom_call" | custom-call | tf_op jit(solution)/shard_map/pallas_call | solution.py:108
  400.2 6.7 %shard_map.294 = (bf16[1024,768]{1,0:T(8,128)(2,1)S(1)}, bf16[1024,768]{1,0:T(8,128)(2,1)S(1)}, bf16[1024,768]{1,0:T(8,128)(2,1)S(1)}, bf16[1024,768]{1,0:T(8,128)(2,1)S(1)}) custom-call(bf16[1024,2048]{1,0:T(8,128)(2,1)S(1)} %copy-done.11, bf16[2,1024,768]{2,1,0:T(8,128)(2,1)S(1)} %copy-done.17), custom_call_target="tpu_custom_call" | custom-call | tf_op jit(solution)/shard_map/pallas_call | solution.py:44
  412.1 4.6 collective-permute-done.74.a
  423.2 8.1 %collective-permute-done.80.a = bf16[128,2048]{1,0:T(8,128)(2,1)S(1)} collective-permute-done((bf16[128,2048]{1,0:T(8,128)(2,1)S(1)}, bf16[128,2048]{1,0:T(8,128)(2,1)S(1)}, u32[]{:S(2)}, u32[]{:S(2)}) %collective-permute-start.80) | collective-permute-done | bytes 524320 | tf_op jit(solution)/shard_map/ppermute | solution.py:147
  435.4 9.7 %collective-permute-done.85 = f32[4,2048]{1,0:T(4,128)S(1)} collective-permute-done((f32[4,2048]{1,0:T(4,128)S(1)}, f32[4,2048]{1,0:T(4,128)S(1)}, u32[]{:S(2)}, u32[]{:S(2)}) %collective-permute-start.85) | collective-permute-done | bytes 32800 | tf_op jit(solution)/shard_map/ppermute | solution.py:133
  449.4 8.8 %collective-permute-done.89 = f32[4,2048]{1,0:T(4,128)S(1)} collective-permute-done((f32[4,2048]{1,0:T(4,128)S(1)}, f32[4,2048]{1,0:T(4,128)S(1)}, u32[]{:S(2)}, u32[]{:S(2)}) %collective-permute-start.89) | collective-permute-done | bytes 32800 | tf_op jit(solution)/shard_map/ppermute | solution.py:133
  461.5 3.6 all-to-all-start.3
  473.9 2.8 shard_map.299
  479.3 19.5 %collective-permute-done.72.a = bf16[128,2048]{1,0:T(8,128)(2,1)S(1)} collective-permute-done((bf16[128,2048]{1,0:T(8,128)(2,1)S(1)}, bf16[128,2048]{1,0:T(8,128)(2,1)S(1)}, u32[]{:S(2)}, u32[]{:S(2)}) %collective-permute-start.72) | collective-permute-done | bytes 524320 | tf_op jit(solution)/shard_map/ppermute | solution.py:147
  500.5 15.2 %collective-permute-done.91 = bf16[2,128,2048]{2,1,0:T(8,128)(2,1)} collective-permute-done((bf16[2,128,2048]{2,1,0:T(8,128)(2,1)S(1)}, bf16[2,128,2048]{2,1,0:T(8,128)(2,1)}, u32[]{:S(2)}, u32[]{:S(2)}) %collective-permute-start.91) | collective-permute-done | bytes 1048608 | tf_op jit(solution)/shard_map/ppermute | solution.py:133
  530.0 2.8 shard_map.302
  532.8 6.7 %shard_map.301 = (f32[256,4096]{1,0:T(8,128)}, f32[256,4096]{1,0:T(8,128)}) custom-call(s32[2]{0:T(128)S(1)} %copy-done.34, bf16[8,128,512]{2,1,0:T(8,128)(2,1)} %all-to-all-done.2.own, bf16[8,128,512]{2,1,0:T(8,128)(2,1)} %collective-permute-done.95.own_c, bf16[8,128,512]{2,1,0:T(8,128)(2,1)} %collective-permute-done.90.other, ...), custom_call_target="tpu_custom_call" | custom-call | tf_op jit(solution)/shard_map/pallas_call | solution.py:432
  541.5 13.2 %collective-permute-done.102.other = bf16[8,128,768]{2,1,0:T(8,128)(2,1)} collective-permute-done((bf16[8,128,768]{2,1,0:T(8,128)(2,1)S(1)}, bf16[8,128,768]{2,1,0:T(8,128)(2,1)}, u32[]{:S(2)}, u32[]{:S(2)}) %collective-permute-start.102) | collective-permute-done | bytes 1572896 | tf_op jit(solution)/shard_map/ppermute | solution.py:133
  558.1 12.5 %collective-permute-done.99.refs_1_ = bf16[128,2048]{1,0:T(8,128)(2,1)S(1)} collective-permute-done((bf16[128,2048]{1,0:T(8,128)(2,1)S(1)}, bf16[128,2048]{1,0:T(8,128)(2,1)S(1)}, u32[]{:S(2)}, u32[]{:S(2)}) %collective-permute-start.99) | collective-permute-done | bytes 524320 | tf_op jit(solution)/shard_map/ppermute | solution.py:147
  573.1 6.5 %shard_map.305 = (f32[256,2048]{1,0:T(8,128)}, f32[256,2048]{1,0:T(8,128)}, f32[256,4096]{1,0:T(8,128)}, f32[256,4096]{1,0:T(8,128)}) custom-call(s32[2]{0:T(128)S(1)} %copy-done.34, bf16[8,128,768]{2,1,0:T(8,128)(2,1)S(1)} %all-to-all-done.3.own, bf16[8,128,768]{2,1,0:T(8,128)(2,1)S(1)} %collective-permute-done.101.own_c, ...), custom_call_target="tpu_custom_call" | custom-call | tf_op jit(solution)/shard_map/pallas_call | solution.py:432
  (376 shorter events, 181.7 us)
Async XLA Ops:
  4.9 46.3 %all-to-all-start = ((bf16[8,128,768]{2,1,0:T(8,128)(2,1)}), bf16[8,128,768]{2,1,0:T(8,128)(2,1)}, u32[]{:S(2)}, u32[]{:S(2)}) async-start(bf16[8,128,768]{2,1,0:T(8,128)(2,1)} %shard_map.272), calls=%async_computation | async-start | bytes 3145728 | tf_op jit(solution)/shard_map/all_to_all | solution.py:377
  12.3 38.9 %collective-permute-start.1 = (bf16[128,2048]{1,0:T(8,128)(2,1)S(1)}, bf16[128,2048]{1,0:T(8,128)(2,1)S(1)}, u32[]{:S(2)}, u32[]{:S(2)}) collective-permute-start(bf16[128,2048]{1,0:T(8,128)(2,1)S(1)} %copy-done.13), channel_id=1, source_target_pairs={{2,0},{4,2},{6,4},{7,6},{5,7},{3,5},{1,3},{0,1},{10,8},{12,10},{14... | collective-permute-start | bytes 1572872 | tf_op jit(solution)/shard_map/ppermute | solution.py:147
  14.3 36.9 %collective-permute-start = (bf16[128,2048]{1,0:T(8,128)(2,1)S(1)}, bf16[128,2048]{1,0:T(8,128)(2,1)S(1)}, u32[]{:S(2)}, u32[]{:S(2)}) collective-permute-start(bf16[128,2048]{1,0:T(8,128)(2,1)S(1)} %copy-done.13), channel_id=1, source_target_pairs={{0,2},{2,4},{4,6},{6,7},{7,5},{5,3},{3,1},{1,0},{8,10},{10,12},{12... | collective-permute-start | bytes 1572872 | tf_op jit(solution)/shard_map/ppermute | solution.py:147
  14.5 28.3 %collective-permute-start.2 = (bf16[4,256]{1,0:T(4,128)(2,1)S(1)}, bf16[4,256]{1,0:T(4,128)(2,1)S(1)}, u32[]{:S(2)}, u32[]{:S(2)}) collective-permute-start(bf16[4,256]{1,0:T(4,128)(2,1)S(1)} %pad_maximum_fusion.4), channel_id=1, source_target_pairs={{0,1},{1,0},{2,3},{3,2},{4,5},{5,4},{6,7},{7,6},{8,9},{9,8},{10,11... | collective-permute-start | bytes 6152 | tf_op jit(solution)/shard_map/ppermute | solution.py:133
  51.2 46.9 %collective-permute-start.12 = (bf16[1024,768]{1,0:T(8,128)(2,1)}, bf16[1024,768]{1,0:T(8,128)(2,1)S(1)}, u32[]{:S(2)}, u32[]{:S(2)}) collective-permute-start(bf16[1024,768]{1,0:T(8,128)(2,1)} %bitcast.4.refs_11_.refs_21_), channel_id=1, source_target_pairs={{0,8},{1,9},{2,10},{3,11},{4,12},{5,13},{6,14},{7,15},{8,0},{9,1},... | collective-permute-start | bytes 4718600 | tf_op jit(solution)/shard_map/ppermute | solution.py:133
  51.3 46.8 %collective-permute-start.11 = (bf16[1024,768]{1,0:T(8,128)(2,1)}, bf16[1024,768]{1,0:T(8,128)(2,1)}, u32[]{:S(2)}, u32[]{:S(2)}) collective-permute-start(bf16[1024,768]{1,0:T(8,128)(2,1)} %bitcast.4.refs_11_.refs_21_), channel_id=1, source_target_pairs={{0,16},{1,17},{2,18},{3,19},{4,20},{5,21},{6,22},{7,23},{8,24},{9,... | collective-permute-start | bytes 4718600 | tf_op jit(solution)/shard_map/ppermute | solution.py:133
  52.8 23.8 %collective-permute-start.3 = (bf16[128,2048]{1,0:T(8,128)(2,1)S(1)}, bf16[128,2048]{1,0:T(8,128)(2,1)}, u32[]{:S(2)}, u32[]{:S(2)}) collective-permute-start(bf16[128,2048]{1,0:T(8,128)(2,1)S(1)} %collective-permute-done.refs_2_), channel_id=1, source_target_pairs={{0,2},{2,4},{4,6},{6,7},{7,5},{5,3},{3,1},{1,0},{8,10},{10,12},{12... | collective-permute-start | bytes 1572872 | tf_op jit(solution)/shard_map/ppermute | solution.py:147
  76.7 14.2 %collective-permute-start.6 = (bf16[128,2048]{1,0:T(8,128)(2,1)}, bf16[128,2048]{1,0:T(8,128)(2,1)S(1)}, u32[]{:S(2)}, u32[]{:S(2)}) collective-permute-start(bf16[128,2048]{1,0:T(8,128)(2,1)} %collective-permute-done.3.refs_3_), channel_id=1, source_target_pairs={{0,2},{2,4},{4,6},{6,7},{7,5},{5,3},{3,1},{1,0},{8,10},{10,12},{12... | collective-permute-start | bytes 1572872 | tf_op jit(solution)/shard_map/ppermute | solution.py:147
  98.2 40.6 %all-to-all-start.1 = ((bf16[8,128,512]{2,1,0:T(8,128)(2,1)}), bf16[8,128,512]{2,1,0:T(8,128)(2,1)S(1)}, u32[]{:S(2)}, u32[]{:S(2)}) async-start(bf16[8,128,512]{2,1,0:T(8,128)(2,1)} %shard_map.273), calls=%async_computation.1 | async-start | bytes 2097152 | tf_op jit(solution)/shard_map/all_to_all | solution.py:377
  160.9 28.3 %collective-permute-start.32 = (bf16[1024,512]{1,0:T(8,128)(2,1)S(1)}, bf16[1024,512]{1,0:T(8,128)(2,1)S(1)}, u32[]{:S(2)}, u32[]{:S(2)}) collective-permute-start(bf16[1024,512]{1,0:T(8,128)(2,1)S(1)} %bitcast.13), channel_id=1, source_target_pairs={{0,16},{1,17},{2,18},{3,19},{4,20},{5,21},{6,22},{7,23},{8,24},{9,... | collective-permute-start | bytes 3145736 | tf_op jit(solution)/shard_map/ppermute | solution.py:133
  162.7 24.5 %collective-permute-start.42 = (bf16[128,2048]{1,0:T(8,128)(2,1)S(1)}, bf16[128,2048]{1,0:T(8,128)(2,1)S(1)}, u32[]{:S(2)}, u32[]{:S(2)}) collective-permute-start(bf16[128,2048]{1,0:T(8,128)(2,1)S(1)} %copy-done.12), channel_id=1, source_target_pairs={{2,0},{4,2},{6,4},{7,6},{5,7},{3,5},{1,3},{0,1},{10,8},{12,10},{14... | collective-permute-start | bytes 1572872 | tf_op jit(solution)/shard_map/ppermute | solution.py:147
  164.3 22.9 %collective-permute-start.41 = (bf16[128,2048]{1,0:T(8,128)(2,1)S(1)}, bf16[128,2048]{1,0:T(8,128)(2,1)S(1)}, u32[]{:S(2)}, u32[]{:S(2)}) collective-permute-start(bf16[128,2048]{1,0:T(8,128)(2,1)S(1)} %copy-done.12), channel_id=1, source_target_pairs={{0,2},{2,4},{4,6},{6,7},{7,5},{5,3},{3,1},{1,0},{8,10},{10,12},{12... | collective-permute-start | bytes 1572872 | tf_op jit(solution)/shard_map/ppermute | solution.py:147
  168.3 14.2 %collective-permute-start.20 = (bf16[128,1024]{1,0:T(8,128)(2,1)S(1)}, bf16[128,1024]{1,0:T(8,128)(2,1)S(1)}, u32[]{:S(2)}, u32[]{:S(2)}) collective-permute-start(bf16[128,1024]{1,0:T(8,128)(2,1)S(1)} %get-tuple-element.295), channel_id=1, source_target_pairs={{0,2},{2,4},{4,6},{6,7},{7,5},{5,3},{3,1},{1,0},{8,10},{10,12},{12... | collective-permute-start | bytes 786440 | tf_op jit(solution)/shard_map/ppermute | solution.py:147
  185.1 14.9 %collective-permute-start.31 = (bf16[128,2048]{1,0:T(8,128)(2,1)S(1)}, bf16[128,2048]{1,0:T(8,128)(2,1)S(1)}, u32[]{:S(2)}, u32[]{:S(2)}) collective-permute-start(bf16[128,2048]{1,0:T(8,128)(2,1)S(1)} %get-tuple-element.313.refs_0_), channel_id=1, source_target_pairs={{2,0},{4,2},{6,4},{7,6},{5,7},{3,5},{1,3},{0,1},{10,8},{12,10},{14... | collective-permute-start | bytes 1572872 | tf_op jit(solution)/shard_map/ppermute | solution.py:147
  185.8 14.9 %collective-permute-start.30 = (bf16[128,2048]{1,0:T(8,128)(2,1)S(1)}, bf16[128,2048]{1,0:T(8,128)(2,1)S(1)}, u32[]{:S(2)}, u32[]{:S(2)}) collective-permute-start(bf16[128,2048]{1,0:T(8,128)(2,1)S(1)} %get-tuple-element.313.refs_0_), channel_id=1, source_target_pairs={{0,2},{2,4},{4,6},{6,7},{7,5},{5,3},{3,1},{1,0},{8,10},{10,12},{12... | collective-permute-start | bytes 1572872 | tf_op jit(solution)/shard_map/ppermute | solution.py:147
  187.2 24.7 %collective-permute-start.43 = (bf16[128,2048]{1,0:T(8,128)(2,1)S(1)}, bf16[128,2048]{1,0:T(8,128)(2,1)S(1)}, u32[]{:S(2)}, u32[]{:S(2)}) collective-permute-start(bf16[128,2048]{1,0:T(8,128)(2,1)S(1)} %collective-permute-done.41.refs_7_.refs_1_), channel_id=1, source_target_pairs={{0,2},{2,4},{4,6},{6,7},{7,5},{5,3},{3,1},{1,0},{8,10},{10,12},{12... | collective-permute-start | bytes 1572872 | tf_op jit(solution)/shard_map/ppermute | solution.py:147
  188.7 23.2 %collective-permute-start.44 = (bf16[128,2048]{1,0:T(8,128)(2,1)S(1)}, bf16[128,2048]{1,0:T(8,128)(2,1)S(1)}, u32[]{:S(2)}, u32[]{:S(2)}) collective-permute-start(bf16[128,2048]{1,0:T(8,128)(2,1)S(1)} %collective-permute-done.42.refs_10_.refs_4_), channel_id=1, source_target_pairs={{2,0},{4,2},{6,4},{7,6},{5,7},{3,5},{1,3},{0,1},{10,8},{12,10},{14... | collective-permute-start | bytes 1572872 | tf_op jit(solution)/shard_map/ppermute | solution.py:147
  200.6 22.5 %collective-permute-start.33 = (bf16[128,2048]{1,0:T(8,128)(2,1)S(1)}, bf16[128,2048]{1,0:T(8,128)(2,1)S(1)}, u32[]{:S(2)}, u32[]{:S(2)}) collective-permute-start(bf16[128,2048]{1,0:T(8,128)(2,1)S(1)} %collective-permute-done.30.refs_1_), channel_id=1, source_target_pairs={{0,2},{2,4},{4,6},{6,7},{7,5},{5,3},{3,1},{1,0},{8,10},{10,12},{12... | collective-permute-start | bytes 1572872 | tf_op jit(solution)/shard_map/ppermute | solution.py:147
  202.0 34.4 %collective-permute-start.37 = (bf16[1024,512]{1,0:T(8,128)(2,1)S(1)}, bf16[1024,512]{1,0:T(8,128)(2,1)S(1)}, u32[]{:S(2)}, u32[]{:S(2)}) collective-permute-start(bf16[1024,512]{1,0:T(8,128)(2,1)S(1)} %bitcast.14), channel_id=1, source_target_pairs={{0,8},{1,9},{2,10},{3,11},{4,12},{5,13},{6,14},{7,15},{8,0},{9,1},... | collective-permute-start | bytes 3145736 | tf_op jit(solution)/shard_map/ppermute | solution.py:133
  212.1 22.2 %collective-permute-start.45 = (bf16[128,2048]{1,0:T(8,128)(2,1)S(1)}, bf16[128,2048]{1,0:T(8,128)(2,1)S(1)}, u32[]{:S(2)}, u32[]{:S(2)}) collective-permute-start(bf16[128,2048]{1,0:T(8,128)(2,1)S(1)} %collective-permute-done.43.refs_8_.refs_2_), channel_id=1, source_target_pairs={{0,2},{2,4},{4,6},{6,7},{7,5},{5,3},{3,1},{1,0},{8,10},{10,12},{12... | collective-permute-start | bytes 1572872 | tf_op jit(solution)/shard_map/ppermute | solution.py:147
  213.9 24.1 %collective-permute-start.38 = (bf16[1024,512]{1,0:T(8,128)(2,1)S(1)}, bf16[1024,512]{1,0:T(8,128)(2,1)S(1)}, u32[]{:S(2)}, u32[]{:S(2)}) collective-permute-start(bf16[1024,512]{1,0:T(8,128)(2,1)S(1)} %collective-permute-done.32.refs_14_.refs_8_), channel_id=1, source_target_pairs={{0,8},{1,9},{2,10},{3,11},{4,12},{5,13},{6,14},{7,15},{8,0},{9,1},... | collective-permute-start | bytes 3145736 | tf_op jit(solution)/shard_map/ppermute | solution.py:133
  224.6 21.0 %collective-permute-start.35 = (bf16[128,2048]{1,0:T(8,128)(2,1)S(1)}, bf16[128,2048]{1,0:T(8,128)(2,1)S(1)}, u32[]{:S(2)}, u32[]{:S(2)}) collective-permute-start(bf16[128,2048]{1,0:T(8,128)(2,1)S(1)} %collective-permute-done.33.refs_2_), channel_id=1, source_target_pairs={{0,2},{2,4},{4,6},{6,7},{7,5},{5,3},{3,1},{1,0},{8,10},{10,12},{12... | collective-permute-start | bytes 1572872 | tf_op jit(solution)/shard_map/ppermute | solution.py:147
  234.3 14.8 %collective-permute-start.36 = (bf16[128,2048]{1,0:T(8,128)(2,1)S(1)}, bf16[128,2048]{1,0:T(8,128)(2,1)S(1)}, u32[]{:S(2)}, u32[]{:S(2)}) collective-permute-start(bf16[128,2048]{1,0:T(8,128)(2,1)S(1)} %collective-permute-done.34.refs_5_), channel_id=1, source_target_pairs={{2,0},{4,2},{6,4},{7,6},{5,7},{3,5},{1,3},{0,1},{10,8},{12,10},{14... | collective-permute-start | bytes 1572872 | tf_op jit(solution)/shard_map/ppermute | solution.py:147
  235.9 26.7 %collective-permute-start.48 = (bf16[64,2048]{1,0:T(8,128)(2,1)S(1)}, bf16[64,2048]{1,0:T(8,128)(2,1)S(1)}, u32[]{:S(2)}, u32[]{:S(2)}) collective-permute-start(bf16[64,2048]{1,0:T(8,128)(2,1)S(1)} %slice.58), channel_id=1, source_target_pairs={{2,0},{4,2},{6,4},{7,6},{5,7},{3,5},{1,3},{0,1},{10,8},{12,10},{14... | collective-permute-start | bytes 786440 | tf_op jit(solution)/shard_map/ppermute | solution.py:147
  236.4 26.2 %collective-permute-start.47 = (bf16[64,2048]{1,0:T(8,128)(2,1)S(1)}, bf16[64,2048]{1,0:T(8,128)(2,1)S(1)}, u32[]{:S(2)}, u32[]{:S(2)}) collective-permute-start(bf16[64,2048]{1,0:T(8,128)(2,1)S(1)} %slice.57), channel_id=1, source_target_pairs={{0,2},{2,4},{4,6},{6,7},{7,5},{5,3},{3,1},{1,0},{8,10},{10,12},{12... | collective-permute-start | bytes 786440 | tf_op jit(solution)/shard_map/ppermute | solution.py:147
  285.4 15.7 %collective-permute-start.55 = (bf16[1024,512]{1,0:T(8,128)(2,1)S(1)}, bf16[1024,512]{1,0:T(8,128)(2,1)S(1)}, u32[]{:S(2)}, u32[]{:S(2)}) collective-permute-start(bf16[1024,512]{1,0:T(8,128)(2,1)S(1)} %get-tuple-element.369), channel_id=1, source_target_pairs={{0,8},{1,9},{2,10},{3,11},{4,12},{5,13},{6,14},{7,15},{8,0},{9,1},... | collective-permute-start | bytes 3145736 | tf_op jit(solution)/shard_map/ppermute | solution.py:133
  301.4 14.4 %collective-permute-start.57 = (bf16[128,2048]{1,0:T(8,128)(2,1)S(1)}, bf16[128,2048]{1,0:T(8,128)(2,1)S(1)}, u32[]{:S(2)}, u32[]{:S(2)}) collective-permute-start(bf16[128,2048]{1,0:T(8,128)(2,1)S(1)} %get-tuple-element.377), channel_id=1, source_target_pairs={{0,2},{2,4},{4,6},{6,7},{7,5},{5,3},{3,1},{1,0},{8,10},{10,12},{12... | collective-permute-start | bytes 1572872 | tf_op jit(solution)/shard_map/ppermute | solution.py:147
  303.5 25.0 %collective-permute-start.62 = (bf16[1024,512]{1,0:T(8,128)(2,1)S(1)}, bf16[1024,512]{1,0:T(8,128)(2,1)S(1)}, u32[]{:S(2)}, u32[]{:S(2)}) collective-permute-start(bf16[1024,512]{1,0:T(8,128)(2,1)S(1)} %add_convert_fusion.7), channel_id=1, source_target_pairs={{0,16},{1,17},{2,18},{3,19},{4,20},{5,21},{6,22},{7,23},{8,24},{9,... | collective-permute-start | bytes 3145736 | tf_op jit(solution)/shard_map/ppermute | solution.py:133
  334.4 30.1 %collective-permute-start.71 = (bf16[2,128,2048]{2,1,0:T(8,128)(2,1)S(1)}, bf16[2,128,2048]{2,1,0:T(8,128)(2,1)S(1)}, u32[]{:S(2)}, u32[]{:S(2)}) collective-permute-start(bf16[2,128,2048]{2,1,0:T(8,128)(2,1)S(1)} %add_convert_fusion.6), channel_id=1, source_target_pairs={{0,16},{1,17},{2,18},{3,19},{4,20},{5,21},{6,22},{7,23},{8,24},{9,... | collective-permute-start | bytes 3145736 | tf_op jit(solution)/shard_map/ppermute | solution.py:133
  344.7 14.9 %collective-permute-start.65 = (bf16[128,2048]{1,0:T(8,128)(2,1)S(1)}, bf16[128,2048]{1,0:T(8,128)(2,1)S(1)}, u32[]{:S(2)}, u32[]{:S(2)}) collective-permute-start(bf16[128,2048]{1,0:T(8,128)(2,1)S(1)} %collective-permute-done.63.refs_3_), channel_id=1, source_target_pairs={{0,2},{2,4},{4,6},{6,7},{7,5},{5,3},{3,1},{1,0},{8,10},{10,12},{12... | collective-permute-start | bytes 1572872 | tf_op jit(solution)/shard_map/ppermute | solution.py:147
  345.4 14.9 %collective-permute-start.66 = (bf16[128,2048]{1,0:T(8,128)(2,1)S(1)}, bf16[128,2048]{1,0:T(8,128)(2,1)S(1)}, u32[]{:S(2)}, u32[]{:S(2)}) collective-permute-start(bf16[128,2048]{1,0:T(8,128)(2,1)S(1)} %collective-permute-done.64.refs_6_), channel_id=1, source_target_pairs={{2,0},{4,2},{6,4},{7,6},{5,7},{3,5},{1,3},{0,1},{10,8},{12,10},{14... | collective-permute-start | bytes 1572872 | tf_op jit(solution)/shard_map/ppermute | solution.py:147
  349.7 14.4 %collective-permute-start.69 = (bf16[64,2048]{1,0:T(8,128)(2,1)S(1)}, bf16[64,2048]{1,0:T(8,128)(2,1)S(1)}, u32[]{:S(2)}, u32[]{:S(2)}) collective-permute-start(bf16[64,2048]{1,0:T(8,128)(2,1)S(1)} %get-tuple-element.394), channel_id=1, source_target_pairs={{0,2},{2,4},{4,6},{6,7},{7,5},{5,3},{3,1},{1,0},{8,10},{10,12},{12... | collective-permute-start | bytes 786440 | tf_op jit(solution)/shard_map/ppermute | solution.py:147
  368.1 27.9 %all-to-all-start.2 = ((bf16[8,128,512]{2,1,0:T(8,128)(2,1)}), bf16[8,128,512]{2,1,0:T(8,128)(2,1)}, u32[]{:S(2)}, u32[]{:S(2)}) async-start(bf16[8,128,512]{2,1,0:T(8,128)(2,1)} %bitcast.18), calls=%async_computation.2 | async-start | bytes 2097152 | tf_op jit(solution)/shard_map/all_to_all | solution.py:410
  420.4 39.4 %collective-permute-start.88 = (bf16[1024,768]{1,0:T(8,128)(2,1)S(1)}, bf16[1024,768]{1,0:T(8,128)(2,1)S(1)}, u32[]{:S(2)}, u32[]{:S(2)}) collective-permute-start(bf16[1024,768]{1,0:T(8,128)(2,1)S(1)} %add_convert_fusion.1), channel_id=1, source_target_pairs={{0,16},{1,17},{2,18},{3,19},{4,20},{5,21},{6,22},{7,23},{8,24},{9,... | collective-permute-start | bytes 4718600 | tf_op jit(solution)/shard_map/ppermute | solution.py:133
  461.5 54.1 %all-to-all-start.3 = ((bf16[8,128,768]{2,1,0:T(8,128)(2,1)}), bf16[8,128,768]{2,1,0:T(8,128)(2,1)S(1)}, u32[]{:S(2)}, u32[]{:S(2)}) async-start(bf16[8,128,768]{2,1,0:T(8,128)(2,1)} %bitcast.17), calls=%async_computation.3 | async-start | bytes 3145728 | tf_op jit(solution)/shard_map/all_to_all | solution.py:410
  467.3 33.2 %collective-permute-start.90 = (bf16[8,128,512]{2,1,0:T(8,128)(2,1)}, bf16[8,128,512]{2,1,0:T(8,128)(2,1)}, u32[]{:S(2)}, u32[]{:S(2)}) collective-permute-start(bf16[8,128,512]{2,1,0:T(8,128)(2,1)} %all-to-all-done.2.own), channel_id=1, source_target_pairs={{0,16},{1,17},{2,18},{3,19},{4,20},{5,21},{6,22},{7,23},{8,24},{9,... | collective-permute-start | bytes 3145736 | tf_op jit(solution)/shard_map/ppermute | solution.py:133
  468.8 46.8 %collective-permute-start.91 = (bf16[2,128,2048]{2,1,0:T(8,128)(2,1)S(1)}, bf16[2,128,2048]{2,1,0:T(8,128)(2,1)}, u32[]{:S(2)}, u32[]{:S(2)}) collective-permute-start(bf16[2,128,2048]{2,1,0:T(8,128)(2,1)S(1)} %copy-done.38), channel_id=1, source_target_pairs={{0,16},{1,17},{2,18},{3,19},{4,20},{5,21},{6,22},{7,23},{8,24},{9,... | collective-permute-start | bytes 3145736 | tf_op jit(solution)/shard_map/ppermute | solution.py:133
  471.6 27.3 %collective-permute-start.72 = (bf16[128,2048]{1,0:T(8,128)(2,1)S(1)}, bf16[128,2048]{1,0:T(8,128)(2,1)S(1)}, u32[]{:S(2)}, u32[]{:S(2)}) collective-permute-start(bf16[128,2048]{1,0:T(8,128)(2,1)S(1)} %get-tuple-element.402), channel_id=1, source_target_pairs={{0,2},{2,4},{4,6},{6,7},{7,5},{5,3},{3,1},{1,0},{8,10},{10,12},{12... | collective-permute-start | bytes 1572872 | tf_op jit(solution)/shard_map/ppermute | solution.py:147
  473.5 26.2 %collective-permute-start.73 = (bf16[128,2048]{1,0:T(8,128)(2,1)S(1)}, bf16[128,2048]{1,0:T(8,128)(2,1)S(1)}, u32[]{:S(2)}, u32[]{:S(2)}) collective-permute-start(bf16[128,2048]{1,0:T(8,128)(2,1)S(1)} %get-tuple-element.403), channel_id=1, source_target_pairs={{2,0},{4,2},{6,4},{7,6},{5,7},{3,5},{1,3},{0,1},{10,8},{12,10},{14... | collective-permute-start | bytes 1572872 | tf_op jit(solution)/shard_map/ppermute | solution.py:147
  476.7 48.1 %collective-permute-start.95 = (bf16[8,128,512]{2,1,0:T(8,128)(2,1)}, bf16[8,128,512]{2,1,0:T(8,128)(2,1)}, u32[]{:S(2)}, u32[]{:S(2)}) collective-permute-start(bf16[8,128,512]{2,1,0:T(8,128)(2,1)} %all-to-all-done.2.own), channel_id=1, source_target_pairs={{0,8},{1,9},{2,10},{3,11},{4,12},{5,13},{6,14},{7,15},{8,0},{9,1},... | collective-permute-start | bytes 3145736 | tf_op jit(solution)/shard_map/ppermute | solution.py:133
  517.7 15.1 %collective-permute-start.96 = (bf16[8,128,512]{2,1,0:T(8,128)(2,1)}, bf16[8,128,512]{2,1,0:T(8,128)(2,1)}, u32[]{:S(2)}, u32[]{:S(2)}) collective-permute-start(bf16[8,128,512]{2,1,0:T(8,128)(2,1)} %collective-permute-done.90.other), channel_id=1, source_target_pairs={{0,8},{1,9},{2,10},{3,11},{4,12},{5,13},{6,14},{7,15},{8,0},{9,1},... | collective-permute-start | bytes 3145736 | tf_op jit(solution)/shard_map/ppermute | solution.py:133
  518.2 36.5 %collective-permute-start.102 = (bf16[8,128,768]{2,1,0:T(8,128)(2,1)S(1)}, bf16[8,128,768]{2,1,0:T(8,128)(2,1)}, u32[]{:S(2)}, u32[]{:S(2)}) collective-permute-start(bf16[8,128,768]{2,1,0:T(8,128)(2,1)S(1)} %all-to-all-done.3.own), channel_id=1, source_target_pairs={{0,16},{1,17},{2,18},{3,19},{4,20},{5,21},{6,22},{7,23},{8,24},{9,... | collective-permute-start | bytes 4718600 | tf_op jit(solution)/shard_map/ppermute | solution.py:133
  522.9 17.4 %collective-permute-start.93 = (bf16[128,2048]{1,0:T(8,128)(2,1)}, bf16[128,2048]{1,0:T(8,128)(2,1)S(1)}, u32[]{:S(2)}, u32[]{:S(2)}) collective-permute-start(bf16[128,2048]{1,0:T(8,128)(2,1)} %get-tuple-element.462), channel_id=1, source_target_pairs={{0,2},{2,4},{4,6},{6,7},{7,5},{5,3},{3,1},{1,0},{8,10},{10,12},{12... | collective-permute-start | bytes 1572872 | tf_op jit(solution)/shard_map/ppermute | solution.py:147
  524.8 15.5 %collective-permute-start.94 = (bf16[128,2048]{1,0:T(8,128)(2,1)}, bf16[128,2048]{1,0:T(8,128)(2,1)}, u32[]{:S(2)}, u32[]{:S(2)}) collective-permute-start(bf16[128,2048]{1,0:T(8,128)(2,1)} %get-tuple-element.463), channel_id=1, source_target_pairs={{2,0},{4,2},{6,4},{7,6},{5,7},{3,5},{1,3},{0,1},{10,8},{12,10},{14... | collective-permute-start | bytes 1572872 | tf_op jit(solution)/shard_map/ppermute | solution.py:147
  525.9 14.4 %collective-permute-start.98 = (f32[4,2048]{1,0:T(4,128)S(1)}, f32[4,2048]{1,0:T(4,128)S(1)}, u32[]{:S(2)}, u32[]{:S(2)}) collective-permute-start(f32[4,2048]{1,0:T(4,128)S(1)} %add.118), channel_id=1, source_target_pairs={{0,4},{1,5},{2,6},{3,7},{4,0},{5,1},{6,2},{7,3},{8,12},{9,13},{10,... | collective-permute-start | bytes 98312 | tf_op jit(solution)/shard_map/ppermute | solution.py:133
  532.8 40.3 %collective-permute-start.101 = (bf16[8,128,768]{2,1,0:T(8,128)(2,1)S(1)}, bf16[8,128,768]{2,1,0:T(8,128)(2,1)S(1)}, u32[]{:S(2)}, u32[]{:S(2)}) collective-permute-start(bf16[8,128,768]{2,1,0:T(8,128)(2,1)S(1)} %all-to-all-done.3.own), channel_id=1, source_target_pairs={{0,8},{1,9},{2,10},{3,11},{4,12},{5,13},{6,14},{7,15},{8,0},{9,1},... | collective-permute-start | bytes 4718600 | tf_op jit(solution)/shard_map/ppermute | solution.py:133
  554.7 18.4 %collective-permute-start.103 = (bf16[8,128,768]{2,1,0:T(8,128)(2,1)}, bf16[8,128,768]{2,1,0:T(8,128)(2,1)S(1)}, u32[]{:S(2)}, u32[]{:S(2)}) collective-permute-start(bf16[8,128,768]{2,1,0:T(8,128)(2,1)} %collective-permute-done.102.other), channel_id=1, source_target_pairs={{0,8},{1,9},{2,10},{3,11},{4,12},{5,13},{6,14},{7,15},{8,0},{9,1},... | collective-permute-start | bytes 4718600 | tf_op jit(solution)/shard_map/ppermute | solution.py:133
  556.0 14.6 %collective-permute-start.99 = (bf16[128,2048]{1,0:T(8,128)(2,1)S(1)}, bf16[128,2048]{1,0:T(8,128)(2,1)S(1)}, u32[]{:S(2)}, u32[]{:S(2)}) collective-permute-start(bf16[128,2048]{1,0:T(8,128)(2,1)S(1)} %get-tuple-element.471), channel_id=1, source_target_pairs={{0,2},{2,4},{4,6},{6,7},{7,5},{5,3},{3,1},{1,0},{8,10},{10,12},{12... | collective-permute-start | bytes 1572872 | tf_op jit(solution)/shard_map/ppermute | solution.py:147
  (123 other events, 1507.4 us)
